TPU v7x, 32 devices: a whole 2x2x4 slice. The times are simulated.
32 devices in a mesh: seq: 16 (over z, y, x), head: 2 (over core).
Axes of the slice: x: 2, y: 2, z: 4, core: 2. Of those that a mesh axis runs over, the one named last changes fastest.
Arguments:
- hidden_in: float32 [4096, 2048], P('seq'), may hold values from -6 to 6
- grad_out: float32 [4096, 2048], P('seq'), may hold values from -6 to 6
- doc_starts: int32 [8], replicated, may hold values from 0 to 4095, as said below
- norm_mixer: float32 [2048], P('seq'), may hold values from 0.5 to 1.5
- norm_ffn: float32 [2048], P('seq'), may hold values from 0.5 to 1.5
- mamba_z: float32 [2048, 3072], P('seq', 'head'), may hold values from -0.125 to 0.125
- mamba_x: float32 [2048, 3072], P('seq', 'head'), may hold values from -0.125 to 0.125
- mamba_bc: float32 [2048, 512], P('seq'), may hold values from -0.015625 to 0.015625
- mamba_dt: float32 [2048, 48], P('seq', 'head'), may hold values from -0.125 to 0.125
- conv_x: float32 [4, 3072], P(None, 'head'), may hold values from -0.5 to 0.5
- conv_bc: float32 [4, 512], replicated, may hold values from -0.5 to 0.5
- a_log: float32 [48], P('head'), may hold values from -16 to -3
- dt_bias: float32 [48], P('head'), may hold values from -1 to 1
- skip_gain: float32 [48], P('head'), may hold values from 0.5 to 1.5
- mamba_out: float32 [3072, 2048], P('head', 'seq'), may hold values from -0.109375 to 0.109375
- attn_query: float32 [2048, 1024], P('seq', 'head'), may hold values from -0.125 to 0.125
- attn_key: float32 [2048, 256], P('seq', 'head'), may hold values from -0.125 to 0.125
- attn_value: float32 [2048, 256], P('seq', 'head'), may hold values from -0.125 to 0.125
- attn_out: float32 [1024, 2048], P('head', 'seq'), may hold values from -0.75 to 0.75
- ffn_gate: float32 [2048, 4096], P('seq', 'head'), may hold values from -0.125 to 0.125
- ffn_up: float32 [2048, 4096], P('seq', 'head'), may hold values from -0.125 to 0.125
- ffn_down: float32 [4096, 2048], P('head', 'seq'), may hold values from -0.09375 to 0.09375
Outputs:
- block_out: float32 [4096, 2048], P('seq')
- grad_in: float32 [4096, 2048], P('seq')
- grad_norm_mixer: float32 [2048], P('seq')
- grad_norm_ffn: float32 [2048], P('seq')
- grad_mamba_z: float32 [2048, 3072], P('seq', 'head')
- grad_mamba_x: float32 [2048, 3072], P('seq', 'head')
- grad_mamba_bc: float32 [2048, 512], P('seq')
- grad_mamba_dt: float32 [2048, 48], P('seq', 'head')
- grad_conv_x: float32 [4, 3072], P(None, 'head')
- grad_conv_bc: float32 [4, 512], replicated
- grad_a_log: float32 [48], P('head')
- grad_dt_bias: float32 [48], P('head')
- grad_skip_gain: float32 [48], P('head')
- grad_mamba_out: float32 [3072, 2048], P('head', 'seq')
- grad_attn_query: float32 [2048, 1024], P('seq', 'head')
- grad_attn_key: float32 [2048, 256], P('seq', 'head')
- grad_attn_value: float32 [2048, 256], P('seq', 'head')
- grad_attn_out: float32 [1024, 2048], P('head', 'seq')
- grad_ffn_gate: float32 [2048, 4096], P('seq', 'head')
- grad_ffn_up: float32 [2048, 4096], P('seq', 'head')
- grad_ffn_down: float32 [4096, 2048], P('head', 'seq')
Inputs may be any that keep to these rules, and one draw needn't show every extreme that they name: `doc_starts`: strictly increasing, the first 0 and the last 4095; 3 of the others lie below 256 and the remaining 3 above 3840.
All inputs are finite; a program needn't handle non-finite values.
Results may differ from a plain program's by a relative error of at most 0.019.
The roundings to bfloat16 on the way count: a program that leaves them out, or rounds other values in their place, can miss the bound.
Values may be sent and summed in bfloat16 or wider, within the bound.
A program may use at most 512 MiB of HBM per device.

v0:
```python
import math

import jax
import jax.numpy as jnp
from jax import lax
from jax.sharding import PartitionSpec as P

MHDIM = 64
NSTATE = 256
HDIM = 128
SPAN = 128


eps_norm = 1e-05
rope_base = 100000000000.0
neg_large = -1e30
top_prec = lax.Precision.HIGHEST


def passed_along(block, axis, distance):
    devices = range(lax.axis_size(axis))
    route = [(i - distance, i) for i in devices if i - distance in devices]
    return lax.ppermute(block, axis, route)


def carried_in(value, axis, join, neutral, backward):
    count, mine = (lax.axis_size(axis), lax.axis_index(axis))
    pieces = jax.tree.map(lambda part: lax.all_gather(part, axis), value)
    if backward:
        pieces = jax.tree.map(lambda part: part[::-1], pieces)
        mine = count - 1 - mine
    running = jax.tree.map(
        lambda part, zero: jnp.full_like(part, 0) + jnp.asarray(zero, part.dtype), value, neutral
    )

    def turn(position, running):
        longer = join(running, jax.tree.map(lambda part: part[position], pieces))
        return jax.tree.map(lambda new, old: jnp.where(position < mine, new, old), longer, running)

    return lax.fori_loop(0, count - 1, turn, running)


def passed_along_2(block, axis, distance):
    devices = range(lax.axis_size(axis))
    route = [((i - distance) % len(devices), i) for i in devices]
    return lax.ppermute(block, axis, route)


def doc_ids(positions, doc_starts):
    return jnp.sum((doc_starts[None, :] <= positions[:, None]).astype(jnp.int32), axis=1) - 1


def rope_tables(positions, head_dim):
    half_dim = head_dim // 2
    freqs = rope_base ** (-2.0 * jnp.arange(half_dim, dtype=jnp.float32) / head_dim)
    angles = positions.astype(jnp.float32)[:, None] * freqs[None, :]
    return (jnp.cos(angles)[:, None, :], jnp.sin(angles)[:, None, :])


def rotate(values, positions):
    half_dim = values.shape[-1] // 2
    cosine, sine = rope_tables(positions, values.shape[-1])
    first_half, second_half = (values[..., :half_dim], values[..., half_dim:])
    return jnp.concatenate(
        [first_half * cosine - second_half * sine, second_half * cosine + first_half * sine],
        axis=-1,
    )


def rotate_back(grads_in, positions):
    half_dim = grads_in.shape[-1] // 2
    cosine, sine = rope_tables(positions, grads_in.shape[-1])
    first_half, second_half = (grads_in[..., :half_dim], grads_in[..., half_dim:])
    return jnp.concatenate(
        [first_half * cosine + second_half * sine, second_half * cosine - first_half * sine],
        axis=-1,
    )


def convolve(extended, weights, ext_docs, tok_count):
    edge_rows = weights.shape[0] - 1
    summed = jnp.zeros((tok_count, extended.shape[1]), jnp.float32)
    for tap_index in range(weights.shape[0]):
        begin_row = edge_rows - tap_index
        same_doc = (ext_docs[begin_row : begin_row + tok_count] == ext_docs[edge_rows:])[:, None]
        summed = (
            summed
            + jnp.where(
                same_doc, extended[begin_row : begin_row + tok_count].astype(jnp.float32), 0.0
            )
            * weights[tap_index][None, :]
        )
    return summed


def convolve_back(d_conv, extended, weights, ext_docs, tok_count):
    edge_rows = weights.shape[0] - 1
    d_extended = jnp.zeros((tok_count + edge_rows, d_conv.shape[1]), jnp.float32)
    tap_grads = []
    for tap_index in range(weights.shape[0]):
        begin_row = edge_rows - tap_index
        same_doc = (ext_docs[begin_row : begin_row + tok_count] == ext_docs[edge_rows:])[:, None]
        masked_grad = jnp.where(same_doc, d_conv, 0.0)
        tap_grads.append(
            jnp.sum(
                masked_grad * extended[begin_row : begin_row + tok_count].astype(jnp.float32),
                axis=0,
            )
        )
        d_extended = d_extended + jnp.pad(
            masked_grad * weights[tap_index][None, :], ((begin_row, edge_rows - begin_row), (0, 0))
        )
    return (d_extended, jnp.stack(tap_grads))


def span_ssd(
    start_state, inputs_x, inputs_b, inputs_c, step_sizes, log_decay, span_docs, before_doc
):
    length = inputs_x.shape[0]
    cumulative = jnp.cumsum(log_decay, axis=0)
    order = jnp.arange(length)
    linked = (span_docs[:, None] == span_docs[None, :]) & (order[:, None] >= order[None, :])
    gaps = jnp.where(linked[:, :, None], cumulative[:, None, :] - cumulative[None, :, :], neg_large)
    inner = jnp.dot(inputs_c, inputs_b.T, precision=top_prec)
    pair_weights = jnp.exp(gaps) * inner[:, :, None] * step_sizes[None, :, :]
    y_inner = jnp.einsum("tsh,shp->thp", pair_weights, inputs_x, precision=top_prec)
    carried = span_docs == before_doc
    entry_decay = jnp.where(carried[:, None], jnp.exp(cumulative), 0.0)
    y_state = (
        jnp.einsum("tn,hpn->thp", inputs_c, start_state, precision=top_prec)
        * entry_decay[:, :, None]
    )
    tail = (
        jnp.where(
            (span_docs == span_docs[-1])[:, None],
            jnp.exp(cumulative[-1][None, :] - cumulative),
            0.0,
        )
        * step_sizes
    )
    new_state = (
        jnp.einsum("sh,shp,sn->hpn", tail, inputs_x, inputs_b, precision=top_prec)
        + entry_decay[-1][:, None, None] * start_state
    )
    return (y_inner + y_state, new_state)


def product(left, right):
    return jnp.dot(left, right, preferred_element_type=jnp.float32)


def product_t(left, right):
    return lax.dot_general(
        left, right, (((0,), (0,)), ((), ())), preferred_element_type=jnp.float32
    )


def product_nt(left, right):
    return lax.dot_general(
        left, right, (((1,), (1,)), ((), ())), preferred_element_type=jnp.float32
    )


def norm_rows(rows, gain):
    row_scale = lax.rsqrt(jnp.mean(rows * rows, axis=1, keepdims=True) + eps_norm)
    return (row_scale, (rows * row_scale * gain.astype(jnp.float32)[None, :]).astype(jnp.bfloat16))


def norm_back(rows, row_scale, gain, d_normed):
    weighted = d_normed * gain.astype(jnp.float32)[None, :]
    grad_gain = jnp.sum(d_normed * rows * row_scale, axis=0)
    d_rows = row_scale * weighted - rows * row_scale**3 * jnp.mean(
        weighted * rows, axis=1, keepdims=True
    )
    return (d_rows, grad_gain)


def silu_slope(values):
    sigma_val = jax.nn.sigmoid(values)
    return sigma_val * (1.0 + values * (1.0 - sigma_val))


def link_states(earlier, later):
    return (earlier[0] * later[0], later[0][:, None, None] * earlier[1] + later[1])


def block_size(row_count, tok_count):
    return math.gcd(row_count, max(tok_count, 1024))


def shards(
    hidden_in,
    grad_out,
    doc_starts,
    norm_mixer,
    norm_ffn,
    mamba_z,
    mamba_x,
    mamba_bc,
    mamba_dt,
    conv_x,
    conv_bc,
    a_log,
    dt_bias,
    skip_gain,
    mamba_out,
    attn_query,
    attn_key,
    attn_value,
    attn_out,
    ffn_gate,
    ffn_up,
    ffn_down,
):
    tok_count = hidden_in.shape[0]
    seq_count = lax.axis_size("seq")
    seq_index = lax.axis_index("seq")
    base_row = seq_index * tok_count
    positions = base_row + jnp.arange(tok_count, dtype=jnp.int32)
    edge_rows = conv_x.shape[0] - 1
    ext_docs = doc_ids(
        base_row - edge_rows + jnp.arange(tok_count + edge_rows, dtype=jnp.int32), doc_starts
    )
    docs_here = ext_docs[edge_rows:]
    prev_doc = ext_docs[edge_rows - 1]
    heads_local = a_log.shape[0]
    q_local = attn_query.shape[1] // HDIM
    kv_local = attn_key.shape[1] // HDIM
    group_size = q_local // kv_local
    score_scale = HDIM ** (-0.5)
    nchunk = tok_count // SPAN

    def head_total(partial_sum):
        return lax.psum(partial_sum, "head")

    def spanned(values):
        return values.reshape((nchunk, SPAN) + values.shape[1:])

    fetched = (
        lax.all_gather(norm_mixer.astype(jnp.bfloat16), "seq", axis=0, tiled=True),
        lax.all_gather(norm_ffn.astype(jnp.bfloat16), "seq", axis=0, tiled=True),
        lax.all_gather(mamba_z.astype(jnp.bfloat16), "seq", axis=0, tiled=True),
        lax.all_gather(mamba_x.astype(jnp.bfloat16), "seq", axis=0, tiled=True),
        lax.all_gather(mamba_bc.astype(jnp.bfloat16), "seq", axis=0, tiled=True),
        lax.all_gather(mamba_dt.astype(jnp.bfloat16), "seq", axis=0, tiled=True),
        lax.all_gather(mamba_out.astype(jnp.bfloat16), "seq", axis=1, tiled=True),
        lax.all_gather(attn_query.astype(jnp.bfloat16), "seq", axis=0, tiled=True),
        lax.all_gather(attn_key.astype(jnp.bfloat16), "seq", axis=0, tiled=True),
        lax.all_gather(attn_value.astype(jnp.bfloat16), "seq", axis=0, tiled=True),
        lax.all_gather(attn_out.astype(jnp.bfloat16), "seq", axis=1, tiled=True),
        lax.all_gather(ffn_gate.astype(jnp.bfloat16), "seq", axis=0, tiled=True),
        lax.all_gather(ffn_up.astype(jnp.bfloat16), "seq", axis=0, tiled=True),
        lax.all_gather(ffn_down.astype(jnp.bfloat16), "seq", axis=1, tiled=True),
    )
    (
        gain_mix,
        gain_ffn,
        full_z,
        full_x,
        full_bc,
        full_dt,
        full_mout,
        full_query,
        full_key,
        full_value,
        full_aout,
        full_gate,
        full_up,
        full_down,
    ) = fetched
    scale_one, normed_one = norm_rows(hidden_in, gain_mix)
    gate_z = product(normed_one, full_z)
    x_pre = product(normed_one, full_x).astype(jnp.bfloat16)
    bc_pre = product(normed_one, full_bc).astype(jnp.bfloat16)
    dt_raw = product(normed_one, full_dt)
    prev_x, prev_bc = passed_along(
        (x_pre[tok_count - edge_rows :], bc_pre[tok_count - edge_rows :]), "seq", 1
    )
    ext_x = jnp.concatenate([prev_x, x_pre], axis=0)
    ext_bc = jnp.concatenate([prev_bc, bc_pre], axis=0)
    conv_xv = convolve(ext_x, conv_x, ext_docs, tok_count)
    conv_bcv = convolve(ext_bc, conv_bc, ext_docs, tok_count)
    x_ssm = jax.nn.silu(conv_xv).astype(jnp.bfloat16)
    bc_ssm = jax.nn.silu(conv_bcv).astype(jnp.bfloat16)
    dt_pre = dt_raw + dt_bias[None, :]
    dt_val = jax.nn.softplus(dt_pre)
    log_decay = -jnp.exp(a_log)[None, :] * dt_val
    x_heads = x_ssm.astype(jnp.float32).reshape(tok_count, heads_local, MHDIM)
    b_mat = bc_ssm[:, :NSTATE].astype(jnp.float32)
    c_mat = bc_ssm[:, NSTATE:].astype(jnp.float32)
    span_prev = jnp.concatenate([prev_doc[None], docs_here[SPAN - 1 :: SPAN][:-1]])

    def forward_step(state_in, inputs):
        xs_c, b_c, c_c, dt_c, la_c, docs_c, before = inputs
        y_c, state_out = span_ssd(state_in, xs_c, b_c, c_c, dt_c, la_c, docs_c, before)
        return (state_out, (y_c, state_in))

    local_state, (y_spans, span_starts) = lax.scan(
        forward_step,
        jnp.zeros((heads_local, MHDIM, NSTATE), jnp.float32),
        (
            spanned(x_heads),
            spanned(b_mat),
            spanned(c_mat),
            spanned(dt_val),
            spanned(log_decay),
            spanned(docs_here),
            span_prev,
        ),
    )
    cum_dev = jnp.cumsum(log_decay, axis=0)
    dev_decay = jnp.where((docs_here == prev_doc)[:, None], jnp.exp(cum_dev), 0.0)
    total_decay = dev_decay[-1]
    in_decay, in_state = carried_in(
        (total_decay, local_state),
        "seq",
        link_states,
        (jnp.ones_like(total_decay), jnp.zeros_like(local_state)),
        False,
    )
    y_carry = jnp.einsum("tn,hpn->thp", c_mat, in_state, precision=top_prec) * dev_decay[:, :, None]
    y_heads = (
        y_spans.reshape(tok_count, heads_local, MHDIM)
        + y_carry
        + skip_gain[None, :, None] * x_heads
    )
    y_flat = y_heads.reshape(tok_count, heads_local * MHDIM)
    silu_z = jax.nn.silu(gate_z)
    gated = (y_flat * silu_z).astype(jnp.bfloat16)
    mixer_part = product(gated, full_mout)
    queries = rotate(
        product(normed_one, full_query).reshape(tok_count, q_local, HDIM), positions
    ).astype(jnp.bfloat16)
    keys = (
        rotate(product(normed_one, full_key).reshape(tok_count, kv_local, HDIM), positions)
        .reshape(tok_count, kv_local * HDIM)
        .astype(jnp.bfloat16)
    )
    values_low = product(normed_one, full_value).astype(jnp.bfloat16)
    query_groups = queries.reshape(tok_count, kv_local, group_size, HDIM)

    def visible_keys(key_first, key_rows):
        key_pos = key_first + jnp.arange(key_rows, dtype=jnp.int32)
        return (positions[:, None] >= key_pos[None, :]) & (
            docs_here[:, None] == doc_ids(key_pos, doc_starts)[None, :]
        )

    start_max = jnp.full((tok_count, kv_local, group_size), neg_large, jnp.float32)
    start_sum = jnp.zeros((tok_count, kv_local, group_size), jnp.float32)
    start_acc = jnp.zeros((tok_count, kv_local, group_size, HDIM), jnp.float32)
    key_piece = lax.all_gather(keys, "seq", axis=0, tiled=True)
    value_piece = lax.all_gather(values_low, "seq", axis=0, tiled=True)
    row_count = key_piece.shape[0]
    block_len = block_size(row_count, tok_count)

    def attend_per_block(current, block_index):
        offset = block_index * block_len
        key_blk = lax.dynamic_slice_in_dim(key_piece, offset, block_len, 0).reshape(
            block_len, kv_local, HDIM
        )
        value_blk = lax.dynamic_slice_in_dim(value_piece, offset, block_len, 0).reshape(
            block_len, kv_local, HDIM
        )
        visible = visible_keys(offset, block_len)
        run_max, run_sum, run_acc = current
        shown_mask = visible[:, None, None, :]
        scores = (
            jnp.einsum("tgrd,kgd->tgrk", query_groups, key_blk, preferred_element_type=jnp.float32)
            * score_scale
        )
        scores = jnp.where(shown_mask, scores, neg_large)
        new_max = jnp.maximum(run_max, jnp.max(scores, axis=3))
        weights = jnp.where(shown_mask, jnp.exp(scores - new_max[..., None]), 0.0)
        rescale = jnp.exp(run_max - new_max)
        new_acc = run_acc * rescale[..., None] + jnp.einsum(
            "tgrk,kgd->tgrd",
            weights.astype(jnp.bfloat16),
            value_blk,
            preferred_element_type=jnp.float32,
        )
        return ((new_max, run_sum * rescale + jnp.sum(weights, axis=3), new_acc), None)

    folded, ignored = lax.scan(
        attend_per_block, (start_max, start_sum, start_acc), jnp.arange(row_count // block_len)
    )
    run_max, run_sum, run_acc = folded
    log_total = run_max + jnp.log(run_sum)
    attn_f32 = run_acc / run_sum[..., None]
    attn_low = attn_f32.reshape(tok_count, q_local * HDIM).astype(jnp.bfloat16)
    attn_part = product(attn_low, full_aout)
    mid = hidden_in + head_total(mixer_part + attn_part)
    scale_two, normed_two = norm_rows(mid, gain_ffn)
    gate_val = product(normed_two, full_gate)
    up_val = product(normed_two, full_up)
    silu_gate = jax.nn.silu(gate_val)
    activated = (silu_gate * up_val).astype(jnp.bfloat16)
    block_out = mid + head_total(product(activated, full_down))
    (
        gain_mix,
        gain_ffn,
        full_z,
        full_x,
        full_bc,
        full_dt,
        full_mout,
        full_query,
        full_key,
        full_value,
        full_aout,
        full_gate,
        full_up,
        full_down,
    ) = fetched
    g_ffn = grad_out.astype(jnp.bfloat16)
    grad_w_down = product_t(activated, g_ffn)
    d_act = product_nt(g_ffn, full_down)
    d_gate = (d_act * up_val * silu_slope(gate_val)).astype(jnp.bfloat16)
    d_up = (d_act * silu_gate).astype(jnp.bfloat16)
    grad_w_gate = product_t(normed_two, d_gate)
    grad_w_up = product_t(normed_two, d_up)
    d_two = head_total(product_nt(d_gate, full_gate) + product_nt(d_up, full_up))
    d_mid_norm, grad_gain_ffn = norm_back(mid, scale_two, gain_ffn, d_two)
    d_mid = grad_out + d_mid_norm
    g_mid = d_mid.astype(jnp.bfloat16)
    grad_w_mout = product_t(gated, g_mid)
    grad_w_aout = product_t(attn_low, g_mid)
    d_gated = product_nt(g_mid, full_mout)
    d_y_flat = d_gated * silu_z
    d_z = (d_gated * y_flat * silu_slope(gate_z)).astype(jnp.bfloat16)
    d_attn_low = product_nt(g_mid, full_aout).astype(jnp.bfloat16)
    d_y_heads = d_y_flat.reshape(tok_count, heads_local, MHDIM)
    grad_skip = jnp.sum(d_y_heads * x_heads, axis=(0, 2))
    d_in_local = jnp.einsum("th,thp,tn->hpn", dev_decay, d_y_heads, c_mat, precision=top_prec)
    out_decay, state_grad = carried_in(
        (total_decay, d_in_local),
        "seq",
        link_states,
        (jnp.ones_like(total_decay), jnp.zeros_like(d_in_local)),
        True,
    )
    before_cum = jnp.concatenate([jnp.zeros((1, heads_local), jnp.float32), cum_dev[:-1]], axis=0)[
        ::SPAN
    ]
    start_decay = jnp.where((span_prev == prev_doc)[:, None], jnp.exp(before_cum), 0.0)
    true_starts = span_starts + start_decay[:, :, None, None] * in_state[None]

    def back_step(grad_state, inputs):
        start_state, xs_c, b_c, c_c, dt_c, la_c, docs_c, before, dy_c = inputs

        def local_span(state_arg, xs_arg, b_arg, c_arg, dt_arg, la_arg):
            return span_ssd(state_arg, xs_arg, b_arg, c_arg, dt_arg, la_arg, docs_c, before)

        ignored, pullback = jax.vjp(local_span, start_state, xs_c, b_c, c_c, dt_c, la_c)
        span_grad = pullback((dy_c, grad_state))
        return (span_grad[0], span_grad[1:])

    ignored_state, (d_xs_c, d_b_c, d_c_c, d_dt_c, d_la_c) = lax.scan(
        back_step,
        state_grad,
        (
            true_starts,
            spanned(x_heads),
            spanned(b_mat),
            spanned(c_mat),
            spanned(dt_val),
            spanned(log_decay),
            spanned(docs_here),
            span_prev,
            spanned(d_y_heads),
        ),
        reverse=True,
    )
    d_xs = d_xs_c.reshape(tok_count, heads_local, MHDIM) + skip_gain[None, :, None] * d_y_heads
    d_log = d_la_c.reshape(tok_count, heads_local)
    grad_a_log = jnp.sum(d_log * log_decay, axis=0)
    d_dt_in = (
        d_dt_c.reshape(tok_count, heads_local) - jnp.exp(a_log)[None, :] * d_log
    ) * jax.nn.sigmoid(dt_pre)
    grad_dt_bias = jnp.sum(d_dt_in, axis=0)
    d_dt_raw = d_dt_in.astype(jnp.bfloat16)
    d_bc_post = head_total(
        jnp.concatenate(
            [d_b_c.reshape(tok_count, NSTATE), d_c_c.reshape(tok_count, NSTATE)], axis=1
        )
    )
    du_x = d_xs.reshape(tok_count, heads_local * MHDIM) * silu_slope(conv_xv)
    du_bc = d_bc_post * silu_slope(conv_bcv)
    dext_x, grad_conv_x = convolve_back(du_x, ext_x, conv_x, ext_docs, tok_count)
    dext_bc, grad_conv_bc = convolve_back(du_bc, ext_bc, conv_bc, ext_docs, tok_count)
    next_x, next_bc = passed_along((dext_x[:edge_rows], dext_bc[:edge_rows]), "seq", -1)
    d_x_pre = (dext_x[edge_rows:] + jnp.pad(next_x, ((tok_count - edge_rows, 0), (0, 0)))).astype(
        jnp.bfloat16
    )
    d_bc_pre = (
        dext_bc[edge_rows:] + jnp.pad(next_bc, ((tok_count - edge_rows, 0), (0, 0)))
    ).astype(jnp.bfloat16)
    dout_groups = d_attn_low.reshape(tok_count, kv_local, group_size, HDIM)
    delta = jnp.sum(dout_groups.astype(jnp.float32) * attn_f32, axis=3)
    query_key_piece = lax.all_gather(keys, "seq", axis=0, tiled=True)
    query_value_piece = lax.all_gather(values_low, "seq", axis=0, tiled=True)
    row_count = query_key_piece.shape[0]
    query_block_len = block_size(row_count, tok_count)

    def query_per_block(current, block_index):
        offset = block_index * query_block_len
        key_blk = lax.dynamic_slice_in_dim(query_key_piece, offset, query_block_len, 0).reshape(
            query_block_len, kv_local, HDIM
        )
        value_blk = lax.dynamic_slice_in_dim(query_value_piece, offset, query_block_len, 0).reshape(
            query_block_len, kv_local, HDIM
        )
        visible = visible_keys(offset, query_block_len)
        shown_mask = visible[:, None, None, :]
        scores = (
            jnp.einsum("tgrd,kgd->tgrk", query_groups, key_blk, preferred_element_type=jnp.float32)
            * score_scale
        )
        probabilities = jnp.exp(jnp.where(shown_mask, scores - log_total[..., None], neg_large))
        d_probs = jnp.einsum(
            "tgrd,kgd->tgrk", dout_groups, value_blk, preferred_element_type=jnp.float32
        )
        d_scores = (probabilities * (d_probs - delta[..., None])).astype(jnp.bfloat16)
        return (
            current
            + jnp.einsum("tgrk,kgd->tgrd", d_scores, key_blk, preferred_element_type=jnp.float32)
            * score_scale,
            None,
        )

    folded, ignored = lax.scan(
        query_per_block,
        jnp.zeros((tok_count, kv_local, group_size, HDIM), jnp.float32),
        jnp.arange(row_count // query_block_len),
    )
    grad_query = folded
    prior_keys, prior_values = passed_along_2((keys, values_low), "seq", 1)
    prior_first = (seq_index + seq_count - 1) % seq_count * tok_count
    prior_positions = prior_first + jnp.arange(tok_count, dtype=jnp.int32)
    prior_docs = doc_ids(prior_positions, doc_starts)
    owned_keys = prior_keys.reshape(tok_count, kv_local, HDIM)
    owned_values = prior_values.reshape(tok_count, kv_local, HDIM)
    query_send = queries.reshape(tok_count, q_local * HDIM).astype(jnp.float32)
    dout_send = d_attn_low.astype(jnp.float32)
    query_piece = lax.all_gather(query_send, "seq", axis=0, tiled=True)
    dout_piece = lax.all_gather(dout_send, "seq", axis=0, tiled=True)
    total_piece = lax.all_gather(log_total.reshape(tok_count, q_local), "seq", axis=0, tiled=True)
    delta_piece = lax.all_gather(delta.reshape(tok_count, q_local), "seq", axis=0, tiled=True)
    row_count = query_piece.shape[0]
    key_block_len = block_size(row_count, tok_count)

    def key_per_block(current, block_index):
        offset = block_index * key_block_len
        query_blk = (
            lax.dynamic_slice_in_dim(query_piece, offset, key_block_len, 0)
            .astype(jnp.bfloat16)
            .reshape(key_block_len, kv_local, group_size, HDIM)
        )
        dout_blk = (
            lax.dynamic_slice_in_dim(dout_piece, offset, key_block_len, 0)
            .astype(jnp.bfloat16)
            .reshape(key_block_len, kv_local, group_size, HDIM)
        )
        total_blk = lax.dynamic_slice_in_dim(total_piece, offset, key_block_len, 0).reshape(
            key_block_len, kv_local, group_size
        )
        delta_blk = lax.dynamic_slice_in_dim(delta_piece, offset, key_block_len, 0).reshape(
            key_block_len, kv_local, group_size
        )
        query_pos = offset + jnp.arange(key_block_len, dtype=jnp.int32)
        visible = (query_pos[:, None] >= prior_positions[None, :]) & (
            doc_ids(query_pos, doc_starts)[:, None] == prior_docs[None, :]
        )
        grad_key, grad_value = current
        shown_mask = visible[:, None, None, :]
        scores = (
            jnp.einsum("qgrd,kgd->qgrk", query_blk, owned_keys, preferred_element_type=jnp.float32)
            * score_scale
        )
        probabilities = jnp.exp(jnp.where(shown_mask, scores - total_blk[..., None], neg_large))
        grad_value = grad_value + jnp.einsum(
            "qgrk,qgrd->kgd",
            probabilities.astype(jnp.bfloat16),
            dout_blk,
            preferred_element_type=jnp.float32,
        )
        d_probs = jnp.einsum(
            "qgrd,kgd->qgrk", dout_blk, owned_values, preferred_element_type=jnp.float32
        )
        d_scores = (probabilities * (d_probs - delta_blk[..., None])).astype(jnp.bfloat16)
        grad_key = (
            grad_key
            + jnp.einsum("qgrk,qgrd->kgd", d_scores, query_blk, preferred_element_type=jnp.float32)
            * score_scale
        )
        return ((grad_key, grad_value), None)

    folded, ignored = lax.scan(
        key_per_block,
        (
            jnp.zeros((tok_count, kv_local, HDIM), jnp.float32),
            jnp.zeros((tok_count, kv_local, HDIM), jnp.float32),
        ),
        jnp.arange(row_count // key_block_len),
    )
    prior_grad_key, prior_grad_value = folded
    grad_key, grad_value = passed_along_2((prior_grad_key, prior_grad_value), "seq", -1)
    d_q_pre = (
        rotate_back(grad_query.reshape(tok_count, q_local, HDIM), positions)
        .reshape(tok_count, q_local * HDIM)
        .astype(jnp.bfloat16)
    )
    d_k_pre = (
        rotate_back(grad_key, positions).reshape(tok_count, kv_local * HDIM).astype(jnp.bfloat16)
    )
    d_v_low = grad_value.reshape(tok_count, kv_local * HDIM).astype(jnp.bfloat16)
    grad_w_z = product_t(normed_one, d_z)
    grad_w_x = product_t(normed_one, d_x_pre)
    grad_w_bc = product_t(normed_one, d_bc_pre)
    grad_w_dt = product_t(normed_one, d_dt_raw)
    grad_w_query = product_t(normed_one, d_q_pre)
    grad_w_key = product_t(normed_one, d_k_pre)
    grad_w_value = product_t(normed_one, d_v_low)
    d_one_part = (
        product_nt(d_z, full_z)
        + product_nt(d_x_pre, full_x)
        + product_nt(d_dt_raw, full_dt)
        + product_nt(d_q_pre, full_query)
        + product_nt(d_k_pre, full_key)
        + product_nt(d_v_low, full_value)
    )
    d_one = head_total(d_one_part) + product_nt(d_bc_pre, full_bc)
    d_in_norm, grad_gain_mix = norm_back(hidden_in, scale_one, gain_mix, d_one)
    grad_in = d_mid + d_in_norm
    small_sent = lax.psum((grad_conv_x, grad_conv_bc, grad_a_log, grad_dt_bias, grad_skip), "seq")
    ordered = (
        lax.psum_scatter(grad_gain_mix, "seq", scatter_dimension=0, tiled=True),
        lax.psum_scatter(grad_gain_ffn, "seq", scatter_dimension=0, tiled=True),
        lax.psum_scatter(grad_w_z, "seq", scatter_dimension=0, tiled=True),
        lax.psum_scatter(grad_w_x, "seq", scatter_dimension=0, tiled=True),
        lax.psum_scatter(grad_w_bc, "seq", scatter_dimension=0, tiled=True),
        lax.psum_scatter(grad_w_dt, "seq", scatter_dimension=0, tiled=True),
        lax.psum_scatter(grad_w_mout, "seq", scatter_dimension=1, tiled=True),
        lax.psum_scatter(grad_w_query, "seq", scatter_dimension=0, tiled=True),
        lax.psum_scatter(grad_w_key, "seq", scatter_dimension=0, tiled=True),
        lax.psum_scatter(grad_w_value, "seq", scatter_dimension=0, tiled=True),
        lax.psum_scatter(grad_w_aout, "seq", scatter_dimension=1, tiled=True),
        lax.psum_scatter(grad_w_gate, "seq", scatter_dimension=0, tiled=True),
        lax.psum_scatter(grad_w_up, "seq", scatter_dimension=0, tiled=True),
        lax.psum_scatter(grad_w_down, "seq", scatter_dimension=1, tiled=True),
    )
    return (
        block_out,
        grad_in,
        ordered[0],
        ordered[1],
        ordered[2],
        ordered[3],
        ordered[4],
        ordered[5],
        small_sent[0],
        small_sent[1],
        small_sent[2],
        small_sent[3],
        small_sent[4],
        ordered[6],
        ordered[7],
        ordered[8],
        ordered[9],
        ordered[10],
        ordered[11],
        ordered[12],
        ordered[13],
    )


def solution(mesh):
    placed = (
        P("seq", None),
        P("seq", None),
        P(),
        P("seq"),
        P("seq"),
        P("seq", "head"),
        P("seq", "head"),
        P("seq", None),
        P("seq", "head"),
        P(None, "head"),
        P(),
        P("head"),
        P("head"),
        P("head"),
        P("head", "seq"),
        P("seq", "head"),
        P("seq", "head"),
        P("seq", "head"),
        P("head", "seq"),
        P("seq", "head"),
        P("seq", "head"),
        P("head", "seq"),
    )
    return jax.shard_map(
        shards,
        mesh=mesh,
        in_specs=placed,
        out_specs=(
            P("seq", None),
            P("seq", None),
            P("seq"),
            P("seq"),
            P("seq", "head"),
            P("seq", "head"),
            P("seq", None),
            P("seq", "head"),
            P(None, "head"),
            P(),
            P("head"),
            P("head"),
            P("head"),
            P("head", "seq"),
            P("seq", "head"),
            P("seq", "head"),
            P("seq", "head"),
            P("head", "seq"),
            P("seq", "head"),
            P("seq", "head"),
            P("head", "seq"),
        ),
        check_vma=False,
    )
```

profile of v0, /device:TPU:0, one launch (start us, length us, event | category | flops | bytes accessed | tf_op | source)
XLA Modules:
  0.0 4236.3 jit_solution(4588101064587588158)
XLA Ops:
  11.1 42.2 all-gather.4
  54.3 39.5 all_gather.87
  96.5 43.2 %all_gather.90 = bf16[2048,128]{1,0:T(8,128)(2,1)S(1)} all-gather(bf16[128,128]{1,0:T(8,128)(2,1)S(1)} %convert_element_type.312), channel_id=1, replica_groups=mesh['seq'=16,'head'=2] {'seq'}, dimensions={0}, use_global_device_ids=true | all-gather | bytes 557056 | tf_op jit(solution)/shard_map/all_gather | solution.py:249
  144.9 37.1 all_gather.79
  213.8 72.6 %while.113 = (s32[]{:T(128)}, f32[24,64,256]{2,1,0:T(8,128)S(1)}, f32[2,128,24,64]{1,0,3,2:T(2,128)}, f32[2,24,64,256]{3,2,1,0:T(8,128)}, s32[2,128]{1,0:T(2,128...) while((s32[]{:T(128)}, f32[24,64,256]{2,1,0:T(8,128)S(1)}, ...), condition=%wide.region_4.5_spmd.clone, body=%wide.region_2.4_spmd.clone.sunk | while | flops 1564861696 | bytes 14346532 | solution.py:298
  231.1 19.0 dynamic_update_slice.74
  267.4 19.1 dynamic_update_slice.74
  295.1 39.1 all-gather.5
  339.9 15.8 all-gather.33.cloned.1.call-done
  355.7 48.0 %while.115 = (s32[]{:T(128)}, f32[256,1,4]{0,2,1:T(4,128)S(1)}, f32[256,1,4]{0,2,1:T(4,128)S(1)}, f32[256,1,4,128]{0,3,2,1:T(8,128)}, s32[4]{0:T(128)S(1)}, /*in...) while((s32[]{:T(128)}, f32[256,1,4]{0,2,1:T(4,128)S(1)}, ...), condition=%wide.region_13.14_spmd.clone, body=%wide.region_9.13_spmd.clone.sunk | while | flops 551714048 | bytes 32341284 | solution.py:383
  408.2 220.2 %all-gather.47.cloned.1.call-done = f32[384,64,256]{2,1,0:T(8,128)} async-done(((f32[24,64,256]{2,1,0:T(8,128)}), f32[384,64,256]{2,1,0:T(8,128)}) %all-gather.47.cloned.1.call-update) | async-done | bytes 25165840 | tf_op jit(solution)/shard_map/all_gather | solution.py:28
  628.4 45.4 %while.114 = (s32[]{:T(128)}, f32[24,64,256]{2,1,0:T(8,128)S(1)}, s32[]{:T(128)}, f32[16,24]{1,0:T(8,128)}, f32[16,24,64,256]{3,2,1,0:T(8,128)}, /*index=5*/s32[]{:T(128)}, s32[]{:T(128)}) while((s32[]{:T(128)}, f32[24,64,256]{2,1,0:T(8,128)S(1)}, s32[]{:T(128)}, f32[16,24]{1,0:T(8,128)}, f32[16,24,64,256]{3,2,1,0:T(8,128)}, ...), condition=%wide.region_8.9_spmd.clone, body=%wide.region_7.8_spmd.clone.sunk | while | flops 1572868 | bytes 4718993 | solution.py:40
  680.8 43.3 %all-gather.27.cloned.1.call-done = bf16[2048,1536]{1,0:T(8,128)(2,1)} async-done(((bf16[128,1536]{1,0:T(8,128)(2,1)}), bf16[2048,1536]{1,0:T(8,128)(2,1)}) %all-gather.27.cloned.1.call-update) | async-done | bytes 6291472 | tf_op jit(solution)/shard_map/all_gather | solution.py:242
  730.5 110.7 %all-gather.29.cloned.1.call-done = bf16[1536,2048]{1,0:T(8,128)(2,1)} async-done(((bf16[1536,128]{1,0:T(8,128)(2,1)}), bf16[1536,2048]{1,0:T(8,128)(2,1)}) %all-gather.29.cloned.1.call-update) | async-done | bytes 6291472 | tf_op jit(solution)/shard_map/all_gather | solution.py:246
  847.4 58.6 %all-gather.35.cloned.1.call-done = bf16[512,2048]{1,0:T(8,128)(2,1)} async-done(((bf16[512,128]{1,0:T(8,128)(2,1)}), bf16[512,2048]{1,0:T(8,128)(2,1)}) %all-gather.35.cloned.1.call-update) | async-done | bytes 2097168 | tf_op jit(solution)/shard_map/all_gather | solution.py:250
  915.8 37.6 all-gather.6
  957.6 90.0 %all-gather.37.cloned.1.call-done = bf16[2048,2048]{1,0:T(8,128)(2,1)} async-done(((bf16[128,2048]{1,0:T(8,128)(2,1)}), bf16[2048,2048]{1,0:T(8,128)(2,1)}) %all-gather.37.cloned.1.call-update) | async-done | bytes 8388624 | tf_op jit(solution)/shard_map/all_gather | solution.py:251
  1047.6 7.1 fusion.339
  1054.7 107.6 %all-gather.39.cloned.1.call-done = bf16[2048,2048]{1,0:T(8,128)(2,1)} async-done(((bf16[128,2048]{1,0:T(8,128)(2,1)}), bf16[2048,2048]{1,0:T(8,128)(2,1)}) %all-gather.39.cloned.1.call-update) | async-done | bytes 8388624 | tf_op jit(solution)/shard_map/all_gather | solution.py:252
  1169.3 137.2 %all-gather.41.cloned.1.call-done = bf16[2048,2048]{1,0:T(8,128)(2,1)} async-done(((bf16[2048,128]{1,0:T(8,128)(2,1)}), bf16[2048,2048]{1,0:T(8,128)(2,1)}) %all-gather.41.cloned.1.call-update) | async-done | bytes 8388624 | tf_op jit(solution)/shard_map/all_gather | solution.py:253
  1306.5 9.1 multiply_convert_fusion
  1327.6 17.9 all-reduce.23.cloned.1.call-done
  1355.2 8.8 multiply_reduce_fusion.7
  1380.0 38.7 all-gather.3
  1422.6 7.1 fusion.341
  1432.4 37.6 while.117
  1476.3 36.9 all_gather.102
  1515.3 78.0 %while.118 = (s32[]{:T(128)}, f32[256,1,128]{0,2,1:T(8,128)S(1)}, f32[256,1,128]{0,2,1:T(8,128)S(1)}, s32[4]{0:T(128)S(1)}, bf16[4096,512]{0,1:T(8,128)(2,1)}, /...) while((s32[]{:T(128)}, f32[256,1,128]{0,2,1:T(8,128)S(1)}, ...), condition=%wide.region_39.40_spmd.clone, body=%wide.region_37.39_spmd.clone.sunk | while | flops 1085203712 | bytes 28851512 | solution.py:597
  1608.9 183.6 %all-gather.51.cloned.1.call-done = f32[384,64,256]{2,1,0:T(8,128)} async-done(((f32[24,64,256]{2,1,0:T(8,128)}), f32[384,64,256]{2,1,0:T(8,128)}) %all-gather.51.cloned.1.call-update) | async-done | bytes 25165840 | tf_op jit(solution)/shard_map/all_gather | solution.py:28
  1792.6 17.4 rev.7
  1810.0 37.4 while.116
  1851.5 97.4 %while.112 = (s32[]{:T(128)}, f32[24,64,256]{2,1,0:T(8,128)S(1)}, f32[2,128,24,64]{1,3,2,0:T(8,128)}, f32[2,128,256]{2,1,0:T(8,128)}, f32[2,128,256]{2,1,0:T(8,1...) while((s32[]{:T(128)}, f32[24,64,256]{2,1,0:T(8,128)S(1)}, ...), condition=%wide.region_31.32_spmd, body=%wide.region_21.31_spmd.sunk | while | flops 3785840896 | bytes 65791424 | solution.py:457
  1998.5 7.3 fusion.345
  2007.5 8.2 fusion.348
  2017.0 8.2 fusion.349
  2026.7 9.5 fusion.270
  2064.8 75.7 %all-reduce.15 = (f32[2048]{0:T(1024)S(1)}, f32[2048]{0:T(1024)S(1)}, f32[4,1536]{1,0:T(4,128)}, f32[4,512]{1,0:T(4,128)}, f32[24]{0:T(128)}, /*index=5*/f32[24]{0:T(128)}, f32[24]{0:T(128)}) all-reduce(f32[2048]{0:T(1024)S(1)} %get-tuple-element.1504, f32[2048]{0:T(1024)S(1)} %copy-done.136, ...), channel_id=6, replica_groups=mesh['seq'=16,'head'=2] {'seq'}, use_global_device_ids=true, to_apply=%region_44.45.clone | all-reduce | flops 12360 | bytes 98880
  2146.6 61.0 %reduce-scatter.29.cloned.1.call-done = f32[512,128]{1,0:T(8,128)} async-done(((f32[512,2048]{1,0:T(8,128)}), f32[512,128]{1,0:T(8,128)}) %reduce-scatter.29.cloned.1.call-update) | async-done | bytes 262160 | tf_op jit(solution)/shard_map/reduce_scatter | solution.py:646
  2207.6 80.1 %reduce-scatter.27.cloned.1.call-done = f32[128,128]{1,0:T(8,128)} async-done(((f32[2048,128]{1,0:T(8,128)}), f32[128,128]{1,0:T(8,128)}) %reduce-scatter.27.cloned.1.call-update) | async-done | bytes 65552 | tf_op jit(solution)/shard_map/reduce_scatter | solution.py:645
  2287.7 76.9 %reduce-scatter.25.cloned.1.call-done = f32[128,128]{1,0:T(8,128)} async-done(((f32[2048,128]{1,0:T(8,128)}), f32[128,128]{1,0:T(8,128)}) %reduce-scatter.25.cloned.1.call-update) | async-done | bytes 65552 | tf_op jit(solution)/shard_map/reduce_scatter | solution.py:644
  2364.6 207.4 %reduce-scatter.13.cloned.1.call-done = f32[128,1536]{1,0:T(8,128)} async-done(((f32[2048,1536]{1,0:T(8,128)}), f32[128,1536]{1,0:T(8,128)}) %reduce-scatter.13.cloned.1.call-update) | async-done | bytes 786448 | tf_op jit(solution)/shard_map/reduce_scatter | solution.py:638
  2572.0 209.7 %reduce-scatter.21.cloned.1.call-done = f32[1536,128]{1,0:T(8,128)} async-done(((f32[1536,2048]{1,0:T(8,128)}), f32[1536,128]{1,0:T(8,128)}) %reduce-scatter.21.cloned.1.call-update) | async-done | bytes 786448 | tf_op jit(solution)/shard_map/reduce_scatter | solution.py:642
  2781.8 349.0 %reduce-scatter.31.cloned.1.call-done = f32[128,2048]{1,0:T(8,128)} async-done(((f32[2048,2048]{1,0:T(8,128)}), f32[128,2048]{1,0:T(8,128)}) %reduce-scatter.31.cloned.1.call-update) | async-done | bytes 1048592 | tf_op jit(solution)/shard_map/reduce_scatter | solution.py:647
  3130.7 354.9 %reduce-scatter.33.cloned.1.call-done = f32[128,2048]{1,0:T(8,128)} async-done(((f32[2048,2048]{1,0:T(8,128)}), f32[128,2048]{1,0:T(8,128)}) %reduce-scatter.33.cloned.1.call-update) | async-done | bytes 1048592 | tf_op jit(solution)/shard_map/reduce_scatter | solution.py:648
  3485.6 354.9 %reduce-scatter.35.cloned.1.call-done = f32[2048,128]{1,0:T(8,128)} async-done(((f32[2048,2048]{1,0:T(8,128)}), f32[2048,128]{1,0:T(8,128)}) %reduce-scatter.35.cloned.1.call-update) | async-done | bytes 1048592 | tf_op jit(solution)/shard_map/reduce_scatter | solution.py:649
  3840.5 84.7 %reduce-scatter.19.cloned.1.call-done = f32[128,24]{0,1:T(8,128)} async-done(((f32[2048,24]{0,1:T(8,128)}), f32[128,24]{0,1:T(8,128)}) %reduce-scatter.19.cloned.1.call-update) | async-done | bytes 12304 | tf_op jit(solution)/shard_map/reduce_scatter | solution.py:641
  3925.2 94.3 %reduce-scatter.17.cloned.1.call-done = f32[128,512]{1,0:T(8,128)} async-done(((f32[2048,512]{1,0:T(8,128)}), f32[128,512]{1,0:T(8,128)}) %reduce-scatter.17.cloned.1.call-update) | async-done | bytes 262160 | tf_op jit(solution)/shard_map/reduce_scatter | solution.py:640
  4019.5 209.8 %reduce-scatter.15.cloned.1.call-done = f32[128,1536]{1,0:T(8,128)} async-done(((f32[2048,1536]{1,0:T(8,128)}), f32[128,1536]{1,0:T(8,128)}) %reduce-scatter.15.cloned.1.call-update) | async-done | bytes 786448 | tf_op jit(solution)/shard_map/reduce_scatter | solution.py:639
  (1009 shorter events, 630.2 us)
Async XLA Ops:
  7.2 176.0 %all-gather.25.cloned.1.call-start = ((), (), s32[]{:S(2)}) async-start(), calls=%async_computation.13 | async-start | bytes 2228224 | tf_op jit(solution)/shard_map/all_gather | solution.py:244
  9.1 184.3 %all-gather.23.cloned.1.call-start = ((), (), s32[]{:S(2)}) async-start(), calls=%async_computation.12 | async-start | bytes 6684672 | tf_op jit(solution)/shard_map/all_gather | solution.py:243
  11.1 323.1 %all-gather.49.cloned.1.call-start = ((), (), s32[]{:S(2)}) async-start(), calls=%async_computation.39 | async-start | bytes 1114112 | tf_op jit(solution)/shard_map/all_gather | solution.py:351
  94.1 630.0 %copy-start.3 = (bf16[256,2048]{1,0:T(8,128)(2,1)}, bf16[256,2048]{1,0:T(8,128)(2,1)S(1)}, u32[]{:S(2)}) copy-start(bf16[256,2048]{1,0:T(8,128)(2,1)S(1)} %multiply_convert_fusion.4) | copy-start | bytes 3145732
  95.7 86.4 %copy-start.169 = (f32[4,512]{1,0:T(4,128)S(1)}, f32[4,512]{1,0:T(4,128)}, u32[]{:S(2)}) copy-start(f32[4,512]{1,0:T(4,128)} %param.46) | copy-start | bytes 24580
  95.7 86.5 %copy-start.176 = (f32[24]{0:T(128)S(1)}, f32[24]{0:T(128)}, u32[]{:S(2)}) copy-start(f32[24]{0:T(128)} %param.48) | copy-start | bytes 292
  95.7 240.7 %all-gather.31.cloned.1.call-start = ((), (), s32[]{:S(2)}) async-start(), calls=%async_computation.16 | async-start | bytes 2228224 | tf_op jit(solution)/shard_map/all_gather | solution.py:247
  96.5 259.2 %all-gather.33.cloned.1.call-start = ((), (), s32[]{:S(2)}) async-start(), calls=%async_computation.17 | async-start | bytes 1114112 | tf_op jit(solution)/shard_map/all_gather | solution.py:352
  141.6 486.8 %all-gather.47.cloned.1.call-start = ((), (), s32[]{:S(2)}) async-start(), calls=%async_computation.38 | async-start | bytes 26738688 | tf_op jit(solution)/shard_map/all_gather | solution.py:28
  143.1 59.2 %copy-start.117 = (f32[1536]{0:T(1024)}, f32[1536]{0:T(1024)S(1)}, u32[]{:S(2)}) copy-start(f32[1536]{0:T(1024)S(1)} %get-tuple-element.1516) | copy-start | bytes 18436
  185.6 6.4 collective-permute-start.1
  198.1 4.1 collective-permute-start
  287.7 436.4 %all-gather.27.cloned.1.call-start = ((), (), s32[]{:S(2)}) async-start(), calls=%async_computation.14 | async-start | bytes 6684672 | tf_op jit(solution)/shard_map/all_gather | solution.py:242
  289.7 551.5 %all-gather.29.cloned.1.call-start = ((), (), s32[]{:S(2)}) async-start(), calls=%async_computation.15 | async-start | bytes 6684672 | tf_op jit(solution)/shard_map/all_gather | solution.py:246
  290.6 615.4 %all-gather.35.cloned.1.call-start = ((), (), s32[]{:S(2)}) async-start(), calls=%async_computation.18 | async-start | bytes 2228224 | tf_op jit(solution)/shard_map/all_gather | solution.py:250
  291.4 662.1 %all-reduce.21.cloned.1.call-start = ((), (), s32[]{:S(2)}) async-start(), calls=%async_computation.19 | async-start | bytes 4194304 | tf_op jit(solution)/shard_map/psum | solution.py:234
  404.8 501.2 %copy-start.46 = (bf16[256,1,4,128]{0,3,2,1:T(8,128)(2,1)}, bf16[256,1,4,128]{0,3,2,1:T(8,128)(2,1)S(1)}, u32[]{:S(2)}) copy-start(bf16[256,1,4,128]{0,3,2,1:T(8,128)(2,1)S(1)} %fusion.277) | copy-start | bytes 786436
  910.3 137.3 %all-gather.37.cloned.1.call-start = ((), (), s32[]{:S(2)}) async-start(), calls=%async_computation.20 | async-start | bytes 8912896 | tf_op jit(solution)/shard_map/all_gather | solution.py:251
  912.4 249.9 %all-gather.39.cloned.1.call-start = ((), (), s32[]{:S(2)}) async-start(), calls=%async_computation.21 | async-start | bytes 8912896 | tf_op jit(solution)/shard_map/all_gather | solution.py:252
  914.6 391.9 %all-gather.41.cloned.1.call-start = ((), (), s32[]{:S(2)}) async-start(), calls=%async_computation.22 | async-start | bytes 8912896 | tf_op jit(solution)/shard_map/all_gather | solution.py:253
  915.5 429.9 %all-reduce.23.cloned.1.call-start = ((), (), s32[]{:S(2)}) async-start(), calls=%async_computation.23 | async-start | bytes 4194304 | tf_op jit(solution)/shard_map/psum | solution.py:234
  957.6 204.7 %copy-start.24 = (bf16[256,2048]{1,0:T(8,128)(2,1)}, bf16[256,2048]{1,0:T(8,128)(2,1)S(1)}, u32[]{:S(2)}) copy-start(bf16[256,2048]{1,0:T(8,128)(2,1)S(1)} %multiply_convert_fusion.3) | copy-start | bytes 3145732
  1325.9 187.2 %all-gather.43.cloned.1.call-start = ((), (), s32[]{:S(2)}) async-start(), calls=%async_computation.24 | async-start | bytes 4456448 | tf_op jit(solution)/shard_map/all_gather | solution.py:544
  1327.6 187.7 %all-gather.45.cloned.1.call-start = ((), (), s32[]{:S(2)}) async-start(), calls=%async_computation.25 | async-start | bytes 4456448 | tf_op jit(solution)/shard_map/all_gather | solution.py:545
  1355.2 437.4 %all-gather.51.cloned.1.call-start = ((), (), s32[]{:S(2)}) async-start(), calls=%async_computation.40 | async-start | bytes 26738688 | tf_op jit(solution)/shard_map/all_gather | solution.py:28
  1369.2 668.2 %all-reduce.25.cloned.1.call-start = ((), (), s32[]{:S(2)}) async-start(), calls=%async_computation.41 | async-start | bytes 9437184 | tf_op jit(solution)/shard_map/psum | solution.py:234
  1369.2 143.9 %collective-permute-start.4 = (bf16[256,128]{1,0:T(8,128)(2,1)}, bf16[256,128]{1,0:T(8,128)(2,1)}, u32[]{:S(2)}, u32[]{:S(2)}) collective-permute-start(bf16[256,128]{1,0:T(8,128)(2,1)} %convolution_convert_fusion.3), channel_id=1, source_target_pairs={{30,0},{0,2},{2,4},{4,6},{6,8},{8,10},{10,12},{12,14},{14,16},{16,... | collective-permute-start | bytes 196616 | tf_op jit(solution)/shard_map/ppermute | solution.py:46
  1371.0 8.0 collective-permute-start.3
  1515.3 79.9 %copy-start.83 = (f32[256,64]{0,1:T(8,128)S(1)}, f32[256,64]{0,1:T(8,128)}, u32[]{:S(2)}) copy-start(f32[256,64]{0,1:T(8,128)} %copy-done.82) | copy-start | bytes 196612
  1515.3 79.9 %copy-start.85 = (f32[256,64]{0,1:T(8,128)S(1)}, f32[256,64]{0,1:T(8,128)}, u32[]{:S(2)}) copy-start(f32[256,64]{0,1:T(8,128)} %copy-done.84) | copy-start | bytes 196612
  1593.3 12.8 collective-permute-start.5
  1604.3 371.5 %collective-permute-start.6 = (bf16[256,1,128]{0,2,1:T(8,128)(2,1)}, bf16[256,1,128]{0,2,1:T(8,128)(2,1)}, u32[]{:S(2)}, u32[]{:S(2)}) collective-permute-start(bf16[256,1,128]{0,2,1:T(8,128)(2,1)} %convert.90), channel_id=1, source_target_pairs={{2,0},{4,2},{6,4},{8,6},{10,8},{12,10},{14,12},{16,14},{18,16},{20... | collective-permute-start | bytes 196616 | tf_op jit(solution)/shard_map/ppermute | solution.py:46
  1962.1 6.0 collective-permute-start.2
  1978.7 167.8 %reduce-scatter.23.cloned.1.call-start = ((), (), s32[]{:S(2)}) async-start(), calls=%async_computation.31 | async-start | bytes 4456448 | tf_op jit(solution)/shard_map/reduce_scatter | solution.py:643
  1982.7 224.8 %reduce-scatter.29.cloned.1.call-start = ((), (), s32[]{:S(2)}) async-start(), calls=%async_computation.34 | async-start | bytes 4456448 | tf_op jit(solution)/shard_map/reduce_scatter | solution.py:646
  1986.9 300.9 %reduce-scatter.27.cloned.1.call-start = ((), (), s32[]{:S(2)}) async-start(), calls=%async_computation.33 | async-start | bytes 1114112 | tf_op jit(solution)/shard_map/reduce_scatter | solution.py:645
  1989.3 375.3 %reduce-scatter.25.cloned.1.call-start = ((), (), s32[]{:S(2)}) async-start(), calls=%async_computation.32 | async-start | bytes 1114112 | tf_op jit(solution)/shard_map/reduce_scatter | solution.py:644
  1990.9 581.2 %reduce-scatter.13.cloned.1.call-start = ((), (), s32[]{:S(2)}) async-start(), calls=%async_computation.26 | async-start | bytes 13369344 | tf_op jit(solution)/shard_map/reduce_scatter | solution.py:638
  1997.4 784.4 %reduce-scatter.21.cloned.1.call-start = ((), (), s32[]{:S(2)}) async-start(), calls=%async_computation.30 | async-start | bytes 13369344 | tf_op jit(solution)/shard_map/reduce_scatter | solution.py:642
  2005.9 1124.9 %reduce-scatter.31.cloned.1.call-start = ((), (), s32[]{:S(2)}) async-start(), calls=%async_computation.35 | async-start | bytes 17825792 | tf_op jit(solution)/shard_map/reduce_scatter | solution.py:647
  2015.8 1469.9 %reduce-scatter.33.cloned.1.call-start = ((), (), s32[]{:S(2)}) async-start(), calls=%async_computation.36 | async-start | bytes 17825792 | tf_op jit(solution)/shard_map/reduce_scatter | solution.py:648
  2025.2 1815.3 %reduce-scatter.35.cloned.1.call-start = ((), (), s32[]{:S(2)}) async-start(), calls=%async_computation.37 | async-start | bytes 17825792 | tf_op jit(solution)/shard_map/reduce_scatter | solution.py:649
  2036.3 1888.9 %reduce-scatter.19.cloned.1.call-start = ((), (), s32[]{:S(2)}) async-start(), calls=%async_computation.29 | async-start | bytes 208896 | tf_op jit(solution)/shard_map/reduce_scatter | solution.py:641
  2037.3 1982.2 %reduce-scatter.17.cloned.1.call-start = ((), (), s32[]{:S(2)}) async-start(), calls=%async_computation.28 | async-start | bytes 4456448 | tf_op jit(solution)/shard_map/reduce_scatter | solution.py:640
  2039.3 6.2 collective-permute-start.7
  2048.3 2181.0 %reduce-scatter.15.cloned.1.call-start = ((), (), s32[]{:S(2)}) async-start(), calls=%async_computation.27 | async-start | bytes 13369344 | tf_op jit(solution)/shard_map/reduce_scatter | solution.py:639
  2062.6 79.1 %copy-start.15 = (f32[256,2048]{1,0:T(8,128)S(1)}, f32[256,2048]{1,0:T(8,128)}, u32[]{:S(2)}) copy-start(f32[256,2048]{1,0:T(8,128)} %param.36) | copy-start | bytes 6291460
  2062.6 79.1 %copy-start.173 = (f32[256]{0:T(256)S(1)}, f32[256]{0:T(256)}, u32[]{:S(2)}) copy-start(f32[256]{0:T(256)} %get-tuple-element.1753) | copy-start | bytes 3076
  (219 other events, 1852.1 us)
Sparse Core Ops, SparseCore 0:
  11.4 65.7 all-gather.24
  80.6 99.0 all-gather.22
  183.0 53.2 all-gather.48
  239.5 59.5 all-gather.30
  301.7 53.9 all-gather.32
  358.3 270.0 all-gather.46
  631.7 92.3 all-gather.26
  727.4 113.8 all-gather.28
  844.5 61.4 all-gather.34
  910.4 19.3 all-reduce.20
  933.6 114.0 all-gather.36
  1051.2 111.0 all-gather.38
  1165.9 140.5 all-gather.40
  1326.1 19.3 all-reduce.22
  1348.6 90.1 all-gather.42
  1442.1 73.1 all-gather.44
  1517.9 274.5 all-gather.50
  1978.9 29.3 all-reduce.24
  2011.2 98.0 reduce-scatter.22
  2112.1 95.4 reduce-scatter.28
  2210.5 77.1 reduce-scatter.26
  2290.5 74.0 reduce-scatter.24
  2371.8 200.1 reduce-scatter.12
  2578.1 203.6 reduce-scatter.20
  2784.7 345.9 reduce-scatter.30
  3133.6 352.0 reduce-scatter.32
  3488.4 352.0 reduce-scatter.34
  3843.4 81.7 reduce-scatter.18
  3928.0 91.4 reduce-scatter.16
  4025.6 203.6 reduce-scatter.14
where the time goes:
time: 4250 us; the launch traced here: 4240 us
  waiting for transfers between devices  3080 us (72%)
  blocking collectives  390 us (9%)
  matrix products  344 us (8%)
  local copies, waits for them, and re-layouts  209 us (5%)
  other arithmetic  167 us (4%)
    all_gather x2, waiting for transfers between devices, carried_in(): pieces = jax.tree.map(lambda part: lax.all_gather(part, axis), value)  404 us
    reduce_scatter x1, waiting for transfers between devices, shards(): lax.psum_scatter(grad_w_up, 'seq', scatter_dimension=0, tiled=True)  355 us
    reduce_scatter x1, waiting for transfers between devices, shards(): lax.psum_scatter(grad_w_down, 'seq', scatter_dimension=1, tiled=True)  355 us
    reduce_scatter x1, waiting for transfers between devices, shards(): lax.psum_scatter(grad_w_gate, 'seq', scatter_dimension=0, tiled=True)  349 us
    reduce_scatter x1, waiting for transfers between devices, shards(): lax.psum_scatter(grad_w_x, 'seq', scatter_dimension=0, tiled=True)  210 us
    reduce_scatter x1, waiting for transfers between devices, shards(): lax.psum_scatter(grad_w_mout, 'seq', scatter_dimension=1, tiled=True)  210 us
    reduce_scatter x1, waiting for transfers between devices, shards(): lax.psum_scatter(grad_w_z, 'seq', scatter_dimension=0, tiled=True)  207 us
    all_gather x1, waiting for transfers between devices, shards(): lax.all_gather(ffn_down.astype(jnp.bfloat16), 'seq', axis=1, tiled=True)  137 us
  transfers between devices with their start and end apart: 38, of which 26 were waited for; matrix products, arithmetic and copies ran while one was open for 16% of the time, Pallas kernels for 0%

commit v1 on v0

v1 whole, which is shorter than its diff:
```python
import math

import jax
import jax.numpy as jnp
import numpy as np
from jax import lax
from jax.sharding import Mesh
from jax.sharding import PartitionSpec as P

MHDIM = 64
NSTATE = 256
HDIM = 128
SPAN = 128

eps_norm = 1e-05
rope_base = 100000000000.0
neg_large = -1e30
top_prec = lax.Precision.HIGHEST
bf16 = jnp.bfloat16
f32 = jnp.float32


def doc_ids(positions, doc_starts):
    return jnp.sum((doc_starts[None, :] <= positions[:, None]).astype(jnp.int32), axis=1) - 1


def product(left, right):
    return jnp.dot(left, right, preferred_element_type=f32)


def product_t(left, right):
    return lax.dot_general(left, right, (((0,), (0,)), ((), ())), preferred_element_type=f32)


def product_nt(left, right):
    return lax.dot_general(left, right, (((1,), (1,)), ((), ())), preferred_element_type=f32)


def norm_rows(rows, gain):
    row_scale = lax.rsqrt(jnp.mean(rows * rows, axis=1, keepdims=True) + eps_norm)
    return (row_scale, (rows * row_scale * gain.astype(f32)[None, :]).astype(bf16))


def norm_back(rows, row_scale, gain, d_normed):
    weighted = d_normed * gain.astype(f32)[None, :]
    grad_gain = jnp.sum(d_normed * rows * row_scale, axis=0)
    d_rows = row_scale * weighted - rows * row_scale**3 * jnp.mean(
        weighted * rows, axis=1, keepdims=True
    )
    return (d_rows, grad_gain)


def silu_slope(values):
    sigma_val = jax.nn.sigmoid(values)
    return sigma_val * (1.0 + values * (1.0 - sigma_val))


def link_states(earlier, later):
    return (earlier[0] * later[0], later[0][:, None, None] * earlier[1] + later[1])


def carried_in(value, axis, join, neutral, backward):
    count, mine = (lax.axis_size(axis), lax.axis_index(axis))
    pieces = jax.tree.map(lambda part: lax.all_gather(part, axis), value)
    if backward:
        pieces = jax.tree.map(lambda part: part[::-1], pieces)
        mine = count - 1 - mine
    running = jax.tree.map(
        lambda part, zero: jnp.full_like(part, 0) + jnp.asarray(zero, part.dtype), value, neutral
    )

    def turn(position, running):
        longer = join(running, jax.tree.map(lambda part: part[position], pieces))
        return jax.tree.map(lambda new, old: jnp.where(position < mine, new, old), longer, running)

    return lax.fori_loop(0, count - 1, turn, running)


def passed_along(block, axis, distance):
    devices = range(lax.axis_size(axis))
    route = [(i - distance, i) for i in devices if i - distance in devices]
    return lax.ppermute(block, axis, route)


def convolve(extended, weights, ext_docs, tok_count):
    edge_rows = weights.shape[0] - 1
    summed = jnp.zeros((tok_count, extended.shape[1]), f32)
    for tap_index in range(weights.shape[0]):
        begin_row = edge_rows - tap_index
        same_doc = (ext_docs[begin_row : begin_row + tok_count] == ext_docs[edge_rows:])[:, None]
        summed = (
            summed
            + jnp.where(same_doc, extended[begin_row : begin_row + tok_count].astype(f32), 0.0)
            * weights[tap_index][None, :]
        )
    return summed


def convolve_back(d_conv, extended, weights, ext_docs, tok_count):
    edge_rows = weights.shape[0] - 1
    d_extended = jnp.zeros((tok_count + edge_rows, d_conv.shape[1]), f32)
    tap_grads = []
    for tap_index in range(weights.shape[0]):
        begin_row = edge_rows - tap_index
        same_doc = (ext_docs[begin_row : begin_row + tok_count] == ext_docs[edge_rows:])[:, None]
        masked_grad = jnp.where(same_doc, d_conv, 0.0)
        tap_grads.append(
            jnp.sum(
                masked_grad * extended[begin_row : begin_row + tok_count].astype(f32), axis=0
            )
        )
        d_extended = d_extended + jnp.pad(
            masked_grad * weights[tap_index][None, :], ((begin_row, edge_rows - begin_row), (0, 0))
        )
    return (d_extended, jnp.stack(tap_grads))


def span_ssd(
    start_state, inputs_x, inputs_b, inputs_c, step_sizes, log_decay, span_docs, before_doc
):
    length = inputs_x.shape[0]
    cumulative = jnp.cumsum(log_decay, axis=0)
    order = jnp.arange(length)
    linked = (span_docs[:, None] == span_docs[None, :]) & (order[:, None] >= order[None, :])
    gaps = jnp.where(linked[:, :, None], cumulative[:, None, :] - cumulative[None, :, :], neg_large)
    inner = jnp.dot(inputs_c, inputs_b.T, precision=top_prec)
    pair_weights = jnp.exp(gaps) * inner[:, :, None] * step_sizes[None, :, :]
    y_inner = jnp.einsum("tsh,shp->thp", pair_weights, inputs_x, precision=top_prec)
    carried = span_docs == before_doc
    entry_decay = jnp.where(carried[:, None], jnp.exp(cumulative), 0.0)
    y_state = (
        jnp.einsum("tn,hpn->thp", inputs_c, start_state, precision=top_prec)
        * entry_decay[:, :, None]
    )
    tail = (
        jnp.where(
            (span_docs == span_docs[-1])[:, None],
            jnp.exp(cumulative[-1][None, :] - cumulative),
            0.0,
        )
        * step_sizes
    )
    new_state = (
        jnp.einsum("sh,shp,sn->hpn", tail, inputs_x, inputs_b, precision=top_prec)
        + entry_decay[-1][:, None, None] * start_state
    )
    return (y_inner + y_state, new_state)


def rope_tables(positions, pairs):
    freqs = rope_base ** (-2.0 * pairs.astype(f32) / HDIM)
    angles = positions.astype(f32)[:, None] * freqs[None, :]
    return jnp.cos(angles), jnp.sin(angles)


def shards(
    hidden_in,
    grad_out,
    doc_starts,
    norm_mixer,
    norm_ffn,
    mamba_z,
    mamba_x,
    mamba_bc,
    mamba_dt,
    conv_x,
    conv_bc,
    a_log,
    dt_bias,
    skip_gain,
    mamba_out,
    attn_query,
    attn_key,
    attn_value,
    attn_out,
    ffn_gate,
    ffn_up,
    ffn_down,
):
    own = hidden_in.shape[0]
    width = hidden_in.shape[1]
    nz, n_p = lax.axis_size("z"), lax.axis_size("p")
    zi, pi, ci = lax.axis_index("z"), lax.axis_index("p"), lax.axis_index("head")
    tok = own * n_p
    base = zi * tok
    positions = base + jnp.arange(tok, dtype=jnp.int32)
    edge = conv_x.shape[0] - 1
    ext_docs = doc_ids(base - edge + jnp.arange(tok + edge, dtype=jnp.int32), doc_starts)
    docs_here = ext_docs[edge:]
    prev_doc = ext_docs[edge - 1]
    rows = mamba_z.shape[0]
    n_heads = a_log.shape[0] // n_p
    xw = n_heads * MHDIM
    bcw = mamba_bc.shape[1] // (2 * n_p)
    kw = HDIM // n_p
    hk = kw // 2
    nchunk = tok // SPAN
    score_scale = HDIM ** (-0.5)

    def cols(w):
        w = w.astype(bf16)
        return w.reshape(w.shape[0], n_p, -1).transpose(1, 0, 2)

    def perm_cols(w):
        w = w.astype(bf16).reshape(rows, 2, n_p, hk)
        return w.transpose(2, 0, 1, 3).reshape(n_p, rows, kw)

    bc_mine = lax.dynamic_slice_in_dim(mamba_bc, ci * (bcw * n_p), bcw * n_p, 1)
    dt_cols = jnp.pad(cols(mamba_dt), ((0, 0), (0, 0), (0, 128 - n_heads)))
    q_cols = attn_query.astype(bf16).reshape(rows, n_p, 2, n_p, hk)
    q_cols = q_cols.transpose(1, 0, 3, 2, 4).reshape(n_p, rows, HDIM)
    pieces = [
        jnp.concatenate(
            [cols(mamba_x), cols(bc_mine), perm_cols(attn_key), cols(attn_value), dt_cols], axis=2
        ),
        jnp.concatenate([q_cols, cols(mamba_z)], axis=2),
        jnp.concatenate([cols(mamba_out.T), cols(attn_out.T)], axis=2),
        jnp.concatenate([cols(ffn_gate), cols(ffn_up)], axis=2),
        cols(ffn_down.T),
    ]

    def fetch(piece):
        piece = lax.all_to_all(piece, "p", 0, 0, tiled=True)
        piece = piece.reshape(n_p * rows, piece.shape[2])
        return lax.all_gather(piece, "z", axis=0, tiled=True)

    w_a, w_b, w_c, w_d, w_e = [fetch(piece) for piece in pieces]

    gains = lax.all_gather(
        jnp.stack([norm_mixer, norm_ffn]).astype(bf16), ("z", "p"), axis=1, tiled=True
    )
    gain_mix, gain_ffn = gains[0], gains[1]
    scale_one, normed_own = norm_rows(hidden_in, gain_mix)
    both = lax.all_gather(
        jnp.stack([normed_own, grad_out.astype(bf16)]), "p", axis=1, tiled=True
    )
    normed_one, g_ffn = both[0], both[1]

    in_a = product(normed_one, w_a)
    in_b = product(normed_one, w_b)
    pre = in_a[:, : xw + bcw].astype(bf16)
    dt_raw = in_a[:, xw + bcw + 2 * kw : xw + bcw + 2 * kw + n_heads]
    gate_z = in_b[:, HDIM:]
    taps = jnp.concatenate(
        [
            lax.dynamic_slice_in_dim(conv_x, pi * xw, xw, 1),
            lax.dynamic_slice_in_dim(conv_bc, (ci * n_p + pi) * bcw, bcw, 1),
        ],
        axis=1,
    )
    prev_rows = passed_along(pre[tok - edge :], "z", 1)
    ext = jnp.concatenate([prev_rows, pre], axis=0)
    conv_in = convolve(ext, taps, ext_docs, tok)
    ssm = jax.nn.silu(conv_in).astype(bf16)
    head_slice = lambda v: lax.dynamic_slice_in_dim(v, pi * n_heads, n_heads, 0)
    my_bias, my_a, my_skip = head_slice(dt_bias), head_slice(a_log), head_slice(skip_gain)
    dt_pre = dt_raw + my_bias[None, :]
    dt_val = jax.nn.softplus(dt_pre)
    log_decay = -jnp.exp(my_a)[None, :] * dt_val
    x_heads = ssm[:, :xw].astype(f32).reshape(tok, n_heads, MHDIM)
    bc_all = lax.all_gather(ssm[:, xw:], ("p", "head"), axis=0)
    bc_all = bc_all.reshape(n_p, 2, tok, bcw).transpose(1, 2, 0, 3).reshape(2, tok, n_p * bcw)
    b_mat, c_mat = bc_all[0].astype(f32), bc_all[1].astype(f32)
    pair_ids = pi * hk + jnp.arange(hk)
    cos_k, sin_k = rope_tables(positions, pair_ids)
    k_pre = in_a[:, xw + bcw : xw + bcw + kw]
    k0, k1 = k_pre[:, :hk], k_pre[:, hk:]
    key_own = jnp.concatenate([k0 * cos_k - k1 * sin_k, k1 * cos_k + k0 * sin_k], axis=1)
    val_own = in_a[:, xw + bcw + kw : xw + bcw + 2 * kw]
    kv_own = jnp.concatenate([key_own, val_own], axis=1).astype(bf16)
    kv = lax.all_gather(kv_own, ("z", "p"), axis=0)
    kv = kv.reshape(nz, n_p, tok, 2 * kw).transpose(0, 2, 1, 3).reshape(nz * tok, n_p, 2 * kw)
    keys = kv[:, :, :kw].reshape(nz * tok, HDIM)
    values = kv[:, :, kw:].reshape(nz * tok, HDIM)
    cos_q, sin_q = rope_tables(positions, jnp.arange(HDIM // 2))
    cos_q, sin_q = cos_q.reshape(tok, n_p, hk), sin_q.reshape(tok, n_p, hk)

    def rope_q(v, sign):
        v = v.reshape(tok, n_p, 2, hk)
        a, b = v[:, :, 0], v[:, :, 1]
        return jnp.stack(
            [a * cos_q - sign * b * sin_q, b * cos_q + sign * a * sin_q], axis=2
        ).reshape(tok, HDIM)

    queries = rope_q(in_b[:, :HDIM], 1.0).astype(bf16)

    span_prev = jnp.concatenate([prev_doc[None], docs_here[SPAN - 1 :: SPAN][:-1]])

    def spanned(v):
        return v.reshape((nchunk, SPAN) + v.shape[1:])

    def forward_step(state_in, inputs):
        xs_c, b_c, c_c, dt_c, la_c, docs_c, before = inputs
        y_c, state_out = span_ssd(state_in, xs_c, b_c, c_c, dt_c, la_c, docs_c, before)
        return (state_out, (y_c, state_in))

    local_state, (y_spans, span_starts) = lax.scan(
        forward_step,
        jnp.zeros((n_heads, MHDIM, NSTATE), f32),
        (
            spanned(x_heads),
            spanned(b_mat),
            spanned(c_mat),
            spanned(dt_val),
            spanned(log_decay),
            spanned(docs_here),
            span_prev,
        ),
    )
    cum_dev = jnp.cumsum(log_decay, axis=0)
    dev_decay = jnp.where((docs_here == prev_doc)[:, None], jnp.exp(cum_dev), 0.0)
    total_decay = dev_decay[-1]
    in_decay, in_state = carried_in(
        (total_decay, local_state),
        "z",
        link_states,
        (jnp.ones_like(total_decay), jnp.zeros_like(local_state)),
        False,
    )
    y_carry = jnp.einsum("tn,hpn->thp", c_mat, in_state, precision=top_prec) * dev_decay[:, :, None]
    y_heads = (
        y_spans.reshape(tok, n_heads, MHDIM) + y_carry + my_skip[None, :, None] * x_heads
    )
    y_flat = y_heads.reshape(tok, xw)
    silu_z = jax.nn.silu(gate_z)
    gated = (y_flat * silu_z).astype(bf16)

    key_pos = jnp.arange(nz * tok, dtype=jnp.int32)
    key_docs = doc_ids(key_pos, doc_starts)
    visible = (positions[:, None] >= key_pos[None, :]) & (docs_here[:, None] == key_docs[None, :])
    scores = product_nt(queries, keys) * score_scale
    scores = jnp.where(visible, scores, neg_large)
    row_max = jnp.max(scores, axis=1, keepdims=True)
    weights = jnp.where(visible, jnp.exp(scores - row_max), 0.0)
    row_sum = jnp.sum(weights, axis=1, keepdims=True)
    probs = weights / row_sum
    probs_low = probs.astype(bf16)
    attn_f32 = product(probs_low, values)
    attn_low = attn_f32.astype(bf16)

    def plane_sum(part):
        part = lax.psum_scatter(part, "p", scatter_dimension=0, tiled=True)
        return lax.psum(part, "head")

    mixed = jnp.concatenate([gated, attn_low], axis=1)
    mid = hidden_in + plane_sum(product_nt(mixed, w_c))
    scale_two, normed_two_own = norm_rows(mid, gain_ffn)
    normed_two = lax.all_gather(normed_two_own, "p", axis=0, tiled=True)
    gu = product(normed_two, w_d)
    ffw = gu.shape[1] // 2
    gate_val, up_val = gu[:, :ffw], gu[:, ffw:]
    silu_gate = jax.nn.silu(gate_val)
    activated = (silu_gate * up_val).astype(bf16)
    block_out = mid + plane_sum(product_nt(activated, w_e))

    grad_e = product_t(g_ffn, activated)
    d_act = product(g_ffn, w_e)
    d_gu = jnp.concatenate(
        [d_act * up_val * silu_slope(gate_val), d_act * silu_gate], axis=1
    ).astype(bf16)
    grad_d = product_t(normed_two, d_gu)
    d_two = plane_sum(product_nt(d_gu, w_d))
    d_mid_norm, grad_gain_ffn = norm_back(mid, scale_two, gain_ffn, d_two)
    d_mid = grad_out + d_mid_norm
    g_mid = lax.all_gather(d_mid.astype(bf16), "p", axis=0, tiled=True)
    grad_c = product_t(g_mid, mixed)
    d_mixed = product(g_mid, w_c)
    d_gated = d_mixed[:, :xw]
    d_attn = d_mixed[:, xw:].astype(bf16)
    d_y_flat = d_gated * silu_z
    d_z = (d_gated * y_flat * silu_slope(gate_z)).astype(bf16)
    d_y_heads = d_y_flat.reshape(tok, n_heads, MHDIM)
    grad_skip = jnp.sum(d_y_heads * x_heads, axis=(0, 2))

    d_in_local = jnp.einsum("th,thp,tn->hpn", dev_decay, d_y_heads, c_mat, precision=top_prec)
    out_decay, state_grad = carried_in(
        (total_decay, d_in_local),
        "z",
        link_states,
        (jnp.ones_like(total_decay), jnp.zeros_like(d_in_local)),
        True,
    )
    before_cum = jnp.concatenate([jnp.zeros((1, n_heads), f32), cum_dev[:-1]], axis=0)[::SPAN]
    start_decay = jnp.where((span_prev == prev_doc)[:, None], jnp.exp(before_cum), 0.0)
    true_starts = span_starts + start_decay[:, :, None, None] * in_state[None]

    def back_step(grad_state, inputs):
        start_state, xs_c, b_c, c_c, dt_c, la_c, docs_c, before, dy_c = inputs

        def local_span(state_arg, xs_arg, b_arg, c_arg, dt_arg, la_arg):
            return span_ssd(state_arg, xs_arg, b_arg, c_arg, dt_arg, la_arg, docs_c, before)

        ignored, pullback = jax.vjp(local_span, start_state, xs_c, b_c, c_c, dt_c, la_c)
        span_grad = pullback((dy_c, grad_state))
        return (span_grad[0], span_grad[1:])

    ignored_state, (d_xs_c, d_b_c, d_c_c, d_dt_c, d_la_c) = lax.scan(
        back_step,
        state_grad,
        (
            true_starts,
            spanned(x_heads),
            spanned(b_mat),
            spanned(c_mat),
            spanned(dt_val),
            spanned(log_decay),
            spanned(docs_here),
            span_prev,
            spanned(d_y_heads),
        ),
        reverse=True,
    )
    d_xs = d_xs_c.reshape(tok, n_heads, MHDIM) + my_skip[None, :, None] * d_y_heads
    d_log = d_la_c.reshape(tok, n_heads)
    grad_a_log = jnp.sum(d_log * log_decay, axis=0)
    d_dt_in = (
        d_dt_c.reshape(tok, n_heads) - jnp.exp(my_a)[None, :] * d_log
    ) * jax.nn.sigmoid(dt_pre)
    grad_dt_bias = jnp.sum(d_dt_in, axis=0)
    d_dt_raw = d_dt_in.astype(bf16)
    d_bc = jnp.stack([d_b_c.reshape(tok, NSTATE), d_c_c.reshape(tok, NSTATE)])
    d_bc = d_bc.reshape(2, tok, n_p, bcw).transpose(2, 0, 1, 3).reshape(2 * n_p * tok, bcw)
    d_bc = lax.psum_scatter(d_bc, ("p", "head"), scatter_dimension=0, tiled=True)
    du = jnp.concatenate([d_xs.reshape(tok, xw), d_bc], axis=1) * silu_slope(conv_in)
    d_ext, grad_taps = convolve_back(du, ext, taps, ext_docs, tok)
    next_rows = passed_along(d_ext[:edge], "z", -1)
    d_pre = (d_ext[edge:] + jnp.pad(next_rows, ((tok - edge, 0), (0, 0)))).astype(bf16)

    d_probs = product_nt(d_attn, values)
    delta = jnp.sum(d_attn.astype(f32) * attn_f32, axis=1, keepdims=True)
    d_scores = (probs * (d_probs - delta)).astype(bf16)
    d_query = product(d_scores, keys) * score_scale
    d_key = product_t(d_scores, queries) * score_scale
    d_value = product_t(probs_low, d_attn)
    d_q_pre = rope_q(d_query, -1.0).astype(bf16)
    d_kv = jnp.concatenate(
        [d_key.reshape(nz * tok, n_p, kw), d_value.reshape(nz * tok, n_p, kw)], axis=2
    )
    d_kv = d_kv.reshape(nz, tok, n_p, 2 * kw).transpose(0, 2, 1, 3)
    d_kv = d_kv.reshape(nz * n_p * tok, 2 * kw)
    d_kv = lax.psum_scatter(d_kv, ("z", "p"), scatter_dimension=0, tiled=True)
    dk0, dk1 = d_kv[:, :hk], d_kv[:, hk:kw]
    d_kv_low = jnp.concatenate(
        [dk0 * cos_k + dk1 * sin_k, dk1 * cos_k - dk0 * sin_k, d_kv[:, kw:]], axis=1
    ).astype(bf16)
    d_a = jnp.concatenate(
        [d_pre, d_kv_low, jnp.pad(d_dt_raw, ((0, 0), (0, 128 - n_heads)))], axis=1
    )
    d_b = jnp.concatenate([d_q_pre, d_z], axis=1)
    grad_a = product_t(normed_one, d_a)
    grad_b = product_t(normed_one, d_b)
    d_one = plane_sum(product_nt(d_a, w_a) + product_nt(d_b, w_b))
    d_in_norm, grad_gain_mix = norm_back(hidden_in, scale_one, gain_mix, d_one)
    grad_in = d_mid + d_in_norm

    def give(grad):
        grad = lax.psum_scatter(grad.astype(bf16), "z", scatter_dimension=0, tiled=True)
        grad = grad.reshape(n_p, rows, grad.shape[1])
        return lax.all_to_all(grad, "p", 0, 0, tiled=True).astype(f32)

    ga, gb, gc, gd, ge = [give(g) for g in (grad_a, grad_b, grad_c, grad_d, grad_e)]

    def uncols(g):
        return g.transpose(1, 0, 2).reshape(rows, -1)

    g_x = uncols(ga[:, :, :xw])
    g_bc = lax.all_gather(uncols(ga[:, :, xw : xw + bcw]), "head", axis=1, tiled=True)
    g_k = ga[:, :, xw + bcw : xw + bcw + kw].reshape(n_p, rows, 2, hk)
    g_k = g_k.transpose(1, 2, 0, 3).reshape(rows, HDIM)
    g_v = uncols(ga[:, :, xw + bcw + kw : xw + bcw + 2 * kw])
    g_dt = uncols(ga[:, :, xw + bcw + 2 * kw : xw + bcw + 2 * kw + n_heads])
    g_q = gb[:, :, :HDIM].reshape(n_p, rows, n_p, 2, hk)
    g_q = g_q.transpose(1, 0, 3, 2, 4).reshape(rows, n_p * HDIM)
    g_z = uncols(gb[:, :, HDIM:])
    g_mout = uncols(gc[:, :, :xw]).T
    g_aout = uncols(gc[:, :, xw:]).T
    g_gate = uncols(gd[:, :, :ffw])
    g_up = uncols(gd[:, :, ffw:])
    g_down = uncols(ge).T

    spread_x = lax.dynamic_update_slice(jnp.zeros(conv_x.shape, f32), grad_taps[:, :xw], (0, pi * xw))
    spread_bc = lax.dynamic_update_slice(
        jnp.zeros(conv_bc.shape, f32), grad_taps[:, xw:], (0, (ci * n_p + pi) * bcw)
    )
    per_head = jnp.stack([grad_a_log, grad_dt_bias, grad_skip])
    spread_h = lax.dynamic_update_slice(
        jnp.zeros((3, a_log.shape[0]), f32), per_head, (0, pi * n_heads)
    )
    s_x, s_h, s_mix, s_ffn = lax.psum(
        (spread_x, spread_h, grad_gain_mix, grad_gain_ffn), ("z", "p")
    )
    s_bc = lax.psum(spread_bc, ("z", "p", "head"))
    si = zi * n_p + pi
    s_mix = lax.dynamic_slice_in_dim(s_mix, si * rows, rows, 0)
    s_ffn = lax.dynamic_slice_in_dim(s_ffn, si * rows, rows, 0)
    return (
        block_out,
        grad_in,
        s_mix,
        s_ffn,
        g_z,
        g_x,
        g_bc,
        g_dt,
        s_x,
        s_bc,
        s_h[0],
        s_h[1],
        s_h[2],
        g_mout,
        g_q,
        g_k,
        g_v,
        g_aout,
        g_gate,
        g_up,
        g_down,
    )


def solution(mesh):
    seq, head = mesh.shape["seq"], mesh.shape["head"]
    plane = math.gcd(seq, 4)
    grid = Mesh(mesh.devices.reshape(seq // plane, plane, head), ("z", "p", "head"))
    s = ("z", "p")
    h = "head"
    placed = (
        P(s, None), P(s, None), P(), P(s), P(s), P(s, h), P(s, h), P(s, None), P(s, h),
        P(None, h), P(), P(h), P(h), P(h), P(h, s), P(s, h), P(s, h), P(s, h), P(h, s),
        P(s, h), P(s, h), P(h, s),
    )
    given = (
        P(s, None), P(s, None), P(s), P(s), P(s, h), P(s, h), P(s, None), P(s, h),
        P(None, h), P(), P(h), P(h), P(h), P(h, s), P(s, h), P(s, h), P(s, h), P(h, s),
        P(s, h), P(s, h), P(h, s),
    )
    return jax.shard_map(shards, mesh=grid, in_specs=placed, out_specs=given, check_vma=False)
```

time: 4250 us -> 2250 us (0.53)
  waiting for transfers between devices: 3080 us -> 954 us
  local copies, waits for them, and re-layouts: 209 us -> 440 us
  blocking collectives: 390 us -> 255 us
  other arithmetic: 167 us -> 215 us
    reduce_scatter x12 -> x11, waiting for transfers between devices: 2080 us -> 574 us  [the longest x4 296 us: plane_sum(): part = lax.psum_scatter(part, 'p', scatter_dimension=0, tiled=True)]
    all_gather x2, waiting for transfers between devices: 404 us -> 31.5 us  [carried_in(): pieces = jax.tree.map(lambda part: lax.all_gather(part, axis), value)]
    all_gather x13 -> x10, waiting for transfers between devices: 565 us -> 306 us  [the longest x5 110 us: fetch(): return lax.all_gather(piece, 'z', axis=0, tiled=True)]
    all_gather x7 -> x2, blocking collectives: 275 us -> 42 us  [the longest x1 40 us: shards(): lax.all_gather(jnp.stack([norm_mixer, norm_ffn]).astype(bf16), ('z', 'p')...]
    dynamic_update_slice x2 -> x51, local copies, waits for them, and re-layouts: 38.1 us -> 188 us  [the longest x16 97.3 us: shards(): lax.scan(forward_step, jnp.zeros((n_heads, MHDIM, NSTATE), f32), (spanned...]
    psum x0 -> x2, blocking collectives: none -> 117 us  [the longest x1 76.1 us: shards(): lax.psum((spread_x, spread_h, grad_gain_mix, grad_gain_ffn), ('z', 'p'))]
    dot_general x39 -> x7, matrix products: 157 us -> 46.4 us  [product(): return jnp.dot(left, right, preferred_element_type=f32)]
    all_to_all x0 -> x6, blocking collectives: none -> 83.7 us  [the longest x4 53.7 us: fetch(): piece = lax.all_to_all(piece, 'p', 0, 0, tiled=True)]
  transfers between devices with their start and end apart: 38 -> 32, of which waited for: 26 -> 21; matrix products, arithmetic and copies ran while one was open for 16% -> 19% of each run, Pallas kernels for 0% -> 0%
where the time goes in v1:
time: 2250 us; the launch traced here: 2230 us
  waiting for transfers between devices  954 us (42%)
  local copies, waits for them, and re-layouts  440 us (20%)
  matrix products  323 us (14%)
  blocking collectives  255 us (11%)
  other arithmetic  215 us (10%)
  starting transfers between devices  22.9 us (1%)
    reduce_scatter x4, waiting for transfers between devices, plane_sum(): part = lax.psum_scatter(part, 'p', scatter_dimension=0, tiled=True)  296 us
    reduce_scatter x5, waiting for transfers between devices, give(): lax.psum_scatter(grad.astype(bf16), 'z', scatter_dimension=0, tiled=True)  226 us
    all_gather x5, waiting for transfers between devices, fetch(): return lax.all_gather(piece, 'z', axis=0, tiled=True)  110 us
    dynamic_update_slice x16, local copies, waits for them, and re-layouts, shards(): lax.scan(forward_step, jnp.zeros((n_heads, MHDIM, NSTATE), f32), (spanned...  97.3 us
    dynamic_update_slice x32, local copies, waits for them, and re-layouts, shards(): lax.scan(back_step, state_grad, (true_starts, spanned(x_heads), spanned(b...  90.3 us
    all_gather x1, waiting for transfers between devices, shards(): lax.all_gather(jnp.stack([normed_own, grad_out.astype(bf16)]), 'p', axis=...  88.8 us
    psum x1, blocking collectives, shards(): lax.psum((spread_x, spread_h, grad_gain_mix, grad_gain_ffn), ('z', 'p'))  76.1 us
    unnamed x245, local copies, waits for them, and re-layouts  57.4 us
  transfers between devices with their start and end apart: 32, of which 21 were waited for; matrix products, arithmetic and copies ran while one was open for 19% of the time, Pallas kernels for 0%

profile of v1, /device:TPU:0, one launch (start us, length us, event | category | flops | bytes accessed | tf_op | source)
XLA Modules:
  0.0 2227.6 jit_solution(3817521618536511206)
XLA Ops:
  13.3 15.1 all_to_all.50
  29.6 40.0 %all_gather.56 = bf16[2,2048]{1,0:T(2,128)(2,1)S(1)} all-gather(bf16[2,128]{1,0:T(2,128)(2,1)S(1)} %pad_maximum_fusion.20), channel_id=1, replica_groups=mesh['z'=4,'p'=4,'head'=2] {'z','p'}, dimensions={1}, use_global_device_ids=true | all-gather | bytes 8704 | tf_op jit(solution)/shard_map/all_gather | solution.py:229
  77.1 7.1 all-gather.19.cloned.1.call-done
  84.3 88.8 %all-gather.17.cloned.1.call-done = bf16[2,1024,2048]{2,1,0:T(8,128)(2,1)} async-done(((bf16[2,256,2048]{2,1,0:T(8,128)(2,1)}), bf16[2,1024,2048]{2,1,0:T(8,128)(2,1)}) %all-gather.17.cloned.1.call-update) | async-done | bytes 8388624 | tf_op jit(solution)/shard_map/all_gather | solution.py:234
  173.0 7.4 fusion.187
  192.4 10.4 all_to_all.51
  233.3 148.7 %while.68 = (s32[]{:T(128)}, f32[6,64,256]{2,1,0:T(8,128)S(1)}, f32[8,128,6,64]{1,0,3,2:T(8,128)}, f32[8,6,64,256]{3,2,1,0:T(8,128)}, s32[8,128]{1,0:T(8,128)}, ...) while((s32[]{:T(128)}, f32[6,64,256]{2,1,0:T(8,128)S(1)}, ...), condition=%wide.region_4.5_spmd.clone, body=%wide.region_2.4_spmd.clone.sunk | while | flops 429001216 | bytes 4107601 | solution.py:297
  391.3 6.2 all-to-all-done.2
  402.0 12.8 all-gather.3
  447.1 6.4 fusion.99
  453.6 10.5 fusion.98
  482.7 7.5 fusion.133
  490.3 83.8 %reduce-scatter.12.cloned.1.call-done = f32[256,2048]{1,0:T(8,128)} async-done(((f32[1024,2048]{1,0:T(8,128)}), f32[256,2048]{1,0:T(8,128)}) %reduce-scatter.12.cloned.1.call-update) | async-done | bytes 2097168 | tf_op jit(solution)/shard_map/reduce_scatter | solution.py:342
  579.8 17.5 all_to_all.52
  604.4 10.7 all_to_all.53
  616.6 64.6 %all-gather.29.cloned.1.call-done = bf16[2048,1024]{1,0:T(8,128)(2,1)} async-done(((bf16[512,1024]{1,0:T(8,128)(2,1)}), bf16[2048,1024]{1,0:T(8,128)(2,1)}) %all-gather.29.cloned.1.call-update) | async-done | bytes 4194320 | tf_op jit(solution)/shard_map/all_gather | solution.py:225
  681.1 53.7 %all-gather.27.cloned.1.call-done = bf16[1024,2048]{1,0:T(8,128)(2,1)} async-done(((bf16[256,2048]{1,0:T(8,128)(2,1)}), bf16[1024,2048]{1,0:T(8,128)(2,1)}) %all-gather.27.cloned.1.call-update) | async-done | bytes 4194320 | tf_op jit(solution)/shard_map/all_gather | solution.py:348
  734.8 10.0 fusion.189
  744.8 38.0 %all-gather.31.cloned.1.call-done = bf16[2048,512]{1,0:T(8,128)(2,1)} async-done(((bf16[512,512]{1,0:T(8,128)(2,1)}), bf16[2048,512]{1,0:T(8,128)(2,1)}) %all-gather.31.cloned.1.call-update) | async-done | bytes 2097168 | tf_op jit(solution)/shard_map/all_gather | solution.py:225
  782.8 8.3 multiply_convert_fusion.2
  792.4 6.9 fusion.127
  799.3 85.2 %reduce-scatter.16.cloned.1.call-done = f32[256,2048]{1,0:T(8,128)} async-done(((f32[1024,2048]{1,0:T(8,128)}), f32[256,2048]{1,0:T(8,128)}) %reduce-scatter.16.cloned.1.call-update) | async-done | bytes 2097168 | tf_op jit(solution)/shard_map/reduce_scatter | solution.py:342
  884.6 23.5 %all-reduce.18.cloned.1.call-done = f32[256,2048]{1,0:T(8,128)} async-done(((f32[256,2048]{1,0:T(8,128)}), f32[256,2048]{1,0:T(8,128)}) %all-reduce.18.cloned.1.call-update) | async-done | bytes 2097168 | tf_op jit(solution)/shard_map/psum | solution.py:343
  913.6 53.8 %all-gather.33.cloned.1.call-done = bf16[1024,2048]{1,0:T(8,128)(2,1)} async-done(((bf16[256,2048]{1,0:T(8,128)(2,1)}), bf16[1024,2048]{1,0:T(8,128)(2,1)}) %all-gather.33.cloned.1.call-update) | async-done | bytes 4194320 | tf_op jit(solution)/shard_map/all_gather | solution.py:365
  985.4 31.5 %all-gather.39.cloned.1.call-done = f32[24,64,256]{2,1,0:T(8,128)} async-done(((f32[6,64,256]{2,1,0:T(8,128)}), f32[24,64,256]{2,1,0:T(8,128)}) %all-gather.39.cloned.1.call-update) | async-done | bytes 1572880 | tf_op jit(solution)/shard_map/all_gather | solution.py:64
  1028.1 442.3 %while.67 = (s32[]{:T(128)}, f32[6,64,256]{2,1,0:T(8,128)S(1)}, f32[8,128,6,64]{1,0,3,2:T(8,128)}, f32[8,128,256]{1,0,2:T(8,128)}, f32[8,128,256]{1,0,2:T(8,128)...) while((s32[]{:T(128)}, f32[6,64,256]{2,1,0:T(8,128)S(1)}, ...), condition=%wide.region_32.33_spmd, body=%wide.region_22.32_spmd.sunk | while | flops 1059780352 | bytes 9995809 | solution.py:397
  1484.3 7.8 multiply_convert_fusion
  1506.0 8.7 fusion.100
  1527.9 6.1 reshape.715
  1535.2 7.3 fusion.190
  1543.3 6.6 convolution_multiply_fusion.3
  1564.5 10.5 collective-permute-done.1
  1575.4 52.2 %reduce-scatter.20.cloned.1.call-done = f32[1024,64]{0,1:T(8,128)} async-done(((f32[16384,64]{0,1:T(8,128)}), f32[1024,64]{0,1:T(8,128)}) %reduce-scatter.20.cloned.1.call-update) | async-done | bytes 262160 | tf_op jit(solution)/shard_map/reduce_scatter | solution.py:441
  1642.4 6.5 fusion.106
  1648.9 9.6 convolution_convert_fusion
  1659.7 6.2 convolution_convert_fusion.2
  1672.2 7.2 convolution_convert_fusion.1
  1679.5 37.6 %reduce-scatter.14.cloned.1.call-done = f32[256,2048]{1,0:T(8,128)} async-done(((f32[1024,2048]{1,0:T(8,128)}), f32[256,2048]{1,0:T(8,128)}) %reduce-scatter.14.cloned.1.call-update) | async-done | bytes 2097168 | tf_op jit(solution)/shard_map/reduce_scatter | solution.py:342
  1717.1 89.3 %reduce-scatter.22.cloned.1.call-done = f32[256,2048]{1,0:T(8,128)} async-done(((f32[1024,2048]{1,0:T(8,128)}), f32[256,2048]{1,0:T(8,128)}) %reduce-scatter.22.cloned.1.call-update) | async-done | bytes 2097168 | tf_op jit(solution)/shard_map/reduce_scatter | solution.py:342
  1806.4 46.3 %reduce-scatter.32.cloned.1.call-done = bf16[512,512]{1,0:T(8,128)(2,1)} async-done(((bf16[2048,512]{1,0:T(8,128)(2,1)}), bf16[512,512]{1,0:T(8,128)(2,1)}) %reduce-scatter.32.cloned.1.call-update) | async-done | bytes 524304 | tf_op jit(solution)/shard_map/reduce_scatter | solution.py:457
  1852.7 12.1 all_to_all.54
  1864.7 66.3 %reduce-scatter.30.cloned.1.call-done = bf16[512,1024]{1,0:T(8,128)(2,1)} async-done(((bf16[2048,1024]{1,0:T(8,128)(2,1)}), bf16[512,1024]{1,0:T(8,128)(2,1)}) %reduce-scatter.30.cloned.1.call-update) | async-done | bytes 1048592 | tf_op jit(solution)/shard_map/reduce_scatter | solution.py:457
  1931.1 17.9 all_to_all.55
  1949.0 28.9 %reduce-scatter.28.cloned.1.call-done = bf16[512,512]{1,0:T(8,128)(2,1)} async-done(((bf16[2048,512]{1,0:T(8,128)(2,1)}), bf16[512,512]{1,0:T(8,128)(2,1)}) %reduce-scatter.28.cloned.1.call-update) | async-done | bytes 524304 | tf_op jit(solution)/shard_map/reduce_scatter | solution.py:457
  1983.7 40.1 %reduce-scatter.24.cloned.1.call-done = bf16[512,512]{1,0:T(8,128)(2,1)} async-done(((bf16[2048,512]{1,0:T(8,128)(2,1)}), bf16[512,512]{1,0:T(8,128)(2,1)}) %reduce-scatter.24.cloned.1.call-update) | async-done | bytes 524304 | tf_op jit(solution)/shard_map/reduce_scatter | solution.py:457
  2033.5 44.1 %reduce-scatter.26.cloned.1.call-done = bf16[512,640]{1,0:T(8,128)(2,1)} async-done(((bf16[2048,640]{1,0:T(8,128)(2,1)}), bf16[512,640]{1,0:T(8,128)(2,1)}) %reduce-scatter.26.cloned.1.call-update) | async-done | bytes 655376 | tf_op jit(solution)/shard_map/reduce_scatter | solution.py:457
  2087.8 40.6 %psum.70 = f32[4,512]{1,0:T(4,128)} all-reduce(f32[4,512]{1,0:T(4,128)S(1)} %dynamic_update_slice.65), channel_id=1, replica_groups=mesh['z'=4,'p'=4,'head'=2] {'z','p','head'}, use_global_device_ids=true, to_apply=%region_50.51 | all-reduce | flops 2048 | bytes 16384 | tf_op jit(solution)/shard_map/psum | solution.py:492
  2136.9 76.1 %all-reduce.10 = (f32[2048]{0:T(1024)S(1)}, f32[2048]{0:T(1024)S(1)}, f32[4,1536]{1,0:T(4,128)}, f32[3,24]{1,0:T(4,128)S(1)}) all-reduce(f32[2048]{0:T(1024)S(1)} %get-tuple-element.891, f32[2048]{0:T(1024)S(1)} %copy-done.64, f32[4,1536]{1,0:T(4,128)S(1)} %slice_dynamic-update-slice_fusion, ...), channel_id=1, replica_groups=mesh['z'=4,'p'=4,'head'=2] {'z','p'}, use_global_device_ids=true, to_apply=%region_40.41 | all-reduce | flops 10312 | bytes 82496 | tf_op jit(solution)/shard_map/psum | solution.py:489
  (1070 shorter events, 889.3 us)
Async XLA Ops:
  7.2 77.0 %all-gather.19.cloned.1.call-start = ((), (), s32[]{:S(2)}) async-start(), calls=%async_computation.22 | async-start | bytes 3276800 | tf_op jit(solution)/shard_map/all_gather | solution.py:225
  10.5 59.1 %copy-start.5 = (f32[256,2048]{1,0:T(8,128)S(1)}, f32[256,2048]{1,0:T(8,128)}, u32[]{:S(2)}) copy-start(f32[256,2048]{1,0:T(8,128)} %param.30) | copy-start | bytes 6291460
  29.5 143.5 %all-gather.17.cloned.1.call-start = ((), (), s32[]{:S(2)}) async-start(), calls=%async_computation.21 | async-start | bytes 10485760 | tf_op jit(solution)/shard_map/all_gather | solution.py:234
  29.6 41.4 %copy-start.14 = (f32[256,2048]{1,0:T(8,128)S(1)}, f32[256,2048]{1,0:T(8,128)}, u32[]{:S(2)}) copy-start(f32[256,2048]{1,0:T(8,128)} %param.31) | copy-start | bytes 6291460
  73.1 144.7 %all-gather.35.cloned.1.call-start = ((), (), s32[]{:S(2)}) async-start(), calls=%async_computation.43 | async-start | bytes 1179648 | tf_op jit(solution)/shard_map/all_gather | solution.py:261
  77.1 109.2 %copy-start.77 = (pred[1024]{0:T(1024)(128)(4,1)}, pred[1024]{0:T(1024)(128)(4,1)S(1)}, u32[]{:S(2)}) copy-start(pred[1024]{0:T(1024)(128)(4,1)S(1)} %get-tuple-element.1039) | copy-start | bytes 3076
  77.1 109.2 %copy-start.79 = (pred[1024]{0:T(1024)(128)(4,1)}, pred[1024]{0:T(1024)(128)(4,1)S(1)}, u32[]{:S(2)}) copy-start(pred[1024]{0:T(1024)(128)(4,1)S(1)} %get-tuple-element.1040) | copy-start | bytes 3076
  77.1 109.2 %copy-start.81 = (pred[1024]{0:T(1024)(128)(4,1)}, pred[1024]{0:T(1024)(128)(4,1)S(1)}, u32[]{:S(2)}) copy-start(pred[1024]{0:T(1024)(128)(4,1)S(1)} %get-tuple-element.1041) | copy-start | bytes 3076
  180.5 5.8 collective-permute-start
  190.9 223.9 %all-gather.21.cloned.1.call-start = ((), (), s32[]{:S(2)}) async-start(), calls=%async_computation.23 | async-start | bytes 2621440 | tf_op jit(solution)/shard_map/all_gather | solution.py:225
  203.8 221.8 %all-gather.23.cloned.1.call-start = ((), (), s32[]{:S(2)}) async-start(), calls=%async_computation.24 | async-start | bytes 2228224 | tf_op jit(solution)/shard_map/all_gather | solution.py:271
  212.9 260.7 %all-gather.37.cloned.1.call-start = ((), (), s32[]{:S(2)}) async-start(), calls=%async_computation.44 | async-start | bytes 1966080 | tf_op jit(solution)/shard_map/all_gather | solution.py:64
  385.8 11.7 all-to-all-start.2
  390.0 92.7 %all-gather.25.cloned.1.call-start = ((), (), s32[]{:S(2)}) async-start(), calls=%async_computation.25 | async-start | bytes 2621440 | tf_op jit(solution)/shard_map/all_gather | solution.py:225
  390.6 30.8 %copy-start.65 = (f32[4,16]{1,0:T(4,128)}, f32[4,16]{1,0:T(4,128)S(1)}, u32[]{:S(2)}) copy-start(f32[4,16]{1,0:T(4,128)S(1)} %multiply_power_fusion) | copy-start | bytes 772
  399.6 174.4 %reduce-scatter.12.cloned.1.call-start = ((), (), s32[]{:S(2)}) async-start(), calls=%async_computation.26 | async-start | bytes 10485760 | tf_op jit(solution)/shard_map/reduce_scatter | solution.py:342
  436.3 27.8 %copy-start.12 = (bf16[4096,4,32]{0,2,1:T(8,128)(2,1)}, bf16[4096,4,32]{0,2,1:T(8,128)(2,1)S(1)}, u32[]{:S(2)}) copy-start(bf16[4096,4,32]{0,2,1:T(8,128)(2,1)S(1)} %get-tuple-element.1019) | copy-start | bytes 3145732
  490.2 109.5 %all-reduce.16.cloned.1.call-start = ((), (), s32[]{:S(2)}) async-start(), calls=%async_computation.27 | async-start | bytes 4194304 | tf_op jit(solution)/shard_map/psum | solution.py:343
  574.1 107.1 %all-gather.29.cloned.1.call-start = ((), (), s32[]{:S(2)}) async-start(), calls=%async_computation.29 | async-start | bytes 5242880 | tf_op jit(solution)/shard_map/all_gather | solution.py:225
  599.7 135.1 %all-gather.27.cloned.1.call-start = ((), (), s32[]{:S(2)}) async-start(), calls=%async_computation.28 | async-start | bytes 5242880 | tf_op jit(solution)/shard_map/all_gather | solution.py:348
  604.2 178.5 %all-gather.31.cloned.1.call-start = ((), (), s32[]{:S(2)}) async-start(), calls=%async_computation.30 | async-start | bytes 2621440 | tf_op jit(solution)/shard_map/all_gather | solution.py:225
  616.1 268.5 %reduce-scatter.16.cloned.1.call-start = ((), (), s32[]{:S(2)}) async-start(), calls=%async_computation.32 | async-start | bytes 10485760 | tf_op jit(solution)/shard_map/reduce_scatter | solution.py:342
  799.3 108.8 %copy-start.8 = (f32[256,2048]{1,0:T(8,128)S(1)}, f32[256,2048]{1,0:T(8,128)}, u32[]{:S(2)}) copy-start(f32[256,2048]{1,0:T(8,128)} %copy-done.7) | copy-start | bytes 6291460
  799.3 108.8 %all-reduce.18.cloned.1.call-start = ((), (), s32[]{:S(2)}) async-start(), calls=%async_computation.33 | async-start | bytes 4194304 | tf_op jit(solution)/shard_map/psum | solution.py:343
  884.6 82.8 %all-gather.33.cloned.1.call-start = ((), (), s32[]{:S(2)}) async-start(), calls=%async_computation.34 | async-start | bytes 5242880 | tf_op jit(solution)/shard_map/all_gather | solution.py:365
  913.4 103.5 %all-gather.39.cloned.1.call-start = ((), (), s32[]{:S(2)}) async-start(), calls=%async_computation.45 | async-start | bytes 1966080 | tf_op jit(solution)/shard_map/all_gather | solution.py:64
  979.7 576.7 %reduce-scatter.18.cloned.1.call-start = ((), (), s32[]{:S(2)}) async-start(), calls=%async_computation.35 | async-start | bytes 2359296 | tf_op jit(solution)/shard_map/reduce_scatter | solution.py:423
  1115.3 23.4 %copy-start.103 = (s32[8]{0:T(128)S(1)}, s32[8]{0:T(128)}, u32[]{:S(2)}) copy-start(s32[8]{0:T(128)} %get-tuple-element.1616) | copy-start | bytes 100 | tf_op jit(solution)/shard_map/while
  1170.6 23.4 %copy-start.103 = (s32[8]{0:T(128)S(1)}, s32[8]{0:T(128)}, u32[]{:S(2)}) copy-start(s32[8]{0:T(128)} %get-tuple-element.1616) | copy-start | bytes 100 | tf_op jit(solution)/shard_map/while
  1281.2 23.4 %copy-start.103 = (s32[8]{0:T(128)S(1)}, s32[8]{0:T(128)}, u32[]{:S(2)}) copy-start(s32[8]{0:T(128)} %get-tuple-element.1616) | copy-start | bytes 100 | tf_op jit(solution)/shard_map/while
  1336.5 23.4 %copy-start.103 = (s32[8]{0:T(128)S(1)}, s32[8]{0:T(128)}, u32[]{:S(2)}) copy-start(s32[8]{0:T(128)} %get-tuple-element.1616) | copy-start | bytes 100 | tf_op jit(solution)/shard_map/while
  1391.7 23.4 %copy-start.103 = (s32[8]{0:T(128)S(1)}, s32[8]{0:T(128)}, u32[]{:S(2)}) copy-start(s32[8]{0:T(128)} %get-tuple-element.1616) | copy-start | bytes 100 | tf_op jit(solution)/shard_map/while
  1447.0 23.4 %copy-start.103 = (s32[8]{0:T(128)S(1)}, s32[8]{0:T(128)}, u32[]{:S(2)}) copy-start(s32[8]{0:T(128)} %get-tuple-element.1616) | copy-start | bytes 100 | tf_op jit(solution)/shard_map/while
  1482.8 144.8 %reduce-scatter.20.cloned.1.call-start = ((), (), s32[]{:S(2)}) async-start(), calls=%async_computation.36 | async-start | bytes 4456448 | tf_op jit(solution)/shard_map/reduce_scatter | solution.py:441
  1534.0 183.1 %reduce-scatter.14.cloned.1.call-start = ((), (), s32[]{:S(2)}) async-start(), calls=%async_computation.31 | async-start | bytes 10485760 | tf_op jit(solution)/shard_map/reduce_scatter | solution.py:342
  1542.6 263.8 %reduce-scatter.22.cloned.1.call-start = ((), (), s32[]{:S(2)}) async-start(), calls=%async_computation.37 | async-start | bytes 10485760 | tf_op jit(solution)/shard_map/reduce_scatter | solution.py:342
  1561.5 13.4 collective-permute-start.1
  1564.5 63.1 %copy-start.89 = (f32[16]{0:T(128)S(1)}, f32[16]{0:T(128)}, u32[]{:S(2)}) copy-start(f32[16]{0:T(128)} %copy-done.88) | copy-start | bytes 196
  1642.1 210.5 %reduce-scatter.32.cloned.1.call-start = ((), (), s32[]{:S(2)}) async-start(), calls=%async_computation.42 | async-start | bytes 2621440 | tf_op jit(solution)/shard_map/reduce_scatter | solution.py:457
  1648.9 282.2 %reduce-scatter.30.cloned.1.call-start = ((), (), s32[]{:S(2)}) async-start(), calls=%async_computation.41 | async-start | bytes 5242880 | tf_op jit(solution)/shard_map/reduce_scatter | solution.py:457
  1658.6 319.3 %reduce-scatter.28.cloned.1.call-start = ((), (), s32[]{:S(2)}) async-start(), calls=%async_computation.40 | async-start | bytes 2621440 | tf_op jit(solution)/shard_map/reduce_scatter | solution.py:457
  1665.9 357.9 %reduce-scatter.24.cloned.1.call-start = ((), (), s32[]{:S(2)}) async-start(), calls=%async_computation.38 | async-start | bytes 2621440 | tf_op jit(solution)/shard_map/reduce_scatter | solution.py:457
  1672.1 405.5 %reduce-scatter.26.cloned.1.call-start = ((), (), s32[]{:S(2)}) async-start(), calls=%async_computation.39 | async-start | bytes 3276800 | tf_op jit(solution)/shard_map/reduce_scatter | solution.py:457
  1679.4 455.3 %all-reduce.20.cloned.1.call-start = ((), (), s32[]{:S(2)}) async-start(), calls=%async_computation.46 | async-start | bytes 8388608 | tf_op jit(solution)/shard_map/psum | solution.py:343
  1977.9 48.0 %all-to-all-start.7 = ((bf16[4,128,512]{2,1,0:T(8,128)(2,1)}), bf16[4,128,512]{2,1,0:T(8,128)(2,1)}, u32[]{:S(2)}, u32[]{:S(2)}) async-start(bf16[4,128,512]{2,1,0:T(8,128)(2,1)} %bitcast.621), calls=%async_computation.16 | async-start | bytes 1048576 | tf_op jit(solution)/shard_map/all_to_all | solution.py:459
  2025.8 54.0 %all-to-all-start.5 = ((bf16[4,128,512]{1,2,0:T(8,128)(2,1)}), bf16[4,128,512]{1,2,0:T(8,128)(2,1)S(1)}, u32[]{:S(2)}, u32[]{:S(2)}) async-start(bf16[4,128,512]{1,2,0:T(8,128)(2,1)} %copy.338), calls=%async_computation.12 | async-start | bytes 1048576 | tf_op jit(solution)/shard_map/all_to_all | solution.py:459
  2032.3 47.6 %copy-start.86 = (f32[3,24]{1,0:T(4,128)}, f32[3,24]{1,0:T(4,128)S(1)}, u32[]{:S(2)}) copy-start(f32[3,24]{1,0:T(4,128)S(1)} %dynamic_update_slice.66) | copy-start | bytes 868
  2079.8 48.6 %all-to-all-start.6 = ((bf16[4,128,640]{1,2,0:T(8,128)(2,1)}), bf16[4,128,640]{1,2,0:T(8,128)(2,1)S(1)}, u32[]{:S(2)}, u32[]{:S(2)}) async-start(bf16[4,128,640]{1,2,0:T(8,128)(2,1)} %copy.339), calls=%async_computation.14 | async-start | bytes 1310720 | tf_op jit(solution)/shard_map/all_to_all | solution.py:459
  (139 other events, 873.8 us)
Sparse Core Ops, SparseCore 0:
  29.6 54.5 all-gather.18
  86.7 86.2 all-gather.16
  191.0 25.4 all-gather.34
  218.5 45.9 all-gather.20
  267.7 59.4 all-gather.22
  382.9 38.9 all-gather.36
  424.0 44.7 all-gather.24
  490.3 83.6 reduce-scatter.11
  576.5 21.1 all-reduce.15
  599.8 81.2 all-gather.28
  683.6 51.2 all-gather.26
  736.8 45.9 all-gather.30
  799.4 85.1 reduce-scatter.15
  886.9 21.1 all-reduce.17
  913.5 53.8 all-gather.32
  979.8 37.0 all-gather.38
  1482.9 40.0 reduce-scatter.17
  1534.1 93.4 reduce-scatter.19
  1631.0 86.0 reduce-scatter.13
  1720.0 86.3 reduce-scatter.21
  1808.8 43.8 reduce-scatter.31
  1855.0 76.0 reduce-scatter.29
  1933.5 44.3 reduce-scatter.27
  1980.6 43.1 reduce-scatter.23
  2026.2 51.4 reduce-scatter.25
  2080.2 28.2 all-reduce.19

commit v2 on v1

v2 whole, which is shorter than its diff:
```python
import functools
import math

import jax
import jax.numpy as jnp
from jax import lax
from jax.experimental import pallas as pl
from jax.experimental.pallas import tpu as pltpu
from jax.sharding import Mesh
from jax.sharding import PartitionSpec as P

MHDIM = 64
NSTATE = 256
HDIM = 128
SPAN = 128

eps_norm = 1e-05
rope_base = 100000000000.0
neg_large = -1e30
top_prec = lax.Precision.HIGHEST
bf16 = jnp.bfloat16
f32 = jnp.float32
MESH = pl.DeviceIdType.MESH
VMEM_LIMIT = 56 * 1024 * 1024


def doc_ids(positions, doc_starts):
    return jnp.sum((doc_starts[None, :] <= positions[:, None]).astype(jnp.int32), axis=1) - 1


def product(left, right):
    return jnp.dot(left, right, preferred_element_type=f32)


def product_t(left, right):
    return lax.dot_general(left, right, (((0,), (0,)), ((), ())), preferred_element_type=f32)


def product_nt(left, right):
    return lax.dot_general(left, right, (((1,), (1,)), ((), ())), preferred_element_type=f32)


def silu_slope(values):
    sigma_val = jax.nn.sigmoid(values)
    return sigma_val * (1.0 + values * (1.0 - sigma_val))


def passed_along(block, axis, distance):
    devices = range(lax.axis_size(axis))
    route = [(i - distance, i) for i in devices if i - distance in devices]
    return lax.ppermute(block, axis, route)


def convolve(extended, weights, ext_docs, tok_count):
    edge_rows = weights.shape[0] - 1
    summed = jnp.zeros((tok_count, extended.shape[1]), f32)
    for tap_index in range(weights.shape[0]):
        begin_row = edge_rows - tap_index
        same_doc = (ext_docs[begin_row : begin_row + tok_count] == ext_docs[edge_rows:])[:, None]
        summed = (
            summed
            + jnp.where(same_doc, extended[begin_row : begin_row + tok_count].astype(f32), 0.0)
            * weights[tap_index][None, :]
        )
    return summed


def convolve_back(d_conv, extended, weights, ext_docs, tok_count):
    edge_rows = weights.shape[0] - 1
    d_extended = jnp.zeros((tok_count + edge_rows, d_conv.shape[1]), f32)
    tap_grads = []
    for tap_index in range(weights.shape[0]):
        begin_row = edge_rows - tap_index
        same_doc = (ext_docs[begin_row : begin_row + tok_count] == ext_docs[edge_rows:])[:, None]
        masked_grad = jnp.where(same_doc, d_conv, 0.0)
        tap_grads.append(
            jnp.sum(
                masked_grad * extended[begin_row : begin_row + tok_count].astype(f32), axis=0
            )
        )
        d_extended = d_extended + jnp.pad(
            masked_grad * weights[tap_index][None, :], ((begin_row, edge_rows - begin_row), (0, 0))
        )
    return (d_extended, jnp.stack(tap_grads))


def tri_dot(a, b, dims=((1,), (0,))):
    return lax.dot_general(a, b, (dims, ((), ())), precision=top_prec, preferred_element_type=f32)


def dot_nn(a, b):
    return lax.dot_general(a, b, (((1,), (0,)), ((), ())), preferred_element_type=f32)


def dot_nt(a, b):
    return lax.dot_general(a, b, (((1,), (1,)), ((), ())), preferred_element_type=f32)


def dot_tn(a, b):
    return lax.dot_general(a, b, (((0,), (0,)), ((), ())), preferred_element_type=f32)


def iota2(shape, dim):
    return lax.broadcasted_iota(jnp.int32, shape, dim)


def docs_of(pos, starts_ref):
    count = jnp.where(starts_ref[0] <= pos, 1, 0)
    for i in range(1, starts_ref.shape[0]):
        count = count + jnp.where(starts_ref[i] <= pos, 1, 0)
    return count - 1


def softplus(v):
    return jnp.maximum(v, 0.0) + jnp.log(1.0 + jnp.exp(-jnp.abs(v)))


def head_maps(xw):
    lane_head = (iota2((128, xw), 1) // MHDIM == iota2((128, xw), 0)).astype(f32)
    row_head = (iota2((xw, 128), 0) // MHDIM == iota2((xw, 128), 1)).astype(f32)
    return lane_head, row_head


def span_setup(k, base_ref, starts_ref, dtp, nega):
    first = base_ref[0] + k * SPAN
    t_idx, s_idx = iota2((SPAN, SPAN), 0), iota2((SPAN, SPAN), 1)
    docs_t = docs_of(first + t_idx, starts_ref)
    docs_s = docs_of(first + s_idx, starts_ref)
    linked = (docs_t == docs_s) & (t_idx >= s_idx)
    dt = softplus(dtp)
    la = nega * dt
    tri = (t_idx >= s_idx).astype(f32)
    cum = tri_dot(tri, la)
    before = docs_of(first - 1, starts_ref)
    last_doc = docs_of(first + SPAN - 1, starts_ref)
    carried = jnp.where(docs_t == before, jnp.exp(cum), 0.0)
    cum_last = cum[SPAN - 1 : SPAN, :]
    tail = jnp.where(docs_t == last_doc, jnp.exp(cum_last - cum), 0.0)
    return docs_t, linked, dt, la, tri, cum, carried, tail


def ssd_forward_kernel(
    n_heads, base_ref, starts_ref, x_ref, b_ref, c_ref, dtp_ref, nega_ref, skip_ref,
    y_ref, span_ref, final_ref, decay_ref, state, running,
):
    k = pl.program_id(0)
    xw = n_heads * MHDIM

    @pl.when(k == 0)
    def _():
        state[...] = jnp.zeros_like(state)
        running[...] = jnp.zeros_like(running)

    docs_t, linked, dt, la, tri, cum, carried, tail = span_setup(
        k, base_ref, starts_ref, dtp_ref[...], nega_ref[...]
    )
    lane_head, row_head = head_maps(xw)
    prev_doc = docs_of(base_ref[0] - 1, starts_ref)
    decay_ref[...] = jnp.where(docs_t == prev_doc, jnp.exp(running[0:1, :] + cum), 0.0)
    running[...] = running[...] + cum[SPAN - 1 : SPAN, :]
    start = state[...]
    span_ref[0] = start
    x, b, c = x_ref[...], b_ref[...], c_ref[...]
    inner = dot_nt(c, b)
    cum_t, dt_t = cum.T, dt.T
    lane = iota2((SPAN, 128), 1)
    pieces = []
    for pair in range(n_heads // 2):
        xp = x[:, pair * 128 : pair * 128 + 128]
        got = []
        for h in (2 * pair, 2 * pair + 1):
            gap = jnp.where(linked, cum[:, h : h + 1] - cum_t[h : h + 1, :], neg_large)
            w = jnp.exp(gap) * inner * dt_t[h : h + 1, :]
            got.append(dot_nn(w.astype(bf16), xp))
        pieces.append(jnp.where(lane < MHDIM, got[0], got[1]))
    y = jnp.concatenate(pieces, axis=1)
    y = y + dot_nt(c, start.astype(bf16)) * tri_dot(carried, lane_head)
    xf = x.astype(f32)
    y_ref[...] = y + skip_ref[...] * xf
    xt = (xf * tri_dot(tail * dt, lane_head)).astype(bf16)
    keep = jnp.sum(row_head * carried[SPAN - 1 : SPAN, :], axis=1, keepdims=True)
    new = dot_tn(xt, b) + keep * start
    state[...] = new
    final_ref[...] = new


def ssd_forward(base, doc_starts, x, b, c, dtp, nega, skip):
    tok, xw = x.shape
    n_heads, nspan = xw // MHDIM, tok // SPAN
    row = lambda n: pl.BlockSpec((SPAN, n), lambda i: (i, 0))
    whole = lambda *s: pl.BlockSpec(s, lambda i: (0,) * len(s))
    smem = pl.BlockSpec(memory_space=pltpu.SMEM)
    return pl.pallas_call(
        functools.partial(ssd_forward_kernel, n_heads),
        grid=(nspan,),
        in_specs=[
            smem, smem, row(xw), row(NSTATE), row(NSTATE), row(128), whole(1, 128), whole(1, xw)
        ],
        out_specs=[
            row(xw),
            pl.BlockSpec((1, xw, NSTATE), lambda i: (i, 0, 0)),
            whole(xw, NSTATE),
            row(128),
        ],
        out_shape=[
            jax.ShapeDtypeStruct((tok, xw), f32),
            jax.ShapeDtypeStruct((nspan, xw, NSTATE), f32),
            jax.ShapeDtypeStruct((xw, NSTATE), f32),
            jax.ShapeDtypeStruct((tok, 128), f32),
        ],
        scratch_shapes=[pltpu.VMEM((xw, NSTATE), f32), pltpu.VMEM((8, 128), f32)],
        compiler_params=pltpu.CompilerParams(vmem_limit_bytes=VMEM_LIMIT),
        cost_estimate=pl.CostEstimate(
            flops=2 * tok * xw * NSTATE * 3, bytes_accessed=8 * tok * xw, transcendentals=0
        ),
        name="ssd_forward",
    )(base, doc_starts, x, b, c, dtp, nega, skip)


def ssd_backward_kernel(
    n_heads, base_ref, starts_ref, x_ref, b_ref, c_ref, dtp_ref, dy_ref, span_ref, decay_ref,
    nega_ref, skip_ref, in_ref, grad_ref,
    dx_ref, dbc_ref, ddt_ref, sums_ref, gskip_ref, gstate,
):
    step = pl.program_id(0)
    k = pl.num_programs(0) - 1 - step
    xw = n_heads * MHDIM

    @pl.when(step == 0)
    def _():
        gstate[...] = grad_ref[...]
        sums_ref[...] = jnp.zeros_like(sums_ref)
        gskip_ref[...] = jnp.zeros_like(gskip_ref)

    nega = nega_ref[...]
    docs_t, linked, dt, la, tri, cum, carried, tail = span_setup(
        k, base_ref, starts_ref, dtp_ref[...], nega
    )
    lane_head, row_head = head_maps(xw)
    begin = jnp.sum(row_head * decay_ref[0], axis=1, keepdims=True)
    start = span_ref[0] + begin * in_ref[...]
    start_low = start.astype(bf16)
    g = gstate[...]
    g_low = g.astype(bf16)
    x, b, c, dy = x_ref[...], b_ref[...], c_ref[...], dy_ref[...]
    dy_low = dy.astype(bf16)
    xf = x.astype(f32)
    inner = dot_nt(c, b)
    cum_t, dt_t = cum.T, dt.T
    lane = iota2((SPAN, 128), 1)
    row8 = iota2((SPAN, 128), 0)
    d_inner = jnp.zeros((SPAN, SPAN), f32)
    r_cols = jnp.zeros((SPAN, 128), f32)
    k_rows = jnp.zeros((SPAN, 128), f32)
    u_pieces = []
    for pair in range(n_heads // 2):
        xp = x[:, pair * 128 : pair * 128 + 128]
        dyp = dy_low[:, pair * 128 : pair * 128 + 128]
        got = []
        for j, h in enumerate((2 * pair, 2 * pair + 1)):
            mine = (lane < MHDIM) if j == 0 else (lane >= MHDIM)
            gap = jnp.where(linked, cum[:, h : h + 1] - cum_t[h : h + 1, :], neg_large)
            e = jnp.exp(gap)
            m = e * inner
            dyx = dot_nt(dyp, jnp.where(mine, xp, jnp.zeros_like(xp)))
            ed = dyx * dt_t[h : h + 1, :]
            d_inner = d_inner + e * ed
            pairs = m * ed
            r_cols = jnp.where(lane == h, jnp.sum(pairs, axis=1, keepdims=True), r_cols)
            k_rows = jnp.where(row8 == h, jnp.sum(pairs, axis=0, keepdims=True), k_rows)
            got.append(dot_tn(m.astype(bf16), dyp))
        u_pieces.append(jnp.where(lane < MHDIM, got[0], got[1]))
    u = jnp.concatenate(u_pieces, axis=1)
    dye = dy * tri_dot(carried, lane_head)
    dye_low = dye.astype(bf16)
    di_low = d_inner.astype(bf16)
    r_state = tri_dot(dye * dot_nt(c, start_low), row_head)
    u_state = dot_nt(b, g_low) * tri_dot(tail, lane_head)
    u = u + u_state
    dt_full = tri_dot(dt, lane_head)
    k_state = dt * tri_dot(xf * u_state, row_head)
    d_dt = tri_dot(xf * u, row_head)
    tail_x = (xf * tri_dot(tail * dt, lane_head)).astype(bf16)
    dx_ref[...] = dt_full * u + skip_ref[...] * dy
    dbc_ref[:, :NSTATE] = dot_nn(tail_x, g_low) + dot_tn(di_low, c)
    dbc_ref[:, NSTATE:] = dot_nn(dye_low, start_low) + dot_nn(di_low, b)
    gs = jnp.sum(g * start, axis=1, keepdims=True)
    gs_row = jnp.sum(row_head * gs, axis=0, keepdims=True)
    last = jnp.sum(k_state, axis=0, keepdims=True) + carried[SPAN - 1 : SPAN, :] * gs_row
    d_cum = r_cols - k_rows.T + r_state - k_state + jnp.where(row8 == SPAN - 1, last, 0.0)
    d_la = tri_dot(tri, d_cum, ((0,), (0,)))
    live = lane < n_heads
    dtp = dtp_ref[...]
    d_in = jnp.where(live, (d_dt + nega * d_la) * jax.nn.sigmoid(dtp), 0.0)
    ddt_ref[...] = d_in
    sum_a = jnp.sum(jnp.where(live, d_la * la, 0.0), axis=0, keepdims=True)
    sum_b = jnp.sum(d_in, axis=0, keepdims=True)
    pick = iota2((8, 128), 0)
    sums_ref[...] += jnp.where(pick == 0, sum_a, jnp.where(pick == 1, sum_b, 0.0))
    gskip_ref[...] += jnp.sum(dy * xf, axis=0, keepdims=True)
    keep = jnp.sum(row_head * carried[SPAN - 1 : SPAN, :], axis=1, keepdims=True)
    gstate[...] = keep * g + dot_tn(dye_low, c)


def ssd_backward(
    base, doc_starts, x, b, c, dtp, dy, span_starts, start_decay, nega, skip, in_state, grad_state
):
    tok, xw = x.shape
    n_heads, nspan = xw // MHDIM, tok // SPAN
    row = lambda n: pl.BlockSpec((SPAN, n), lambda i: (nspan - 1 - i, 0))
    whole = lambda *s: pl.BlockSpec(s, lambda i: (0,) * len(s))
    smem = pl.BlockSpec(memory_space=pltpu.SMEM)
    return pl.pallas_call(
        functools.partial(ssd_backward_kernel, n_heads),
        grid=(nspan,),
        in_specs=[
            smem, smem, row(xw), row(NSTATE), row(NSTATE), row(128), row(xw),
            pl.BlockSpec((1, xw, NSTATE), lambda i: (nspan - 1 - i, 0, 0)),
            pl.BlockSpec((1, 1, 128), lambda i: (nspan - 1 - i, 0, 0)),
            whole(1, 128), whole(1, xw), whole(xw, NSTATE), whole(xw, NSTATE),
        ],
        out_specs=[row(xw), row(2 * NSTATE), row(128), whole(8, 128), whole(1, xw)],
        out_shape=[
            jax.ShapeDtypeStruct((tok, xw), f32),
            jax.ShapeDtypeStruct((tok, 2 * NSTATE), f32),
            jax.ShapeDtypeStruct((tok, 128), f32),
            jax.ShapeDtypeStruct((8, 128), f32),
            jax.ShapeDtypeStruct((1, xw), f32),
        ],
        scratch_shapes=[pltpu.VMEM((xw, NSTATE), f32)],
        compiler_params=pltpu.CompilerParams(vmem_limit_bytes=VMEM_LIMIT),
        cost_estimate=pl.CostEstimate(
            flops=2 * tok * xw * NSTATE * 8, bytes_accessed=16 * tok * xw, transcendentals=0
        ),
        name="ssd_backward",
    )(base, doc_starts, x, b, c, dtp, dy, span_starts, start_decay, nega, skip, in_state, grad_state)


QB = 256
KB = 512


def seen(base_ref, starts_ref, q_first, k_first):
    q_pos = base_ref[0] + q_first + iota2((QB, KB), 0)
    k_pos = k_first + iota2((QB, KB), 1)
    return (q_pos >= k_pos) & (docs_of(q_pos, starts_ref) == docs_of(k_pos, starts_ref))


def attend_kernel(scale, base_ref, starts_ref, q_ref, k_ref, v_ref, o_ref, lse_ref):
    i = pl.program_id(0)
    q = q_ref[...]
    blocks = (base_ref[0] + (i + 1) * QB + KB - 1) // KB

    def turn(j, carry):
        m, l, acc = carry
        at = pl.ds(pl.multiple_of(j * KB, KB), KB)
        s = dot_nt(q, k_ref[at, :]) * scale
        visible = seen(base_ref, starts_ref, i * QB, j * KB)
        s = jnp.where(visible, s, neg_large)
        m_new = jnp.maximum(m, jnp.max(s, axis=1, keepdims=True))
        w = jnp.where(visible, jnp.exp(s - m_new), 0.0)
        r = jnp.exp(m - m_new)
        l = l * r + jnp.sum(w, axis=1, keepdims=True)
        return m_new, l, acc * r + dot_nn(w.astype(bf16), v_ref[at, :])

    m, l, acc = lax.fori_loop(
        0,
        blocks,
        turn,
        (jnp.full((QB, 1), neg_large, f32), jnp.zeros((QB, 1), f32), jnp.zeros((QB, HDIM), f32)),
    )
    o_ref[...] = acc / l
    lse_ref[...] = jnp.broadcast_to(m + jnp.log(l), (QB, 128))


def attend(base, doc_starts, q, k, v):
    tok = q.shape[0]
    row = pl.BlockSpec((QB, HDIM), lambda i: (i, 0))
    whole = pl.BlockSpec(k.shape, lambda i: (0, 0))
    smem = pl.BlockSpec(memory_space=pltpu.SMEM)
    return pl.pallas_call(
        functools.partial(attend_kernel, HDIM ** (-0.5)),
        grid=(tok // QB,),
        in_specs=[smem, smem, row, whole, whole],
        out_specs=[row, row],
        out_shape=[jax.ShapeDtypeStruct((tok, HDIM), f32)] * 2,
        compiler_params=pltpu.CompilerParams(vmem_limit_bytes=VMEM_LIMIT),
        cost_estimate=pl.CostEstimate(
            flops=4 * tok * k.shape[0] * HDIM, bytes_accessed=8 * k.size, transcendentals=0
        ),
        name="attend",
    )(base, doc_starts, q, k, v)


def attend_back_kernel(
    scale, base_ref, starts_ref, q_ref, do_ref, o_ref, lse_ref, k_ref, v_ref,
    dq_ref, dk_ref, dv_ref,
):
    i = pl.program_id(0)

    @pl.when(i == 0)
    def _():
        dk_ref[...] = jnp.zeros_like(dk_ref)
        dv_ref[...] = jnp.zeros_like(dv_ref)

    q, do = q_ref[...], do_ref[...]
    delta = jnp.sum(do.astype(f32) * o_ref[...], axis=1, keepdims=True)
    lse = lse_ref[:, 0:1]
    blocks = (base_ref[0] + (i + 1) * QB + KB - 1) // KB

    def turn(j, dq):
        at = pl.ds(pl.multiple_of(j * KB, KB), KB)
        k, v = k_ref[at, :], v_ref[at, :]
        visible = seen(base_ref, starts_ref, i * QB, j * KB)
        s = dot_nt(q, k) * scale
        p = jnp.exp(jnp.where(visible, s - lse, neg_large))
        ds = (p * (dot_nt(do, v) - delta)).astype(bf16)
        dv_ref[at, :] += dot_tn(p.astype(bf16), do)
        dk_ref[at, :] += dot_tn(ds, q) * scale
        return dq + dot_nn(ds, k)

    dq_ref[...] = lax.fori_loop(0, blocks, turn, jnp.zeros((QB, HDIM), f32)) * scale


def attend_back(base, doc_starts, q, do, o, lse, k, v):
    tok = q.shape[0]
    row = pl.BlockSpec((QB, HDIM), lambda i: (i, 0))
    whole = pl.BlockSpec(k.shape, lambda i: (0, 0))
    smem = pl.BlockSpec(memory_space=pltpu.SMEM)
    return pl.pallas_call(
        functools.partial(attend_back_kernel, HDIM ** (-0.5)),
        grid=(tok // QB,),
        in_specs=[smem, smem, row, row, row, row, whole, whole],
        out_specs=[row, whole, whole],
        out_shape=[
            jax.ShapeDtypeStruct((tok, HDIM), f32),
            jax.ShapeDtypeStruct(k.shape, f32),
            jax.ShapeDtypeStruct(k.shape, f32),
        ],
        compiler_params=pltpu.CompilerParams(vmem_limit_bytes=VMEM_LIMIT),
        cost_estimate=pl.CostEstimate(
            flops=10 * tok * k.shape[0] * HDIM, bytes_accessed=20 * k.size, transcendentals=0
        ),
        name="attend_back",
    )(base, doc_starts, q, do, o, lse, k, v)


def at_rows(first, count):
    return pl.ds(pl.multiple_of(first, count), count)


def place():
    return lax.axis_index("z"), lax.axis_index("p"), lax.axis_index("head")


def hop(p, d):
    x, y = lax.rem(p, 2), p // 2
    return lax.rem(y + d // 2, 2) * 2 + lax.rem(x + d % 2, 2)


def chip(z, p, c):
    return (z, p, c)


def meet(others):
    barrier = pltpu.get_barrier_semaphore()
    for other in others:
        pl.semaphore_signal(barrier, inc=1, device_id=other, device_id_type=MESH)
    pl.semaphore_wait(barrier, len(others))


def send(src, dst, send_sem, recv_sem, to):
    copy = pltpu.make_async_remote_copy(
        src_ref=src, dst_ref=dst, send_sem=send_sem, recv_sem=recv_sem,
        device_id=to, device_id_type=MESH,
    )
    copy.start()
    return copy


HOPS = (3, 1, 2)


def share_rows(full_ref, half, own_sems, far_sems, near_sems):
    z, p, c = place()
    other = chip(z, p, 1 - c)
    mine = full_ref.at[at_rows((p * 2 + c) * half, half), :]
    copies = []
    for i, d in enumerate(HOPS):
        copies.append(send(mine, mine, far_sems.at[0, i], far_sems.at[1, i], chip(z, hop(p, d), c)))
    copies.append(send(mine, mine, own_sems.at[0], own_sems.at[1], other))
    onward = []
    for i, d in ((1, 1), (2, 2), (0, 3)):
        copies[i].wait_recv()
        came = full_ref.at[at_rows((hop(p, d) * 2 + c) * half, half), :]
        onward.append(send(came, came, near_sems.at[0, i], near_sems.at[1, i], other))
    return copies, onward


def finish_share(copies, onward):
    for copy in copies[:3]:
        copy.wait_send()
    copies[3].wait()
    for copy in onward:
        copy.wait()


def reduce_blocks(pairs, part, keep, sib_out, sib_in, out, came, near_sems, far_sems):
    z, p, c = place()
    other = chip(z, p, 1 - c)
    half = keep.shape[1]
    width = keep.shape[2]
    tile = part.shape[1]
    near, far = [], []

    def pass_on(i, d):
        near[i].wait_recv()

        @pl.loop(0, half // 16)
        def _(r):
            at = at_rows(r * 16, 16)
            out[i, at, :] = (keep[i, at, :] + sib_in[i, at, :].astype(f32)).astype(bf16)

        far.append(
            send(out.at[i], came.at[i], far_sems.at[0, i], far_sems.at[1, i], chip(z, hop(p, d), c))
        )

    order = HOPS + (0,)
    for i, d in enumerate(order):
        rows = at_rows(hop(p, d) * (2 * half), 2 * half)

        @pl.loop(0, width // tile)
        def _(n):
            cols = at_rows(n * tile, tile)
            total = dot_nt(pairs[0][0][rows, :], pairs[0][1][cols, :])
            for left, right in pairs[1:]:
                total = total + dot_nt(left[rows, :], right[cols, :])
            part[...] = total
            keep[i, :, cols] = part[at_rows(c * half, half), :]
            sib_out[i, :, cols] = part[at_rows((1 - c) * half, half), :].astype(bf16)

        near.append(
            send(sib_out.at[i], sib_in.at[i], near_sems.at[0, i], near_sems.at[1, i], other)
        )
        if i:
            pass_on(i - 1, order[i - 1])
    near[3].wait_recv()
    for copy in far:
        copy.wait_recv()

    def total_rows(at):
        total = keep[3, at, :] + sib_in[3, at, :].astype(f32)
        return total + came[0, at, :].astype(f32) + came[1, at, :].astype(f32) + came[2, at, :].astype(f32)

    def done():
        for copy in near + far:
            copy.wait_send()

    return total_rows, done


def greet():
    z, p, c = place()
    meet([chip(z, p, 1 - c)] + [chip(z, hop(p, d), c) for d in HOPS])


def rms(rows):
    return lax.rsqrt(jnp.mean(rows * rows, axis=1, keepdims=True) + eps_norm)


def mid_kernel(
    left, right, resid, gain, mid_ref, full_ref,
    part, keep, sib_out, sib_in, out, came, n_sems, f_sems, own_sems, far_sems, near_sems,
):
    greet()
    z, p, c = place()
    half = keep.shape[1]
    total_rows, done = reduce_blocks(
        [(left, right)], part, keep, sib_out, sib_in, out, came, n_sems, f_sems
    )
    g = gain[...]

    @pl.loop(0, half // 16)
    def _(r):
        at = at_rows(r * 16, 16)
        mid = resid[at, :] + total_rows(at)
        mid_ref[at, :] = mid
        full_ref[at_rows((p * 2 + c) * half + r * 16, 16), :] = (mid * rms(mid) * g).astype(bf16)

    copies, onward = share_rows(full_ref, half, own_sems, far_sems, near_sems)
    done()
    finish_share(copies, onward)


def two_kernel(
    left, right, mid_own, grad_own, gain, dmid_ref, ggain_ref, full_ref,
    part, keep, sib_out, sib_in, out, came, n_sems, f_sems, own_sems, far_sems, near_sems,
):
    greet()
    z, p, c = place()
    half = keep.shape[1]
    total_rows, done = reduce_blocks(
        [(left, right)], part, keep, sib_out, sib_in, out, came, n_sems, f_sems
    )
    g = gain[...]
    ggain_ref[...] = jnp.zeros_like(ggain_ref)

    @pl.loop(0, half // 16)
    def _(r):
        at = at_rows(r * 16, 16)
        d_two, mid = total_rows(at), mid_own[at, :]
        scale = rms(mid)
        w = d_two * g
        d_mid = grad_own[at, :] + scale * w - mid * (scale * scale * scale) * jnp.mean(
            w * mid, axis=1, keepdims=True
        )
        ggain_ref[...] += jnp.sum(d_two * mid * scale, axis=0, keepdims=True)
        dmid_ref[at, :] = d_mid
        full_ref[at_rows((p * 2 + c) * half + r * 16, 16), :] = d_mid.astype(bf16)

    copies, onward = share_rows(full_ref, half, own_sems, far_sems, near_sems)
    done()
    finish_share(copies, onward)


def one_kernel(
    left_a, right_a, left_b, right_b, hidden_own, dmid_own, gain, grad_ref, ggain_ref,
    part, keep, sib_out, sib_in, out, came, n_sems, f_sems, own_sems,
):
    greet()
    z, p, c = place()
    half = keep.shape[1]
    total_rows, done = reduce_blocks(
        [(left_a, right_a), (left_b, right_b)],
        part, keep, sib_out, sib_in, out, came, n_sems, f_sems,
    )
    g = gain[...]
    ggain_ref[...] = jnp.zeros_like(ggain_ref)

    @pl.loop(0, half // 16)
    def _(r):
        at = at_rows(r * 16, 16)
        d_one, hid = total_rows(at), hidden_own[at, :]
        scale = rms(hid)
        w = d_one * g
        d_in = dmid_own[at, :] + scale * w - hid * (scale * scale * scale) * jnp.mean(
            w * hid, axis=1, keepdims=True
        )
        ggain_ref[...] += jnp.sum(d_one * hid * scale, axis=0, keepdims=True)
        grad_ref[at_rows(c * half + r * 16, 16), :] = d_in

    mine = grad_ref.at[at_rows(c * half, half), :]
    copy = send(mine, mine, own_sems.at[0], own_sems.at[1], chip(z, p, 1 - c))
    done()
    copy.wait()


VM = pl.BlockSpec(memory_space=pltpu.VMEM)


def reduce_scratch(half, width):
    return [
        pltpu.VMEM((2 * half, 512), f32),
        pltpu.VMEM((4, half, width), f32),
        pltpu.VMEM((4, half, width), bf16),
        pltpu.VMEM((4, half, width), bf16),
        pltpu.VMEM((3, half, width), bf16),
        pltpu.VMEM((3, half, width), bf16),
        pltpu.SemaphoreType.DMA((2, 4)),
        pltpu.SemaphoreType.DMA((2, 3)),
    ]


SHARE_SEMS = [
    pltpu.SemaphoreType.DMA((2,)),
    pltpu.SemaphoreType.DMA((2, 3)),
    pltpu.SemaphoreType.DMA((2, 3)),
]


def plane_call(kernel, name, number, args, shapes, scratch, flops=0):
    return pl.pallas_call(
        kernel,
        in_specs=[VM] * len(args),
        out_specs=[VM] * len(shapes),
        out_shape=[jax.ShapeDtypeStruct(s, t) for s, t in shapes],
        scratch_shapes=scratch,
        compiler_params=pltpu.CompilerParams(
            collective_id=number, has_side_effects=True, vmem_limit_bytes=VMEM_LIMIT
        ),
        cost_estimate=pl.CostEstimate(flops=flops, bytes_accessed=150_000_000, transcendentals=0),
        name=name,
    )(*args)


def mid_step(mixed, w, resid_own, gain):
    tok, width = mixed.shape[0], w.shape[0]
    half = resid_own.shape[0]
    return plane_call(
        mid_kernel, "mid_step", 1, (mixed, w, resid_own, gain),
        [((half, width), f32), ((tok, width), bf16)],
        reduce_scratch(half, width) + SHARE_SEMS,
    )


def two_step(d_gu, w, mid_own, grad_own, gain):
    tok, width = d_gu.shape[0], w.shape[0]
    half = mid_own.shape[0]
    return plane_call(
        two_kernel, "two_step", 2, (d_gu, w, mid_own, grad_own, gain),
        [((half, width), f32), ((1, width), f32), ((tok, width), bf16)],
        reduce_scratch(half, width) + SHARE_SEMS,
    )


def one_step(d_a, w_a, d_b, w_b, hidden_own, dmid_own, gain):
    width = w_a.shape[0]
    half = hidden_own.shape[0]
    return plane_call(
        one_kernel, "one_step", 3, (d_a, w_a, d_b, w_b, hidden_own, dmid_own, gain),
        [((2 * half, width), f32), ((1, width), f32)],
        reduce_scratch(half, width) + [pltpu.SemaphoreType.DMA((2,))],
    )


def open_kernel(gains_ref, a_ref, gain_out, a_out, z_sems, p_sems, a_sems, loc_sems):
    z, p, c = place()
    nz = gain_out.shape[1]
    ups = [chip(lax.rem(z + d, nz), p, c) for d in range(1, nz)]
    meet(ups + [chip(z, hop(p, d), c) for d in HOPS])
    gain_out[p, z] = gains_ref[...]
    copies = []
    for d in range(1, nz):
        copies.append(
            send(gain_out.at[p, z], gain_out.at[p, z], z_sems.at[0, d - 1], z_sems.at[1, d - 1], ups[d - 1])
        )
    for i, d in enumerate(HOPS):
        q = hop(p, d)
        copies.append(
            send(a_ref.at[q], a_out.at[p], a_sems.at[0, i], a_sems.at[1, i], chip(z, q, c))
        )
    local = pltpu.make_async_copy(a_ref.at[p], a_out.at[p], loc_sems.at[0])
    local.start()
    for copy in copies[: nz - 1]:
        copy.wait_recv()
    late = []
    for i, d in enumerate(HOPS):
        late.append(
            send(gain_out.at[p], gain_out.at[p], p_sems.at[0, i], p_sems.at[1, i], chip(z, hop(p, d), c))
        )
    for copy in copies[: nz - 1]:
        copy.wait_send()
    for copy in copies[nz - 1 :] + late:
        copy.wait()
    local.wait()


def open_step(gains, piece, nz):
    n_p = piece.shape[0]
    return plane_call(
        open_kernel, "open_step", 4, (gains, piece),
        [((n_p, nz) + gains.shape, f32), (piece.shape, bf16)],
        [
            pltpu.SemaphoreType.DMA((2, nz - 1)),
            pltpu.SemaphoreType.DMA((2, 3)),
            pltpu.SemaphoreType.DMA((2, 3)),
            pltpu.SemaphoreType.DMA((1,)),
        ],
    )


def share_kernel(n, *refs):
    hid, grad, gain = refs[:3]
    w_refs, (full_ref, gfull_ref), w_outs = refs[3 : 3 + n], refs[3 + n : 5 + n], refs[5 + n : 5 + 2 * n]
    own_sems, far_sems, near_sems, own_g, far_g, near_g, w_sems, loc_sems = refs[5 + 2 * n :]
    greet()
    z, p, c = place()
    half = hid.shape[0]
    g = gain[...]

    @pl.loop(0, half // 16)
    def _(r):
        at = at_rows(r * 16, 16)
        to = at_rows((p * 2 + c) * half + r * 16, 16)
        rows = hid[at, :]
        full_ref[to, :] = (rows * rms(rows) * g).astype(bf16)
        gfull_ref[to, :] = grad[at, :].astype(bf16)

    local = []
    for j in range(n):
        local.append(pltpu.make_async_copy(w_refs[j].at[p], w_outs[j].at[p], loc_sems.at[j]))
        local[j].start()
    copies, onward = share_rows(full_ref, half, own_sems, far_sems, near_sems)
    moved = []
    for j in range(n):
        for i, d in enumerate(HOPS):
            q = hop(p, d)
            moved.append(
                send(
                    w_refs[j].at[q], w_outs[j].at[p], w_sems.at[0, j, i], w_sems.at[1, j, i],
                    chip(z, q, c),
                )
            )
    copies_g, onward_g = share_rows(gfull_ref, half, own_g, far_g, near_g)
    finish_share(copies, onward)
    finish_share(copies_g, onward_g)
    for copy in moved:
        copy.wait()
    for copy in local:
        copy.wait()


def share_step(hid, grad, gain, rest, tok):
    width, n = hid.shape[1], len(rest)
    anywhere = pl.BlockSpec(memory_space=pl.ANY)
    return pl.pallas_call(
        functools.partial(share_kernel, n),
        in_specs=[VM, VM, VM] + [anywhere] * n,
        out_specs=[VM, VM] + [anywhere] * n,
        out_shape=[jax.ShapeDtypeStruct((tok, width), bf16)] * 2
        + [jax.ShapeDtypeStruct(r.shape, bf16) for r in rest],
        scratch_shapes=SHARE_SEMS
        + SHARE_SEMS
        + [pltpu.SemaphoreType.DMA((2, n, 3)), pltpu.SemaphoreType.DMA((n,))],
        compiler_params=pltpu.CompilerParams(
            collective_id=5, has_side_effects=True, vmem_limit_bytes=VMEM_LIMIT
        ),
        cost_estimate=pl.CostEstimate(flops=0, bytes_accessed=200_000_000, transcendentals=0),
        name="share_step",
    )(hid, grad, gain, *rest)


def sums_kernel(v_ref, out_ref, came, z_sems, p_sems, c_sems):
    z, p, c = place()
    nz = came.shape[0]
    ups = [chip(lax.rem(z + d, nz), p, c) for d in range(1, nz)]
    other = chip(z, p, 1 - c)
    meet(ups + [chip(z, hop(p, d), c) for d in HOPS] + [other])
    copies = []
    for d in range(1, nz):
        copies.append(
            send(v_ref, came.at[d], z_sems.at[0, d - 1], z_sems.at[1, d - 1], ups[d - 1])
        )
    total = v_ref[...]
    for d in range(1, nz):
        copies[d - 1].wait_recv()
        total = total + came[d]
    out_ref[c, p] = total
    far = []
    for i, d in enumerate(HOPS):
        far.append(
            send(out_ref.at[c, p], out_ref.at[c, p], p_sems.at[0, i], p_sems.at[1, i], chip(z, hop(p, d), c))
        )
    for copy in far:
        copy.wait_recv()
    near = send(out_ref.at[c], out_ref.at[c], c_sems.at[0], c_sems.at[1], other)
    for copy in copies + far:
        copy.wait_send()
    near.wait()


def sums_step(v, nz, n_p):
    return plane_call(
        sums_kernel, "sums_step", 6, (v,),
        [((2, n_p) + v.shape, f32)],
        [
            pltpu.VMEM((nz,) + v.shape, f32),
            pltpu.SemaphoreType.DMA((2, nz - 1)),
            pltpu.SemaphoreType.DMA((2, 3)),
            pltpu.SemaphoreType.DMA((2,)),
        ],
    )[0]


def rope_tables(positions, pairs):
    freqs = rope_base ** (-2.0 * pairs.astype(f32) / HDIM)
    angles = positions.astype(f32)[:, None] * freqs[None, :]
    return jnp.cos(angles), jnp.sin(angles)


def plane_swap(x):
    n_p = lax.axis_size("p")
    p = lax.axis_index("p")
    out = x
    for d in range(1, n_p):
        other = jnp.bitwise_xor(p, d)
        block = lax.dynamic_index_in_dim(x, other, 0, keepdims=True)
        came = lax.ppermute(block, "p", [(i, i ^ d) for i in range(n_p)])
        out = lax.dynamic_update_slice_in_dim(out, came, other, 0)
    return out


def plane_gather(x):
    n_p = lax.axis_size("p")
    p = lax.axis_index("p")
    out = jnp.zeros((n_p,) + x.shape, x.dtype)
    out = lax.dynamic_update_slice_in_dim(out, x[None], p, 0)
    for d in range(1, n_p):
        came = lax.ppermute(x, "p", [(i, i ^ d) for i in range(n_p)])
        out = lax.dynamic_update_slice_in_dim(out, came[None], jnp.bitwise_xor(p, d), 0)
    return out


def plane_sum(x):
    n_p = lax.axis_size("p")
    p = lax.axis_index("p")
    total = lax.dynamic_index_in_dim(x, p, 0, keepdims=False).astype(f32)
    for d in range(1, n_p):
        block = lax.dynamic_index_in_dim(x, jnp.bitwise_xor(p, d), 0, keepdims=False)
        came = lax.ppermute(block.astype(bf16), "p", [(i, i ^ d) for i in range(n_p)])
        total = total + came.astype(f32)
    return total


def swap_core(x):
    return lax.ppermute(x, "head", [(0, 1), (1, 0)])


def block_sum(part):
    ci = lax.axis_index("head")
    mine = lax.dynamic_index_in_dim(part, ci, 1, keepdims=False)
    other = lax.dynamic_index_in_dim(part, 1 - ci, 1, keepdims=False)
    return plane_sum(mine + swap_core(other.astype(bf16)).astype(f32))


def join_cores(mine):
    ci = lax.axis_index("head")
    other = swap_core(mine)
    out = jnp.concatenate([mine, mine])
    return lax.dynamic_update_slice_in_dim(out, other, (1 - ci) * mine.shape[0], 0)


def carry_states(state, decays, sign):
    nz = lax.axis_size("z")
    low = state.astype(bf16)
    total, factor = None, None
    for d in range(1, nz):
        route = [(i, i + sign * d) for i in range(nz) if 0 <= i + sign * d < nz]
        came = lax.ppermute(low, "z", route).astype(f32)
        rate = lax.ppermute(decays, "z", route)
        total = came if total is None else total + factor * came
        factor = rate if factor is None else factor * rate
    return total


def shards(
    hidden_in,
    grad_out,
    doc_starts,
    norm_mixer,
    norm_ffn,
    mamba_z,
    mamba_x,
    mamba_bc,
    mamba_dt,
    conv_x,
    conv_bc,
    a_log,
    dt_bias,
    skip_gain,
    mamba_out,
    attn_query,
    attn_key,
    attn_value,
    attn_out,
    ffn_gate,
    ffn_up,
    ffn_down,
):
    own = hidden_in.shape[0]
    width = hidden_in.shape[1]
    half = own // 2
    nz, n_p = lax.axis_size("z"), lax.axis_size("p")
    zi, pi, ci = lax.axis_index("z"), lax.axis_index("p"), lax.axis_index("head")
    tok = own * n_p
    base = zi * tok
    positions = base + jnp.arange(tok, dtype=jnp.int32)
    edge = conv_x.shape[0] - 1
    ext_docs = doc_ids(base - edge + jnp.arange(tok + edge, dtype=jnp.int32), doc_starts)
    rows = mamba_z.shape[0]
    n_heads = a_log.shape[0] // n_p
    xw = n_heads * MHDIM
    bw = mamba_bc.shape[1] // (2 * n_p)
    cw = xw + 2 * bw
    kw = HDIM // n_p
    hk = kw // 2
    tail_w = 128 - 2 * kw - n_heads

    def cols(w):
        w = w.astype(bf16)
        return w.reshape(w.shape[0], n_p, -1).transpose(1, 0, 2)

    k_cols = attn_key.astype(bf16).reshape(rows, 2, n_p, hk)
    k_cols = k_cols.transpose(2, 0, 1, 3).reshape(n_p, rows, kw)
    bc_cols = mamba_bc.astype(bf16).reshape(rows, 2, n_p, bw)
    bc_cols = bc_cols.transpose(2, 0, 1, 3).reshape(n_p, rows, 2 * bw)
    q_cols = attn_query.astype(bf16).reshape(rows, n_p, 2, n_p, hk)
    q_cols = q_cols.transpose(1, 0, 3, 2, 4).reshape(n_p, rows, HDIM)
    piece_a = jnp.concatenate(
        [
            cols(mamba_x), bc_cols, k_cols, cols(attn_value), cols(mamba_dt),
            jnp.zeros((n_p, rows, tail_w), bf16),
        ],
        axis=2,
    )
    rest = [
        jnp.concatenate([q_cols, cols(mamba_z)], axis=2),
        jnp.concatenate([cols(mamba_out.T), cols(attn_out.T)], axis=2),
        jnp.concatenate([cols(ffn_gate), cols(ffn_up)], axis=2),
        cols(ffn_down.T),
    ]

    def along_z(piece):
        piece = piece.reshape(n_p * rows, piece.shape[2])
        return lax.all_gather(piece, "z", axis=0, tiled=True)

    gains_own = jnp.pad(
        jnp.stack([norm_mixer, norm_ffn]).astype(bf16).astype(f32), ((0, 6), (0, 128 - rows))
    )
    gains, piece_a = open_step(gains_own, piece_a, nz)
    w_a = along_z(piece_a)
    gains = gains.transpose(2, 1, 0, 3)[:, :, :, :rows].reshape(8, 1, width)
    gain_mix, gain_ffn = gains[0], gains[1]
    my_half = lambda v: lax.dynamic_slice_in_dim(v, ci * half, half, 0)
    hidden_own, grad_own = my_half(hidden_in), my_half(grad_out)
    normed_one, g_ffn, *rest = share_step(hidden_own, grad_own, gain_mix, rest, tok)
    w_b, w_c, w_d, w_e = [along_z(piece) for piece in rest]

    in_a = product(normed_one, w_a)
    in_b = product(normed_one, w_b)
    pre = in_a[:, :cw].astype(bf16)
    gate_z = in_b[:, HDIM:]
    slice_1 = lambda v, at, n: lax.dynamic_slice_in_dim(v, at, n, 1)
    taps = jnp.concatenate(
        [
            slice_1(conv_x, pi * xw, xw),
            slice_1(conv_bc, pi * bw, bw),
            slice_1(conv_bc, (n_p + pi) * bw, bw),
        ],
        axis=1,
    )
    prev_rows = passed_along(pre[tok - edge :], "z", 1)
    ext = jnp.concatenate([prev_rows, pre], axis=0)
    conv_in = convolve(ext, taps, ext_docs, tok)
    ssm = jax.nn.silu(conv_in).astype(bf16)
    head_slice = lambda v: lax.dynamic_slice_in_dim(v, pi * n_heads, n_heads, 0)
    my_bias, my_a, my_skip = head_slice(dt_bias), head_slice(a_log), head_slice(skip_gain)
    lanes = lambda v: jnp.pad(v, (0, 128 - n_heads))[None, :]
    dt_at = cw + 2 * kw
    dt_pre = jnp.pad(in_a[:, dt_at : dt_at + n_heads], ((0, 0), (0, 128 - n_heads))) + lanes(my_bias)
    neg_rate = lanes(-jnp.exp(my_a))
    skip_full = jnp.repeat(my_skip, MHDIM)[None, :]
    x_low = ssm[:, :xw]
    bc_all = plane_gather(ssm[:, xw:]).reshape(n_p, tok, 2, bw)
    bc_all = bc_all.transpose(2, 1, 0, 3).reshape(2, tok, n_p * bw)
    b_mat, c_mat = bc_all[0], bc_all[1]
    pair_ids = pi * hk + jnp.arange(hk)
    cos_k, sin_k = rope_tables(positions, pair_ids)
    k0, k1 = in_a[:, cw : cw + hk], in_a[:, cw + hk : cw + kw]
    key_own = jnp.concatenate([k0 * cos_k - k1 * sin_k, k1 * cos_k + k0 * sin_k], axis=1)
    val_own = in_a[:, cw + kw : cw + 2 * kw]
    kv_own = jnp.concatenate([key_own, val_own], axis=1).astype(bf16)
    kv = jnp.zeros((nz, tok, 2 * kw), bf16)
    kv = lax.dynamic_update_slice_in_dim(kv, kv_own[None], zi, 0)
    for d in range(1, nz):
        came = passed_along(kv_own, "z", d)
        kv = lax.dynamic_update_slice_in_dim(kv, came[None], (zi - d) % nz, 0)
    kv = plane_gather(kv).transpose(1, 2, 0, 3).reshape(nz * tok, n_p, 2 * kw)
    keys = kv[:, :, :kw].reshape(nz * tok, HDIM)
    values = kv[:, :, kw:].reshape(nz * tok, HDIM)
    cos_q, sin_q = rope_tables(positions, jnp.arange(HDIM // 2))
    cos_q, sin_q = cos_q.reshape(tok, n_p, hk), sin_q.reshape(tok, n_p, hk)

    def rope_q(v, sign):
        v = v.reshape(tok, n_p, 2, hk)
        a, b = v[:, :, 0], v[:, :, 1]
        return jnp.stack(
            [a * cos_q - sign * b * sin_q, b * cos_q + sign * a * sin_q], axis=2
        ).reshape(tok, HDIM)

    queries = rope_q(in_b[:, :HDIM], 1.0).astype(bf16)

    base_arr = jnp.reshape(base, (1,)).astype(jnp.int32)
    y_local, span_starts, local_state, dev_decay = ssd_forward(
        base_arr, doc_starts, x_low, b_mat, c_mat, dt_pre, neg_rate, skip_full
    )
    decay_full = jnp.repeat(dev_decay[:, :n_heads], MHDIM, axis=1)
    total_decay = decay_full[-1][:, None]
    in_state = carry_states(local_state, total_decay, 1)

    attn_f32, lse = attend(base_arr, doc_starts, queries, keys, values)
    attn_low = attn_f32.astype(bf16)
    y_flat = y_local + product_nt(c_mat, in_state.astype(bf16)) * decay_full
    silu_z = jax.nn.silu(gate_z)
    gated = (y_flat * silu_z).astype(bf16)
    mixed = jnp.concatenate([gated, attn_low], axis=1)

    mid_own, normed_two = mid_step(mixed, w_c, hidden_own, gain_ffn)
    gu = product(normed_two, w_d)
    ffw = gu.shape[1] // 2
    gate_val, up_val = gu[:, :ffw], gu[:, ffw:]
    silu_gate = jax.nn.silu(gate_val)
    activated = (silu_gate * up_val).astype(bf16)
    d_act = product(g_ffn, w_e)
    d_gu = jnp.concatenate(
        [d_act * up_val * silu_slope(gate_val), d_act * silu_gate], axis=1
    ).astype(bf16)
    grad_e = product_t(g_ffn, activated).astype(bf16)
    grad_d = product_t(normed_two, d_gu).astype(bf16)
    d_gu, grad_e, grad_d = lax.optimization_barrier((d_gu, grad_e, grad_d))

    def scattered(grad):
        grad = lax.psum_scatter(grad, "z", scatter_dimension=0, tiled=True)
        return plane_swap(grad.reshape(n_p, rows, grad.shape[1])).astype(f32)

    ge = scattered(grad_e)
    gd = scattered(grad_d)
    d_mid_own, grad_gain_ffn, g_mid = two_step(d_gu, w_d, mid_own, grad_own, gain_ffn)
    out_part = product_nt(activated, w_e).reshape(n_p, 2, half, width)
    block_out = join_cores(mid_own + block_sum(out_part))

    d_mixed = product(g_mid, w_c)
    grad_c = product_t(g_mid, mixed).astype(bf16)
    gc = scattered(grad_c)
    d_gated = d_mixed[:, :xw]
    d_attn = d_mixed[:, xw:].astype(bf16)
    d_y_flat = d_gated * silu_z
    d_z = (d_gated * y_flat * silu_slope(gate_z)).astype(bf16)
    d_in_local = product_t((d_y_flat * decay_full).astype(bf16), c_mat)
    state_grad = carry_states(d_in_local, total_decay, -1)
    d_query, d_key, d_value = attend_back(
        base_arr, doc_starts, queries, d_attn, attn_f32, lse, keys, values
    )
    d_q_pre = rope_q(d_query, -1.0).astype(bf16)
    d_b = jnp.concatenate([d_q_pre, d_z], axis=1)
    grad_b = product_t(normed_one, d_b).astype(bf16)
    gb = scattered(grad_b)
    d_kv = jnp.concatenate(
        [d_key.reshape(nz, tok, n_p, kw), d_value.reshape(nz, tok, n_p, kw)], axis=3
    )
    d_kv = plane_sum(d_kv.transpose(2, 0, 1, 3))
    d_kv_own = lax.dynamic_index_in_dim(d_kv, zi, 0, keepdims=False)
    for d in range(1, nz):
        block = lax.dynamic_index_in_dim(d_kv, (zi - d) % nz, 0, keepdims=False)
        d_kv_own = d_kv_own + passed_along(block.astype(bf16), "z", -d).astype(f32)
    dk0, dk1 = d_kv_own[:, :hk], d_kv_own[:, hk:kw]
    d_kv_low = jnp.concatenate(
        [dk0 * cos_k + dk1 * sin_k, dk1 * cos_k - dk0 * sin_k, d_kv_own[:, kw:]], axis=1
    ).astype(bf16)

    start_decay = jnp.concatenate([jnp.ones((1, 128), f32), dev_decay[SPAN - 1 :: SPAN][:-1]])
    d_xs, d_bc, d_dt, sums, skip_sums = ssd_backward(
        base_arr, doc_starts, x_low, b_mat, c_mat, dt_pre, d_y_flat, span_starts,
        start_decay[:, None, :], neg_rate, skip_full, in_state, state_grad,
    )
    d_bc = d_bc.reshape(2, tok // 2, 2, n_p, bw).transpose(3, 0, 1, 2, 4)
    d_bc = join_cores(block_sum(d_bc.reshape(n_p, 2, tok // 2, 2 * bw)))
    du = jnp.concatenate([d_xs, d_bc], axis=1) * silu_slope(conv_in)
    d_ext, grad_taps = convolve_back(du, ext, taps, ext_docs, tok)
    next_rows = passed_along(d_ext[:edge], "z", -1)
    d_pre = (d_ext[edge:] + jnp.pad(next_rows, ((tok - edge, 0), (0, 0)))).astype(bf16)
    d_last = jnp.concatenate(
        [d_kv_low, d_dt[:, :n_heads].astype(bf16), jnp.zeros((tok, tail_w), bf16)], axis=1
    )
    d_a = jnp.concatenate([d_pre, d_last], axis=1)
    grad_a = product_t(normed_one, d_a).astype(bf16)
    ga = scattered(grad_a)
    once = jnp.where(ci == 0, d_pre[:, xw:], jnp.zeros((), bf16))
    d_a_once = jnp.concatenate([d_pre[:, :xw], once, d_last], axis=1)
    d_a_once, grad_a = lax.optimization_barrier((d_a_once, grad_a))
    grad_in, grad_gain_mix = one_step(
        d_a_once, w_a, d_b, w_b, hidden_own, d_mid_own, gain_mix
    )

    flat = jnp.concatenate(
        [
            grad_gain_mix.reshape(-1, 128),
            grad_gain_ffn.reshape(-1, 128),
            grad_taps.reshape(-1, 128),
            sums[:2],
            jnp.pad(jnp.sum(skip_sums.reshape(n_heads, MHDIM), axis=1), (0, 128 - n_heads))[None],
        ]
    )
    flat = jnp.pad(flat, ((0, -flat.shape[0] % 8), (0, 0)))
    summed = sums_step(flat, nz, n_p)
    g_rows = width // 128
    t_rows = grad_taps.size // 128
    si = zi * n_p + pi
    gains_sum = jnp.sum(summed[:, :, : 2 * g_rows], axis=(0, 1)).reshape(2, width)
    gains_sum = lax.dynamic_slice_in_dim(gains_sum, si * rows, rows, 1)
    mine = lax.dynamic_index_in_dim(summed, ci, 0, keepdims=False)
    s_taps = mine[:, 2 * g_rows : 2 * g_rows + t_rows].reshape(n_p, edge + 1, cw).transpose(1, 0, 2)
    s_heads = mine[:, 2 * g_rows + t_rows : 2 * g_rows + t_rows + 3, :n_heads]
    s_heads = s_heads.transpose(1, 0, 2).reshape(3, n_p * n_heads)
    s_x = s_taps[:, :, :xw].reshape(edge + 1, n_p * xw)
    s_bc = summed[0][:, 2 * g_rows : 2 * g_rows + t_rows].reshape(n_p, edge + 1, cw)
    s_bc = s_bc[:, :, xw:].reshape(n_p, edge + 1, 2, bw).transpose(1, 2, 0, 3)
    s_bc = s_bc.reshape(edge + 1, 2 * n_p * bw)

    def uncols(g):
        return g.transpose(1, 0, 2).reshape(rows, -1)

    g_x = uncols(ga[:, :, :xw])
    g_bc = ga[:, :, xw:cw].reshape(n_p, rows, 2, bw).transpose(1, 2, 0, 3).reshape(rows, -1)
    g_k = ga[:, :, cw : cw + kw].reshape(n_p, rows, 2, hk)
    g_k = g_k.transpose(1, 2, 0, 3).reshape(rows, HDIM)
    g_v = uncols(ga[:, :, cw + kw : cw + 2 * kw])
    g_dt = uncols(ga[:, :, dt_at : dt_at + n_heads])
    g_q = gb[:, :, :HDIM].reshape(n_p, rows, n_p, 2, hk)
    g_q = g_q.transpose(1, 0, 3, 2, 4).reshape(rows, n_p * HDIM)
    g_z = uncols(gb[:, :, HDIM:])
    g_mout = uncols(gc[:, :, :xw]).T
    g_aout = uncols(gc[:, :, xw:]).T
    g_gate = uncols(gd[:, :, :ffw])
    g_up = uncols(gd[:, :, ffw:])
    g_down = uncols(ge).T
    return (
        block_out,
        grad_in,
        gains_sum[0],
        gains_sum[1],
        g_z,
        g_x,
        g_bc,
        g_dt,
        s_x,
        s_bc,
        s_heads[0],
        s_heads[1],
        s_heads[2],
        g_mout,
        g_q,
        g_k,
        g_v,
        g_aout,
        g_gate,
        g_up,
        g_down,
    )


def solution(mesh):
    seq, head = mesh.shape["seq"], mesh.shape["head"]
    plane = math.gcd(seq, 4)
    grid = Mesh(mesh.devices.reshape(seq // plane, plane, head), ("z", "p", "head"))
    s = ("z", "p")
    h = "head"
    placed = (
        P(s, None), P(s, None), P(), P(s), P(s), P(s, h), P(s, h), P(s, None), P(s, h),
        P(None, h), P(), P(h), P(h), P(h), P(h, s), P(s, h), P(s, h), P(s, h), P(h, s),
        P(s, h), P(s, h), P(h, s),
    )
    given = (
        P(s, None), P(s, None), P(s), P(s), P(s, h), P(s, h), P(s, None), P(s, h),
        P(None, h), P(), P(h), P(h), P(h), P(h, s), P(s, h), P(s, h), P(s, h), P(h, s),
        P(s, h), P(s, h), P(h, s),
    )
    return jax.shard_map(shards, mesh=grid, in_specs=placed, out_specs=given, check_vma=False)
```

time: 2250 us -> 976 us (0.43)
  waiting for transfers between devices: 954 us -> 220 us
  Pallas kernels: 0 us -> 347 us
  local copies, waits for them, and re-layouts: 440 us -> 171 us
  blocking collectives: 255 us -> 0 us
  matrix products: 323 us -> 73.1 us
  other arithmetic: 215 us -> 51.1 us
  starting transfers between devices: 22.9 us -> 85.1 us
    reduce_scatter x11 -> x5, waiting for transfers between devices: 574 us -> 0.01 us  [scattered(): grad = lax.psum_scatter(grad, 'z', scatter_dimension=0, tiled=True)]
    pallas_call x0 -> x10, Pallas kernels: none -> 347 us  [the longest x5 209 us: plane_call(): pl.pallas_call(kernel, in_specs=[VM] * len(args), out_specs=[VM] * len(sh...]
    all_gather x12 -> x5, waiting for transfers between devices: 337 us -> 85 us  [along_z(): return lax.all_gather(piece, 'z', axis=0, tiled=True)]
    dot_general x114 -> x0, matrix products: 183 us -> none  [the longest x24 54.1 us: span_ssd(): jnp.einsum('tsh,shp->thp', pair_weights, inputs_x, precision=top_prec)]
    dynamic_update_slice x51 -> x26, local copies, waits for them, and re-layouts: 188 us -> 6.53 us  [the longest x12 2.46 us: plane_swap(): out = lax.dynamic_update_slice_in_dim(out, came, other, 0)]
    psum x2 -> x0, blocking collectives: 117 us -> none  [the longest x1 76.1 us: shards(): lax.psum((spread_x, spread_h, grad_gain_mix, grad_gain_ffn), ('z', 'p'))]
    all_to_all x6 -> x0, blocking collectives: 83.7 us -> none  [the longest x4 53.7 us: fetch(): piece = lax.all_to_all(piece, 'p', 0, 0, tiled=True)]
    ppermute x0 -> x44, starting transfers between devices: none -> 70 us  [the longest x4 24.3 us: carry_states(): rate = lax.ppermute(decays, 'z', route)]
  transfers between devices with their start and end apart: 32 -> 62, of which waited for: 21 -> 21; matrix products, arithmetic and copies ran while one was open for 19% -> 23% of each run, Pallas kernels for 0% -> 19%
where the time goes in v2:
time: 976 us; the launch traced here: 964 us
  Pallas kernels  347 us (36%)
  waiting for transfers between devices  220 us (23%)
  local copies, waits for them, and re-layouts  171 us (18%)
  starting transfers between devices  85.1 us (9%)
  matrix products  73.1 us (7%)
  other arithmetic  51.1 us (5%)
  between operations  16.4 us (2%)
    pallas_call x5, Pallas kernels, plane_call(): pl.pallas_call(kernel, in_specs=[VM] * len(args), out_specs=[VM] * len(sh...  209 us
    pallas_call x1, Pallas kernels, share_step(): pl.pallas_call(functools.partial(share_kernel, n), in_specs=[VM, VM, VM]...  86 us
    all_gather x5, waiting for transfers between devices, along_z(): return lax.all_gather(piece, 'z', axis=0, tiled=True)  85 us
    ppermute x8, waiting for transfers between devices, passed_along(): return lax.ppermute(block, axis, route)  75.5 us
    dot_general x5, matrix products, product(): return jnp.dot(left, right, preferred_element_type=f32)  34.2 us
    unnamed x173, local copies, waits for them, and re-layouts  32.8 us
    dot_general x6, matrix products, product_t(): lax.dot_general(left, right, (((0,), (0,)), ((), ())), preferred_element_...  29.9 us
    ppermute x4, starting transfers between devices, carry_states(): rate = lax.ppermute(decays, 'z', route)  24.3 us
  transfers between devices with their start and end apart: 62, of which 21 were waited for; matrix products, arithmetic and copies ran while one was open for 23% of the time, Pallas kernels for 19%

profile of v2, /device:TPU:0, one launch (start us, length us, event | category | flops | bytes accessed | tf_op | source)
XLA Modules:
  0.0 964.2 jit_solution(17772702277135882655)
XLA Ops:
  21.7 17.6 %open_step.1 = (f32[4,4,8,128]{3,2,1,0:T(8,128)}, bf16[4,128,640]{2,1,0:T(8,128)(2,1)}) custom-call(f32[8,128]{1,0:T(8,128)} %fusion.73.gains_ref, bf16[4,128,640]{2,1,0:T(8,128)(2,1)} %concatenate.79.a_ref), custom_call_target="tpu_custom_call" | custom-call | bytes 150000000 | tf_op jit(solution)/shard_map/open_step/pallas_call | solution.py:682
  55.1 86.0 %share_step.1 = (bf16[1024,2048]{1,0:T(8,128)(2,1)}, bf16[1024,2048]{1,0:T(8,128)(2,1)}, bf16[4,128,512]{2,1,0:T(8,128)(2,1)}, bf16[4,128,512]{2,1,0:T(8,128)(2,...) custom-call(f32[128,2048]{1,0:T(8,128)} %constant_dynamic-slice_fusion.23.refs_0_.resid.hidden_own, ...), custom_call_target="tpu_custom_call" | custom-call | bytes 200000000 | tf_op jit(solution)/shard_map/share_step/pallas_call | solution.py:816
  147.2 38.9 %all-gather.8.cloned.1.call-done.right_b = bf16[2048,512]{1,0:T(8,128)(2,1)} async-done(((bf16[512,512]{1,0:T(8,128)(2,1)}), bf16[2048,512]{1,0:T(8,128)(2,1)}) %all-gather.8.cloned.1.call-update) | async-done | bytes 2097168 | tf_op jit(solution)/shard_map/all_gather | solution.py:1015
  186.2 5.2 fusion.84
  195.3 46.0 %all-gather.6.cloned.1.call-done.right_a = bf16[2048,640]{1,0:T(8,128)(2,1)} async-done(((bf16[512,640]{1,0:T(8,128)(2,1)}), bf16[2048,640]{1,0:T(8,128)(2,1)}) %all-gather.6.cloned.1.call-update) | async-done | bytes 2621456 | tf_op jit(solution)/shard_map/all_gather | solution.py:1015
  241.3 6.0 fusion.83
  251.2 3.4 collective-permute-start.11
  262.0 26.7 %collective-permute-done = bf16[3,512]{1,0:T(4,128)(2,1)S(1)} collective-permute-done((bf16[3,512]{1,0:T(4,128)(2,1)S(1)}, bf16[3,512]{1,0:T(4,128)(2,1)S(1)}, u32[]{:S(2)}, u32[]{:S(2)}) %collective-permute-start) | collective-permute-done | bytes 3104 | tf_op jit(solution)/shard_map/ppermute | solution.py:51
  288.8 3.6 multiply_convert_fusion.3
  313.0 12.6 %ssd_forward.1 = (f32[1024,384]{1,0:T(8,128)}, f32[8,384,256]{2,1,0:T(8,128)}, f32[384,256]{1,0:T(8,128)}, f32[1024,128]{1,0:T(8,128)}) custom-call(s32[1]{0:T(128)} %bitcast.base_ref, s32[8]{0:T(128)} %starts_ref.7, bf16[1024,384]{1,0:T(8,128)(2,1)} %slice.336.x_ref, bf16[1024,256]{1,0:T(8,128)(2,1)} %copy.389.b_ref, bf16[1024,256]{1,0:T(8,128)(2,1)} %copy.390.c_ref, ...), custom_call_target="tpu_custom_call" | custom-call | flops 603979776 | bytes 3145728 | tf_op jit(solution)/shard_map/ssd_forward/pallas_call | solution.py:193
  327.0 19.9 %collective-permute-start.7 = (f32[384,1]{0,1:T(1,128)}, f32[384,1]{0,1:T(1,128)S(1)}, u32[]{:S(2)}, u32[]{:S(2)}) collective-permute-start(f32[384,1]{0,1:T(1,128)} %broadcast_in_dim.145), channel_id=1, source_target_pairs={{0,16},{8,24},{1,17},{9,25},{2,18},{10,26},{3,19},{11,27},{4,20},{... | collective-permute-start | bytes 4616 | tf_op jit(solution)/shard_map/ppermute | solution.py:940
  361.1 3.1 copy.393
  368.9 7.6 collective-permute-done.4
  377.9 4.7 multiply_convert_fusion.6
  382.6 6.2 collective-permute-done.12
  391.5 3.7 reshape.425
  400.3 6.8 attend.1
  409.3 63.9 %mid_step.1 = (f32[128,2048]{1,0:T(8,128)}, bf16[1024,2048]{1,0:T(8,128)(2,1)}) custom-call(bf16[1024,512]{1,0:T(8,128)(2,1)} %pad_maximum_fusion.4.left, bf16[2048,512]{1,0:T(8,128)(2,1)} %all-gather.10.cloned.1.call-done.right, f32[128,2048]{1,0:T(8,128)} %constant_dynamic-slice_fusion.23.refs_0_.resid.hidden_own, f32[1,2048]{1,0:T(1,128)} %bitcast.337), custom_call_target="tpu_custom_call" | custom-call | bytes 150000000 | tf_op jit(solution)/shard_map/mid_step/pallas_call | solution.py:682
  473.2 10.0 %fusion.85 = f32[1024,1024]{1,0:T(8,128)} fusion(bf16[1024,2048]{1,0:T(8,128)(2,1)} %get-tuple-element.64, bf16[2048,1024]{1,0:T(8,128)(2,1)} %all-gather.12.cloned.1.call-done.right), kind=kOutput, calls=%fused_computation.258 | convolution fusion | flops 4294967296 | bytes 12582912 | tf_op jit(solution)/shard_map/dot_general | solution.py:32
  483.2 8.3 multiply_convert_fusion.1
  491.5 6.5 convolution_convert_fusion
  501.0 5.0 convolution_convert_fusion.4
  506.0 65.0 %two_step.1 = (f32[128,2048]{1,0:T(8,128)}, f32[1,2048]{1,0:T(1,128)}, bf16[1024,2048]{1,0:T(8,128)(2,1)}) custom-call(bf16[1024,1024]{1,0:T(8,128)(2,1)} %pad_maximum_fusion.1.left, bf16[2048,1024]{1,0:T(8,128)(2,1)} %all-gather.12.cloned.1.call-done.right, f32[128,2048]{1,0:T(8,128)} %get-tuple-element.63.mid_own, ...), custom_call_target="tpu_custom_call" | custom-call | bytes 150000000 | tf_op jit(solution)/shard_map/two_step/pallas_call | solution.py:682
  571.0 5.9 convolution_convert_fusion.2
  582.0 16.8 %collective-permute-done.23 = f32[384,1]{0,1:T(1,128)S(1)} collective-permute-done((f32[384,1]{0,1:T(1,128)}, f32[384,1]{0,1:T(1,128)S(1)}, u32[]{:S(2)}, u32[]{:S(2)}) %collective-permute-start.23) | collective-permute-done | bytes 1568 | tf_op jit(solution)/shard_map/ppermute | solution.py:940
  598.8 4.7 fusion.87
  611.1 10.1 %attend_back.1 = (f32[1024,128]{1,0:T(8,128)}, f32[4096,128]{1,0:T(8,128)}, f32[4096,128]{1,0:T(8,128)}) custom-call(s32[1]{0:T(128)} %bitcast.base_ref, s32[8]{0:T(128)} %starts_ref.7, bf16[1024,128]{1,0:T(8,128)(2,1)} %copy.404.q_ref, bf16[1024,128]{1,0:T(8,128)(2,1)} %slice.465.do_ref, f32[1024,128]{1,0:T(8,128)} %get-tuple-element.61.o_ref, ...), custom_call_target="tpu_custom_call" | custom-call | flops 5368709120 | bytes 10485760 | tf_op jit(solution)/shard_map/attend_back/pallas_call | solution.py:430
  621.2 2.9 copy.425
  631.9 2.9 copy.426
  634.8 3.7 reshape.435
  647.6 3.8 convolution_convert_fusion.3
  658.2 22.9 %ssd_backward.1 = (f32[1024,384]{1,0:T(8,128)}, f32[1024,512]{1,0:T(8,128)}, f32[1024,128]{1,0:T(8,128)}, f32[8,128]{1,0:T(8,128)}, f32[1,384]{1,0:T(1,128)}) custom-call(s32[1]{0:T(128)} %bitcast.base_ref, s32[8]{0:T(128)} %starts_ref.7, bf16[1024,384]{1,0:T(8,128)(2,1)} %slice.336.x_ref, bf16[1024,256]{1,0:T(8,128)(2,1)} %copy.389.b_ref, ...), custom_call_target="tpu_custom_call" | custom-call | flops 1610612736 | bytes 6291456 | tf_op jit(solution)/shard_map/ssd_backward/pallas_call | solution.py:313
  682.2 3.0 copy.417
  685.1 4.0 reshape.432
  717.6 25.8 %collective-permute-done.34 = bf16[1024,64]{1,0:T(8,128)(2,1)S(1)} collective-permute-done((bf16[1024,64]{1,0:T(8,128)(2,1)S(1)}, bf16[1024,64]{1,0:T(8,128)(2,1)S(1)}, u32[]{:S(2)}, u32[]{:S(2)}) %collective-permute-start.34) | collective-permute-done | bytes 131104 | tf_op jit(solution)/shard_map/ppermute | solution.py:51
  744.5 10.0 %collective-permute-done.36 = bf16[1024,64]{1,0:T(8,128)(2,1)S(1)} collective-permute-done((bf16[1024,64]{1,0:T(8,128)(2,1)S(1)}, bf16[1024,64]{1,0:T(8,128)(2,1)S(1)}, u32[]{:S(2)}, u32[]{:S(2)}) %collective-permute-start.36) | collective-permute-done | bytes 131104 | tf_op jit(solution)/shard_map/ppermute | solution.py:51
  754.5 9.8 %collective-permute-done.35 = bf16[1024,64]{1,0:T(8,128)(2,1)S(1)} collective-permute-done((bf16[1024,64]{1,0:T(8,128)(2,1)S(1)}, bf16[1024,64]{1,0:T(8,128)(2,1)S(1)}, u32[]{:S(2)}, u32[]{:S(2)}) %collective-permute-start.35) | collective-permute-done | bytes 131104 | tf_op jit(solution)/shard_map/ppermute | solution.py:51
  765.6 3.1 fusion.36
  774.9 3.2 collective-permute-done.30
  780.7 7.5 convolution_convert_fusion.1
  788.9 4.3 fusion.86
  793.2 3.3 copy-done.11
  802.6 3.5 bitcast_add_fusion
  815.3 49.3 %one_step.1 = (f32[256,2048]{1,0:T(8,128)}, f32[1,2048]{1,0:T(1,128)}) custom-call(bf16[1024,640]{1,0:T(8,128)(2,1)} %concatenate.97.left_a, bf16[2048,640]{1,0:T(8,128)(2,1)} %all-gather.6.cloned.1.call-done.right_a, bf16[1024,512]{1,0:T(8,128)(2,1)} %pad_maximum_fusion.5.left_b, bf16[2048,512]{1,0:T(8,128)(2,1)} %all-gather.8.cloned.1.call-done.right_b, ...), custom_call_target="tpu_custom_call" | custom-call | bytes 150000000 | tf_op jit(solution)/shard_map/one_step/pallas_call | solution.py:682
  865.9 13.1 %sums_step.1 = f32[2,4,56,128]{3,2,1,0:T(8,128)} custom-call(f32[56,128]{1,0:T(8,128)} %pad.56.v_ref), custom_call_target="tpu_custom_call" | custom-call | bytes 150000000 | tf_op jit(solution)/shard_map/sums_step/pallas_call | solution.py:682
  909.8 2.9 collective-permute-done.44
  930.3 5.0 collective-permute-done.41
  948.5 3.7 collective-permute-done.48
  (519 shorter events, 266.0 us)
Async XLA Ops:
  7.2 178.9 %all-gather.8.cloned.1.call-start = ((), (), s32[]{:S(2)}) async-start(), calls=%async_computation.6 | async-start | bytes 2621440 | tf_op jit(solution)/shard_map/all_gather | solution.py:1015
  141.2 100.1 %all-gather.6.cloned.1.call-start = ((), (), s32[]{:S(2)}) async-start(), calls=%async_computation.5 | async-start | bytes 3276800 | tf_op jit(solution)/shard_map/all_gather | solution.py:1015
  141.9 267.4 %all-gather.10.cloned.1.call-start = ((), (), s32[]{:S(2)}) async-start(), calls=%async_computation.7 | async-start | bytes 2621440 | tf_op jit(solution)/shard_map/all_gather | solution.py:1015
  142.7 330.6 %all-gather.12.cloned.1.call-start = ((), (), s32[]{:S(2)}) async-start(), calls=%async_computation.8 | async-start | bytes 5242880 | tf_op jit(solution)/shard_map/all_gather | solution.py:1015
  143.2 340.0 %all-gather.14.cloned.1.call-start = ((), (), s32[]{:S(2)}) async-start(), calls=%async_computation.9 | async-start | bytes 2621440 | tf_op jit(solution)/shard_map/all_gather | solution.py:1015
  143.8 745.2 %reduce-scatter.10.cloned.1.call-start = ((), (), s32[]{:S(2)}) async-start(), calls=%async_computation.12 | async-start | bytes 2621440 | tf_op jit(solution)/shard_map/reduce_scatter | solution.py:1113
  251.2 47.1 %collective-permute-start.11 = (bf16[1024,64]{1,0:T(8,128)(2,1)}, bf16[1024,64]{1,0:T(8,128)(2,1)}, u32[]{:S(2)}, u32[]{:S(2)}) collective-permute-start(bf16[1024,64]{1,0:T(8,128)(2,1)} %pad_maximum_fusion.11), channel_id=1, source_target_pairs={{0,24},{1,25},{2,26},{3,27},{4,28},{5,29},{6,30},{7,31}} | collective-permute-start | bytes 393224 | tf_op jit(solution)/shard_map/ppermute | solution.py:51
  254.6 44.8 %collective-permute-start.10 = (bf16[1024,64]{1,0:T(8,128)(2,1)}, bf16[1024,64]{1,0:T(8,128)(2,1)}, u32[]{:S(2)}, u32[]{:S(2)}) collective-permute-start(bf16[1024,64]{1,0:T(8,128)(2,1)} %pad_maximum_fusion.11), channel_id=1, source_target_pairs={{0,16},{8,24},{1,17},{9,25},{2,18},{10,26},{3,19},{11,27},{4,20},{... | collective-permute-start | bytes 393224 | tf_op jit(solution)/shard_map/ppermute | solution.py:51
  256.6 40.2 %collective-permute-start.9 = (bf16[1024,64]{1,0:T(8,128)(2,1)}, bf16[1024,64]{1,0:T(8,128)(2,1)}, u32[]{:S(2)}, u32[]{:S(2)}) collective-permute-start(bf16[1024,64]{1,0:T(8,128)(2,1)} %pad_maximum_fusion.11), channel_id=1, source_target_pairs={{0,8},{8,16},{16,24},{1,9},{9,17},{17,25},{2,10},{10,18},{18,26},{... | collective-permute-start | bytes 393224 | tf_op jit(solution)/shard_map/ppermute | solution.py:51
  259.1 29.6 %collective-permute-start = (bf16[3,512]{1,0:T(4,128)(2,1)S(1)}, bf16[3,512]{1,0:T(4,128)(2,1)S(1)}, u32[]{:S(2)}, u32[]{:S(2)}) collective-permute-start(bf16[3,512]{1,0:T(4,128)(2,1)S(1)} %slice.326), channel_id=1, source_target_pairs={{0,8},{8,16},{16,24},{1,9},{9,17},{17,25},{2,10},{10,18},{18,26},{... | collective-permute-start | bytes 9224 | tf_op jit(solution)/shard_map/ppermute | solution.py:51
  296.8 10.8 %collective-permute-start.3 = (bf16[1024,128]{1,0:T(8,128)(2,1)S(1)}, bf16[1024,128]{1,0:T(8,128)(2,1)}, u32[]{:S(2)}, u32[]{:S(2)}) collective-permute-start(bf16[1024,128]{1,0:T(8,128)(2,1)S(1)} %get-tuple-element.217), channel_id=1, source_target_pairs={{0,6},{2,4},{4,2},{6,0},{1,7},{3,5},{5,3},{7,1},{8,14},{10,12},{12... | collective-permute-start | bytes 786440 | tf_op jit(solution)/shard_map/ppermute | solution.py:899
  327.0 37.2 %collective-permute-start.7 = (f32[384,1]{0,1:T(1,128)}, f32[384,1]{0,1:T(1,128)S(1)}, u32[]{:S(2)}, u32[]{:S(2)}) collective-permute-start(f32[384,1]{0,1:T(1,128)} %broadcast_in_dim.145), channel_id=1, source_target_pairs={{0,16},{8,24},{1,17},{9,25},{2,18},{10,26},{3,19},{11,27},{4,20},{... | collective-permute-start | bytes 4616 | tf_op jit(solution)/shard_map/ppermute | solution.py:940
  346.9 19.9 %collective-permute-start.5 = (f32[384,1]{0,1:T(1,128)}, f32[384,1]{0,1:T(1,128)}, u32[]{:S(2)}, u32[]{:S(2)}) collective-permute-start(f32[384,1]{0,1:T(1,128)} %broadcast_in_dim.145), channel_id=1, source_target_pairs={{0,8},{8,16},{16,24},{1,9},{9,17},{17,25},{2,10},{10,18},{18,26},{... | collective-permute-start | bytes 4616 | tf_op jit(solution)/shard_map/ppermute | solution.py:940
  349.7 18.3 %collective-permute-start.8 = (bf16[384,256]{1,0:T(8,128)(2,1)S(1)}, bf16[384,256]{1,0:T(8,128)(2,1)S(1)}, u32[]{:S(2)}, u32[]{:S(2)}) collective-permute-start(bf16[384,256]{1,0:T(8,128)(2,1)S(1)} %convert_element_type.351), channel_id=1, source_target_pairs={{0,24},{1,25},{2,26},{3,27},{4,28},{5,29},{6,30},{7,31}} | collective-permute-start | bytes 589832 | tf_op jit(solution)/shard_map/ppermute | solution.py:939
  351.1 17.9 %collective-permute-start.6 = (bf16[384,256]{1,0:T(8,128)(2,1)S(1)}, bf16[384,256]{1,0:T(8,128)(2,1)}, u32[]{:S(2)}, u32[]{:S(2)}) collective-permute-start(bf16[384,256]{1,0:T(8,128)(2,1)S(1)} %convert_element_type.351), channel_id=1, source_target_pairs={{0,16},{8,24},{1,17},{9,25},{2,18},{10,26},{3,19},{11,27},{4,20},{... | collective-permute-start | bytes 589832 | tf_op jit(solution)/shard_map/ppermute | solution.py:939
  353.1 23.5 %collective-permute-start.4 = (bf16[384,256]{1,0:T(8,128)(2,1)S(1)}, bf16[384,256]{1,0:T(8,128)(2,1)}, u32[]{:S(2)}, u32[]{:S(2)}) collective-permute-start(bf16[384,256]{1,0:T(8,128)(2,1)S(1)} %convert_element_type.351), channel_id=1, source_target_pairs={{0,8},{8,16},{16,24},{1,9},{9,17},{17,25},{2,10},{10,18},{18,26},{... | collective-permute-start | bytes 589832 | tf_op jit(solution)/shard_map/ppermute | solution.py:939
  364.2 25.6 %collective-permute-start.14 = (bf16[4,1024,64]{1,2,0:T(8,128)(2,1)}, bf16[4,1024,64]{1,2,0:T(8,128)(2,1)S(1)}, u32[]{:S(2)}, u32[]{:S(2)}) collective-permute-start(bf16[4,1024,64]{1,2,0:T(8,128)(2,1)} %copy-done.27), channel_id=1, source_target_pairs={{0,6},{2,4},{4,2},{6,0},{1,7},{3,5},{5,3},{7,1},{8,14},{10,12},{12... | collective-permute-start | bytes 1572872 | tf_op jit(solution)/shard_map/ppermute | solution.py:899
  366.7 22.5 %collective-permute-start.13 = (bf16[4,1024,64]{1,2,0:T(8,128)(2,1)}, bf16[4,1024,64]{1,2,0:T(8,128)(2,1)S(1)}, u32[]{:S(2)}, u32[]{:S(2)}) collective-permute-start(bf16[4,1024,64]{1,2,0:T(8,128)(2,1)} %copy-done.27), channel_id=1, source_target_pairs={{0,4},{2,6},{4,0},{6,2},{1,5},{3,7},{5,1},{7,3},{8,12},{10,14},{12... | collective-permute-start | bytes 1572872 | tf_op jit(solution)/shard_map/ppermute | solution.py:899
  368.0 20.8 %collective-permute-start.12 = (bf16[4,1024,64]{1,2,0:T(8,128)(2,1)}, bf16[4,1024,64]{1,2,0:T(8,128)(2,1)S(1)}, u32[]{:S(2)}, u32[]{:S(2)}) collective-permute-start(bf16[4,1024,64]{1,2,0:T(8,128)(2,1)} %copy-done.27), channel_id=1, source_target_pairs={{0,2},{2,0},{4,6},{6,4},{1,3},{3,1},{5,7},{7,5},{8,10},{10,8},{12,... | collective-permute-start | bytes 1572872 | tf_op jit(solution)/shard_map/ppermute | solution.py:899
  577.0 313.9 %reduce-scatter.14.cloned.1.call-start = ((), (), s32[]{:S(2)}) async-start(), calls=%async_computation.14 | async-start | bytes 2621440 | tf_op jit(solution)/shard_map/reduce_scatter | solution.py:1113
  577.7 315.3 %reduce-scatter.6.cloned.1.call-start = ((), (), s32[]{:S(2)}) async-start(), calls=%async_computation.10 | async-start | bytes 2621440 | tf_op jit(solution)/shard_map/reduce_scatter | solution.py:1113
  577.8 21.0 %collective-permute-start.23 = (f32[384,1]{0,1:T(1,128)}, f32[384,1]{0,1:T(1,128)S(1)}, u32[]{:S(2)}, u32[]{:S(2)}) collective-permute-start(f32[384,1]{0,1:T(1,128)} %broadcast_in_dim.145), channel_id=1, source_target_pairs={{16,0},{24,8},{17,1},{25,9},{18,2},{26,10},{19,3},{27,11},{20,4},{... | collective-permute-start | bytes 4616 | tf_op jit(solution)/shard_map/ppermute | solution.py:940
  579.1 19.7 %collective-permute-start.21 = (f32[384,1]{0,1:T(1,128)}, f32[384,1]{0,1:T(1,128)S(1)}, u32[]{:S(2)}, u32[]{:S(2)}) collective-permute-start(f32[384,1]{0,1:T(1,128)} %broadcast_in_dim.145), channel_id=1, source_target_pairs={{8,0},{16,8},{24,16},{9,1},{17,9},{25,17},{10,2},{18,10},{26,18},{... | collective-permute-start | bytes 4616 | tf_op jit(solution)/shard_map/ppermute | solution.py:940
  607.2 48.2 %collective-permute-start.24 = (bf16[384,256]{1,0:T(8,128)(2,1)}, bf16[384,256]{1,0:T(8,128)(2,1)}, u32[]{:S(2)}, u32[]{:S(2)}) collective-permute-start(bf16[384,256]{1,0:T(8,128)(2,1)} %convolution_convert_fusion.5), channel_id=1, source_target_pairs={{24,0},{25,1},{26,2},{27,3},{28,4},{29,5},{30,6},{31,7}} | collective-permute-start | bytes 589832 | tf_op jit(solution)/shard_map/ppermute | solution.py:939
  608.5 47.7 %collective-permute-start.22 = (bf16[384,256]{1,0:T(8,128)(2,1)}, bf16[384,256]{1,0:T(8,128)(2,1)}, u32[]{:S(2)}, u32[]{:S(2)}) collective-permute-start(bf16[384,256]{1,0:T(8,128)(2,1)} %convolution_convert_fusion.5), channel_id=1, source_target_pairs={{16,0},{24,8},{17,1},{25,9},{18,2},{26,10},{19,3},{27,11},{20,4},{... | collective-permute-start | bytes 589832 | tf_op jit(solution)/shard_map/ppermute | solution.py:939
  609.8 46.4 %collective-permute-start.20 = (bf16[384,256]{1,0:T(8,128)(2,1)}, bf16[384,256]{1,0:T(8,128)(2,1)}, u32[]{:S(2)}, u32[]{:S(2)}) collective-permute-start(bf16[384,256]{1,0:T(8,128)(2,1)} %convolution_convert_fusion.5), channel_id=1, source_target_pairs={{8,0},{16,8},{24,16},{9,1},{17,9},{25,17},{10,2},{18,10},{26,18},{... | collective-permute-start | bytes 589832 | tf_op jit(solution)/shard_map/ppermute | solution.py:939
  644.7 55.4 %collective-permute-start.32 = (bf16[4,1024,64]{1,2,0:T(8,128)(2,1)}, bf16[4,1024,64]{1,2,0:T(8,128)(2,1)}, u32[]{:S(2)}, u32[]{:S(2)}) collective-permute-start(bf16[4,1024,64]{1,2,0:T(8,128)(2,1)} %copy.430), channel_id=1, source_target_pairs={{0,4},{2,6},{4,0},{6,2},{1,5},{3,7},{5,1},{7,3},{8,12},{10,14},{12... | collective-permute-start | bytes 1572872 | tf_op jit(solution)/shard_map/ppermute | solution.py:910
  646.1 56.4 %collective-permute-start.33 = (bf16[4,1024,64]{1,2,0:T(8,128)(2,1)}, bf16[4,1024,64]{1,2,0:T(8,128)(2,1)}, u32[]{:S(2)}, u32[]{:S(2)}) collective-permute-start(bf16[4,1024,64]{1,2,0:T(8,128)(2,1)} %copy.432), channel_id=1, source_target_pairs={{0,6},{2,4},{4,2},{6,0},{1,7},{3,5},{5,3},{7,1},{8,14},{10,12},{12... | collective-permute-start | bytes 1572872 | tf_op jit(solution)/shard_map/ppermute | solution.py:910
  655.4 262.5 %reduce-scatter.8.cloned.1.call-start = ((), (), s32[]{:S(2)}) async-start(), calls=%async_computation.11 | async-start | bytes 3276800 | tf_op jit(solution)/shard_map/reduce_scatter | solution.py:1113
  655.4 49.4 %collective-permute-start.31 = (bf16[4,1024,64]{1,2,0:T(8,128)(2,1)}, bf16[4,1024,64]{1,2,0:T(8,128)(2,1)}, u32[]{:S(2)}, u32[]{:S(2)}) collective-permute-start(bf16[4,1024,64]{1,2,0:T(8,128)(2,1)} %copy.428), channel_id=1, source_target_pairs={{0,2},{2,0},{4,6},{6,4},{1,3},{3,1},{5,7},{7,5},{8,10},{10,8},{12,... | collective-permute-start | bytes 1572872 | tf_op jit(solution)/shard_map/ppermute | solution.py:910
  700.1 13.6 %collective-permute-start.25 = (bf16[4,512,128]{2,1,0:T(8,128)(2,1)}, bf16[4,512,128]{2,1,0:T(8,128)(2,1)}, u32[]{:S(2)}, u32[]{:S(2)}) collective-permute-start(bf16[4,512,128]{2,1,0:T(8,128)(2,1)} %bitcast.320), channel_id=1, source_target_pairs={{0,1},{1,0},{2,3},{3,2},{4,5},{5,4},{6,7},{7,6},{8,9},{9,8},{10,11... | collective-permute-start | bytes 1572872 | tf_op jit(solution)/shard_map/ppermute | solution.py:916
  709.7 33.7 %collective-permute-start.34 = (bf16[1024,64]{1,0:T(8,128)(2,1)S(1)}, bf16[1024,64]{1,0:T(8,128)(2,1)S(1)}, u32[]{:S(2)}, u32[]{:S(2)}) collective-permute-start(bf16[1024,64]{1,0:T(8,128)(2,1)S(1)} %get-tuple-element.200), channel_id=1, source_target_pairs={{8,0},{16,8},{24,16},{9,1},{17,9},{25,17},{10,2},{18,10},{26,18},{... | collective-permute-start | bytes 393224 | tf_op jit(solution)/shard_map/ppermute | solution.py:51
  711.1 43.4 %collective-permute-start.36 = (bf16[1024,64]{1,0:T(8,128)(2,1)S(1)}, bf16[1024,64]{1,0:T(8,128)(2,1)S(1)}, u32[]{:S(2)}, u32[]{:S(2)}) collective-permute-start(bf16[1024,64]{1,0:T(8,128)(2,1)S(1)} %get-tuple-element.201), channel_id=1, source_target_pairs={{24,0},{25,1},{26,2},{27,3},{28,4},{29,5},{30,6},{31,7}} | collective-permute-start | bytes 393224 | tf_op jit(solution)/shard_map/ppermute | solution.py:51
  712.4 51.9 %collective-permute-start.35 = (bf16[1024,64]{1,0:T(8,128)(2,1)S(1)}, bf16[1024,64]{1,0:T(8,128)(2,1)S(1)}, u32[]{:S(2)}, u32[]{:S(2)}) collective-permute-start(bf16[1024,64]{1,0:T(8,128)(2,1)S(1)} %get-tuple-element.202), channel_id=1, source_target_pairs={{16,0},{24,8},{17,1},{25,9},{18,2},{26,10},{19,3},{27,11},{20,4},{... | collective-permute-start | bytes 393224 | tf_op jit(solution)/shard_map/ppermute | solution.py:51
  715.0 50.3 %collective-permute-start.26 = (bf16[512,128]{1,0:T(8,128)(2,1)S(1)}, bf16[512,128]{1,0:T(8,128)(2,1)S(1)}, u32[]{:S(2)}, u32[]{:S(2)}) collective-permute-start(bf16[512,128]{1,0:T(8,128)(2,1)S(1)} %get-tuple-element.212), channel_id=1, source_target_pairs={{0,2},{2,0},{4,6},{6,4},{1,3},{3,1},{5,7},{7,5},{8,10},{10,8},{12,... | collective-permute-start | bytes 393224 | tf_op jit(solution)/shard_map/ppermute | solution.py:910
  716.1 49.2 %collective-permute-start.28 = (bf16[512,128]{1,0:T(8,128)(2,1)S(1)}, bf16[512,128]{1,0:T(8,128)(2,1)S(1)}, u32[]{:S(2)}, u32[]{:S(2)}) collective-permute-start(bf16[512,128]{1,0:T(8,128)(2,1)S(1)} %get-tuple-element.213), channel_id=1, source_target_pairs={{0,6},{2,4},{4,2},{6,0},{1,7},{3,5},{5,3},{7,1},{8,14},{10,12},{12... | collective-permute-start | bytes 393224 | tf_op jit(solution)/shard_map/ppermute | solution.py:910
  743.4 21.9 %collective-permute-start.27 = (bf16[512,128]{1,0:T(8,128)(2,1)S(1)}, bf16[512,128]{1,0:T(8,128)(2,1)S(1)}, u32[]{:S(2)}, u32[]{:S(2)}) collective-permute-start(bf16[512,128]{1,0:T(8,128)(2,1)S(1)} %get-tuple-element.214), channel_id=1, source_target_pairs={{0,4},{2,6},{4,0},{6,2},{1,5},{3,7},{5,1},{7,3},{8,12},{10,14},{12... | collective-permute-start | bytes 393224 | tf_op jit(solution)/shard_map/ppermute | solution.py:910
  788.3 139.7 %reduce-scatter.12.cloned.1.call-start = ((), (), s32[]{:S(2)}) async-start(), calls=%async_computation.13 | async-start | bytes 5242880 | tf_op jit(solution)/shard_map/reduce_scatter | solution.py:1113
  809.3 70.7 %collective-permute-start.16 = (bf16[128,2048]{1,0:T(8,128)(2,1)}, bf16[128,2048]{1,0:T(8,128)(2,1)}, u32[]{:S(2)}, u32[]{:S(2)}) collective-permute-start(bf16[128,2048]{1,0:T(8,128)(2,1)} %get-tuple-element.191), channel_id=1, source_target_pairs={{0,2},{2,0},{4,6},{6,4},{1,3},{3,1},{5,7},{7,5},{8,10},{10,8},{12,... | collective-permute-start | bytes 1572872 | tf_op jit(solution)/shard_map/ppermute | solution.py:910
  810.8 69.2 %collective-permute-start.18 = (bf16[128,2048]{1,0:T(8,128)(2,1)}, bf16[128,2048]{1,0:T(8,128)(2,1)}, u32[]{:S(2)}, u32[]{:S(2)}) collective-permute-start(bf16[128,2048]{1,0:T(8,128)(2,1)} %get-tuple-element.192), channel_id=1, source_target_pairs={{0,6},{2,4},{4,2},{6,0},{1,7},{3,5},{5,3},{7,1},{8,14},{10,12},{12... | collective-permute-start | bytes 1572872 | tf_op jit(solution)/shard_map/ppermute | solution.py:910
  812.3 67.8 %collective-permute-start.17 = (bf16[128,2048]{1,0:T(8,128)(2,1)}, bf16[128,2048]{1,0:T(8,128)(2,1)}, u32[]{:S(2)}, u32[]{:S(2)}) collective-permute-start(bf16[128,2048]{1,0:T(8,128)(2,1)} %get-tuple-element.193), channel_id=1, source_target_pairs={{0,4},{2,6},{4,0},{6,2},{1,5},{3,7},{5,1},{7,3},{8,12},{10,14},{12... | collective-permute-start | bytes 1572872 | tf_op jit(solution)/shard_map/ppermute | solution.py:910
  894.4 10.5 %collective-permute-start.39 = (bf16[1,128,512]{1,2,0:T(8,128)(2,1)S(1)}, bf16[1,128,512]{1,2,0:T(8,128)(2,1)S(1)}, u32[]{:S(2)}, u32[]{:S(2)}) collective-permute-start(bf16[1,128,512]{1,2,0:T(8,128)(2,1)S(1)} %get-tuple-element.236), channel_id=1, source_target_pairs={{0,6},{2,4},{4,2},{6,0},{1,7},{3,5},{5,3},{7,1},{8,14},{10,12},{12... | collective-permute-start | bytes 393224 | tf_op jit(solution)/shard_map/ppermute | solution.py:888
  895.6 9.3 collective-permute-start.38
  898.0 14.7 %collective-permute-start.45 = (bf16[1,128,512]{2,1,0:T(8,128)(2,1)S(1)}, bf16[1,128,512]{2,1,0:T(8,128)(2,1)S(1)}, u32[]{:S(2)}, u32[]{:S(2)}) collective-permute-start(bf16[1,128,512]{2,1,0:T(8,128)(2,1)S(1)} %get-tuple-element.233), channel_id=1, source_target_pairs={{0,6},{2,4},{4,2},{6,0},{1,7},{3,5},{5,3},{7,1},{8,14},{10,12},{12... | collective-permute-start | bytes 393224 | tf_op jit(solution)/shard_map/ppermute | solution.py:888
  899.2 13.5 %collective-permute-start.44 = (bf16[1,128,512]{2,1,0:T(8,128)(2,1)S(1)}, bf16[1,128,512]{2,1,0:T(8,128)(2,1)S(1)}, u32[]{:S(2)}, u32[]{:S(2)}) collective-permute-start(bf16[1,128,512]{2,1,0:T(8,128)(2,1)S(1)} %get-tuple-element.234), channel_id=1, source_target_pairs={{0,4},{2,6},{4,0},{6,2},{1,5},{3,7},{5,1},{7,3},{8,12},{10,14},{12... | collective-permute-start | bytes 393224 | tf_op jit(solution)/shard_map/ppermute | solution.py:888
  905.1 10.0 %collective-permute-start.51 = (bf16[1,128,512]{2,1,0:T(8,128)(2,1)S(1)}, bf16[1,128,512]{2,1,0:T(8,128)(2,1)S(1)}, u32[]{:S(2)}, u32[]{:S(2)}) collective-permute-start(bf16[1,128,512]{2,1,0:T(8,128)(2,1)S(1)} %get-tuple-element.230), channel_id=1, source_target_pairs={{0,6},{2,4},{4,2},{6,0},{1,7},{3,5},{5,3},{7,1},{8,14},{10,12},{12... | collective-permute-start | bytes 393224 | tf_op jit(solution)/shard_map/ppermute | solution.py:888
  920.0 10.2 %collective-permute-start.40 = (bf16[1,128,640]{1,2,0:T(8,128)(2,1)}, bf16[1,128,640]{1,2,0:T(8,128)(2,1)S(1)}, u32[]{:S(2)}, u32[]{:S(2)}) collective-permute-start(bf16[1,128,640]{1,2,0:T(8,128)(2,1)} %get-tuple-element.223), channel_id=1, source_target_pairs={{0,2},{2,0},{4,6},{6,4},{1,3},{3,1},{5,7},{7,5},{8,10},{10,8},{12,... | collective-permute-start | bytes 491528 | tf_op jit(solution)/shard_map/ppermute | solution.py:888
  925.7 9.6 collective-permute-start.42
  (91 other events, 1782.7 us)
Sparse Core Ops, SparseCore 0:
  141.3 44.8 all-gather.7
  187.7 53.5 all-gather.5
  242.9 57.9 all-gather.9
  302.3 97.2 all-gather.11
  401.0 52.2 all-gather.13
  577.1 71.7 reduce-scatter.9
  651.3 46.2 reduce-scatter.13
  699.9 47.7 reduce-scatter.5
  788.4 50.2 reduce-scatter.7
  840.9 78.2 reduce-scatter.11

commit v3 on v2

--- a/solution.py
+++ b/solution.py
@@ -139,9 +139,18 @@
     return docs_t, linked, dt, la, tri, cum, carried, tail
 
 
+def split_bc(bc_ref):
+    parts = [bc_ref[q] for q in range(bc_ref.shape[0])]
+    half = parts[0].shape[1] // 2
+    return (
+        jnp.concatenate([part[:, :half] for part in parts], axis=1),
+        jnp.concatenate([part[:, half:] for part in parts], axis=1),
+    )
+
+
 def ssd_forward_kernel(
-    n_heads, base_ref, starts_ref, x_ref, b_ref, c_ref, dtp_ref, nega_ref, skip_ref,
-    y_ref, span_ref, final_ref, decay_ref, state, running,
+    n_heads, base_ref, starts_ref, x_ref, bc_ref, dtp_ref, nega_ref, skip_ref,
+    y_ref, span_ref, final_ref, decay_ref, wide_ref, c_out, state, running,
 ):
     k = pl.program_id(0)
     xw = n_heads * MHDIM
@@ -156,11 +165,14 @@
     )
     lane_head, row_head = head_maps(xw)
     prev_doc = docs_of(base_ref[0] - 1, starts_ref)
-    decay_ref[...] = jnp.where(docs_t == prev_doc, jnp.exp(running[0:1, :] + cum), 0.0)
+    since = jnp.where(docs_t == prev_doc, jnp.exp(running[0:1, :] + cum), 0.0)
+    decay_ref[...] = since
+    wide_ref[...] = tri_dot(since, lane_head)
     running[...] = running[...] + cum[SPAN - 1 : SPAN, :]
     start = state[...]
     span_ref[0] = start
-    x, b, c = x_ref[...], b_ref[...], c_ref[...]
+    x, (b, c) = x_ref[...], split_bc(bc_ref)
+    c_out[...] = c
     inner = dot_nt(c, b)
     cum_t, dt_t = cum.T, dt.T
     lane = iota2((SPAN, 128), 1)
@@ -184,8 +196,8 @@
     final_ref[...] = new
 
 
-def ssd_forward(base, doc_starts, x, b, c, dtp, nega, skip):
-    tok, xw = x.shape
+def ssd_forward(base, doc_starts, x, bc, dtp, nega, skip):
+    tok, xw, n_p = x.shape[0], skip.shape[1], bc.shape[0]
     n_heads, nspan = xw // MHDIM, tok // SPAN
     row = lambda n: pl.BlockSpec((SPAN, n), lambda i: (i, 0))
     whole = lambda *s: pl.BlockSpec(s, lambda i: (0,) * len(s))
@@ -194,31 +206,36 @@
         functools.partial(ssd_forward_kernel, n_heads),
         grid=(nspan,),
         in_specs=[
-            smem, smem, row(xw), row(NSTATE), row(NSTATE), row(128), whole(1, 128), whole(1, xw)
+            smem, smem, row(xw), pl.BlockSpec((n_p, SPAN, 128), lambda i: (0, i, 0)), row(128),
+            whole(1, 128), whole(1, xw),
         ],
         out_specs=[
             row(xw),
             pl.BlockSpec((1, xw, NSTATE), lambda i: (i, 0, 0)),
             whole(xw, NSTATE),
             row(128),
+            row(xw),
+            row(NSTATE),
         ],
         out_shape=[
             jax.ShapeDtypeStruct((tok, xw), f32),
             jax.ShapeDtypeStruct((nspan, xw, NSTATE), f32),
             jax.ShapeDtypeStruct((xw, NSTATE), f32),
             jax.ShapeDtypeStruct((tok, 128), f32),
+            jax.ShapeDtypeStruct((tok, xw), f32),
+            jax.ShapeDtypeStruct((tok, NSTATE), bf16),
         ],
         scratch_shapes=[pltpu.VMEM((xw, NSTATE), f32), pltpu.VMEM((8, 128), f32)],
         compiler_params=pltpu.CompilerParams(vmem_limit_bytes=VMEM_LIMIT),
         cost_estimate=pl.CostEstimate(
-            flops=2 * tok * xw * NSTATE * 3, bytes_accessed=8 * tok * xw, transcendentals=0
+            flops=2 * tok * xw * NSTATE * 3, bytes_accessed=40_000_000, transcendentals=0
         ),
         name="ssd_forward",
-    )(base, doc_starts, x, b, c, dtp, nega, skip)
+    )(base, doc_starts, x, bc, dtp, nega, skip)
 
 
 def ssd_backward_kernel(
-    n_heads, base_ref, starts_ref, x_ref, b_ref, c_ref, dtp_ref, dy_ref, span_ref, decay_ref,
+    n_heads, base_ref, starts_ref, x_ref, bc_ref, dtp_ref, dy_ref, span_ref, decay_ref,
     nega_ref, skip_ref, in_ref, grad_ref,
     dx_ref, dbc_ref, ddt_ref, sums_ref, gskip_ref, gstate,
 ):
@@ -242,7 +259,7 @@
     start_low = start.astype(bf16)
     g = gstate[...]
     g_low = g.astype(bf16)
-    x, b, c, dy = x_ref[...], b_ref[...], c_ref[...], dy_ref[...]
+    x, (b, c), dy = x_ref[...], split_bc(bc_ref), dy_ref[...]
     dy_low = dy.astype(bf16)
     xf = x.astype(f32)
     inner = dot_nt(c, b)
@@ -282,8 +299,12 @@
     d_dt = tri_dot(xf * u, row_head)
     tail_x = (xf * tri_dot(tail * dt, lane_head)).astype(bf16)
     dx_ref[...] = dt_full * u + skip_ref[...] * dy
-    dbc_ref[:, :NSTATE] = dot_nn(tail_x, g_low) + dot_tn(di_low, c)
-    dbc_ref[:, NSTATE:] = dot_nn(dye_low, start_low) + dot_nn(di_low, b)
+    d_b = dot_nn(tail_x, g_low) + dot_tn(di_low, c)
+    d_c = dot_nn(dye_low, start_low) + dot_nn(di_low, b)
+    bw = 64
+    for q in range(dbc_ref.shape[0]):
+        cut = slice(q * bw, q * bw + bw)
+        dbc_ref[q] = jnp.concatenate([d_b[:, cut], d_c[:, cut]], axis=1)
     gs = jnp.sum(g * start, axis=1, keepdims=True)
     gs_row = jnp.sum(row_head * gs, axis=0, keepdims=True)
     last = jnp.sum(k_state, axis=0, keepdims=True) + carried[SPAN - 1 : SPAN, :] * gs_row
@@ -303,9 +324,10 @@
 
 
 def ssd_backward(
-    base, doc_starts, x, b, c, dtp, dy, span_starts, start_decay, nega, skip, in_state, grad_state
+    base, doc_starts, x, bc, dtp, dy, span_starts, start_decay, nega, skip, in_state, grad_state
 ):
-    tok, xw = x.shape
+    tok, xw, n_p = x.shape[0], skip.shape[1], bc.shape[0]
+    wide = pl.BlockSpec((n_p, SPAN, 128), lambda i: (0, nspan - 1 - i, 0))
     n_heads, nspan = xw // MHDIM, tok // SPAN
     row = lambda n: pl.BlockSpec((SPAN, n), lambda i: (nspan - 1 - i, 0))
     whole = lambda *s: pl.BlockSpec(s, lambda i: (0,) * len(s))
@@ -314,15 +336,15 @@
         functools.partial(ssd_backward_kernel, n_heads),
         grid=(nspan,),
         in_specs=[
-            smem, smem, row(xw), row(NSTATE), row(NSTATE), row(128), row(xw),
+            smem, smem, row(xw), wide, row(128), row(xw),
             pl.BlockSpec((1, xw, NSTATE), lambda i: (nspan - 1 - i, 0, 0)),
             pl.BlockSpec((1, 1, 128), lambda i: (nspan - 1 - i, 0, 0)),
             whole(1, 128), whole(1, xw), whole(xw, NSTATE), whole(xw, NSTATE),
         ],
-        out_specs=[row(xw), row(2 * NSTATE), row(128), whole(8, 128), whole(1, xw)],
+        out_specs=[row(xw), wide, row(128), whole(8, 128), whole(1, xw)],
         out_shape=[
             jax.ShapeDtypeStruct((tok, xw), f32),
-            jax.ShapeDtypeStruct((tok, 2 * NSTATE), f32),
+            jax.ShapeDtypeStruct((n_p, tok, 128), f32),
             jax.ShapeDtypeStruct((tok, 128), f32),
             jax.ShapeDtypeStruct((8, 128), f32),
             jax.ShapeDtypeStruct((1, xw), f32),
@@ -330,10 +352,10 @@
         scratch_shapes=[pltpu.VMEM((xw, NSTATE), f32)],
         compiler_params=pltpu.CompilerParams(vmem_limit_bytes=VMEM_LIMIT),
         cost_estimate=pl.CostEstimate(
-            flops=2 * tok * xw * NSTATE * 8, bytes_accessed=16 * tok * xw, transcendentals=0
+            flops=2 * tok * xw * NSTATE * 8, bytes_accessed=80_000_000, transcendentals=0
         ),
         name="ssd_backward",
-    )(base, doc_starts, x, b, c, dtp, dy, span_starts, start_decay, nega, skip, in_state, grad_state)
+    )(base, doc_starts, x, bc, dtp, dy, span_starts, start_decay, nega, skip, in_state, grad_state)
 
 
 QB = 256
@@ -346,8 +368,23 @@
     return (q_pos >= k_pos) & (docs_of(q_pos, starts_ref) == docs_of(k_pos, starts_ref))
 
 
-def attend_kernel(scale, base_ref, starts_ref, q_ref, k_ref, v_ref, o_ref, lse_ref):
+def attend_kernel(scale, base_ref, starts_ref, q_ref, kv_ref, o_ref, lse_ref, k_ref, v_ref):
     i = pl.program_id(0)
+
+    @pl.when(i == 0)
+    def _():
+        n_p, nz, rows, _ = kv_ref.shape
+        kw = HDIM // n_p
+
+        @pl.loop(0, nz)
+        def _(z):
+            parts = [kv_ref[q, z] for q in range(n_p)]
+            for t in range(2):
+                at = pl.ds(pl.multiple_of((2 * z + t) * rows, rows), rows)
+                lo = 2 * kw * t
+                k_ref[at, :] = jnp.concatenate([v[:, lo : lo + kw] for v in parts], axis=1)
+                v_ref[at, :] = jnp.concatenate([v[:, lo + kw : lo + 2 * kw] for v in parts], axis=1)
+
     q = q_ref[...]
     blocks = (base_ref[0] + (i + 1) * QB + KB - 1) // KB
 
@@ -373,28 +410,30 @@
     lse_ref[...] = jnp.broadcast_to(m + jnp.log(l), (QB, 128))
 
 
-def attend(base, doc_starts, q, k, v):
+def attend(base, doc_starts, q, kv):
     tok = q.shape[0]
+    keys = kv.shape[1] * kv.shape[2] * 2
     row = pl.BlockSpec((QB, HDIM), lambda i: (i, 0))
-    whole = pl.BlockSpec(k.shape, lambda i: (0, 0))
+    whole = lambda s: pl.BlockSpec(s, lambda i: (0,) * len(s))
     smem = pl.BlockSpec(memory_space=pltpu.SMEM)
     return pl.pallas_call(
         functools.partial(attend_kernel, HDIM ** (-0.5)),
         grid=(tok // QB,),
-        in_specs=[smem, smem, row, whole, whole],
-        out_specs=[row, row],
-        out_shape=[jax.ShapeDtypeStruct((tok, HDIM), f32)] * 2,
+        in_specs=[smem, smem, row, whole(kv.shape)],
+        out_specs=[row, row, whole((keys, HDIM)), whole((keys, HDIM))],
+        out_shape=[jax.ShapeDtypeStruct((tok, HDIM), f32)] * 2
+        + [jax.ShapeDtypeStruct((keys, HDIM), bf16)] * 2,
         compiler_params=pltpu.CompilerParams(vmem_limit_bytes=VMEM_LIMIT),
         cost_estimate=pl.CostEstimate(
-            flops=4 * tok * k.shape[0] * HDIM, bytes_accessed=8 * k.size, transcendentals=0
+            flops=4 * tok * keys * HDIM, bytes_accessed=30_000_000, transcendentals=0
         ),
         name="attend",
-    )(base, doc_starts, q, k, v)
+    )(base, doc_starts, q, kv)
 
 
 def attend_back_kernel(
     scale, base_ref, starts_ref, q_ref, do_ref, o_ref, lse_ref, k_ref, v_ref,
-    dq_ref, dk_ref, dv_ref,
+    dq_ref, dkv_ref, dk_ref, dv_ref,
 ):
     i = pl.program_id(0)
 
@@ -421,25 +460,40 @@
 
     dq_ref[...] = lax.fori_loop(0, blocks, turn, jnp.zeros((QB, HDIM), f32)) * scale
 
-
-def attend_back(base, doc_starts, q, do, o, lse, k, v):
+    @pl.when(i == pl.num_programs(0) - 1)
+    def _():
+        n_p, nz, rows, _ = dkv_ref.shape
+        kw = HDIM // n_p
+
+        @pl.loop(0, nz)
+        def _(z):
+            got = []
+            for t in range(2):
+                at = pl.ds(pl.multiple_of((2 * z + t) * rows, rows), rows)
+                got += [dk_ref[at, :].astype(bf16), dv_ref[at, :].astype(bf16)]
+            for q in range(n_p):
+                cut = slice(q * kw, q * kw + kw)
+                dkv_ref[q, z] = jnp.concatenate([v[:, cut] for v in got], axis=1)
+
+
+def attend_back(base, doc_starts, q, do, o, lse, k, v, packed):
     tok = q.shape[0]
     row = pl.BlockSpec((QB, HDIM), lambda i: (i, 0))
-    whole = pl.BlockSpec(k.shape, lambda i: (0, 0))
+    whole = lambda s: pl.BlockSpec(s, lambda i: (0,) * len(s))
     smem = pl.BlockSpec(memory_space=pltpu.SMEM)
     return pl.pallas_call(
         functools.partial(attend_back_kernel, HDIM ** (-0.5)),
         grid=(tok // QB,),
-        in_specs=[smem, smem, row, row, row, row, whole, whole],
-        out_specs=[row, whole, whole],
+        in_specs=[smem, smem, row, row, row, row, whole(k.shape), whole(k.shape)],
+        out_specs=[row, whole(packed)],
         out_shape=[
             jax.ShapeDtypeStruct((tok, HDIM), f32),
-            jax.ShapeDtypeStruct(k.shape, f32),
-            jax.ShapeDtypeStruct(k.shape, f32),
+            jax.ShapeDtypeStruct(packed, bf16),
         ],
+        scratch_shapes=[pltpu.VMEM(k.shape, f32), pltpu.VMEM(k.shape, f32)],
         compiler_params=pltpu.CompilerParams(vmem_limit_bytes=VMEM_LIMIT),
         cost_estimate=pl.CostEstimate(
-            flops=10 * tok * k.shape[0] * HDIM, bytes_accessed=20 * k.size, transcendentals=0
+            flops=10 * tok * k.shape[0] * HDIM, bytes_accessed=40_000_000, transcendentals=0
         ),
         name="attend_back",
     )(base, doc_starts, q, do, o, lse, k, v)
@@ -678,7 +732,7 @@
 ]
 
 
-def plane_call(kernel, name, number, args, shapes, scratch, flops=0):
+def plane_call(kernel, name, number, args, shapes, scratch, nbytes=150_000_000):
     return pl.pallas_call(
         kernel,
         in_specs=[VM] * len(args),
@@ -688,7 +742,7 @@
         compiler_params=pltpu.CompilerParams(
             collective_id=number, has_side_effects=True, vmem_limit_bytes=VMEM_LIMIT
         ),
-        cost_estimate=pl.CostEstimate(flops=flops, bytes_accessed=150_000_000, transcendentals=0),
+        cost_estimate=pl.CostEstimate(flops=0, bytes_accessed=nbytes, transcendentals=0),
         name=name,
     )(*args)
 
@@ -723,111 +777,310 @@
     )
 
 
-def open_kernel(gains_ref, a_ref, gain_out, a_out, z_sems, p_sems, a_sems, loc_sems):
+HALO = 16
+
+
+def open_kernel(n, *refs):
+    hid, grad, gains_ref, a_ref = refs[:4]
+    w_refs = refs[4 : 4 + n]
+    gain_out, full_ref, gfull_ref, a_out = refs[4 + n : 8 + n]
+    w_outs = refs[8 + n : 8 + 2 * n]
+    (
+        g_vec, gz_sems, gp_sems, a_sems, up_sems, down_sems, own_sems, far_sems, near_sems,
+        own_g, far_g, near_g, w_sems, loc_sems, halo_sems,
+    ) = refs[8 + 2 * n :]
     z, p, c = place()
-    nz = gain_out.shape[1]
+    nz, half, rows = a_out.shape[0], hid.shape[0], a_ref.shape[1]
+    tok = gfull_ref.shape[0]
     ups = [chip(lax.rem(z + d, nz), p, c) for d in range(1, nz)]
-    meet(ups + [chip(z, hop(p, d), c) for d in HOPS])
+    flat = [chip(z, hop(p, d), c) for d in HOPS]
+    meet(ups + flat + [chip(z, p, 1 - c)])
     gain_out[p, z] = gains_ref[...]
-    copies = []
-    for d in range(1, nz):
-        copies.append(
-            send(gain_out.at[p, z], gain_out.at[p, z], z_sems.at[0, d - 1], z_sems.at[1, d - 1], ups[d - 1])
+    gz = [
+        send(gain_out.at[p, z], gain_out.at[p, z], gz_sems.at[0, d], gz_sems.at[1, d], ups[d])
+        for d in range(nz - 1)
+    ]
+    to_plane = []
+    for i, d in enumerate(HOPS):
+        to_plane.append(
+            send(a_ref.at[hop(p, d)], a_out.at[z, p], a_sems.at[0, i], a_sems.at[1, i], flat[i])
+        )
+    local = [pltpu.make_async_copy(a_ref.at[p], a_out.at[z, p], loc_sems.at[n])]
+    for j in range(n):
+        local.append(pltpu.make_async_copy(w_refs[j].at[p], w_outs[j].at[p], loc_sems.at[j]))
+    for copy in local:
+        copy.start()
+
+    @pl.loop(0, half // 16)
+    def _(r):
+        at = at_rows(r * 16, 16)
+        gfull_ref[at_rows((p * 2 + c) * half + r * 16, 16), :] = grad[at, :].astype(bf16)
+
+    for copy in gz:
+        copy.wait_recv()
+    gp = [
+        send(gain_out.at[p], gain_out.at[p], gp_sems.at[0, i], gp_sems.at[1, i], flat[i])
+        for i in range(3)
+    ]
+    for copy in gp:
+        copy.wait_recv()
+    for i in range(nz):
+        for j in range(gain_out.shape[0]):
+            first = (i * gain_out.shape[0] + j) * rows
+            g_vec[:, first : first + rows] = gain_out[j, i][:, :rows]
+    g = g_vec[0:1, :]
+
+    @pl.loop(0, half // 16)
+    def _(r):
+        rows_in = hid[at_rows(r * 16, 16), :]
+        full_ref[at_rows((p * 2 + c) * half + r * 16, 16), :] = (
+            rows_in * rms(rows_in) * g
+        ).astype(bf16)
+
+    other = chip(z, p, 1 - c)
+    mine = full_ref.at[at_rows((p * 2 + c) * half, half), :]
+    rows_out = [
+        send(mine, mine, far_sems.at[0, i], far_sems.at[1, i], flat[i]) for i in range(3)
+    ] + [send(mine, mine, own_sems.at[0], own_sems.at[1], other)]
+
+    def block_up(k):
+        at = a_out.at[z - k]
+        return pltpu.make_async_remote_copy(
+            src_ref=at, dst_ref=at, send_sem=up_sems.at[0, k], recv_sem=up_sems.at[1, k],
+            device_id=chip(z + 1, p, c), device_id_type=MESH,
+        )
+
+    def block_down(k):
+        at = a_out.at[z + k]
+        return pltpu.make_async_remote_copy(
+            src_ref=at, dst_ref=at, send_sem=down_sems.at[0, k], recv_sem=down_sems.at[1, k],
+            device_id=chip(z - 1, p, c), device_id_type=MESH,
+        )
+
+    def got_up(k):
+        at = a_out.at[z - k]
+        pltpu.make_async_remote_copy(
+            src_ref=at, dst_ref=at, send_sem=up_sems.at[0, k - 1], recv_sem=up_sems.at[1, k - 1],
+            device_id=chip(z - 1, p, c), device_id_type=MESH,
+        ).wait_recv()
+
+    def got_down(k):
+        at = a_out.at[z + k]
+        pltpu.make_async_remote_copy(
+            src_ref=at, dst_ref=at, send_sem=down_sems.at[0, k - 1],
+            recv_sem=down_sems.at[1, k - 1],
+            device_id=chip(z + 1, p, c), device_id_type=MESH,
+        ).wait_recv()
+
+    def stage(k):
+        if k:
+
+            @pl.when(z - k >= 0)
+            def _():
+                got_up(k)
+
+        @pl.when((z - k >= 0) & (z + 1 < nz))
+        def _():
+            block_up(k).start()
+
+        if k:
+
+            @pl.when(z + k < nz)
+            def _():
+                got_down(k)
+
+        @pl.when((z + k < nz) & (z > 0))
+        def _():
+            block_down(k).start()
+
+    for copy in to_plane:
+        copy.wait_recv()
+    for copy in local:
+        copy.wait()
+    stage(0)
+    if nz > 2:
+        stage(1)
+    onward = []
+    for i, d in ((1, 1), (2, 2), (0, 3)):
+        rows_out[i].wait_recv()
+        came = full_ref.at[at_rows((hop(p, d) * 2 + c) * half, half), :]
+        onward.append(send(came, came, near_sems.at[0, i], near_sems.at[1, i], other))
+    moved = []
+    for j in range(n):
+        for i, d in enumerate(HOPS):
+            moved.append(
+                send(
+                    w_refs[j].at[hop(p, d)], w_outs[j].at[p], w_sems.at[0, j, i],
+                    w_sems.at[1, j, i], flat[i],
+                )
+            )
+    finish_share(rows_out, onward)
+    halo_from = full_ref.at[at_rows(tok - HALO, HALO), :]
+    halo_to = full_ref.at[at_rows(tok, HALO), :]
+
+    def halo(to):
+        return pltpu.make_async_remote_copy(
+            src_ref=halo_from, dst_ref=halo_to, send_sem=halo_sems.at[0],
+            recv_sem=halo_sems.at[1], device_id=to, device_id_type=MESH,
+        )
+
+    @pl.when(z + 1 < nz)
+    def _():
+        halo(chip(z + 1, p, c)).start()
+
+    @pl.when(z == 0)
+    def _():
+        full_ref[at_rows(tok, HALO), :] = jnp.zeros((HALO, full_ref.shape[1]), bf16)
+
+    for k in range(2, nz):
+        stage(k)
+    copies_g, onward_g = share_rows(gfull_ref, half, own_g, far_g, near_g)
+
+    @pl.when(z > 0)
+    def _():
+        halo(chip(z - 1, p, c)).wait_recv()
+
+    @pl.when(z + 1 < nz)
+    def _():
+        halo(chip(z + 1, p, c)).wait_send()
+
+    for k in range(nz):
+
+        @pl.when((z - k >= 0) & (z + 1 < nz))
+        def _():
+            block_up(k).wait_send()
+
+        @pl.when((z + k < nz) & (z > 0))
+        def _():
+            block_down(k).wait_send()
+
+    finish_share(copies_g, onward_g)
+    for copy in moved:
+        copy.wait()
+    for copy in gz + gp + to_plane:
+        copy.wait_send()
+
+
+def open_step(hid, grad, gains, piece, rest, tok, nz):
+    width, n, n_p = hid.shape[1], len(rest), piece.shape[0]
+    anywhere = pl.BlockSpec(memory_space=pl.ANY)
+    dma = pltpu.SemaphoreType.DMA
+    return pl.pallas_call(
+        functools.partial(open_kernel, n),
+        in_specs=[VM, VM, VM] + [anywhere] * (n + 1),
+        out_specs=[VM, VM, VM] + [anywhere] * (n + 1),
+        out_shape=[
+            jax.ShapeDtypeStruct((n_p, nz) + gains.shape, f32),
+            jax.ShapeDtypeStruct((tok + HALO, width), bf16),
+            jax.ShapeDtypeStruct((tok, width), bf16),
+            jax.ShapeDtypeStruct((nz,) + piece.shape, bf16),
+        ]
+        + [jax.ShapeDtypeStruct(r.shape, bf16) for r in rest],
+        scratch_shapes=[
+            pltpu.VMEM((8, width), f32), dma((2, nz - 1)), dma((2, 3)), dma((2, 3)), dma((2, nz)),
+            dma((2, nz)),
+        ]
+        + SHARE_SEMS
+        + SHARE_SEMS
+        + [dma((2, n, 3)), dma((n + 1,)), dma((2,))],
+        compiler_params=pltpu.CompilerParams(
+            collective_id=4, has_side_effects=True, vmem_limit_bytes=VMEM_LIMIT
+        ),
+        cost_estimate=pl.CostEstimate(flops=0, bytes_accessed=250_000_000, transcendentals=0),
+        name="open_step",
+    )(hid, grad, gains, piece, *rest)
+
+
+def gather_bc_kernel(x_ref, full_ref, far_sems, near_sems):
+    greet()
+    z, p, c = place()
+    half = x_ref.shape[0] // 2
+    full_ref[p] = x_ref[...]
+    rows = at_rows(c * half, half)
+    mine = full_ref.at[p, rows, :]
+    copies = [
+        send(mine, mine, far_sems.at[0, i], far_sems.at[1, i], chip(z, hop(p, d), c))
+        for i, d in enumerate(HOPS)
+    ]
+    onward = []
+    for i, d in ((1, 1), (2, 2), (0, 3)):
+        copies[i].wait_recv()
+        came = full_ref.at[hop(p, d), rows, :]
+        onward.append(
+            send(came, came, near_sems.at[0, i], near_sems.at[1, i], chip(z, p, 1 - c))
+        )
+    for copy in copies:
+        copy.wait_send()
+    for copy in onward:
+        copy.wait()
+
+
+def gather_bc(x, at, n_p):
+    tok = x.shape[0]
+    return pl.pallas_call(
+        gather_bc_kernel,
+        grid=(1,),
+        in_specs=[pl.BlockSpec((tok, 128), lambda i: (0, at))],
+        out_specs=pl.BlockSpec((n_p, tok, 128), lambda i: (0, 0, 0)),
+        out_shape=jax.ShapeDtypeStruct((n_p, tok, 128), bf16),
+        scratch_shapes=[pltpu.SemaphoreType.DMA((2, 3)), pltpu.SemaphoreType.DMA((2, 3))],
+        compiler_params=pltpu.CompilerParams(
+            collective_id=5, has_side_effects=True, vmem_limit_bytes=VMEM_LIMIT
+        ),
+        cost_estimate=pl.CostEstimate(flops=0, bytes_accessed=30_000_000, transcendentals=0),
+        name="gather_bc",
+    )(x)
+
+
+def reduce_bc_kernel(x_ref, out_ref, sib_out, sib_in, out, came, n_sems, f_sems, own_sems):
+    greet()
+    z, p, c = place()
+    half = x_ref.shape[1] // 2
+    other = chip(z, p, 1 - c)
+    near, far = [], []
+    order = HOPS + (0,)
+    for i, d in enumerate(order):
+        q = hop(p, d)
+        sib_out[i] = x_ref[q, at_rows((1 - c) * half, half), :].astype(bf16)
+        near.append(
+            send(sib_out.at[i], sib_in.at[i], n_sems.at[0, i], n_sems.at[1, i], other)
         )
     for i, d in enumerate(HOPS):
         q = hop(p, d)
-        copies.append(
-            send(a_ref.at[q], a_out.at[p], a_sems.at[0, i], a_sems.at[1, i], chip(z, q, c))
+        near[i].wait_recv()
+        out[i] = (x_ref[q, at_rows(c * half, half), :] + sib_in[i].astype(f32)).astype(bf16)
+        far.append(
+            send(out.at[i], came.at[i], f_sems.at[0, i], f_sems.at[1, i], chip(z, q, c))
         )
-    local = pltpu.make_async_copy(a_ref.at[p], a_out.at[p], loc_sems.at[0])
-    local.start()
-    for copy in copies[: nz - 1]:
-        copy.wait_recv()
-    late = []
-    for i, d in enumerate(HOPS):
-        late.append(
-            send(gain_out.at[p], gain_out.at[p], p_sems.at[0, i], p_sems.at[1, i], chip(z, hop(p, d), c))
-        )
-    for copy in copies[: nz - 1]:
-        copy.wait_send()
-    for copy in copies[nz - 1 :] + late:
-        copy.wait()
-    local.wait()
-
-
-def open_step(gains, piece, nz):
-    n_p = piece.shape[0]
+    near[3].wait_recv()
+    total = x_ref[p, at_rows(c * half, half), :] + sib_in[3].astype(f32)
+    for i in (1, 2, 0):
+        far[i].wait_recv()
+        total = total + came[i].astype(f32)
+    mine = out_ref.at[at_rows(c * half, half), :]
+    out_ref[at_rows(c * half, half), :] = total
+    copy = send(mine, mine, own_sems.at[0], own_sems.at[1], other)
+    for done in near + far:
+        done.wait_send()
+    copy.wait()
+
+
+def reduce_bc(x):
+    n_p, tok, _ = x.shape
+    half = tok // 2
     return plane_call(
-        open_kernel, "open_step", 4, (gains, piece),
-        [((n_p, nz) + gains.shape, f32), (piece.shape, bf16)],
+        reduce_bc_kernel, "reduce_bc", 7, (x,), [((tok, 128), f32)],
         [
-            pltpu.SemaphoreType.DMA((2, nz - 1)),
+            pltpu.VMEM((4, half, 128), bf16),
+            pltpu.VMEM((4, half, 128), bf16),
+            pltpu.VMEM((3, half, 128), bf16),
+            pltpu.VMEM((3, half, 128), bf16),
+            pltpu.SemaphoreType.DMA((2, 4)),
             pltpu.SemaphoreType.DMA((2, 3)),
-            pltpu.SemaphoreType.DMA((2, 3)),
-            pltpu.SemaphoreType.DMA((1,)),
+            pltpu.SemaphoreType.DMA((2,)),
         ],
-    )
-
-
-def share_kernel(n, *refs):
-    hid, grad, gain = refs[:3]
-    w_refs, (full_ref, gfull_ref), w_outs = refs[3 : 3 + n], refs[3 + n : 5 + n], refs[5 + n : 5 + 2 * n]
-    own_sems, far_sems, near_sems, own_g, far_g, near_g, w_sems, loc_sems = refs[5 + 2 * n :]
-    greet()
-    z, p, c = place()
-    half = hid.shape[0]
-    g = gain[...]
-
-    @pl.loop(0, half // 16)
-    def _(r):
-        at = at_rows(r * 16, 16)
-        to = at_rows((p * 2 + c) * half + r * 16, 16)
-        rows = hid[at, :]
-        full_ref[to, :] = (rows * rms(rows) * g).astype(bf16)
-        gfull_ref[to, :] = grad[at, :].astype(bf16)
-
-    local = []
-    for j in range(n):
-        local.append(pltpu.make_async_copy(w_refs[j].at[p], w_outs[j].at[p], loc_sems.at[j]))
-        local[j].start()
-    copies, onward = share_rows(full_ref, half, own_sems, far_sems, near_sems)
-    moved = []
-    for j in range(n):
-        for i, d in enumerate(HOPS):
-            q = hop(p, d)
-            moved.append(
-                send(
-                    w_refs[j].at[q], w_outs[j].at[p], w_sems.at[0, j, i], w_sems.at[1, j, i],
-                    chip(z, q, c),
-                )
-            )
-    copies_g, onward_g = share_rows(gfull_ref, half, own_g, far_g, near_g)
-    finish_share(copies, onward)
-    finish_share(copies_g, onward_g)
-    for copy in moved:
-        copy.wait()
-    for copy in local:
-        copy.wait()
-
-
-def share_step(hid, grad, gain, rest, tok):
-    width, n = hid.shape[1], len(rest)
-    anywhere = pl.BlockSpec(memory_space=pl.ANY)
-    return pl.pallas_call(
-        functools.partial(share_kernel, n),
-        in_specs=[VM, VM, VM] + [anywhere] * n,
-        out_specs=[VM, VM] + [anywhere] * n,
-        out_shape=[jax.ShapeDtypeStruct((tok, width), bf16)] * 2
-        + [jax.ShapeDtypeStruct(r.shape, bf16) for r in rest],
-        scratch_shapes=SHARE_SEMS
-        + SHARE_SEMS
-        + [pltpu.SemaphoreType.DMA((2, n, 3)), pltpu.SemaphoreType.DMA((n,))],
-        compiler_params=pltpu.CompilerParams(
-            collective_id=5, has_side_effects=True, vmem_limit_bytes=VMEM_LIMIT
-        ),
-        cost_estimate=pl.CostEstimate(flops=0, bytes_accessed=200_000_000, transcendentals=0),
-        name="share_step",
-    )(hid, grad, gain, *rest)
+        nbytes=40_000_000,
+    )[0]
 
 
 def sums_kernel(v_ref, out_ref, came, z_sems, p_sems, c_sems):
@@ -1017,18 +1270,20 @@
     gains_own = jnp.pad(
         jnp.stack([norm_mixer, norm_ffn]).astype(bf16).astype(f32), ((0, 6), (0, 128 - rows))
     )
-    gains, piece_a = open_step(gains_own, piece_a, nz)
-    w_a = along_z(piece_a)
+    my_half = lambda v: lax.dynamic_slice_in_dim(v, ci * half, half, 0)
+    hidden_own, grad_own = my_half(hidden_in), my_half(grad_out)
+    gains, normed_one, g_ffn, w_a, *rest = open_step(
+        hidden_own, grad_own, gains_own, piece_a, rest, tok, nz
+    )
+    w_a = w_a.reshape(nz * n_p * rows, w_a.shape[3])
     gains = gains.transpose(2, 1, 0, 3)[:, :, :, :rows].reshape(8, 1, width)
     gain_mix, gain_ffn = gains[0], gains[1]
-    my_half = lambda v: lax.dynamic_slice_in_dim(v, ci * half, half, 0)
-    hidden_own, grad_own = my_half(hidden_in), my_half(grad_out)
-    normed_one, g_ffn, *rest = share_step(hidden_own, grad_own, gain_mix, rest, tok)
     w_b, w_c, w_d, w_e = [along_z(piece) for piece in rest]
 
-    in_a = product(normed_one, w_a)
-    in_b = product(normed_one, w_b)
-    pre = in_a[:, :cw].astype(bf16)
+    in_ext = product(normed_one, w_a)
+    in_b = product(normed_one, w_b)[:tok]
+    in_a = in_ext[:tok]
+    pre_ext = in_ext[:, :cw].astype(bf16)
     gate_z = in_b[:, HDIM:]
     slice_1 = lambda v, at, n: lax.dynamic_slice_in_dim(v, at, n, 1)
     taps = jnp.concatenate(
@@ -1039,8 +1294,7 @@
         ],
         axis=1,
     )
-    prev_rows = passed_along(pre[tok - edge :], "z", 1)
-    ext = jnp.concatenate([prev_rows, pre], axis=0)
+    ext = jnp.concatenate([pre_ext[tok + HALO - edge :], pre_ext[:tok]], axis=0)
     conv_in = convolve(ext, taps, ext_docs, tok)
     ssm = jax.nn.silu(conv_in).astype(bf16)
     head_slice = lambda v: lax.dynamic_slice_in_dim(v, pi * n_heads, n_heads, 0)
@@ -1050,24 +1304,20 @@
     dt_pre = jnp.pad(in_a[:, dt_at : dt_at + n_heads], ((0, 0), (0, 128 - n_heads))) + lanes(my_bias)
     neg_rate = lanes(-jnp.exp(my_a))
     skip_full = jnp.repeat(my_skip, MHDIM)[None, :]
-    x_low = ssm[:, :xw]
-    bc_all = plane_gather(ssm[:, xw:]).reshape(n_p, tok, 2, bw)
-    bc_all = bc_all.transpose(2, 1, 0, 3).reshape(2, tok, n_p * bw)
-    b_mat, c_mat = bc_all[0], bc_all[1]
+    bc_all = gather_bc(ssm, xw // 128, n_p)
     pair_ids = pi * hk + jnp.arange(hk)
     cos_k, sin_k = rope_tables(positions, pair_ids)
     k0, k1 = in_a[:, cw : cw + hk], in_a[:, cw + hk : cw + kw]
     key_own = jnp.concatenate([k0 * cos_k - k1 * sin_k, k1 * cos_k + k0 * sin_k], axis=1)
     val_own = in_a[:, cw + kw : cw + 2 * kw]
     kv_own = jnp.concatenate([key_own, val_own], axis=1).astype(bf16)
-    kv = jnp.zeros((nz, tok, 2 * kw), bf16)
+    kv_own = jnp.concatenate([kv_own[: tok // 2], kv_own[tok // 2 :]], axis=1)
+    kv = jnp.zeros((nz, tok // 2, 4 * kw), bf16)
     kv = lax.dynamic_update_slice_in_dim(kv, kv_own[None], zi, 0)
     for d in range(1, nz):
         came = passed_along(kv_own, "z", d)
         kv = lax.dynamic_update_slice_in_dim(kv, came[None], (zi - d) % nz, 0)
-    kv = plane_gather(kv).transpose(1, 2, 0, 3).reshape(nz * tok, n_p, 2 * kw)
-    keys = kv[:, :, :kw].reshape(nz * tok, HDIM)
-    values = kv[:, :, kw:].reshape(nz * tok, HDIM)
+    kv = plane_gather(kv)
     cos_q, sin_q = rope_tables(positions, jnp.arange(HDIM // 2))
     cos_q, sin_q = cos_q.reshape(tok, n_p, hk), sin_q.reshape(tok, n_p, hk)
 
@@ -1081,14 +1331,13 @@
     queries = rope_q(in_b[:, :HDIM], 1.0).astype(bf16)
 
     base_arr = jnp.reshape(base, (1,)).astype(jnp.int32)
-    y_local, span_starts, local_state, dev_decay = ssd_forward(
-        base_arr, doc_starts, x_low, b_mat, c_mat, dt_pre, neg_rate, skip_full
-    )
-    decay_full = jnp.repeat(dev_decay[:, :n_heads], MHDIM, axis=1)
+    y_local, span_starts, local_state, dev_decay, decay_full, c_mat = ssd_forward(
+        base_arr, doc_starts, ssm, bc_all, dt_pre, neg_rate, skip_full
+    )
     total_decay = decay_full[-1][:, None]
     in_state = carry_states(local_state, total_decay, 1)
 
-    attn_f32, lse = attend(base_arr, doc_starts, queries, keys, values)
+    attn_f32, lse, keys, values = attend(base_arr, doc_starts, queries, kv)
     attn_low = attn_f32.astype(bf16)
     y_flat = y_local + product_nt(c_mat, in_state.astype(bf16)) * decay_full
     silu_z = jax.nn.silu(gate_z)
@@ -1110,12 +1359,16 @@
     d_gu, grad_e, grad_d = lax.optimization_barrier((d_gu, grad_e, grad_d))
 
     def scattered(grad):
-        grad = lax.psum_scatter(grad, "z", scatter_dimension=0, tiled=True)
+        return lax.psum_scatter(grad, "z", scatter_dimension=0, tiled=True)
+
+    def swapped(grad):
         return plane_swap(grad.reshape(n_p, rows, grad.shape[1])).astype(f32)
 
     ge = scattered(grad_e)
     gd = scattered(grad_d)
     d_mid_own, grad_gain_ffn, g_mid = two_step(d_gu, w_d, mid_own, grad_own, gain_ffn)
+    g_mid, ge = lax.optimization_barrier((g_mid, ge))
+    ge = swapped(ge)
     out_part = product_nt(activated, w_e).reshape(n_p, 2, half, width)
     block_out = join_cores(mid_own + block_sum(out_part))
 
@@ -1128,33 +1381,35 @@
     d_z = (d_gated * y_flat * silu_slope(gate_z)).astype(bf16)
     d_in_local = product_t((d_y_flat * decay_full).astype(bf16), c_mat)
     state_grad = carry_states(d_in_local, total_decay, -1)
-    d_query, d_key, d_value = attend_back(
-        base_arr, doc_starts, queries, d_attn, attn_f32, lse, keys, values
+    d_query, d_kv = attend_back(
+        base_arr, doc_starts, queries, d_attn, attn_f32, lse, keys, values, kv.shape
     )
     d_q_pre = rope_q(d_query, -1.0).astype(bf16)
     d_b = jnp.concatenate([d_q_pre, d_z], axis=1)
-    grad_b = product_t(normed_one, d_b).astype(bf16)
+    more = lambda v: jnp.pad(v, ((0, HALO), (0, 0)))
+    grad_b = product_t(normed_one, more(d_b)).astype(bf16)
     gb = scattered(grad_b)
-    d_kv = jnp.concatenate(
-        [d_key.reshape(nz, tok, n_p, kw), d_value.reshape(nz, tok, n_p, kw)], axis=3
-    )
-    d_kv = plane_sum(d_kv.transpose(2, 0, 1, 3))
+    d_kv = plane_sum(d_kv)
     d_kv_own = lax.dynamic_index_in_dim(d_kv, zi, 0, keepdims=False)
     for d in range(1, nz):
         block = lax.dynamic_index_in_dim(d_kv, (zi - d) % nz, 0, keepdims=False)
         d_kv_own = d_kv_own + passed_along(block.astype(bf16), "z", -d).astype(f32)
+    d_kv_own = jnp.concatenate([d_kv_own[:, : 2 * kw], d_kv_own[:, 2 * kw :]], axis=0)
     dk0, dk1 = d_kv_own[:, :hk], d_kv_own[:, hk:kw]
     d_kv_low = jnp.concatenate(
         [dk0 * cos_k + dk1 * sin_k, dk1 * cos_k - dk0 * sin_k, d_kv_own[:, kw:]], axis=1
     ).astype(bf16)
 
     start_decay = jnp.concatenate([jnp.ones((1, 128), f32), dev_decay[SPAN - 1 :: SPAN][:-1]])
+    d_y_flat, gd = lax.optimization_barrier((d_y_flat, gd))
+    gd = swapped(gd)
     d_xs, d_bc, d_dt, sums, skip_sums = ssd_backward(
-        base_arr, doc_starts, x_low, b_mat, c_mat, dt_pre, d_y_flat, span_starts,
+        base_arr, doc_starts, ssm, bc_all, dt_pre, d_y_flat, span_starts,
         start_decay[:, None, :], neg_rate, skip_full, in_state, state_grad,
     )
-    d_bc = d_bc.reshape(2, tok // 2, 2, n_p, bw).transpose(3, 0, 1, 2, 4)
-    d_bc = join_cores(block_sum(d_bc.reshape(n_p, 2, tok // 2, 2 * bw)))
+    d_bc, gc = lax.optimization_barrier((d_bc, gc))
+    gc = swapped(gc)
+    d_bc = reduce_bc(d_bc)
     du = jnp.concatenate([d_xs, d_bc], axis=1) * silu_slope(conv_in)
     d_ext, grad_taps = convolve_back(du, ext, taps, ext_docs, tok)
     next_rows = passed_along(d_ext[:edge], "z", -1)
@@ -1163,11 +1418,12 @@
         [d_kv_low, d_dt[:, :n_heads].astype(bf16), jnp.zeros((tok, tail_w), bf16)], axis=1
     )
     d_a = jnp.concatenate([d_pre, d_last], axis=1)
-    grad_a = product_t(normed_one, d_a).astype(bf16)
-    ga = scattered(grad_a)
+    grad_a = product_t(normed_one, more(d_a)).astype(bf16)
+    ga = swapped(scattered(grad_a))
     once = jnp.where(ci == 0, d_pre[:, xw:], jnp.zeros((), bf16))
     d_a_once = jnp.concatenate([d_pre[:, :xw], once, d_last], axis=1)
-    d_a_once, grad_a = lax.optimization_barrier((d_a_once, grad_a))
+    d_a_once, grad_a, gb = lax.optimization_barrier((d_a_once, grad_a, gb))
+    gb = swapped(gb)
     grad_in, grad_gain_mix = one_step(
         d_a_once, w_a, d_b, w_b, hidden_own, d_mid_own, gain_mix
     )

time: 976 us -> 832 us (0.85)
  local copies, waits for them, and re-layouts: 171 us -> 86.4 us
  waiting for transfers between devices: 220 us -> 164 us
  starting transfers between devices: 85.1 us -> 57.1 us
  Pallas kernels: 347 us -> 373 us
    ppermute x8 -> x7, waiting for transfers between devices: 75.5 us -> 23.1 us  [passed_along(): return lax.ppermute(block, axis, route)]
    all_gather x5 -> x4, waiting for transfers between devices: 85 us -> 45.8 us  [along_z(): return lax.all_gather(piece, 'z', axis=0, tiled=True)]
    ppermute x6, waiting for transfers between devices: 7.89 us -> 45.4 us  [carry_states(): came = lax.ppermute(low, 'z', route).astype(f32)]
    pallas_call x1 -> x2, Pallas kernels: 86 us -> 120 us  [the longest x1 107 us: open_step(): pl.pallas_call(functools.partial(open_kernel, n), in_specs=[VM, VM, VM] +...]
    reshape x9 -> x2, local copies, waits for them, and re-layouts: 23.4 us -> 2.72 us  [swapped(): return plane_swap(grad.reshape(n_p, rows, grad.shape[1])).astype(f32)]
    ppermute x4, starting transfers between devices: 24.3 us -> 5.15 us  [carry_states(): rate = lax.ppermute(decays, 'z', route)]
    ppermute x4, waiting for transfers between devices: 16.8 us -> 2.96 us  [carry_states(): rate = lax.ppermute(decays, 'z', route)]
    ppermute x15, waiting for transfers between devices: 17.9 us -> 31.7 us  [plane_swap(): came = lax.ppermute(block, 'p', [(i, i ^ d) for i in range(n_p)])]
  transfers between devices with their start and end apart: 62 -> 52, of which waited for: 21 -> 20; matrix products, arithmetic and copies ran while one was open for 23% -> 18% of each run, Pallas kernels for 19% -> 32%
where the time goes in v3:
time: 832 us; the launch traced here: 821 us
  Pallas kernels  373 us (45%)
  waiting for transfers between devices  164 us (20%)
  local copies, waits for them, and re-layouts  86.4 us (10%)
  matrix products  75.3 us (9%)
  starting transfers between devices  57.1 us (7%)
  other arithmetic  49.1 us (6%)
  between operations  15.9 us (2%)
    pallas_call x5, Pallas kernels, plane_call(): pl.pallas_call(kernel, in_specs=[VM] * len(args), out_specs=[VM] * len(sh...  196 us
    pallas_call x1, Pallas kernels, open_step(): pl.pallas_call(functools.partial(open_kernel, n), in_specs=[VM, VM, VM] +...  107 us
    all_gather x4, waiting for transfers between devices, along_z(): return lax.all_gather(piece, 'z', axis=0, tiled=True)  45.8 us
    ppermute x6, waiting for transfers between devices, carry_states(): came = lax.ppermute(low, 'z', route).astype(f32)  45.4 us
    dot_general x5, matrix products, product(): return jnp.dot(left, right, preferred_element_type=f32)  34.6 us
    dot_general x6, matrix products, product_t(): lax.dot_general(left, right, (((0,), (0,)), ((), ())), preferred_element_...  33.8 us
    ppermute x15, waiting for transfers between devices, plane_swap(): came = lax.ppermute(block, 'p', [(i, i ^ d) for i in range(n_p)])  31.7 us
    unnamed x122, local copies, waits for them, and re-layouts  24.9 us
  transfers between devices with their start and end apart: 52, of which 20 were waited for; matrix products, arithmetic and copies ran while one was open for 18% of the time, Pallas kernels for 32%

profile of v3, /device:TPU:0, one launch (start us, length us, event | category | flops | bytes accessed | tf_op | source)
XLA Modules:
  0.0 821.1 jit_solution(12821324965914876042)
XLA Ops:
  22.4 2.9 constant_dynamic-slice_fusion.19
  27.5 107.4 %open_step.1 = (f32[4,4,8,128]{3,2,1,0:T(8,128)}, bf16[1040,2048]{1,0:T(8,128)(2,1)}, bf16[1024,2048]{1,0:T(8,128)(2,1)}, bf16[4,4,128,640]{3,2,1,0:T(8,128)(2,1...) custom-call(f32[128,2048]{1,0:T(8,128)} %get-tuple-element.255.refs_, ...), custom_call_target="tpu_custom_call" | custom-call | bytes 250000000 | tf_op jit(solution)/shard_map/open_step/pallas_call | solution.py:968
  136.5 8.0 fusion.81
  144.7 4.1 fusion.34
  150.7 3.8 collective-permute-start.6
  154.6 4.3 collective-permute-start.5
  162.8 3.8 multiply_convert_fusion.3
  166.6 12.5 %gather_bc.1.bc_ref = bf16[4,1024,128]{2,1,0:T(8,128)(2,1)} custom-call(bf16[1024,512]{1,0:T(8,128)(2,1)} %get-tuple-element.182.x_ref), custom_call_target="tpu_custom_call" | custom-call | bytes 30000000 | tf_op jit(solution)/shard_map/gather_bc/pallas_call | solution.py:1020
  180.5 13.7 %ssd_forward.1 = (f32[1024,384]{1,0:T(8,128)}, f32[8,384,256]{2,1,0:T(8,128)}, f32[384,256]{1,0:T(8,128)}, f32[1024,128]{1,0:T(8,128)}, f32[1024,384]{1,0:T(8,128)}, /*index=5*/bf16[1024,256]{1,0:T(8,128)(2,1)}) custom-call(s32[1]{0:T(128)} %bitcast.base_ref, s32[8]{0:T(128)} %starts_ref.7, bf16[1024,512]{1,0:T(8,128)(2,1)} %get-tuple-element.182.x_ref, ...), custom_call_target="tpu_custom_call" | custom-call | flops 603979776 | bytes 40000000 | tf_op jit(solution)/shard_map/ssd_forward/pallas_call | solution.py:205
  213.7 5.8 collective-permute-done.2
  219.5 8.3 %collective-permute-done = bf16[384,256]{1,0:T(8,128)(2,1)S(1)} collective-permute-done((bf16[384,256]{1,0:T(8,128)(2,1)S(1)}, bf16[384,256]{1,0:T(8,128)(2,1)S(1)}, u32[]{:S(2)}, u32[]{:S(2)}) %collective-permute-start) | collective-permute-done | bytes 196640 | tf_op jit(solution)/shard_map/ppermute | solution.py:1192
  228.8 5.7 collective-permute-done.9
  234.7 6.0 fusion.82
  246.2 9.5 %attend.1 = (f32[1024,128]{1,0:T(8,128)}, f32[1024,128]{1,0:T(8,128)}, bf16[4096,128]{1,0:T(8,128)(2,1)}, bf16[4096,128]{1,0:T(8,128)(2,1)}) custom-call(s32[1]{0:T(128)} %bitcast.base_ref, s32[8]{0:T(128)} %starts_ref.7, bf16[1024,128]{1,0:T(8,128)(2,1)} %copy.218.q_ref, bf16[4,4,512,128]{3,2,1,0:T(8,128)(2,1)} %copy-done.19), custom_call_target="tpu_custom_call" | custom-call | flops 2147483648 | bytes 30000000 | tf_op jit(solution)/shard_map/attend/pallas_call | solution.py:419
  256.8 3.3 multiply_convert_fusion.6
  261.2 64.3 %mid_step.1 = (f32[128,2048]{1,0:T(8,128)}, bf16[1024,2048]{1,0:T(8,128)(2,1)}) custom-call(bf16[1024,512]{1,0:T(8,128)(2,1)} %pad_maximum_fusion.4.left, bf16[2048,512]{1,0:T(8,128)(2,1)} %all-gather.7.cloned.1.call-done.right, f32[128,2048]{1,0:T(8,128)} %get-tuple-element.255.refs_0_.resid.hidden_own, f32[1,2048]{1,0:T(1,128)} %bitcast.276), custom_call_target="tpu_custom_call" | custom-call | bytes 150000000 | tf_op jit(solution)/shard_map/mid_step/pallas_call | solution.py:736
  325.5 9.8 %all-gather.9.cloned.1.call-done.right = bf16[2048,1024]{1,0:T(8,128)(2,1)} async-done(((bf16[512,1024]{1,0:T(8,128)(2,1)}), bf16[2048,1024]{1,0:T(8,128)(2,1)}) %all-gather.9.cloned.1.call-update) | async-done | bytes 4194320 | tf_op jit(solution)/shard_map/all_gather | solution.py:1268
  335.3 10.0 %fusion.83 = f32[1024,1024]{1,0:T(8,128)} fusion(bf16[1024,2048]{1,0:T(8,128)(2,1)} %get-tuple-element.75, bf16[2048,1024]{1,0:T(8,128)(2,1)} %all-gather.9.cloned.1.call-done.right), kind=kOutput, calls=%fused_computation.240 | convolution fusion | flops 4294967296 | bytes 12582912 | tf_op jit(solution)/shard_map/dot_general | solution.py:32
  345.3 36.0 %all-gather.11.cloned.1.call-done = bf16[2048,512]{1,0:T(8,128)(2,1)} async-done(((bf16[512,512]{1,0:T(8,128)(2,1)}), bf16[2048,512]{1,0:T(8,128)(2,1)}) %all-gather.11.cloned.1.call-update) | async-done | bytes 2097168 | tf_op jit(solution)/shard_map/all_gather | solution.py:1268
  381.2 8.3 %multiply_convert_fusion.1 = (bf16[1024,512]{1,0:T(8,128)(2,1)S(1)}, bf16[1024,512]{1,0:T(8,128)(2,1)S(1)}, bf16[1024,512]{1,0:T(8,128)(2,1)}) fusion(f32[1024,1024]{1,0:T(8,128)} %fusion.83, bf16[1024,2048]{1,0:T(8,128)(2,1)} %get-tuple-element.78, bf16[2048,512]{1,0:T(8,128)(2,1)} %all-gather.11.cloned.1.call-done), kind=kOutput, calls=%fused_computation.33 | convolution fusion | flops 2155347968 | bytes 13631488 | tf_op jit(solution)/shard_map/dot_general | solution.py:32
  389.5 6.4 convolution_convert_fusion
  398.8 5.0 convolution_convert_fusion.4
  405.5 3.6 fusion.84
  409.1 3.3 copy-done.5
  412.8 66.1 %two_step.1 = (f32[128,2048]{1,0:T(8,128)}, f32[1,2048]{1,0:T(1,128)}, bf16[1024,2048]{1,0:T(8,128)(2,1)}) custom-call(bf16[1024,1024]{1,0:T(8,128)(2,1)} %pad_maximum_fusion.1.left, bf16[2048,1024]{1,0:T(8,128)(2,1)} %all-gather.9.cloned.1.call-done.right, f32[128,2048]{1,0:T(8,128)} %get-tuple-element.74.mid_own, ...), custom_call_target="tpu_custom_call" | custom-call | bytes 150000000 | tf_op jit(solution)/shard_map/two_step/pallas_call | solution.py:736
  479.0 6.1 convolution_convert_fusion.3
  492.4 3.7 bitcast_add_fusion
  503.9 11.2 %attend_back.1 = (f32[1024,128]{1,0:T(8,128)}, bf16[4,4,512,128]{3,2,1,0:T(8,128)(2,1)}) custom-call(s32[1]{0:T(128)} %bitcast.base_ref, s32[8]{0:T(128)} %starts_ref.7, bf16[1024,128]{1,0:T(8,128)(2,1)} %copy.218.q_ref, bf16[1024,128]{1,0:T(8,128)(2,1)} %slice.481.do_ref, f32[1024,128]{1,0:T(8,128)} %get-tuple-element.71.o_ref, ...), custom_call_target="tpu_custom_call" | custom-call | flops 5368709120 | bytes 40000000 | tf_op jit(solution)/shard_map/attend_back/pallas_call | solution.py:484
  525.0 2.8 multiply_convert_fusion.4
  528.9 6.3 convolution_convert_fusion.2
  538.7 7.6 collective-permute-done.24
  550.7 20.2 %collective-permute-done.20 = bf16[384,256]{1,0:T(8,128)(2,1)S(1)} collective-permute-done((bf16[384,256]{1,0:T(8,128)(2,1)S(1)}, bf16[384,256]{1,0:T(8,128)(2,1)S(1)}, u32[]{:S(2)}, u32[]{:S(2)}) %collective-permute-start.20) | collective-permute-done | bytes 196640 | tf_op jit(solution)/shard_map/ppermute | solution.py:1192
  572.2 11.1 %collective-permute-done.18 = bf16[384,256]{1,0:T(8,128)(2,1)S(1)} collective-permute-done((bf16[384,256]{1,0:T(8,128)(2,1)S(1)}, bf16[384,256]{1,0:T(8,128)(2,1)S(1)}, u32[]{:S(2)}, u32[]{:S(2)}) %collective-permute-start.18) | collective-permute-done | bytes 196640 | tf_op jit(solution)/shard_map/ppermute | solution.py:1192
  588.5 3.7 collective-permute-done.27
  592.2 16.6 %collective-permute-done.26 = bf16[512,128]{1,0:T(8,128)(2,1)S(1)} collective-permute-done((bf16[512,128]{1,0:T(8,128)(2,1)S(1)}, bf16[512,128]{1,0:T(8,128)(2,1)S(1)}, u32[]{:S(2)}, u32[]{:S(2)}) %collective-permute-start.26) | collective-permute-done | bytes 131104 | tf_op jit(solution)/shard_map/ppermute | solution.py:51
  609.1 2.8 fusion.40
  612.0 22.6 %ssd_backward.1 = (f32[1024,384]{1,0:T(8,128)}, f32[4,1024,128]{2,1,0:T(8,128)}, f32[1024,128]{1,0:T(8,128)}, f32[8,128]{1,0:T(8,128)}, f32[1,384]{1,0:T(1,128)}) custom-call(s32[1]{0:T(128)} %bitcast.base_ref, s32[8]{0:T(128)} %starts_ref.7, bf16[1024,512]{1,0:T(8,128)(2,1)} %get-tuple-element.182.x_ref, bf16[4,1024,128]{2,1,0:T(8,128)(2,1)} %gather_bc.1.bc_ref, ...), custom_call_target="tpu_custom_call" | custom-call | flops 1610612736 | bytes 80000000 | tf_op jit(solution)/shard_map/ssd_backward/pallas_call | solution.py:335
  634.7 14.2 %reduce_bc.1 = f32[1024,128]{1,0:T(8,128)} custom-call(f32[4,1024,128]{2,1,0:T(8,128)} %get-tuple-element.89.x_ref), custom_call_target="tpu_custom_call" | custom-call | bytes 40000000 | tf_op jit(solution)/shard_map/reduce_bc/pallas_call | solution.py:736
  648.9 4.2 fusion.5
  662.2 8.0 convolution_convert_fusion.1
  675.8 5.2 collective-permute-done.40
  684.4 5.7 collective-permute-done.41
  701.4 39.5 %one_step.1 = (f32[256,2048]{1,0:T(8,128)}, f32[1,2048]{1,0:T(1,128)}) custom-call(bf16[1024,640]{1,0:T(8,128)(2,1)} %concatenate.77.left_a, bf16[2048,640]{1,0:T(8,128)(2,1)} %bitcast.225, bf16[1024,512]{1,0:T(8,128)(2,1)} %copy-done.9, bf16[2048,512]{1,0:T(8,128)(2,1)} %all-gather.5.cloned.1.call-done.right_b, ...), custom_call_target="tpu_custom_call" | custom-call | bytes 150000000 | tf_op jit(solution)/shard_map/one_step/pallas_call | solution.py:736
  742.3 11.8 %sums_step.1 = f32[2,4,56,128]{3,2,1,0:T(8,128)} custom-call(f32[56,128]{1,0:T(8,128)} %pad.66.v_ref), custom_call_target="tpu_custom_call" | custom-call | bytes 150000000 | tf_op jit(solution)/shard_map/sums_step/pallas_call | solution.py:736
  766.9 6.1 collective-permute-done.29
  781.9 9.7 %collective-permute-done.38 = bf16[1,128,1024]{2,1,0:T(8,128)(2,1)S(1)} collective-permute-done((bf16[1,128,1024]{2,1,0:T(8,128)(2,1)S(1)}, bf16[1,128,1024]{2,1,0:T(8,128)(2,1)S(1)}, u32[]{:S(2)}, u32[]{:S(2)}) %collective-permute-start.38) | collective-permute-done | bytes 262176 | tf_op jit(solution)/shard_map/ppermute | solution.py:1141
  803.2 3.8 collective-permute-done.33
  811.3 3.1 copy.289
  (396 shorter events, 167.3 us)
Async XLA Ops:
  7.2 227.5 %all-gather.5.cloned.1.call-start = ((), (), s32[]{:S(2)}) async-start(), calls=%async_computation.5 | async-start | bytes 2621440 | tf_op jit(solution)/shard_map/all_gather | solution.py:1268
  134.9 126.3 %all-gather.7.cloned.1.call-start = ((), (), s32[]{:S(2)}) async-start(), calls=%async_computation.6 | async-start | bytes 2621440 | tf_op jit(solution)/shard_map/all_gather | solution.py:1268
  135.7 199.6 %all-gather.9.cloned.1.call-start = ((), (), s32[]{:S(2)}) async-start(), calls=%async_computation.7 | async-start | bytes 5242880 | tf_op jit(solution)/shard_map/all_gather | solution.py:1268
  136.4 244.8 %all-gather.11.cloned.1.call-start = ((), (), s32[]{:S(2)}) async-start(), calls=%async_computation.8 | async-start | bytes 2621440 | tf_op jit(solution)/shard_map/all_gather | solution.py:1268
  150.7 52.4 %collective-permute-start.6 = (bf16[512,128]{1,0:T(8,128)(2,1)S(1)}, bf16[512,128]{1,0:T(8,128)(2,1)}, u32[]{:S(2)}, u32[]{:S(2)}) collective-permute-start(bf16[512,128]{1,0:T(8,128)(2,1)S(1)} %get-tuple-element.185), channel_id=1, source_target_pairs={{0,16},{8,24},{1,17},{9,25},{2,18},{10,26},{3,19},{11,27},{4,20},{... | collective-permute-start | bytes 393224 | tf_op jit(solution)/shard_map/ppermute | solution.py:51
  154.6 45.7 %collective-permute-start.5 = (bf16[512,128]{1,0:T(8,128)(2,1)S(1)}, bf16[512,128]{1,0:T(8,128)(2,1)}, u32[]{:S(2)}, u32[]{:S(2)}) collective-permute-start(bf16[512,128]{1,0:T(8,128)(2,1)S(1)} %get-tuple-element.185), channel_id=1, source_target_pairs={{0,8},{8,16},{16,24},{1,9},{9,17},{17,25},{2,10},{10,18},{18,26},{... | collective-permute-start | bytes 393224 | tf_op jit(solution)/shard_map/ppermute | solution.py:51
  158.9 47.1 %collective-permute-start.7 = (bf16[512,128]{1,0:T(8,128)(2,1)S(1)}, bf16[512,128]{1,0:T(8,128)(2,1)S(1)}, u32[]{:S(2)}, u32[]{:S(2)}) collective-permute-start(bf16[512,128]{1,0:T(8,128)(2,1)S(1)} %get-tuple-element.185), channel_id=1, source_target_pairs={{0,24},{1,25},{2,26},{3,27},{4,28},{5,29},{6,30},{7,31}} | collective-permute-start | bytes 393224 | tf_op jit(solution)/shard_map/ppermute | solution.py:51
  195.0 13.6 %collective-permute-start.3 = (f32[384,1]{0,1:T(1,128)S(1)}, f32[384,1]{0,1:T(1,128)S(1)}, u32[]{:S(2)}, u32[]{:S(2)}) collective-permute-start(f32[384,1]{0,1:T(1,128)S(1)} %slice_bitcast_fusion.7), channel_id=1, source_target_pairs={{0,16},{8,24},{1,17},{9,25},{2,18},{10,26},{3,19},{11,27},{4,20},{... | collective-permute-start | bytes 4616 | tf_op jit(solution)/shard_map/ppermute | solution.py:1193
  196.2 12.9 %collective-permute-start.1 = (f32[384,1]{0,1:T(1,128)S(1)}, f32[384,1]{0,1:T(1,128)S(1)}, u32[]{:S(2)}, u32[]{:S(2)}) collective-permute-start(f32[384,1]{0,1:T(1,128)S(1)} %slice_bitcast_fusion.7), channel_id=1, source_target_pairs={{0,8},{8,16},{16,24},{1,9},{9,17},{17,25},{2,10},{10,18},{18,26},{... | collective-permute-start | bytes 4616 | tf_op jit(solution)/shard_map/ppermute | solution.py:1193
  197.6 281.4 %reduce-scatter.6.cloned.1.call-start = ((), (), s32[]{:S(2)}) async-start(), calls=%async_computation.9 | async-start | bytes 2621440 | tf_op jit(solution)/shard_map/reduce_scatter | solution.py:1362
  200.3 11.7 %collective-permute-start.4 = (bf16[384,256]{1,0:T(8,128)(2,1)S(1)}, bf16[384,256]{1,0:T(8,128)(2,1)S(1)}, u32[]{:S(2)}, u32[]{:S(2)}) collective-permute-start(bf16[384,256]{1,0:T(8,128)(2,1)S(1)} %convert_element_type.300), channel_id=1, source_target_pairs={{0,24},{1,25},{2,26},{3,27},{4,28},{5,29},{6,30},{7,31}} | collective-permute-start | bytes 589832 | tf_op jit(solution)/shard_map/ppermute | solution.py:1192
  203.2 16.3 %collective-permute-start.2 = (bf16[384,256]{1,0:T(8,128)(2,1)S(1)}, bf16[384,256]{1,0:T(8,128)(2,1)S(1)}, u32[]{:S(2)}, u32[]{:S(2)}) collective-permute-start(bf16[384,256]{1,0:T(8,128)(2,1)S(1)} %convert_element_type.300), channel_id=1, source_target_pairs={{0,16},{8,24},{1,17},{9,25},{2,18},{10,26},{3,19},{11,27},{4,20},{... | collective-permute-start | bytes 589832 | tf_op jit(solution)/shard_map/ppermute | solution.py:1192
  206.1 21.7 %collective-permute-start = (bf16[384,256]{1,0:T(8,128)(2,1)S(1)}, bf16[384,256]{1,0:T(8,128)(2,1)S(1)}, u32[]{:S(2)}, u32[]{:S(2)}) collective-permute-start(bf16[384,256]{1,0:T(8,128)(2,1)S(1)} %convert_element_type.300), channel_id=1, source_target_pairs={{0,8},{8,16},{16,24},{1,9},{9,17},{17,25},{2,10},{10,18},{18,26},{... | collective-permute-start | bytes 589832 | tf_op jit(solution)/shard_map/ppermute | solution.py:1192
  208.5 20.3 %collective-permute-start.8 = (bf16[4,512,128]{2,1,0:T(8,128)(2,1)}, bf16[4,512,128]{2,1,0:T(8,128)(2,1)S(1)}, u32[]{:S(2)}, u32[]{:S(2)}) collective-permute-start(bf16[4,512,128]{2,1,0:T(8,128)(2,1)} %bitcast_dynamic-update-slice_fusion.4), channel_id=1, source_target_pairs={{0,2},{2,0},{4,6},{6,4},{1,3},{3,1},{5,7},{7,5},{8,10},{10,8},{12,... | collective-permute-start | bytes 1572872 | tf_op jit(solution)/shard_map/ppermute | solution.py:1152
  209.1 25.4 %collective-permute-start.9 = (bf16[4,512,128]{2,1,0:T(8,128)(2,1)}, bf16[4,512,128]{2,1,0:T(8,128)(2,1)S(1)}, u32[]{:S(2)}, u32[]{:S(2)}) collective-permute-start(bf16[4,512,128]{2,1,0:T(8,128)(2,1)} %bitcast_dynamic-update-slice_fusion.4), channel_id=1, source_target_pairs={{0,4},{2,6},{4,0},{6,2},{1,5},{3,7},{5,1},{7,3},{8,12},{10,14},{12... | collective-permute-start | bytes 1572872 | tf_op jit(solution)/shard_map/ppermute | solution.py:1152
  212.0 22.6 %collective-permute-start.10 = (bf16[4,512,128]{2,1,0:T(8,128)(2,1)}, bf16[4,512,128]{2,1,0:T(8,128)(2,1)S(1)}, u32[]{:S(2)}, u32[]{:S(2)}) collective-permute-start(bf16[4,512,128]{2,1,0:T(8,128)(2,1)} %bitcast_dynamic-update-slice_fusion.4), channel_id=1, source_target_pairs={{0,6},{2,4},{4,2},{6,0},{1,7},{3,5},{5,3},{7,1},{8,14},{10,12},{12... | collective-permute-start | bytes 1572872 | tf_op jit(solution)/shard_map/ppermute | solution.py:1152
  403.9 208.1 %reduce-scatter.8.cloned.1.call-start = ((), (), s32[]{:S(2)}) async-start(), calls=%async_computation.10 | async-start | bytes 5242880 | tf_op jit(solution)/shard_map/reduce_scatter | solution.py:1362
  404.5 230.2 %reduce-scatter.10.cloned.1.call-start = ((), (), s32[]{:S(2)}) async-start(), calls=%async_computation.11 | async-start | bytes 2621440 | tf_op jit(solution)/shard_map/reduce_scatter | solution.py:1362
  412.7 79.6 %collective-permute-start.11 = (bf16[4,128,2048]{2,1,0:T(8,128)(2,1)S(1)}, bf16[4,128,2048]{2,1,0:T(8,128)(2,1)}, u32[]{:S(2)}, u32[]{:S(2)}) collective-permute-start(bf16[4,128,2048]{2,1,0:T(8,128)(2,1)S(1)} %fusion.10), channel_id=1, source_target_pairs={{0,1},{1,0},{2,3},{3,2},{4,5},{5,4},{6,7},{7,6},{8,9},{9,8},{10,11... | collective-permute-start | bytes 6291464 | tf_op jit(solution)/shard_map/ppermute | solution.py:1169
  485.1 215.0 %reduce-scatter.12.cloned.1.call-start = ((), (), s32[]{:S(2)}) async-start(), calls=%async_computation.12 | async-start | bytes 2621440 | tf_op jit(solution)/shard_map/reduce_scatter | solution.py:1362
  485.1 6.6 collective-permute-start.19
  497.2 173.0 %collective-permute-start.12 = (bf16[128,2048]{1,0:T(8,128)(2,1)}, bf16[128,2048]{1,0:T(8,128)(2,1)}, u32[]{:S(2)}, u32[]{:S(2)}) collective-permute-start(bf16[128,2048]{1,0:T(8,128)(2,1)} %get-tuple-element.191), channel_id=1, source_target_pairs={{0,2},{2,0},{4,6},{6,4},{1,3},{3,1},{5,7},{7,5},{8,10},{10,8},{12,... | collective-permute-start | bytes 1572872 | tf_op jit(solution)/shard_map/ppermute | solution.py:1163
  497.6 172.6 %collective-permute-start.14 = (bf16[128,2048]{1,0:T(8,128)(2,1)}, bf16[128,2048]{1,0:T(8,128)(2,1)}, u32[]{:S(2)}, u32[]{:S(2)}) collective-permute-start(bf16[128,2048]{1,0:T(8,128)(2,1)} %get-tuple-element.192), channel_id=1, source_target_pairs={{0,6},{2,4},{4,2},{6,0},{1,7},{3,5},{5,3},{7,1},{8,14},{10,12},{12... | collective-permute-start | bytes 1572872 | tf_op jit(solution)/shard_map/ppermute | solution.py:1163
  521.5 15.9 %collective-permute-start.22 = (bf16[4,512,128]{2,1,0:T(8,128)(2,1)}, bf16[4,512,128]{2,1,0:T(8,128)(2,1)S(1)}, u32[]{:S(2)}, u32[]{:S(2)}) collective-permute-start(bf16[4,512,128]{2,1,0:T(8,128)(2,1)} %get-tuple-element.198), channel_id=1, source_target_pairs={{0,2},{2,0},{4,6},{6,4},{1,3},{3,1},{5,7},{7,5},{8,10},{10,8},{12,... | collective-permute-start | bytes 1572872 | tf_op jit(solution)/shard_map/ppermute | solution.py:1163
  521.8 24.5 %collective-permute-start.24 = (bf16[4,512,128]{2,1,0:T(8,128)(2,1)}, bf16[4,512,128]{2,1,0:T(8,128)(2,1)}, u32[]{:S(2)}, u32[]{:S(2)}) collective-permute-start(bf16[4,512,128]{2,1,0:T(8,128)(2,1)} %get-tuple-element.199), channel_id=1, source_target_pairs={{0,6},{2,4},{4,2},{6,0},{1,7},{3,5},{5,3},{7,1},{8,14},{10,12},{12... | collective-permute-start | bytes 1572872 | tf_op jit(solution)/shard_map/ppermute | solution.py:1163
  523.6 24.1 %collective-permute-start.23 = (bf16[4,512,128]{2,1,0:T(8,128)(2,1)}, bf16[4,512,128]{2,1,0:T(8,128)(2,1)}, u32[]{:S(2)}, u32[]{:S(2)}) collective-permute-start(bf16[4,512,128]{2,1,0:T(8,128)(2,1)} %get-tuple-element.200), channel_id=1, source_target_pairs={{0,4},{2,6},{4,0},{6,2},{1,5},{3,7},{5,1},{7,3},{8,12},{10,14},{12... | collective-permute-start | bytes 1572872 | tf_op jit(solution)/shard_map/ppermute | solution.py:1163
  535.3 259.3 %reduce-scatter.14.cloned.1.call-start = ((), (), s32[]{:S(2)}) async-start(), calls=%async_computation.13 | async-start | bytes 3276800 | tf_op jit(solution)/shard_map/reduce_scatter | solution.py:1362
  537.4 33.5 %collective-permute-start.20 = (bf16[384,256]{1,0:T(8,128)(2,1)S(1)}, bf16[384,256]{1,0:T(8,128)(2,1)S(1)}, u32[]{:S(2)}, u32[]{:S(2)}) collective-permute-start(bf16[384,256]{1,0:T(8,128)(2,1)S(1)} %convolution_convert_fusion.5), channel_id=1, source_target_pairs={{24,0},{25,1},{26,2},{27,3},{28,4},{29,5},{30,6},{31,7}} | collective-permute-start | bytes 589832 | tf_op jit(solution)/shard_map/ppermute | solution.py:1192
  546.3 37.0 %collective-permute-start.18 = (bf16[384,256]{1,0:T(8,128)(2,1)S(1)}, bf16[384,256]{1,0:T(8,128)(2,1)S(1)}, u32[]{:S(2)}, u32[]{:S(2)}) collective-permute-start(bf16[384,256]{1,0:T(8,128)(2,1)S(1)} %convolution_convert_fusion.5), channel_id=1, source_target_pairs={{16,0},{24,8},{17,1},{25,9},{18,2},{26,10},{19,3},{27,11},{20,4},{... | collective-permute-start | bytes 589832 | tf_op jit(solution)/shard_map/ppermute | solution.py:1192
  547.7 36.9 %collective-permute-start.16 = (bf16[384,256]{1,0:T(8,128)(2,1)S(1)}, bf16[384,256]{1,0:T(8,128)(2,1)S(1)}, u32[]{:S(2)}, u32[]{:S(2)}) collective-permute-start(bf16[384,256]{1,0:T(8,128)(2,1)S(1)} %convolution_convert_fusion.5), channel_id=1, source_target_pairs={{8,0},{16,8},{24,16},{9,1},{17,9},{25,17},{10,2},{18,10},{26,18},{... | collective-permute-start | bytes 589832 | tf_op jit(solution)/shard_map/ppermute | solution.py:1192
  570.9 15.9 %collective-permute-start.25 = (bf16[512,128]{1,0:T(8,128)(2,1)S(1)}, bf16[512,128]{1,0:T(8,128)(2,1)S(1)}, u32[]{:S(2)}, u32[]{:S(2)}) collective-permute-start(bf16[512,128]{1,0:T(8,128)(2,1)S(1)} %get-tuple-element.208), channel_id=1, source_target_pairs={{8,0},{16,8},{24,16},{9,1},{17,9},{25,17},{10,2},{18,10},{26,18},{... | collective-permute-start | bytes 393224 | tf_op jit(solution)/shard_map/ppermute | solution.py:51
  583.3 8.9 %collective-permute-start.27 = (bf16[512,128]{1,0:T(8,128)(2,1)S(1)}, bf16[512,128]{1,0:T(8,128)(2,1)S(1)}, u32[]{:S(2)}, u32[]{:S(2)}) collective-permute-start(bf16[512,128]{1,0:T(8,128)(2,1)S(1)} %get-tuple-element.209), channel_id=1, source_target_pairs={{24,0},{25,1},{26,2},{27,3},{28,4},{29,5},{30,6},{31,7}} | collective-permute-start | bytes 393224 | tf_op jit(solution)/shard_map/ppermute | solution.py:51
  584.6 24.1 %collective-permute-start.26 = (bf16[512,128]{1,0:T(8,128)(2,1)S(1)}, bf16[512,128]{1,0:T(8,128)(2,1)S(1)}, u32[]{:S(2)}, u32[]{:S(2)}) collective-permute-start(bf16[512,128]{1,0:T(8,128)(2,1)S(1)} %get-tuple-element.210), channel_id=1, source_target_pairs={{16,0},{24,8},{17,1},{25,9},{18,2},{26,10},{19,3},{27,11},{20,4},{... | collective-permute-start | bytes 393224 | tf_op jit(solution)/shard_map/ppermute | solution.py:51
  586.9 83.4 %collective-permute-start.13 = (bf16[128,2048]{1,0:T(8,128)(2,1)}, bf16[128,2048]{1,0:T(8,128)(2,1)}, u32[]{:S(2)}, u32[]{:S(2)}) collective-permute-start(bf16[128,2048]{1,0:T(8,128)(2,1)} %get-tuple-element.193), channel_id=1, source_target_pairs={{0,4},{2,6},{4,0},{6,2},{1,5},{3,7},{5,1},{7,3},{8,12},{10,14},{12... | collective-permute-start | bytes 1572872 | tf_op jit(solution)/shard_map/ppermute | solution.py:1163
  673.5 9.5 %collective-permute-start.15 = (f32[128,2048]{1,0:T(8,128)S(1)}, f32[128,2048]{1,0:T(8,128)}, u32[]{:S(2)}, u32[]{:S(2)}) collective-permute-start(f32[128,2048]{1,0:T(8,128)S(1)} %fusion.22), channel_id=1, source_target_pairs={{0,1},{1,0},{2,3},{3,2},{4,5},{5,4},{6,7},{7,6},{8,9},{9,8},{10,11... | collective-permute-start | bytes 3145736 | tf_op jit(solution)/shard_map/ppermute | solution.py:1169
  681.1 9.0 %collective-permute-start.42 = (bf16[1,128,512]{2,1,0:T(8,128)(2,1)S(1)}, bf16[1,128,512]{2,1,0:T(8,128)(2,1)S(1)}, u32[]{:S(2)}, u32[]{:S(2)}) collective-permute-start(bf16[1,128,512]{2,1,0:T(8,128)(2,1)S(1)} %get-tuple-element.222), channel_id=1, source_target_pairs={{0,6},{2,4},{4,2},{6,0},{1,7},{3,5},{5,3},{7,1},{8,14},{10,12},{12... | collective-permute-start | bytes 393224 | tf_op jit(solution)/shard_map/ppermute | solution.py:1141
  682.6 7.4 collective-permute-start.41
  694.1 69.4 %collective-permute-start.34 = (bf16[1,128,512]{2,1,0:T(8,128)(2,1)}, bf16[1,128,512]{2,1,0:T(8,128)(2,1)}, u32[]{:S(2)}, u32[]{:S(2)}) collective-permute-start(bf16[1,128,512]{2,1,0:T(8,128)(2,1)} %constant_dynamic-slice_fusion.8), channel_id=1, source_target_pairs={{0,2},{2,0},{4,6},{6,4},{1,3},{3,1},{5,7},{7,5},{8,10},{10,8},{12,... | collective-permute-start | bytes 393224 | tf_op jit(solution)/shard_map/ppermute | solution.py:1141
  696.2 78.9 %collective-permute-start.37 = (bf16[1,128,1024]{2,1,0:T(8,128)(2,1)}, bf16[1,128,1024]{2,1,0:T(8,128)(2,1)}, u32[]{:S(2)}, u32[]{:S(2)}) collective-permute-start(bf16[1,128,1024]{2,1,0:T(8,128)(2,1)} %constant_dynamic-slice_fusion.5), channel_id=1, source_target_pairs={{0,2},{2,0},{4,6},{6,4},{1,3},{3,1},{5,7},{7,5},{8,10},{10,8},{12,... | collective-permute-start | bytes 786440 | tf_op jit(solution)/shard_map/ppermute | solution.py:1141
  756.7 9.3 %collective-permute-start.28 = (bf16[1,128,512]{1,2,0:T(8,128)(2,1)S(1)}, bf16[1,128,512]{1,2,0:T(8,128)(2,1)S(1)}, u32[]{:S(2)}, u32[]{:S(2)}) collective-permute-start(bf16[1,128,512]{1,2,0:T(8,128)(2,1)S(1)} %get-tuple-element.230), channel_id=1, source_target_pairs={{0,2},{2,0},{4,6},{6,4},{1,3},{3,1},{5,7},{7,5},{8,10},{10,8},{12,... | collective-permute-start | bytes 393224 | tf_op jit(solution)/shard_map/ppermute | solution.py:1141
  760.9 12.1 %collective-permute-start.30 = (bf16[1,128,512]{1,2,0:T(8,128)(2,1)S(1)}, bf16[1,128,512]{1,2,0:T(8,128)(2,1)S(1)}, u32[]{:S(2)}, u32[]{:S(2)}) collective-permute-start(bf16[1,128,512]{1,2,0:T(8,128)(2,1)S(1)} %get-tuple-element.228), channel_id=1, source_target_pairs={{0,6},{2,4},{4,2},{6,0},{1,7},{3,5},{5,3},{7,1},{8,14},{10,12},{12... | collective-permute-start | bytes 393224 | tf_op jit(solution)/shard_map/ppermute | solution.py:1141
  762.4 10.6 %collective-permute-start.29 = (bf16[1,128,512]{1,2,0:T(8,128)(2,1)S(1)}, bf16[1,128,512]{1,2,0:T(8,128)(2,1)S(1)}, u32[]{:S(2)}, u32[]{:S(2)}) collective-permute-start(bf16[1,128,512]{1,2,0:T(8,128)(2,1)S(1)} %get-tuple-element.229), channel_id=1, source_target_pairs={{0,4},{2,6},{4,0},{6,2},{1,5},{3,7},{5,1},{7,3},{8,12},{10,14},{12... | collective-permute-start | bytes 393224 | tf_op jit(solution)/shard_map/ppermute | solution.py:1141
  764.5 15.2 %collective-permute-start.36 = (bf16[1,128,512]{2,1,0:T(8,128)(2,1)S(1)}, bf16[1,128,512]{2,1,0:T(8,128)(2,1)S(1)}, u32[]{:S(2)}, u32[]{:S(2)}) collective-permute-start(bf16[1,128,512]{2,1,0:T(8,128)(2,1)S(1)} %get-tuple-element.225), channel_id=1, source_target_pairs={{0,6},{2,4},{4,2},{6,0},{1,7},{3,5},{5,3},{7,1},{8,14},{10,12},{12... | collective-permute-start | bytes 393224 | tf_op jit(solution)/shard_map/ppermute | solution.py:1141
  766.0 13.7 %collective-permute-start.35 = (bf16[1,128,512]{2,1,0:T(8,128)(2,1)S(1)}, bf16[1,128,512]{2,1,0:T(8,128)(2,1)S(1)}, u32[]{:S(2)}, u32[]{:S(2)}) collective-permute-start(bf16[1,128,512]{2,1,0:T(8,128)(2,1)S(1)} %get-tuple-element.226), channel_id=1, source_target_pairs={{0,4},{2,6},{4,0},{6,2},{1,5},{3,7},{5,1},{7,3},{8,12},{10,14},{12... | collective-permute-start | bytes 393224 | tf_op jit(solution)/shard_map/ppermute | solution.py:1141
  777.0 15.4 %collective-permute-start.39 = (bf16[1,128,1024]{2,1,0:T(8,128)(2,1)S(1)}, bf16[1,128,1024]{2,1,0:T(8,128)(2,1)S(1)}, u32[]{:S(2)}, u32[]{:S(2)}) collective-permute-start(bf16[1,128,1024]{2,1,0:T(8,128)(2,1)S(1)} %get-tuple-element.205), channel_id=1, source_target_pairs={{0,6},{2,4},{4,2},{6,0},{1,7},{3,5},{5,3},{7,1},{8,14},{10,12},{12... | collective-permute-start | bytes 786440 | tf_op jit(solution)/shard_map/ppermute | solution.py:1141
  778.5 13.2 %collective-permute-start.38 = (bf16[1,128,1024]{2,1,0:T(8,128)(2,1)S(1)}, bf16[1,128,1024]{2,1,0:T(8,128)(2,1)S(1)}, u32[]{:S(2)}, u32[]{:S(2)}) collective-permute-start(bf16[1,128,1024]{2,1,0:T(8,128)(2,1)S(1)} %get-tuple-element.206), channel_id=1, source_target_pairs={{0,4},{2,6},{4,0},{6,2},{1,5},{3,7},{5,1},{7,3},{8,12},{10,14},{12... | collective-permute-start | bytes 786440 | tf_op jit(solution)/shard_map/ppermute | solution.py:1141
  796.1 7.1 collective-permute-start.32
  800.5 6.5 collective-permute-start.33
  (57 other events, 736.6 us)
Sparse Core Ops, SparseCore 0:
  135.0 50.1 all-gather.4
  186.8 59.8 all-gather.6
  248.2 87.0 all-gather.8
  336.7 44.4 all-gather.10
  404.0 42.5 reduce-scatter.5
  448.9 76.1 reduce-scatter.7
  527.3 53.1 reduce-scatter.9
  583.0 47.5 reduce-scatter.11
  670.3 49.2 reduce-scatter.13

commit v4 on v3

--- a/solution.py
+++ b/solution.py
@@ -45,43 +45,33 @@
     return sigma_val * (1.0 + values * (1.0 - sigma_val))
 
 
-def passed_along(block, axis, distance):
-    devices = range(lax.axis_size(axis))
-    route = [(i - distance, i) for i in devices if i - distance in devices]
-    return lax.ppermute(block, axis, route)
-
-
 def convolve(extended, weights, ext_docs, tok_count):
     edge_rows = weights.shape[0] - 1
+    here = ext_docs[edge_rows : edge_rows + tok_count]
     summed = jnp.zeros((tok_count, extended.shape[1]), f32)
     for tap_index in range(weights.shape[0]):
         begin_row = edge_rows - tap_index
-        same_doc = (ext_docs[begin_row : begin_row + tok_count] == ext_docs[edge_rows:])[:, None]
-        summed = (
-            summed
-            + jnp.where(same_doc, extended[begin_row : begin_row + tok_count].astype(f32), 0.0)
-            * weights[tap_index][None, :]
-        )
+        same_doc = (ext_docs[begin_row : begin_row + tok_count] == here)[:, None]
+        rows = extended[begin_row : begin_row + tok_count].astype(f32)
+        summed = summed + jnp.where(same_doc, rows, 0.0) * weights[tap_index][None, :]
     return summed
 
 
 def convolve_back(d_conv, extended, weights, ext_docs, tok_count):
     edge_rows = weights.shape[0] - 1
-    d_extended = jnp.zeros((tok_count + edge_rows, d_conv.shape[1]), f32)
+    here = ext_docs[edge_rows : edge_rows + tok_count]
+    d_rows = jnp.zeros((tok_count, d_conv.shape[1]), f32)
     tap_grads = []
     for tap_index in range(weights.shape[0]):
         begin_row = edge_rows - tap_index
-        same_doc = (ext_docs[begin_row : begin_row + tok_count] == ext_docs[edge_rows:])[:, None]
-        masked_grad = jnp.where(same_doc, d_conv, 0.0)
-        tap_grads.append(
-            jnp.sum(
-                masked_grad * extended[begin_row : begin_row + tok_count].astype(f32), axis=0
-            )
-        )
-        d_extended = d_extended + jnp.pad(
-            masked_grad * weights[tap_index][None, :], ((begin_row, edge_rows - begin_row), (0, 0))
-        )
-    return (d_extended, jnp.stack(tap_grads))
+        before = (ext_docs[begin_row : begin_row + tok_count] == here)[:, None]
+        rows = extended[begin_row : begin_row + tok_count].astype(f32)
+        tap_grads.append(jnp.sum(jnp.where(before, d_conv[:tok_count] * rows, 0.0), axis=0))
+        last = edge_rows + tap_index
+        after = (ext_docs[last : last + tok_count] == here)[:, None]
+        ahead = d_conv[tap_index : tap_index + tok_count]
+        d_rows = d_rows + jnp.where(after, ahead, 0.0) * weights[tap_index][None, :]
+    return (d_rows, jnp.stack(tap_grads))
 
 
 def tri_dot(a, b, dims=((1,), (0,))):
@@ -358,14 +348,21 @@
     )(base, doc_starts, x, bc, dtp, dy, span_starts, start_decay, nega, skip, in_state, grad_state)
 
 
-QB = 256
+QB = 512
 KB = 512
 
 
-def seen(base_ref, starts_ref, q_first, k_first):
-    q_pos = base_ref[0] + q_first + iota2((QB, KB), 0)
+def sight(base_ref, starts_ref, q_first):
+    q_pos = base_ref[0] + q_first + iota2((QB, 1), 0)
+    low = jnp.zeros((QB, 1), jnp.int32)
+    for i in range(starts_ref.shape[0]):
+        low = jnp.where(starts_ref[i] <= q_pos, starts_ref[i], low)
+    return jnp.broadcast_to(low, (QB, KB)), jnp.broadcast_to(q_pos, (QB, KB))
+
+
+def seen(low, high, k_first):
     k_pos = k_first + iota2((QB, KB), 1)
-    return (q_pos >= k_pos) & (docs_of(q_pos, starts_ref) == docs_of(k_pos, starts_ref))
+    return (k_pos >= low) & (k_pos <= high)
 
 
 def attend_kernel(scale, base_ref, starts_ref, q_ref, kv_ref, o_ref, lse_ref, k_ref, v_ref):
@@ -386,16 +383,16 @@
                 v_ref[at, :] = jnp.concatenate([v[:, lo + kw : lo + 2 * kw] for v in parts], axis=1)
 
     q = q_ref[...]
+    low, high = sight(base_ref, starts_ref, i * QB)
     blocks = (base_ref[0] + (i + 1) * QB + KB - 1) // KB
 
     def turn(j, carry):
         m, l, acc = carry
         at = pl.ds(pl.multiple_of(j * KB, KB), KB)
         s = dot_nt(q, k_ref[at, :]) * scale
-        visible = seen(base_ref, starts_ref, i * QB, j * KB)
-        s = jnp.where(visible, s, neg_large)
+        s = jnp.where(seen(low, high, j * KB), s, neg_large)
         m_new = jnp.maximum(m, jnp.max(s, axis=1, keepdims=True))
-        w = jnp.where(visible, jnp.exp(s - m_new), 0.0)
+        w = jnp.exp(s - m_new)
         r = jnp.exp(m - m_new)
         l = l * r + jnp.sum(w, axis=1, keepdims=True)
         return m_new, l, acc * r + dot_nn(w.astype(bf16), v_ref[at, :])
@@ -404,7 +401,7 @@
         0,
         blocks,
         turn,
-        (jnp.full((QB, 1), neg_large, f32), jnp.zeros((QB, 1), f32), jnp.zeros((QB, HDIM), f32)),
+        (jnp.full((QB, 1), 0.1 * neg_large, f32), jnp.zeros((QB, 1), f32), jnp.zeros((QB, HDIM), f32)),
     )
     o_ref[...] = acc / l
     lse_ref[...] = jnp.broadcast_to(m + jnp.log(l), (QB, 128))
@@ -445,12 +442,13 @@
     q, do = q_ref[...], do_ref[...]
     delta = jnp.sum(do.astype(f32) * o_ref[...], axis=1, keepdims=True)
     lse = lse_ref[:, 0:1]
+    low, high = sight(base_ref, starts_ref, i * QB)
     blocks = (base_ref[0] + (i + 1) * QB + KB - 1) // KB
 
     def turn(j, dq):
         at = pl.ds(pl.multiple_of(j * KB, KB), KB)
         k, v = k_ref[at, :], v_ref[at, :]
-        visible = seen(base_ref, starts_ref, i * QB, j * KB)
+        visible = seen(low, high, j * KB)
         s = dot_nt(q, k) * scale
         p = jnp.exp(jnp.where(visible, s - lse, neg_large))
         ds = (p * (dot_nt(do, v) - delta)).astype(bf16)
@@ -499,6 +497,128 @@
     )(base, doc_starts, q, do, o, lse, k, v)
 
 
+def one_at(shape, source, where=True):
+    lane = iota2(shape, 1)
+    return ((iota2(shape, 0) == source(lane)) & where).astype(bf16)
+
+
+def eye(n):
+    return one_at((n, n), lambda lane: lane)
+
+
+def q_order(kw):
+    hk = kw // 2
+    return one_at(
+        (HDIM, HDIM), lambda l: ((l % kw) // hk) * (HDIM // 2) + (l // kw) * hk + l % hk
+    )
+
+
+def bc_order(p, bw, n_p):
+    return one_at((2 * n_p * bw, 2 * bw), lambda l: (l // bw) * (n_p * bw) + p * bw + l % bw)
+
+
+def last_order(p, kw, n_heads, dt_rows):
+    hk = kw // 2
+    lane = iota2((HDIM, 128), 1)
+    lane_dt = iota2((dt_rows, 128), 1)
+    key = one_at((HDIM, 128), lambda l: (l // hk) * (HDIM // 2) + p * hk + l % hk, lane < kw)
+    value = one_at((HDIM, 128), lambda l: p * kw + l - kw, (lane >= kw) & (lane < 2 * kw))
+    step = one_at(
+        (dt_rows, 128),
+        lambda l: p * n_heads + l - 2 * kw,
+        (lane_dt >= 2 * kw) & (lane_dt < 2 * kw + n_heads),
+    )
+    return key, value, step
+
+
+def pack_kernel(
+    x_ref, bc_ref, k_ref, v_ref, dt_ref, q_ref, z_ref, mout_ref, aout_ref, gate_ref, up_ref,
+    down_ref, a_ref, b_ref, c_ref, d_ref, e_ref,
+):
+    n_p = a_ref.shape[0]
+    xw, bw, kw = x_ref.shape[1] // n_p, bc_ref.shape[1] // (2 * n_p), HDIM // n_p
+    n_heads, ff, aw = dt_ref.shape[1] // n_p, gate_ref.shape[1] // n_p, q_ref.shape[1] // n_p
+    bc, key, value = bc_ref[...].astype(bf16), k_ref[...].astype(bf16), v_ref[...].astype(bf16)
+    step = dt_ref[...].astype(bf16)
+    order = q_order(kw)
+    for p in range(n_p):
+        cut = lambda ref, n: ref[:, p * n : p * n + n].astype(bf16)
+        flip = lambda ref, n: dot_tn(ref[p * n : p * n + n, :].astype(bf16), eye(n)).astype(bf16)
+        a_ref[p, :, :xw] = cut(x_ref, xw)
+        a_ref[p, :, xw : xw + 2 * bw] = dot_nn(bc, bc_order(p, bw, n_p)).astype(bf16)
+        s_key, s_value, s_step = last_order(p, kw, n_heads, dt_ref.shape[1])
+        a_ref[p, :, xw + 2 * bw :] = (
+            dot_nn(key, s_key) + dot_nn(value, s_value) + dot_nn(step, s_step)
+        ).astype(bf16)
+        b_ref[p, :, :HDIM] = dot_nn(cut(q_ref, aw), order).astype(bf16)
+        b_ref[p, :, HDIM:] = cut(z_ref, xw)
+        c_ref[p, :, :xw] = flip(mout_ref, xw)
+        c_ref[p, :, xw:] = flip(aout_ref, aw)
+        d_ref[p, :, :ff] = cut(gate_ref, ff)
+        d_ref[p, :, ff:] = cut(up_ref, ff)
+        e_ref[p] = flip(down_ref, ff)
+
+
+def pack(n_p, *weights):
+    x, bc, k, v, dt, q, z, mout, aout, gate, up, down = weights
+    rows = x.shape[0]
+    ff, xw = gate.shape[1] // n_p, x.shape[1] // n_p
+    widths = (xw + bc.shape[1] // n_p + 128, HDIM + xw, xw + HDIM, 2 * ff, ff)
+    vm = pl.BlockSpec(memory_space=pltpu.VMEM)
+    return pl.pallas_call(
+        pack_kernel,
+        in_specs=[vm] * 12,
+        out_specs=[vm] * 5,
+        out_shape=[jax.ShapeDtypeStruct((n_p, rows, w), bf16) for w in widths],
+        compiler_params=pltpu.CompilerParams(vmem_limit_bytes=VMEM_LIMIT),
+        cost_estimate=pl.CostEstimate(flops=0, bytes_accessed=10_000_000, transcendentals=0),
+        name="pack",
+    )(*weights)
+
+
+def unpack_kernel(
+    a_ref, b_ref, c_ref, d_ref, e_ref,
+    x_ref, bc_ref, k_ref, v_ref, dt_ref, q_ref, z_ref, mout_ref, aout_ref, gate_ref, up_ref,
+    down_ref,
+):
+    n_p, rows = a_ref.shape[0], a_ref.shape[1]
+    xw, bw, kw = x_ref.shape[1] // n_p, bc_ref.shape[1] // (2 * n_p), HDIM // n_p
+    n_heads, ff, aw = dt_ref.shape[1] // n_p, gate_ref.shape[1] // n_p, q_ref.shape[1] // n_p
+    order, turn = q_order(kw), eye(rows)
+    bc, key = jnp.zeros(bc_ref.shape, f32), jnp.zeros(k_ref.shape, f32)
+    value, step = jnp.zeros(v_ref.shape, f32), jnp.zeros(dt_ref.shape, f32)
+    for p in range(n_p):
+        cut = lambda n: slice(p * n, p * n + n)
+        x_ref[:, cut(xw)] = a_ref[p, :, :xw].astype(f32)
+        bc = bc + dot_nt(a_ref[p, :, xw : xw + 2 * bw], bc_order(p, bw, n_p))
+        last = a_ref[p, :, xw + 2 * bw :]
+        s_key, s_value, s_step = last_order(p, kw, n_heads, dt_ref.shape[1])
+        key, value = key + dot_nt(last, s_key), value + dot_nt(last, s_value)
+        step = step + dot_nt(last, s_step)
+        q_ref[:, cut(aw)] = dot_nt(b_ref[p, :, :HDIM], order)
+        z_ref[:, cut(xw)] = b_ref[p, :, HDIM:].astype(f32)
+        mout_ref[cut(xw), :] = dot_tn(c_ref[p, :, :xw], turn)
+        aout_ref[cut(aw), :] = dot_tn(c_ref[p, :, xw:], turn)
+        gate_ref[:, cut(ff)] = d_ref[p, :, :ff].astype(f32)
+        up_ref[:, cut(ff)] = d_ref[p, :, ff:].astype(f32)
+        down_ref[cut(ff), :] = dot_tn(e_ref[p], turn)
+    bc_ref[...] = bc
+    k_ref[...], v_ref[...], dt_ref[...] = key, value, step
+
+
+def unpack(pieces, like):
+    vm = pl.BlockSpec(memory_space=pltpu.VMEM)
+    return pl.pallas_call(
+        unpack_kernel,
+        in_specs=[vm] * 5,
+        out_specs=[vm] * 12,
+        out_shape=[jax.ShapeDtypeStruct(w.shape, f32) for w in like],
+        compiler_params=pltpu.CompilerParams(vmem_limit_bytes=VMEM_LIMIT),
+        cost_estimate=pl.CostEstimate(flops=0, bytes_accessed=10_000_000, transcendentals=0),
+        name="unpack",
+    )(*pieces)
+
+
 def at_rows(first, count):
     return pl.ds(pl.multiple_of(first, count), count)
 
@@ -535,7 +655,75 @@
 HOPS = (3, 1, 2)
 
 
-def share_rows(full_ref, half, own_sems, far_sems, near_sems):
+def z_chain(ref, up_sems, down_sems):
+    z, p, c = place()
+    nz = ref.shape[0]
+
+    def block_up(k):
+        at = ref.at[z - k]
+        return pltpu.make_async_remote_copy(
+            src_ref=at, dst_ref=at, send_sem=up_sems.at[0, k], recv_sem=up_sems.at[1, k],
+            device_id=chip(z + 1, p, c), device_id_type=MESH,
+        )
+
+    def block_down(k):
+        at = ref.at[z + k]
+        return pltpu.make_async_remote_copy(
+            src_ref=at, dst_ref=at, send_sem=down_sems.at[0, k], recv_sem=down_sems.at[1, k],
+            device_id=chip(z - 1, p, c), device_id_type=MESH,
+        )
+
+    def got_up(k):
+        at = ref.at[z - k]
+        pltpu.make_async_remote_copy(
+            src_ref=at, dst_ref=at, send_sem=up_sems.at[0, k - 1], recv_sem=up_sems.at[1, k - 1],
+            device_id=chip(z - 1, p, c), device_id_type=MESH,
+        ).wait_recv()
+
+    def got_down(k):
+        at = ref.at[z + k]
+        pltpu.make_async_remote_copy(
+            src_ref=at, dst_ref=at, send_sem=down_sems.at[0, k - 1],
+            recv_sem=down_sems.at[1, k - 1],
+            device_id=chip(z + 1, p, c), device_id_type=MESH,
+        ).wait_recv()
+
+    def stage(k):
+        if k:
+
+            @pl.when(z - k >= 0)
+            def _():
+                got_up(k)
+
+        @pl.when((z - k >= 0) & (z + 1 < nz))
+        def _():
+            block_up(k).start()
+
+        if k:
+
+            @pl.when(z + k < nz)
+            def _():
+                got_down(k)
+
+        @pl.when((z + k < nz) & (z > 0))
+        def _():
+            block_down(k).start()
+
+    def done():
+        for k in range(nz):
+
+            @pl.when((z - k >= 0) & (z + 1 < nz))
+            def _():
+                block_up(k).wait_send()
+
+            @pl.when((z + k < nz) & (z > 0))
+            def _():
+                block_down(k).wait_send()
+
+    return stage, done
+
+
+def share_rows(full_ref, half, own_sems, far_sems, near_sems, between=None):
     z, p, c = place()
     other = chip(z, p, 1 - c)
     mine = full_ref.at[at_rows((p * 2 + c) * half, half), :]
@@ -543,6 +731,8 @@
     for i, d in enumerate(HOPS):
         copies.append(send(mine, mine, far_sems.at[0, i], far_sems.at[1, i], chip(z, hop(p, d), c)))
     copies.append(send(mine, mine, own_sems.at[0], own_sems.at[1], other))
+    if between is not None:
+        between()
     onward = []
     for i, d in ((1, 1), (2, 2), (0, 3)):
         copies[i].wait_recv()
@@ -598,9 +788,10 @@
         )
         if i:
             pass_on(i - 1, order[i - 1])
-    near[3].wait_recv()
-    for copy in far:
-        copy.wait_recv()
+    def finish():
+        near[3].wait_recv()
+        for copy in far:
+            copy.wait_recv()
 
     def total_rows(at):
         total = keep[3, at, :] + sib_in[3, at, :].astype(f32)
@@ -610,7 +801,7 @@
         for copy in near + far:
             copy.wait_send()
 
-    return total_rows, done
+    return total_rows, finish, done
 
 
 def greet():
@@ -623,15 +814,28 @@
 
 
 def mid_kernel(
-    left, right, resid, gain, mid_ref, full_ref,
+    left, right, resid, gain, w_ref, mid_ref, full_ref, w_out,
     part, keep, sib_out, sib_in, out, came, n_sems, f_sems, own_sems, far_sems, near_sems,
+    up_sems, down_sems, loc_sems,
 ):
-    greet()
     z, p, c = place()
+    nz = w_out.shape[0]
+    meet(
+        [chip(z, p, 1 - c)]
+        + [chip(z, hop(p, d), c) for d in HOPS]
+        + [chip(lax.rem(z + d, nz), p, c) for d in (1, nz - 1)]
+    )
+    local = pltpu.make_async_copy(w_ref, w_out.at[z], loc_sems.at[0])
+    local.start()
+    local.wait()
+    stage, chain_done = z_chain(w_out, up_sems, down_sems)
+    stage(0)
     half = keep.shape[1]
-    total_rows, done = reduce_blocks(
+    total_rows, finish, done = reduce_blocks(
         [(left, right)], part, keep, sib_out, sib_in, out, came, n_sems, f_sems
     )
+    stage(1)
+    finish()
     g = gain[...]
 
     @pl.loop(0, half // 16)
@@ -641,9 +845,13 @@
         mid_ref[at, :] = mid
         full_ref[at_rows((p * 2 + c) * half + r * 16, 16), :] = (mid * rms(mid) * g).astype(bf16)
 
-    copies, onward = share_rows(full_ref, half, own_sems, far_sems, near_sems)
+    between = lambda: stage(2) if nz > 2 else None
+    copies, onward = share_rows(full_ref, half, own_sems, far_sems, near_sems, between)
+    for k in range(3, nz):
+        stage(k)
     done()
     finish_share(copies, onward)
+    chain_done()
 
 
 def two_kernel(
@@ -653,9 +861,10 @@
     greet()
     z, p, c = place()
     half = keep.shape[1]
-    total_rows, done = reduce_blocks(
+    total_rows, finish, done = reduce_blocks(
         [(left, right)], part, keep, sib_out, sib_in, out, came, n_sems, f_sems
     )
+    finish()
     g = gain[...]
     ggain_ref[...] = jnp.zeros_like(ggain_ref)
 
@@ -678,18 +887,20 @@
 
 
 def one_kernel(
-    left_a, right_a, left_b, right_b, hidden_own, dmid_own, gain, grad_ref, ggain_ref,
-    part, keep, sib_out, sib_in, out, came, n_sems, f_sems, own_sems,
+    n, left_a, right_a, left_b, right_b, hidden_own, dmid_own, gain, act, w_act, mid_own, *refs
 ):
+    ins, (grad_ref, block_ref, ggain_ref), outs = refs[:n], refs[n : n + 3], refs[n + 3 : 2 * n + 3]
+    first, second = refs[2 * n + 3 : 2 * n + 11], refs[2 * n + 11 : 2 * n + 19]
+    own_sems, w_sems, loc_sems = refs[2 * n + 19 :]
     greet()
     z, p, c = place()
-    half = keep.shape[1]
-    total_rows, done = reduce_blocks(
-        [(left_a, right_a), (left_b, right_b)],
-        part, keep, sib_out, sib_in, out, came, n_sems, f_sems,
-    )
+    half = hidden_own.shape[0]
+    total_rows, finish, done = reduce_blocks([(left_a, right_a), (left_b, right_b)], *first)
+    total_out, finish_out, done_out = reduce_blocks([(act, w_act)], *second)
+    moved = swap_begin(ins, outs, w_sems, loc_sems)
     g = gain[...]
     ggain_ref[...] = jnp.zeros_like(ggain_ref)
+    finish()
 
     @pl.loop(0, half // 16)
     def _(r):
@@ -703,13 +914,48 @@
         ggain_ref[...] += jnp.sum(d_one * hid * scale, axis=0, keepdims=True)
         grad_ref[at_rows(c * half + r * 16, 16), :] = d_in
 
-    mine = grad_ref.at[at_rows(c * half, half), :]
-    copy = send(mine, mine, own_sems.at[0], own_sems.at[1], chip(z, p, 1 - c))
+    mine = at_rows(c * half, half)
+    other = chip(z, p, 1 - c)
+    copies = [
+        send(grad_ref.at[mine, :], grad_ref.at[mine, :], own_sems.at[0, 0], own_sems.at[1, 0], other)
+    ]
+    finish_out()
+
+    @pl.loop(0, half // 16)
+    def _(r):
+        at = at_rows(r * 16, 16)
+        block_ref[at_rows(c * half + r * 16, 16), :] = mid_own[at, :] + total_out(at)
+
+    copies.append(
+        send(block_ref.at[mine, :], block_ref.at[mine, :], own_sems.at[0, 1], own_sems.at[1, 1], other)
+    )
     done()
-    copy.wait()
+    done_out()
+    for copy in copies + moved:
+        copy.wait()
 
 
 VM = pl.BlockSpec(memory_space=pltpu.VMEM)
+ANYWHERE = pl.BlockSpec(memory_space=pl.ANY)
+
+
+def swap_begin(ins, outs, sems, loc_sems):
+    z, p, c = place()
+    copies = []
+    for j, (src, dst) in enumerate(zip(ins, outs)):
+        for i, d in enumerate(HOPS):
+            q = hop(p, d)
+            copies.append(
+                send(src.at[q], dst.at[p], sems.at[0, j, i], sems.at[1, j, i], chip(z, q, c))
+            )
+        local = pltpu.make_async_copy(src.at[p], dst.at[p], loc_sems.at[j])
+        local.start()
+        copies.append(local)
+    return copies
+
+
+def swap_sems(n):
+    return [pltpu.SemaphoreType.DMA((2, n, 3)), pltpu.SemaphoreType.DMA((n,))]
 
 
 def reduce_scratch(half, width):
@@ -732,29 +978,48 @@
 ]
 
 
-def plane_call(kernel, name, number, args, shapes, scratch, nbytes=150_000_000):
+def plane_call(kernel, name, number, args, shapes, scratch, nbytes=150_000_000, moved=()):
+    n = len(moved)
+    if n:
+        kernel = functools.partial(kernel, n)
+        scratch = scratch + swap_sems(n)
     return pl.pallas_call(
         kernel,
-        in_specs=[VM] * len(args),
-        out_specs=[VM] * len(shapes),
-        out_shape=[jax.ShapeDtypeStruct(s, t) for s, t in shapes],
+        in_specs=[VM] * len(args) + [ANYWHERE] * n,
+        out_specs=[VM] * len(shapes) + [ANYWHERE] * n,
+        out_shape=[jax.ShapeDtypeStruct(s, t) for s, t in shapes]
+        + [jax.ShapeDtypeStruct(m.shape, m.dtype) for m in moved],
         scratch_shapes=scratch,
         compiler_params=pltpu.CompilerParams(
             collective_id=number, has_side_effects=True, vmem_limit_bytes=VMEM_LIMIT
         ),
         cost_estimate=pl.CostEstimate(flops=0, bytes_accessed=nbytes, transcendentals=0),
         name=name,
-    )(*args)
-
-
-def mid_step(mixed, w, resid_own, gain):
+    )(*args, *moved)
+
+
+def mid_step(mixed, w, resid_own, gain, piece, nz):
     tok, width = mixed.shape[0], w.shape[0]
     half = resid_own.shape[0]
-    return plane_call(
-        mid_kernel, "mid_step", 1, (mixed, w, resid_own, gain),
-        [((half, width), f32), ((tok, width), bf16)],
-        reduce_scratch(half, width) + SHARE_SEMS,
-    )
+    dma = pltpu.SemaphoreType.DMA
+    return pl.pallas_call(
+        mid_kernel,
+        in_specs=[VM] * 4 + [ANYWHERE],
+        out_specs=[VM] * 2 + [ANYWHERE],
+        out_shape=[
+            jax.ShapeDtypeStruct((half, width), f32),
+            jax.ShapeDtypeStruct((tok, width), bf16),
+            jax.ShapeDtypeStruct((nz,) + piece.shape, bf16),
+        ],
+        scratch_shapes=reduce_scratch(half, width)
+        + SHARE_SEMS
+        + [dma((2, nz)), dma((2, nz)), dma((1,))],
+        compiler_params=pltpu.CompilerParams(
+            collective_id=1, has_side_effects=True, vmem_limit_bytes=VMEM_LIMIT
+        ),
+        cost_estimate=pl.CostEstimate(flops=0, bytes_accessed=150_000_000, transcendentals=0),
+        name="mid_step",
+    )(mixed, w, resid_own, gain, piece)
 
 
 def two_step(d_gu, w, mid_own, grad_own, gain):
@@ -767,13 +1032,17 @@
     )
 
 
-def one_step(d_a, w_a, d_b, w_b, hidden_own, dmid_own, gain):
+def one_step(d_a, w_a, d_b, w_b, hidden_own, dmid_own, gain, act, w_act, mid_own, moved):
     width = w_a.shape[0]
     half = hidden_own.shape[0]
     return plane_call(
-        one_kernel, "one_step", 3, (d_a, w_a, d_b, w_b, hidden_own, dmid_own, gain),
-        [((2 * half, width), f32), ((1, width), f32)],
-        reduce_scratch(half, width) + [pltpu.SemaphoreType.DMA((2,))],
+        one_kernel, "one_step", 3,
+        (d_a, w_a, d_b, w_b, hidden_own, dmid_own, gain, act, w_act, mid_own),
+        [((2 * half, width), f32), ((2 * half, width), f32), ((1, width), f32)],
+        reduce_scratch(half, width)
+        + reduce_scratch(half, width)
+        + [pltpu.SemaphoreType.DMA((2, 2))],
+        moved=moved,
     )
 
 
@@ -781,17 +1050,17 @@
 
 
 def open_kernel(n, *refs):
-    hid, grad, gains_ref, a_ref = refs[:4]
-    w_refs = refs[4 : 4 + n]
-    gain_out, full_ref, gfull_ref, a_out = refs[4 + n : 8 + n]
-    w_outs = refs[8 + n : 8 + 2 * n]
+    hid, gains_ref, a_ref = refs[:3]
+    w_refs = refs[3 : 3 + n]
+    gain_out, full_ref, a_out = refs[3 + n : 6 + n]
+    w_outs = refs[6 + n : 6 + 2 * n]
     (
         g_vec, gz_sems, gp_sems, a_sems, up_sems, down_sems, own_sems, far_sems, near_sems,
-        own_g, far_g, near_g, w_sems, loc_sems, halo_sems,
-    ) = refs[8 + 2 * n :]
+        w_sems, loc_sems, halo_sems,
+    ) = refs[6 + 2 * n :]
     z, p, c = place()
     nz, half, rows = a_out.shape[0], hid.shape[0], a_ref.shape[1]
-    tok = gfull_ref.shape[0]
+    tok = full_ref.shape[0] - HALO
     ups = [chip(lax.rem(z + d, nz), p, c) for d in range(1, nz)]
     flat = [chip(z, hop(p, d), c) for d in HOPS]
     meet(ups + flat + [chip(z, p, 1 - c)])
@@ -811,11 +1080,6 @@
     for copy in local:
         copy.start()
 
-    @pl.loop(0, half // 16)
-    def _(r):
-        at = at_rows(r * 16, 16)
-        gfull_ref[at_rows((p * 2 + c) * half + r * 16, 16), :] = grad[at, :].astype(bf16)
-
     for copy in gz:
         copy.wait_recv()
     gp = [
@@ -843,56 +1107,7 @@
         send(mine, mine, far_sems.at[0, i], far_sems.at[1, i], flat[i]) for i in range(3)
     ] + [send(mine, mine, own_sems.at[0], own_sems.at[1], other)]
 
-    def block_up(k):
-        at = a_out.at[z - k]
-        return pltpu.make_async_remote_copy(
-            src_ref=at, dst_ref=at, send_sem=up_sems.at[0, k], recv_sem=up_sems.at[1, k],
-            device_id=chip(z + 1, p, c), device_id_type=MESH,
-        )
-
-    def block_down(k):
-        at = a_out.at[z + k]
-        return pltpu.make_async_remote_copy(
-            src_ref=at, dst_ref=at, send_sem=down_sems.at[0, k], recv_sem=down_sems.at[1, k],
-            device_id=chip(z - 1, p, c), device_id_type=MESH,
-        )
-
-    def got_up(k):
-        at = a_out.at[z - k]
-        pltpu.make_async_remote_copy(
-            src_ref=at, dst_ref=at, send_sem=up_sems.at[0, k - 1], recv_sem=up_sems.at[1, k - 1],
-            device_id=chip(z - 1, p, c), device_id_type=MESH,
-        ).wait_recv()
-
-    def got_down(k):
-        at = a_out.at[z + k]
-        pltpu.make_async_remote_copy(
-            src_ref=at, dst_ref=at, send_sem=down_sems.at[0, k - 1],
-            recv_sem=down_sems.at[1, k - 1],
-            device_id=chip(z + 1, p, c), device_id_type=MESH,
-        ).wait_recv()
-
-    def stage(k):
-        if k:
-
-            @pl.when(z - k >= 0)
-            def _():
-                got_up(k)
-
-        @pl.when((z - k >= 0) & (z + 1 < nz))
-        def _():
-            block_up(k).start()
-
-        if k:
-
-            @pl.when(z + k < nz)
-            def _():
-                got_down(k)
-
-        @pl.when((z + k < nz) & (z > 0))
-        def _():
-            block_down(k).start()
-
+    stage, chain_done = z_chain(a_out, up_sems, down_sems)
     for copy in to_plane:
         copy.wait_recv()
     for copy in local:
@@ -934,7 +1149,6 @@
 
     for k in range(2, nz):
         stage(k)
-    copies_g, onward_g = share_rows(gfull_ref, half, own_g, far_g, near_g)
 
     @pl.when(z > 0)
     def _():
@@ -944,35 +1158,24 @@
     def _():
         halo(chip(z + 1, p, c)).wait_send()
 
-    for k in range(nz):
-
-        @pl.when((z - k >= 0) & (z + 1 < nz))
-        def _():
-            block_up(k).wait_send()
-
-        @pl.when((z + k < nz) & (z > 0))
-        def _():
-            block_down(k).wait_send()
-
-    finish_share(copies_g, onward_g)
+    chain_done()
     for copy in moved:
         copy.wait()
     for copy in gz + gp + to_plane:
         copy.wait_send()
 
 
-def open_step(hid, grad, gains, piece, rest, tok, nz):
+def open_step(hid, gains, piece, rest, tok, nz):
     width, n, n_p = hid.shape[1], len(rest), piece.shape[0]
     anywhere = pl.BlockSpec(memory_space=pl.ANY)
     dma = pltpu.SemaphoreType.DMA
     return pl.pallas_call(
         functools.partial(open_kernel, n),
-        in_specs=[VM, VM, VM] + [anywhere] * (n + 1),
-        out_specs=[VM, VM, VM] + [anywhere] * (n + 1),
+        in_specs=[VM, VM] + [anywhere] * (n + 1),
+        out_specs=[VM, VM] + [anywhere] * (n + 1),
         out_shape=[
             jax.ShapeDtypeStruct((n_p, nz) + gains.shape, f32),
             jax.ShapeDtypeStruct((tok + HALO, width), bf16),
-            jax.ShapeDtypeStruct((tok, width), bf16),
             jax.ShapeDtypeStruct((nz,) + piece.shape, bf16),
         ]
         + [jax.ShapeDtypeStruct(r.shape, bf16) for r in rest],
@@ -981,19 +1184,41 @@
             dma((2, nz)),
         ]
         + SHARE_SEMS
-        + SHARE_SEMS
         + [dma((2, n, 3)), dma((n + 1,)), dma((2,))],
         compiler_params=pltpu.CompilerParams(
             collective_id=4, has_side_effects=True, vmem_limit_bytes=VMEM_LIMIT
         ),
         cost_estimate=pl.CostEstimate(flops=0, bytes_accessed=250_000_000, transcendentals=0),
         name="open_step",
-    )(hid, grad, gains, piece, *rest)
-
-
-def gather_bc_kernel(x_ref, full_ref, far_sems, near_sems):
-    greet()
+    )(hid, gains, piece, *rest)
+
+
+def gather_bc_kernel(
+    x_ref, kv_ref, grad_ref, full_ref, kvz_ref, g_ref,
+    far_sems, near_sems, z_sems, own_g, far_g, near_g,
+):
     z, p, c = place()
+    nz = kvz_ref.shape[0]
+    other = chip(z, p, 1 - c)
+    meet(
+        [other]
+        + [chip(z, hop(p, d), c) for d in HOPS]
+        + [chip(lax.rem(z + d, nz), p, c) for d in range(1, nz)]
+    )
+    kvz_ref[z] = kv_ref[...]
+
+    def up(d):
+        return pltpu.make_async_remote_copy(
+            src_ref=kv_ref, dst_ref=kvz_ref.at[z], send_sem=z_sems.at[0, d - 1],
+            recv_sem=z_sems.at[1, d - 1], device_id=chip(z + d, p, c), device_id_type=MESH,
+        )
+
+    for d in range(1, nz):
+
+        @pl.when(z + d < nz)
+        def _():
+            up(d).start()
+
     half = x_ref.shape[0] // 2
     full_ref[p] = x_ref[...]
     rows = at_rows(c * half, half)
@@ -1006,37 +1231,168 @@
     for i, d in ((1, 1), (2, 2), (0, 3)):
         copies[i].wait_recv()
         came = full_ref.at[hop(p, d), rows, :]
-        onward.append(
-            send(came, came, near_sems.at[0, i], near_sems.at[1, i], chip(z, p, 1 - c))
-        )
+        onward.append(send(came, came, near_sems.at[0, i], near_sems.at[1, i], other))
+    g_half = grad_ref.shape[0]
+    g_ref[at_rows((p * 2 + c) * g_half, g_half), :] = grad_ref[...].astype(bf16)
+    g_copies, g_onward = share_rows(g_ref, g_half, own_g, far_g, near_g)
+    for d in range(1, nz):
+
+        @pl.when(z - d >= 0)
+        def _():
+            pltpu.make_async_remote_copy(
+                src_ref=kv_ref, dst_ref=kvz_ref.at[z - d], send_sem=z_sems.at[0, d - 1],
+                recv_sem=z_sems.at[1, d - 1], device_id=chip(z - d, p, c), device_id_type=MESH,
+            ).wait_recv()
+
+        @pl.when(z + d < nz)
+        def _():
+            kvz_ref[z + d] = jnp.zeros(kv_ref.shape, kv_ref.dtype)
+            up(d).wait_send()
+
     for copy in copies:
         copy.wait_send()
     for copy in onward:
         copy.wait()
-
-
-def gather_bc(x, at, n_p):
+    finish_share(g_copies, g_onward)
+
+
+def gather_bc(x, at, n_p, kv, nz, grad):
     tok = x.shape[0]
+    dma = pltpu.SemaphoreType.DMA
+    whole = lambda s: pl.BlockSpec(s, lambda i: (0,) * len(s))
     return pl.pallas_call(
         gather_bc_kernel,
         grid=(1,),
-        in_specs=[pl.BlockSpec((tok, 128), lambda i: (0, at))],
-        out_specs=pl.BlockSpec((n_p, tok, 128), lambda i: (0, 0, 0)),
-        out_shape=jax.ShapeDtypeStruct((n_p, tok, 128), bf16),
-        scratch_shapes=[pltpu.SemaphoreType.DMA((2, 3)), pltpu.SemaphoreType.DMA((2, 3))],
+        in_specs=[
+            pl.BlockSpec((tok, 128), lambda i: (0, at)), whole(kv.shape), whole(grad.shape)
+        ],
+        out_specs=[
+            whole((n_p, tok, 128)), whole((nz,) + kv.shape), whole((tok, grad.shape[1]))
+        ],
+        out_shape=[
+            jax.ShapeDtypeStruct((n_p, tok, 128), bf16),
+            jax.ShapeDtypeStruct((nz,) + kv.shape, bf16),
+            jax.ShapeDtypeStruct((tok, grad.shape[1]), bf16),
+        ],
+        scratch_shapes=[dma((2, 3)), dma((2, 3)), dma((2, nz - 1))] + SHARE_SEMS,
         compiler_params=pltpu.CompilerParams(
             collective_id=5, has_side_effects=True, vmem_limit_bytes=VMEM_LIMIT
         ),
-        cost_estimate=pl.CostEstimate(flops=0, bytes_accessed=30_000_000, transcendentals=0),
+        cost_estimate=pl.CostEstimate(flops=0, bytes_accessed=40_000_000, transcendentals=0),
         name="gather_bc",
-    )(x)
-
-
-def reduce_bc_kernel(x_ref, out_ref, sib_out, sib_in, out, came, n_sems, f_sems, own_sems):
-    greet()
+    )(x, kv, grad)
+
+
+def carry_kernel(state_ref, rate_ref, kvz_ref, in_ref, kv_ref, low, came, rates, factor, s_sems, r_sems, p_sems):
     z, p, c = place()
+    nz = kvz_ref.shape[0]
+    meet(
+        [chip(z, hop(p, d), c) for d in HOPS]
+        + [chip(lax.rem(z + d, nz), p, c) for d in range(1, nz)]
+    )
+    low[...] = state_ref[...].astype(bf16)
+
+    def up(d):
+        to = chip(z + d, p, c)
+        return (
+            pltpu.make_async_remote_copy(
+                src_ref=low, dst_ref=came.at[d - 1], send_sem=s_sems.at[0, d - 1],
+                recv_sem=s_sems.at[1, d - 1], device_id=to, device_id_type=MESH,
+            ),
+            pltpu.make_async_remote_copy(
+                src_ref=rate_ref, dst_ref=rates.at[d - 1], send_sem=r_sems.at[0, d - 1],
+                recv_sem=r_sems.at[1, d - 1], device_id=to, device_id_type=MESH,
+            ),
+        )
+
+    for d in range(1, nz):
+
+        @pl.when(z + d < nz)
+        def _():
+            for copy in up(d):
+                copy.start()
+
+    kv_ref[p] = kvz_ref[...]
+    mine = kv_ref.at[p]
+    copies = [
+        send(mine, mine, p_sems.at[0, i], p_sems.at[1, i], chip(z, hop(p, d), c))
+        for i, d in enumerate(HOPS)
+    ]
+    in_ref[...] = jnp.zeros_like(in_ref)
+    factor[...] = jnp.ones_like(factor)
+    lane_head, row_head = head_maps(state_ref.shape[0])
+    for d in range(1, nz):
+
+        @pl.when(z - d >= 0)
+        def _():
+            fro = chip(z - d, p, c)
+            pltpu.make_async_remote_copy(
+                src_ref=low, dst_ref=came.at[d - 1], send_sem=s_sems.at[0, d - 1],
+                recv_sem=s_sems.at[1, d - 1], device_id=fro, device_id_type=MESH,
+            ).wait_recv()
+            pltpu.make_async_remote_copy(
+                src_ref=rate_ref, dst_ref=rates.at[d - 1], send_sem=r_sems.at[0, d - 1],
+                recv_sem=r_sems.at[1, d - 1], device_id=fro, device_id_type=MESH,
+            ).wait_recv()
+            scale = jnp.sum(row_head * factor[0:1, :], axis=1, keepdims=True)
+            in_ref[...] += scale * came[d - 1].astype(f32)
+            factor[...] = factor[...] * rates[d - 1]
+
+        @pl.when(z + d < nz)
+        def _():
+            for copy in up(d):
+                copy.wait_send()
+
+    for copy in copies:
+        copy.wait()
+
+
+def carry_step(state, rate, kvz, n_p):
+    nz = kvz.shape[0]
+    dma = pltpu.SemaphoreType.DMA
+    return plane_call(
+        carry_kernel, "carry_step", 8, (state, rate, kvz),
+        [(state.shape, f32), ((n_p,) + kvz.shape, bf16)],
+        [
+            pltpu.VMEM(state.shape, bf16),
+            pltpu.VMEM((nz - 1,) + state.shape, bf16),
+            pltpu.VMEM((nz - 1,) + rate.shape, f32),
+            pltpu.VMEM(rate.shape, f32),
+            dma((2, nz - 1)), dma((2, nz - 1)), dma((2, 3)),
+        ],
+        nbytes=80_000_000,
+    )
+
+
+def reduce_bc_kernel(n, x_ref, dkv_ref, dx_ref, slope_ref, *refs):
+    ins, (out_ref, own_ref, next_ref), outs = refs[:n], refs[n : n + 3], refs[n + 3 : 2 * n + 3]
+    (
+        sib_out, sib_in, out, came, z_came, first, n_sems, f_sems, own_sems, z_sems, h_sems,
+        w_sems, loc_sems,
+    ) = refs[2 * n + 3 :]
+    z, p, c = place()
+    nz = dkv_ref.shape[0]
     half = x_ref.shape[1] // 2
+    xw = dx_ref.shape[1]
     other = chip(z, p, 1 - c)
+    meet(
+        [other]
+        + [chip(z, hop(p, d), c) for d in HOPS]
+        + [chip(lax.rem(z + d, nz), p, c) for d in range(1, nz)]
+    )
+
+    def down(d):
+        return pltpu.make_async_remote_copy(
+            src_ref=dkv_ref.at[z - d], dst_ref=z_came.at[d - 1], send_sem=z_sems.at[0, d - 1],
+            recv_sem=z_sems.at[1, d - 1], device_id=chip(z - d, p, c), device_id_type=MESH,
+        )
+
+    for d in range(1, nz):
+
+        @pl.when(z - d >= 0)
+        def _():
+            down(d).start()
+
     near, far = [], []
     order = HOPS + (0,)
     for i, d in enumerate(order):
@@ -1052,6 +1408,7 @@
         far.append(
             send(out.at[i], came.at[i], f_sems.at[0, i], f_sems.at[1, i], chip(z, q, c))
         )
+    moved = swap_begin(ins, outs, w_sems, loc_sems)
     near[3].wait_recv()
     total = x_ref[p, at_rows(c * half, half), :] + sib_in[3].astype(f32)
     for i in (1, 2, 0):
@@ -1060,35 +1417,83 @@
     mine = out_ref.at[at_rows(c * half, half), :]
     out_ref[at_rows(c * half, half), :] = total
     copy = send(mine, mine, own_sems.at[0], own_sems.at[1], other)
+    copy.wait()
+    first[:, :xw] = dx_ref[...] * slope_ref[:, :xw]
+    first[:, xw:] = out_ref[0:8, :] * slope_ref[:, xw:]
+
+    def edge(to):
+        return pltpu.make_async_remote_copy(
+            src_ref=first, dst_ref=next_ref, send_sem=h_sems.at[0], recv_sem=h_sems.at[1],
+            device_id=to, device_id_type=MESH,
+        )
+
+    @pl.when(z > 0)
+    def _():
+        edge(chip(z - 1, p, c)).start()
+
+    own_ref[...] = dkv_ref[z].astype(f32)
+    for d in range(1, nz):
+
+        @pl.when(z + d < nz)
+        def _():
+            pltpu.make_async_remote_copy(
+                src_ref=dkv_ref.at[z], dst_ref=z_came.at[d - 1], send_sem=z_sems.at[0, d - 1],
+                recv_sem=z_sems.at[1, d - 1], device_id=chip(z + d, p, c), device_id_type=MESH,
+            ).wait_recv()
+            own_ref[...] += z_came[d - 1].astype(f32)
+
+        @pl.when(z - d >= 0)
+        def _():
+            down(d).wait_send()
+
+    @pl.when(z + 1 == nz)
+    def _():
+        next_ref[...] = jnp.zeros_like(next_ref)
+
+    @pl.when(z + 1 < nz)
+    def _():
+        edge(chip(z + 1, p, c)).wait_recv()
+
+    @pl.when(z > 0)
+    def _():
+        edge(chip(z - 1, p, c)).wait_send()
+
     for done in near + far:
         done.wait_send()
-    copy.wait()
-
-
-def reduce_bc(x):
+    for copy in moved:
+        copy.wait()
+
+
+def reduce_bc(x, dkv, dx, slope, moved):
     n_p, tok, _ = x.shape
-    half = tok // 2
+    half, nz = tok // 2, dkv.shape[0]
+    dma = pltpu.SemaphoreType.DMA
     return plane_call(
-        reduce_bc_kernel, "reduce_bc", 7, (x,), [((tok, 128), f32)],
+        reduce_bc_kernel, "reduce_bc", 7, (x, dkv, dx, slope),
+        [((tok, 128), f32), (dkv.shape[1:], f32), (slope.shape, f32)],
         [
             pltpu.VMEM((4, half, 128), bf16),
             pltpu.VMEM((4, half, 128), bf16),
             pltpu.VMEM((3, half, 128), bf16),
             pltpu.VMEM((3, half, 128), bf16),
-            pltpu.SemaphoreType.DMA((2, 4)),
-            pltpu.SemaphoreType.DMA((2, 3)),
-            pltpu.SemaphoreType.DMA((2,)),
+            pltpu.VMEM((nz - 1,) + dkv.shape[1:], bf16),
+            pltpu.VMEM(slope.shape, f32),
+            dma((2, 4)), dma((2, 3)), dma((2,)), dma((2, nz - 1)), dma((2,)),
         ],
-        nbytes=40_000_000,
-    )[0]
-
-
-def sums_kernel(v_ref, out_ref, came, z_sems, p_sems, c_sems):
+        nbytes=100_000_000,
+        moved=moved,
+    )
+
+
+def sums_kernel(n, v_ref, *refs):
+    ins, out_ref, outs = refs[:n], refs[n], refs[n + 1 : 2 * n + 1]
+    came, z_sems, p_sems, c_sems, w_sems, loc_sems = refs[2 * n + 1 :]
     z, p, c = place()
     nz = came.shape[0]
     ups = [chip(lax.rem(z + d, nz), p, c) for d in range(1, nz)]
     other = chip(z, p, 1 - c)
     meet(ups + [chip(z, hop(p, d), c) for d in HOPS] + [other])
+    moved = swap_begin(ins, outs, w_sems, loc_sems)
     copies = []
     for d in range(1, nz):
         copies.append(
@@ -1110,9 +1515,11 @@
     for copy in copies + far:
         copy.wait_send()
     near.wait()
-
-
-def sums_step(v, nz, n_p):
+    for copy in moved:
+        copy.wait()
+
+
+def sums_step(v, nz, n_p, moved):
     return plane_call(
         sums_kernel, "sums_step", 6, (v,),
         [((2, n_p) + v.shape, f32)],
@@ -1122,65 +1529,14 @@
             pltpu.SemaphoreType.DMA((2, 3)),
             pltpu.SemaphoreType.DMA((2,)),
         ],
-    )[0]
+        moved=moved,
+    )
 
 
 def rope_tables(positions, pairs):
     freqs = rope_base ** (-2.0 * pairs.astype(f32) / HDIM)
     angles = positions.astype(f32)[:, None] * freqs[None, :]
     return jnp.cos(angles), jnp.sin(angles)
-
-
-def plane_swap(x):
-    n_p = lax.axis_size("p")
-    p = lax.axis_index("p")
-    out = x
-    for d in range(1, n_p):
-        other = jnp.bitwise_xor(p, d)
-        block = lax.dynamic_index_in_dim(x, other, 0, keepdims=True)
-        came = lax.ppermute(block, "p", [(i, i ^ d) for i in range(n_p)])
-        out = lax.dynamic_update_slice_in_dim(out, came, other, 0)
-    return out
-
-
-def plane_gather(x):
-    n_p = lax.axis_size("p")
-    p = lax.axis_index("p")
-    out = jnp.zeros((n_p,) + x.shape, x.dtype)
-    out = lax.dynamic_update_slice_in_dim(out, x[None], p, 0)
-    for d in range(1, n_p):
-        came = lax.ppermute(x, "p", [(i, i ^ d) for i in range(n_p)])
-        out = lax.dynamic_update_slice_in_dim(out, came[None], jnp.bitwise_xor(p, d), 0)
-    return out
-
-
-def plane_sum(x):
-    n_p = lax.axis_size("p")
-    p = lax.axis_index("p")
-    total = lax.dynamic_index_in_dim(x, p, 0, keepdims=False).astype(f32)
-    for d in range(1, n_p):
-        block = lax.dynamic_index_in_dim(x, jnp.bitwise_xor(p, d), 0, keepdims=False)
-        came = lax.ppermute(block.astype(bf16), "p", [(i, i ^ d) for i in range(n_p)])
-        total = total + came.astype(f32)
-    return total
-
-
-def swap_core(x):
-    return lax.ppermute(x, "head", [(0, 1), (1, 0)])
-
-
-def block_sum(part):
-    ci = lax.axis_index("head")
-    mine = lax.dynamic_index_in_dim(part, ci, 1, keepdims=False)
-    other = lax.dynamic_index_in_dim(part, 1 - ci, 1, keepdims=False)
-    return plane_sum(mine + swap_core(other.astype(bf16)).astype(f32))
-
-
-def join_cores(mine):
-    ci = lax.axis_index("head")
-    other = swap_core(mine)
-    out = jnp.concatenate([mine, mine])
-    return lax.dynamic_update_slice_in_dim(out, other, (1 - ci) * mine.shape[0], 0)
 
 
 def carry_states(state, decays, sign):
@@ -1229,7 +1585,7 @@
     base = zi * tok
     positions = base + jnp.arange(tok, dtype=jnp.int32)
     edge = conv_x.shape[0] - 1
-    ext_docs = doc_ids(base - edge + jnp.arange(tok + edge, dtype=jnp.int32), doc_starts)
+    ext_docs = doc_ids(base - edge + jnp.arange(tok + 2 * edge, dtype=jnp.int32), doc_starts)
     rows = mamba_z.shape[0]
     n_heads = a_log.shape[0] // n_p
     xw = n_heads * MHDIM
@@ -1239,29 +1595,11 @@
     hk = kw // 2
     tail_w = 128 - 2 * kw - n_heads
 
-    def cols(w):
-        w = w.astype(bf16)
-        return w.reshape(w.shape[0], n_p, -1).transpose(1, 0, 2)
-
-    k_cols = attn_key.astype(bf16).reshape(rows, 2, n_p, hk)
-    k_cols = k_cols.transpose(2, 0, 1, 3).reshape(n_p, rows, kw)
-    bc_cols = mamba_bc.astype(bf16).reshape(rows, 2, n_p, bw)
-    bc_cols = bc_cols.transpose(2, 0, 1, 3).reshape(n_p, rows, 2 * bw)
-    q_cols = attn_query.astype(bf16).reshape(rows, n_p, 2, n_p, hk)
-    q_cols = q_cols.transpose(1, 0, 3, 2, 4).reshape(n_p, rows, HDIM)
-    piece_a = jnp.concatenate(
-        [
-            cols(mamba_x), bc_cols, k_cols, cols(attn_value), cols(mamba_dt),
-            jnp.zeros((n_p, rows, tail_w), bf16),
-        ],
-        axis=2,
-    )
-    rest = [
-        jnp.concatenate([q_cols, cols(mamba_z)], axis=2),
-        jnp.concatenate([cols(mamba_out.T), cols(attn_out.T)], axis=2),
-        jnp.concatenate([cols(ffn_gate), cols(ffn_up)], axis=2),
-        cols(ffn_down.T),
-    ]
+    weights = (
+        mamba_x, mamba_bc, attn_key, attn_value, mamba_dt, attn_query, mamba_z, mamba_out, attn_out,
+        ffn_gate, ffn_up, ffn_down,
+    )
+    piece_a, *rest = pack(n_p, *weights)
 
     def along_z(piece):
         piece = piece.reshape(n_p * rows, piece.shape[2])
@@ -1272,13 +1610,11 @@
     )
     my_half = lambda v: lax.dynamic_slice_in_dim(v, ci * half, half, 0)
     hidden_own, grad_own = my_half(hidden_in), my_half(grad_out)
-    gains, normed_one, g_ffn, w_a, *rest = open_step(
-        hidden_own, grad_own, gains_own, piece_a, rest, tok, nz
-    )
+    gains, normed_one, w_a, *rest = open_step(hidden_own, gains_own, piece_a, rest, tok, nz)
     w_a = w_a.reshape(nz * n_p * rows, w_a.shape[3])
     gains = gains.transpose(2, 1, 0, 3)[:, :, :, :rows].reshape(8, 1, width)
     gain_mix, gain_ffn = gains[0], gains[1]
-    w_b, w_c, w_d, w_e = [along_z(piece) for piece in rest]
+    w_b, w_c, w_d = [along_z(piece) for piece in rest[:3]]
 
     in_ext = product(normed_one, w_a)
     in_b = product(normed_one, w_b)[:tok]
@@ -1304,7 +1640,6 @@
     dt_pre = jnp.pad(in_a[:, dt_at : dt_at + n_heads], ((0, 0), (0, 128 - n_heads))) + lanes(my_bias)
     neg_rate = lanes(-jnp.exp(my_a))
     skip_full = jnp.repeat(my_skip, MHDIM)[None, :]
-    bc_all = gather_bc(ssm, xw // 128, n_p)
     pair_ids = pi * hk + jnp.arange(hk)
     cos_k, sin_k = rope_tables(positions, pair_ids)
     k0, k1 = in_a[:, cw : cw + hk], in_a[:, cw + hk : cw + kw]
@@ -1312,12 +1647,7 @@
     val_own = in_a[:, cw + kw : cw + 2 * kw]
     kv_own = jnp.concatenate([key_own, val_own], axis=1).astype(bf16)
     kv_own = jnp.concatenate([kv_own[: tok // 2], kv_own[tok // 2 :]], axis=1)
-    kv = jnp.zeros((nz, tok // 2, 4 * kw), bf16)
-    kv = lax.dynamic_update_slice_in_dim(kv, kv_own[None], zi, 0)
-    for d in range(1, nz):
-        came = passed_along(kv_own, "z", d)
-        kv = lax.dynamic_update_slice_in_dim(kv, came[None], (zi - d) % nz, 0)
-    kv = plane_gather(kv)
+    bc_all, kvz, g_ffn = gather_bc(ssm, xw // 128, n_p, kv_own, nz, grad_own)
     cos_q, sin_q = rope_tables(positions, jnp.arange(HDIM // 2))
     cos_q, sin_q = cos_q.reshape(tok, n_p, hk), sin_q.reshape(tok, n_p, hk)
 
@@ -1335,7 +1665,8 @@
         base_arr, doc_starts, ssm, bc_all, dt_pre, neg_rate, skip_full
     )
     total_decay = decay_full[-1][:, None]
-    in_state = carry_states(local_state, total_decay, 1)
+    rate = jnp.broadcast_to(dev_decay[tok - 1 :], (8, 128))
+    in_state, kv = carry_step(local_state, rate, kvz, n_p)
 
     attn_f32, lse, keys, values = attend(base_arr, doc_starts, queries, kv)
     attn_low = attn_f32.astype(bf16)
@@ -1344,7 +1675,8 @@
     gated = (y_flat * silu_z).astype(bf16)
     mixed = jnp.concatenate([gated, attn_low], axis=1)
 
-    mid_own, normed_two = mid_step(mixed, w_c, hidden_own, gain_ffn)
+    mid_own, normed_two, w_e = mid_step(mixed, w_c, hidden_own, gain_ffn, rest[3], nz)
+    w_e = w_e.reshape(width, -1)
     gu = product(normed_two, w_d)
     ffw = gu.shape[1] // 2
     gate_val, up_val = gu[:, :ffw], gu[:, ffw:]
@@ -1361,16 +1693,13 @@
     def scattered(grad):
         return lax.psum_scatter(grad, "z", scatter_dimension=0, tiled=True)
 
-    def swapped(grad):
-        return plane_swap(grad.reshape(n_p, rows, grad.shape[1])).astype(f32)
+    def by_owner(grad):
+        return grad.reshape(n_p, rows, grad.shape[1])
 
     ge = scattered(grad_e)
     gd = scattered(grad_d)
     d_mid_own, grad_gain_ffn, g_mid = two_step(d_gu, w_d, mid_own, grad_own, gain_ffn)
     g_mid, ge = lax.optimization_barrier((g_mid, ge))
-    ge = swapped(ge)
-    out_part = product_nt(activated, w_e).reshape(n_p, 2, half, width)
-    block_out = join_cores(mid_own + block_sum(out_part))
 
     d_mixed = product(g_mid, w_c)
     grad_c = product_t(g_mid, mixed).astype(bf16)
@@ -1380,52 +1709,55 @@
     d_y_flat = d_gated * silu_z
     d_z = (d_gated * y_flat * silu_slope(gate_z)).astype(bf16)
     d_in_local = product_t((d_y_flat * decay_full).astype(bf16), c_mat)
+    d_in_local, d_attn = lax.optimization_barrier((d_in_local, d_attn))
     state_grad = carry_states(d_in_local, total_decay, -1)
     d_query, d_kv = attend_back(
         base_arr, doc_starts, queries, d_attn, attn_f32, lse, keys, values, kv.shape
     )
     d_q_pre = rope_q(d_query, -1.0).astype(bf16)
     d_b = jnp.concatenate([d_q_pre, d_z], axis=1)
+    d_b, state_grad = lax.optimization_barrier((d_b, state_grad))
     more = lambda v: jnp.pad(v, ((0, HALO), (0, 0)))
     grad_b = product_t(normed_one, more(d_b)).astype(bf16)
     gb = scattered(grad_b)
-    d_kv = plane_sum(d_kv)
-    d_kv_own = lax.dynamic_index_in_dim(d_kv, zi, 0, keepdims=False)
-    for d in range(1, nz):
-        block = lax.dynamic_index_in_dim(d_kv, (zi - d) % nz, 0, keepdims=False)
-        d_kv_own = d_kv_own + passed_along(block.astype(bf16), "z", -d).astype(f32)
+    d_kv_parts = [lax.dynamic_index_in_dim(d_kv, pi, 0, keepdims=False)]
+    for d in range(1, n_p):
+        part = lax.dynamic_index_in_dim(d_kv, jnp.bitwise_xor(pi, d), 0, keepdims=False)
+        d_kv_parts.append(lax.ppermute(part, "p", [(i, i ^ d) for i in range(n_p)]))
+
+    start_decay = jnp.concatenate([jnp.ones((1, 128), f32), dev_decay[SPAN - 1 :: SPAN][:-1]])
+    d_y_flat, gd = lax.optimization_barrier((d_y_flat, gd))
+    d_xs, d_bc, d_dt, sums, skip_sums = ssd_backward(
+        base_arr, doc_starts, ssm, bc_all, dt_pre, d_y_flat, span_starts,
+        start_decay[:, None, :], neg_rate, skip_full, in_state, state_grad,
+    )
+    d_bc, d_kv_parts = lax.optimization_barrier((d_bc, d_kv_parts))
+    d_kv = sum(part.astype(f32) for part in d_kv_parts).astype(bf16)
+    slope = silu_slope(conv_in)
+    d_bc, d_kv_own, du_next, ge, gd = reduce_bc(
+        d_bc, d_kv, d_xs[:8], slope[:8], (by_owner(ge), by_owner(gd))
+    )
     d_kv_own = jnp.concatenate([d_kv_own[:, : 2 * kw], d_kv_own[:, 2 * kw :]], axis=0)
     dk0, dk1 = d_kv_own[:, :hk], d_kv_own[:, hk:kw]
     d_kv_low = jnp.concatenate(
         [dk0 * cos_k + dk1 * sin_k, dk1 * cos_k - dk0 * sin_k, d_kv_own[:, kw:]], axis=1
     ).astype(bf16)
-
-    start_decay = jnp.concatenate([jnp.ones((1, 128), f32), dev_decay[SPAN - 1 :: SPAN][:-1]])
-    d_y_flat, gd = lax.optimization_barrier((d_y_flat, gd))
-    gd = swapped(gd)
-    d_xs, d_bc, d_dt, sums, skip_sums = ssd_backward(
-        base_arr, doc_starts, ssm, bc_all, dt_pre, d_y_flat, span_starts,
-        start_decay[:, None, :], neg_rate, skip_full, in_state, state_grad,
-    )
-    d_bc, gc = lax.optimization_barrier((d_bc, gc))
-    gc = swapped(gc)
-    d_bc = reduce_bc(d_bc)
-    du = jnp.concatenate([d_xs, d_bc], axis=1) * silu_slope(conv_in)
-    d_ext, grad_taps = convolve_back(du, ext, taps, ext_docs, tok)
-    next_rows = passed_along(d_ext[:edge], "z", -1)
-    d_pre = (d_ext[edge:] + jnp.pad(next_rows, ((tok - edge, 0), (0, 0)))).astype(bf16)
+    du = jnp.concatenate([d_xs, d_bc], axis=1) * slope
+    du = jnp.concatenate([du, du_next[:edge]], axis=0)
+    d_pre, grad_taps = convolve_back(du, ext, taps, ext_docs, tok)
+    d_pre = d_pre.astype(bf16)
     d_last = jnp.concatenate(
         [d_kv_low, d_dt[:, :n_heads].astype(bf16), jnp.zeros((tok, tail_w), bf16)], axis=1
     )
     d_a = jnp.concatenate([d_pre, d_last], axis=1)
     grad_a = product_t(normed_one, more(d_a)).astype(bf16)
-    ga = swapped(scattered(grad_a))
+    ga = scattered(grad_a)
     once = jnp.where(ci == 0, d_pre[:, xw:], jnp.zeros((), bf16))
     d_a_once = jnp.concatenate([d_pre[:, :xw], once, d_last], axis=1)
-    d_a_once, grad_a, gb = lax.optimization_barrier((d_a_once, grad_a, gb))
-    gb = swapped(gb)
-    grad_in, grad_gain_mix = one_step(
-        d_a_once, w_a, d_b, w_b, hidden_own, d_mid_own, gain_mix
+    d_a_once, grad_a, gc = lax.optimization_barrier((d_a_once, grad_a, gc))
+    grad_in, block_out, grad_gain_mix, gc = one_step(
+        d_a_once, w_a, d_b, w_b, hidden_own, d_mid_own, gain_mix, activated, w_e, mid_own,
+        (by_owner(gc),),
     )
 
     flat = jnp.concatenate(
@@ -1438,7 +1770,7 @@
         ]
     )
     flat = jnp.pad(flat, ((0, -flat.shape[0] % 8), (0, 0)))
-    summed = sums_step(flat, nz, n_p)
+    summed, ga, gb = sums_step(flat, nz, n_p, (by_owner(ga), by_owner(gb)))
     g_rows = width // 128
     t_rows = grad_taps.size // 128
     si = zi * n_p + pi
@@ -1453,23 +1785,9 @@
     s_bc = s_bc[:, :, xw:].reshape(n_p, edge + 1, 2, bw).transpose(1, 2, 0, 3)
     s_bc = s_bc.reshape(edge + 1, 2 * n_p * bw)
 
-    def uncols(g):
-        return g.transpose(1, 0, 2).reshape(rows, -1)
-
-    g_x = uncols(ga[:, :, :xw])
-    g_bc = ga[:, :, xw:cw].reshape(n_p, rows, 2, bw).transpose(1, 2, 0, 3).reshape(rows, -1)
-    g_k = ga[:, :, cw : cw + kw].reshape(n_p, rows, 2, hk)
-    g_k = g_k.transpose(1, 2, 0, 3).reshape(rows, HDIM)
-    g_v = uncols(ga[:, :, cw + kw : cw + 2 * kw])
-    g_dt = uncols(ga[:, :, dt_at : dt_at + n_heads])
-    g_q = gb[:, :, :HDIM].reshape(n_p, rows, n_p, 2, hk)
-    g_q = g_q.transpose(1, 0, 3, 2, 4).reshape(rows, n_p * HDIM)
-    g_z = uncols(gb[:, :, HDIM:])
-    g_mout = uncols(gc[:, :, :xw]).T
-    g_aout = uncols(gc[:, :, xw:]).T
-    g_gate = uncols(gd[:, :, :ffw])
-    g_up = uncols(gd[:, :, ffw:])
-    g_down = uncols(ge).T
+    g_x, g_bc, g_k, g_v, g_dt, g_q, g_z, g_mout, g_aout, g_gate, g_up, g_down = unpack(
+        (ga, gb, gc, gd, ge), weights
+    )
     return (
         block_out,
         grad_in,

time: 832 us -> 727 us (0.87)
  waiting for transfers between devices: 164 us -> 20 us
  Pallas kernels: 373 us -> 509 us
  starting transfers between devices: 57.1 us -> 10.2 us
  local copies, waits for them, and re-layouts: 86.4 us -> 53.2 us
    pallas_call x6 -> x9, Pallas kernels: 303 us -> 416 us  [the longest x5 227 us: plane_call(): pl.pallas_call(kernel, in_specs=[VM] * len(args) + [ANYWHERE] * n, out_sp...]
    ppermute x33 -> x3, waiting for transfers between devices: 68.2 us -> 0.01 us  [shards(): d_kv_parts.append(lax.ppermute(part, 'p', [(i, i ^ d) for i in range(n_p)]))]
    all_gather x4 -> x3, waiting for transfers between devices: 45.8 us -> 0.04 us  [along_z(): return lax.all_gather(piece, 'z', axis=0, tiled=True)]
    ppermute x33 -> x3, starting transfers between devices: 43.4 us -> 3.49 us  [shards(): d_kv_parts.append(lax.ppermute(part, 'p', [(i, i ^ d) for i in range(n_p)]))]
    ppermute x6 -> x3, waiting for transfers between devices: 45.4 us -> 12.6 us  [carry_states(): came = lax.ppermute(low, 'z', route).astype(f32)]
    pallas_call x1, Pallas kernels: 12.5 us -> 38 us  [gather_bc(): pl.pallas_call(gather_bc_kernel, grid=(1,), in_specs=[pl.BlockSpec((tok,...]
    unnamed x122 -> x74, local copies, waits for them, and re-layouts: 24.9 us -> 12.5 us
    reshape x18 -> x0, local copies, waits for them, and re-layouts: 9.12 us -> none  [the longest x3 2.73 us: uncols(): return g.transpose(1, 0, 2).reshape(rows, -1)]
  transfers between devices with their start and end apart: 52 -> 16, of which waited for: 20 -> 5; matrix products, arithmetic and copies ran while one was open for 18% -> 16% of each run, Pallas kernels for 32% -> 55%
where the time goes in v4:
time: 727 us; the launch traced here: 717 us
  Pallas kernels  509 us (70%)
  matrix products  67.9 us (9%)
  local copies, waits for them, and re-layouts  53.2 us (7%)
  other arithmetic  41.5 us (6%)
  waiting for transfers between devices  20 us (3%)
  between operations  15.3 us (2%)
  starting transfers between devices  10.2 us (1%)
    pallas_call x5, Pallas kernels, plane_call(): pl.pallas_call(kernel, in_specs=[VM] * len(args) + [ANYWHERE] * n, out_sp...  227 us
    pallas_call x1, Pallas kernels, mid_step(): pl.pallas_call(mid_kernel, in_specs=[VM] * 4 + [ANYWHERE], out_specs=[VM]...  97.8 us
    pallas_call x1, Pallas kernels, open_step(): pl.pallas_call(functools.partial(open_kernel, n), in_specs=[VM, VM] + [an...  81 us
    pallas_call x1, Pallas kernels, gather_bc(): pl.pallas_call(gather_bc_kernel, grid=(1,), in_specs=[pl.BlockSpec((tok,...  38 us
    dot_general x6, matrix products, product_t(): lax.dot_general(left, right, (((0,), (0,)), ((), ())), preferred_element_...  34 us
    dot_general x5, matrix products, product(): return jnp.dot(left, right, preferred_element_type=f32)  30.4 us
    pallas_call x1, Pallas kernels, ssd_backward(): pl.pallas_call(functools.partial(ssd_backward_kernel, n_heads), grid=(nsp...  22.4 us
  transfers between devices with their start and end apart: 16, of which 5 were waited for; matrix products, arithmetic and copies ran while one was open for 16% of the time, Pallas kernels for 55%

profile of v4, /device:TPU:0, one launch (start us, length us, event | category | flops | bytes accessed | tf_op | source)
XLA Modules:
  0.0 717.1 jit_solution(11822113235549816442)
XLA Ops:
  11.2 5.5 pack.1
  16.7 81.0 %open_step.1 = (f32[4,4,8,128]{3,2,1,0:T(8,128)}, bf16[1040,2048]{1,0:T(8,128)(2,1)}, bf16[4,4,128,640]{3,2,1,0:T(8,128)(2,1)}, bf16[4,128,512]{2,1,0:T(8,128)(2...) custom-call(f32[128,2048]{1,0:T(8,128)} %constant_dynamic-slice_fusion.5.refs_0_.resi, ...), custom_call_target="tpu_custom_call" | custom-call | bytes 250000000 | tf_op jit(solution)/shard_map/open_step/pallas_call | solution.py:1172
  99.3 8.0 %fusion.80 = (bf16[1040,640]{1,0:T(8,128)(2,1)S(1)}, f32[1040,640]{1,0:T(8,128)}) fusion(bf16[1040,2048]{1,0:T(8,128)(2,1)} %get-tuple-element.108, bf16[2048,640]{1,0:T(8,128)(2,1)} %bitcast.83), kind=kOutput, calls=%fused_computation.177 | convolution fusion | flops 2726963200 | bytes 10874880 | tf_op jit(solution)/shard_map/dot_general | solution.py:32
  110.3 2.0 slice.314
  113.4 3.8 fusion.43
  119.5 3.7 add_multiply_fusion
  124.7 38.0 %gather_bc.1 = (bf16[4,1024,128]{2,1,0:T(8,128)(2,1)}, bf16[4,512,128]{2,1,0:T(8,128)(2,1)}, bf16[1024,2048]{1,0:T(8,128)(2,1)}) custom-call(bf16[1024,512]{1,0:T(8,128)(2,1)} %multiply_convert_fusion.3.x_ref, bf16[512,128]{1,0:T(8,128)(2,1)} %pad_maximum_fusion.9.kv_ref, f32[128,2048]{1,0:T(8,128)} %constant_dynamic-slice_fusion.1.grad_ref.grad_own), custom_call_target="tpu_custom_call" | custom-call | bytes 40000000 | tf_op jit(solution)/shard_map/gather_bc/pallas_call | solution.py:1263
  164.1 13.7 %ssd_forward.1 = (f32[1024,384]{1,0:T(8,128)}, f32[8,384,256]{2,1,0:T(8,128)}, f32[384,256]{1,0:T(8,128)}, f32[1024,128]{1,0:T(8,128)}, f32[1024,384]{1,0:T(8,128)}, /*index=5*/bf16[1024,256]{1,0:T(8,128)(2,1)}) custom-call(s32[1]{0:T(128)} %bitcast.base_ref, s32[8]{0:T(128)} %starts_ref.7, bf16[1024,512]{1,0:T(8,128)(2,1)} %multiply_convert_fusion.3.x_ref, ...), custom_call_target="tpu_custom_call" | custom-call | flops 603979776 | bytes 40000000 | tf_op jit(solution)/shard_map/ssd_forward/pallas_call | solution.py:195
  179.1 32.4 %carry_step.1 = (f32[384,256]{1,0:T(8,128)}, bf16[4,4,512,128]{3,2,1,0:T(8,128)(2,1)}) custom-call(f32[384,256]{1,0:T(8,128)} %get-tuple-element.114.state_ref, f32[8,128]{1,0:T(8,128)} %broadcast_in_dim.119.rate_ref, bf16[4,512,128]{2,1,0:T(8,128)(2,1)} %get-tuple-element.116.kvz_ref), custom_call_target="tpu_custom_call" | custom-call | bytes 80000000 | tf_op jit(solution)/shard_map/carry_step/pallas_call | solution.py:986
  211.6 5.3 fusion.81
  219.1 2.0 copy.94
  221.2 2.6 fusion.60
  224.6 8.5 %attend.1 = (f32[1024,128]{1,0:T(8,128)}, f32[1024,128]{1,0:T(8,128)}, bf16[4096,128]{1,0:T(8,128)(2,1)}, bf16[4096,128]{1,0:T(8,128)(2,1)}) custom-call(s32[1]{0:T(128)} %bitcast.base_ref, s32[8]{0:T(128)} %starts_ref.7, bf16[1024,128]{1,0:T(8,128)(2,1)} %copy.95.q_ref, bf16[4,4,512,128]{3,2,1,0:T(8,128)(2,1)} %get-tuple-element.120.kv_ref), custom_call_target="tpu_custom_call" | custom-call | flops 2147483648 | bytes 30000000 | tf_op jit(solution)/shard_map/attend/pallas_call | solution.py:416
  234.2 3.4 multiply_convert_fusion.6
  239.6 97.8 %mid_step.1 = (f32[128,2048]{1,0:T(8,128)}, bf16[1024,2048]{1,0:T(8,128)(2,1)}, bf16[4,4,128,512]{3,2,1,0:T(8,128)(2,1)}) custom-call(bf16[1024,512]{1,0:T(8,128)(2,1)} %pad_maximum_fusion.3.left, bf16[2048,512]{1,0:T(8,128)(2,1)} %all-gather.6.cloned.1.call-done.right, f32[128,2048]{1,0:T(8,128)} %constant_dynamic-slice_fusion.5.refs_0_.resid.hidden_own, ...), custom_call_target="tpu_custom_call" | custom-call | bytes 150000000 | tf_op jit(solution)/shard_map/mid_step/pallas_call | solution.py:1005
  337.5 7.7 %fusion.82 = f32[1024,1024]{1,0:T(8,128)S(1)} fusion(bf16[1024,2048]{1,0:T(8,128)(2,1)} %get-tuple-element.126, bf16[2048,1024]{1,0:T(8,128)(2,1)} %all-gather.8.cloned.1.call-done.right), kind=kOutput, calls=%fused_computation.179 | convolution fusion | flops 4294967296 | bytes 12582912 | tf_op jit(solution)/shard_map/dot_general | solution.py:32
  345.1 4.2 multiply_convert_fusion.2
  350.7 6.5 convolution_convert_fusion
  357.2 3.2 pad_maximum_fusion.1.left
  360.4 5.9 convolution_convert_fusion.4
  367.0 65.9 %two_step.1 = (f32[128,2048]{1,0:T(8,128)}, f32[1,2048]{1,0:T(1,128)}, bf16[1024,2048]{1,0:T(8,128)(2,1)}) custom-call(bf16[1024,1024]{1,0:T(8,128)(2,1)} %pad_maximum_fusion.1.left, bf16[2048,1024]{1,0:T(8,128)(2,1)} %all-gather.8.cloned.1.call-done.right, f32[128,2048]{1,0:T(8,128)} %get-tuple-element.129.mid_own, ...), custom_call_target="tpu_custom_call" | custom-call | bytes 150000000 | tf_op jit(solution)/shard_map/two_step/pallas_call | solution.py:986
  432.9 6.1 convolution_convert_fusion.3
  442.4 5.2 collective-permute-done.3
  447.8 5.3 fusion.83
  453.9 1.7 multiply_convert_fusion.4
  461.7 9.8 %attend_back.1 = (f32[1024,128]{1,0:T(8,128)}, bf16[4,4,512,128]{3,2,1,0:T(8,128)(2,1)}) custom-call(s32[1]{0:T(128)} %bitcast.base_ref, s32[8]{0:T(128)} %starts_ref.7, bf16[1024,128]{1,0:T(8,128)(2,1)} %copy.95.q_ref, bf16[1024,128]{1,0:T(8,128)(2,1)} %slice.483.do_ref, f32[1024,128]{1,0:T(8,128)} %get-tuple-element.121.o_ref, ...), custom_call_target="tpu_custom_call" | custom-call | flops 5368709120 | bytes 40000000 | tf_op jit(solution)/shard_map/attend_back/pallas_call | solution.py:482
  471.5 2.1 copy.104
  473.6 2.1 fusion.64
  477.9 2.3 collective-permute-done.2
  480.3 10.2 %collective-permute-done.4 = bf16[384,256]{1,0:T(8,128)(2,1)} collective-permute-done((bf16[384,256]{1,0:T(8,128)(2,1)}, bf16[384,256]{1,0:T(8,128)(2,1)}, u32[]{:S(2)}, u32[]{:S(2)}) %collective-permute-start.4) | collective-permute-done | bytes 196640 | tf_op jit(solution)/shard_map/ppermute | solution.py:1548
  490.5 2.0 multiply_add_fusion.1.grad_ref
  492.6 6.3 convolution_convert_fusion.2
  499.0 2.9 dynamic-slice_bitcast_fusion
  501.9 2.3 collective-permute-start.7
  508.3 22.4 %ssd_backward.1 = (f32[1024,384]{1,0:T(8,128)}, f32[4,1024,128]{2,1,0:T(8,128)}, f32[1024,128]{1,0:T(8,128)}, f32[8,128]{1,0:T(8,128)}, f32[1,384]{1,0:T(1,128)}) custom-call(s32[1]{0:T(128)} %bitcast.base_ref, s32[8]{0:T(128)} %starts_ref.7, bf16[1024,512]{1,0:T(8,128)(2,1)} %multiply_convert_fusion.3.x_ref, ...), custom_call_target="tpu_custom_call" | custom-call | flops 1610612736 | bytes 80000000 | tf_op jit(solution)/shard_map/ssd_backward/pallas_call | solution.py:325
  532.1 1.8 slice.482
  533.9 2.4 add_convert_fusion.dkv_ref
  536.3 39.7 %reduce_bc.1 = (f32[1024,128]{1,0:T(8,128)}, f32[512,128]{1,0:T(8,128)}, f32[8,512]{1,0:T(8,128)}, bf16[4,128,512]{2,1,0:T(8,128)(2,1)}, bf16[4,128,1024]{2,1,0:T(8,128)(2,1)}) custom-call(f32[4,1024,128]{2,1,0:T(8,128)} %get-tuple-element.146.x_ref, bf16[4,512,128]{2,1,0:T(8,128)(2,1)} %add_convert_fusion.dkv_ref, f32[8,384]{1,0:T(8,128)} %slice.264.dx_ref, ...), custom_call_target="tpu_custom_call" | custom-call | bytes 100000000 | tf_op jit(solution)/shard_map/reduce_bc/pallas_call | solution.py:986
  578.2 3.7 fusion.49
  581.9 3.8 fusion.6
  585.8 2.7 fusion.18
  588.5 2.1 concatenate.63
  590.6 8.1 %convolution_convert_fusion.1 = bf16[2048,640]{1,0:T(8,128)(2,1)} fusion(bf16[1040,2048]{1,0:T(8,128)(2,1)} %get-tuple-element.108, bf16[1024,640]{1,0:T(8,128)(2,1)} %concatenate.63), kind=kOutput, calls=%fused_computation.1 | convolution fusion | flops 2727608320 | bytes 8192000 | tf_op jit(solution)/shard_map/dot_general | solution.py:36
  600.4 2.1 concatenate.62.left_a
  602.5 67.5 %one_step.1 = (f32[256,2048]{1,0:T(8,128)}, f32[256,2048]{1,0:T(8,128)}, f32[1,2048]{1,0:T(1,128)}, bf16[4,128,512]{2,1,0:T(8,128)(2,1)}) custom-call(bf16[1024,640]{1,0:T(8,128)(2,1)} %concatenate.62.left_a, bf16[2048,640]{1,0:T(8,128)(2,1)} %bitcast.84, bf16[1024,512]{1,0:T(8,128)(2,1)} %copy-done.5, ...), custom_call_target="tpu_custom_call" | custom-call | bytes 150000000 | tf_op jit(solution)/shard_map/one_step/pallas_call | solution.py:986
  671.4 21.1 %sums_step.1 = (f32[2,4,56,128]{3,2,1,0:T(8,128)}, bf16[4,128,640]{2,1,0:T(8,128)(2,1)}, bf16[4,128,512]{2,1,0:T(8,128)(2,1)}) custom-call(f32[56,128]{1,0:T(8,128)} %pad.40.v_ref, bf16[4,128,640]{2,1,0:T(8,128)(2,1)} %bitcast.93, bf16[4,128,512]{2,1,0:T(8,128)(2,1)} %bitcast.96), custom_call_target="tpu_custom_call" | custom-call | bytes 150000000 | tf_op jit(solution)/shard_map/sums_step/pallas_call | solution.py:986
  698.4 5.3 unpack.1
  705.2 3.3 copy.118
  (194 shorter events, 56.1 us)
Async XLA Ops:
  7.2 2.9 copy-start
  7.2 204.4 %all-gather.4.cloned.1.call-start = ((), (), s32[]{:S(2)}) async-start(), calls=%async_computation.5 | async-start | bytes 2621440 | tf_op jit(solution)/shard_map/all_gather | solution.py:1606
  97.7 141.8 %all-gather.6.cloned.1.call-start = ((), (), s32[]{:S(2)}) async-start(), calls=%async_computation.6 | async-start | bytes 2621440 | tf_op jit(solution)/shard_map/all_gather | solution.py:1606
  98.5 238.9 %all-gather.8.cloned.1.call-start = ((), (), s32[]{:S(2)}) async-start(), calls=%async_computation.7 | async-start | bytes 5242880 | tf_op jit(solution)/shard_map/all_gather | solution.py:1606
  99.2 333.7 %reduce-scatter.6.cloned.1.call-start = ((), (), s32[]{:S(2)}) async-start(), calls=%async_computation.8 | async-start | bytes 2621440 | tf_op jit(solution)/shard_map/reduce_scatter | solution.py:1694
  107.3 9.9 %copy-start.3 = (bf16[1040,640]{1,0:T(8,128)(2,1)}, bf16[1040,640]{1,0:T(8,128)(2,1)S(1)}, u32[]{:S(2)}) copy-start(bf16[1040,640]{1,0:T(8,128)(2,1)S(1)} %get-tuple-element.320) | copy-start | bytes 3993604
  107.3 1.5 copy-start.32
  107.3 1.6 copy-start.33
  107.3 5.0 copy-start.28
  107.3 6.0 copy-start.27
  112.3 6.1 copy-start.24
  123.2 39.5 %copy-start.34 = (f32[24]{0:T(128)S(1)}, f32[24]{0:T(128)}, u32[]{:S(2)}) copy-start(f32[24]{0:T(128)} %param.33) | copy-start | bytes 292
  123.2 40.1 %copy-start.10 = (f32[1024,6]{1,0:T(8,128)S(1)}, f32[1024,6]{1,0:T(8,128)}, u32[]{:S(2)}) copy-start(f32[1024,6]{1,0:T(8,128)} %slice.314) | copy-start | bytes 73732
  216.9 1.4 copy-start.13
  224.6 9.5 %copy-start.14 = (f32[1040,512]{1,0:T(8,128)S(1)}, f32[1040,512]{1,0:T(8,128)}, u32[]{:S(2)}) copy-start(f32[1040,512]{1,0:T(8,128)} %copy-done.13) | copy-start | bytes 6389764
  224.6 9.5 %copy-start.17 = (f32[1024,384]{1,0:T(8,128)S(1)}, f32[1024,384]{1,0:T(8,128)}, u32[]{:S(2)}) copy-start(f32[1024,384]{1,0:T(8,128)} %get-tuple-element.118) | copy-start | bytes 4718596
  337.4 7.7 %copy-start.11 = (bf16[4,4,128,512]{3,2,1,0:T(8,128)(2,1)S(1)}, bf16[4,4,128,512]{3,2,1,0:T(8,128)(2,1)}, u32[]{:S(2)}) copy-start(bf16[4,4,128,512]{3,2,1,0:T(8,128)(2,1)} %get-tuple-element.125) | copy-start | bytes 6291460
  337.4 7.7 %copy-start.30 = (bf16[1024,2048]{1,0:T(8,128)(2,1)S(1)}, bf16[1024,2048]{1,0:T(8,128)(2,1)}, u32[]{:S(2)}) copy-start(bf16[1024,2048]{1,0:T(8,128)(2,1)} %get-tuple-element.111) | copy-start | bytes 12582916
  345.1 5.5 copy-start.31
  349.3 1.3 copy-start.22
  357.2 3.2 copy-start.20
  366.3 142.0 %reduce-scatter.8.cloned.1.call-start = ((), (), s32[]{:S(2)}) async-start(), calls=%async_computation.9 | async-start | bytes 5242880 | tf_op jit(solution)/shard_map/reduce_scatter | solution.py:1694
  366.9 235.6 %reduce-scatter.10.cloned.1.call-start = ((), (), s32[]{:S(2)}) async-start(), calls=%async_computation.10 | async-start | bytes 2621440 | tf_op jit(solution)/shard_map/reduce_scatter | solution.py:1694
  439.1 232.4 %reduce-scatter.14.cloned.1.call-start = ((), (), s32[]{:S(2)}) async-start(), calls=%async_computation.12 | async-start | bytes 2621440 | tf_op jit(solution)/shard_map/reduce_scatter | solution.py:1694
  439.8 7.8 %collective-permute-start.3 = (f32[384,1]{0,1:T(1,128)S(1)}, f32[384,1]{0,1:T(1,128)S(1)}, u32[]{:S(2)}, u32[]{:S(2)}) collective-permute-start(f32[384,1]{0,1:T(1,128)S(1)} %slice_bitcast_fusion.2), channel_id=1, source_target_pairs={{16,0},{24,8},{17,1},{25,9},{18,2},{26,10},{19,3},{27,11},{20,4},{... | collective-permute-start | bytes 4616 | tf_op jit(solution)/shard_map/ppermute | solution.py:1549
  441.1 6.6 collective-permute-start.1
  447.7 6.1 copy-start.15
  447.8 6.1 copy-start.19
  453.9 2.8 copy-start.18
  453.9 2.9 copy-start.25
  457.8 22.4 %collective-permute-start.2 = (bf16[384,256]{1,0:T(8,128)(2,1)}, bf16[384,256]{1,0:T(8,128)(2,1)}, u32[]{:S(2)}, u32[]{:S(2)}) collective-permute-start(bf16[384,256]{1,0:T(8,128)(2,1)} %fusion.31), channel_id=1, source_target_pairs={{16,0},{24,8},{17,1},{25,9},{18,2},{26,10},{19,3},{27,11},{20,4},{... | collective-permute-start | bytes 589832 | tf_op jit(solution)/shard_map/ppermute | solution.py:1548
  459.1 21.2 %collective-permute-start = (bf16[384,256]{1,0:T(8,128)(2,1)}, bf16[384,256]{1,0:T(8,128)(2,1)}, u32[]{:S(2)}, u32[]{:S(2)}) collective-permute-start(bf16[384,256]{1,0:T(8,128)(2,1)} %fusion.31), channel_id=1, source_target_pairs={{8,0},{16,8},{24,16},{9,1},{17,9},{25,17},{10,2},{18,10},{26,18},{... | collective-permute-start | bytes 589832 | tf_op jit(solution)/shard_map/ppermute | solution.py:1548
  460.4 30.1 %collective-permute-start.4 = (bf16[384,256]{1,0:T(8,128)(2,1)}, bf16[384,256]{1,0:T(8,128)(2,1)}, u32[]{:S(2)}, u32[]{:S(2)}) collective-permute-start(bf16[384,256]{1,0:T(8,128)(2,1)} %fusion.31), channel_id=1, source_target_pairs={{24,0},{25,1},{26,2},{27,3},{28,4},{29,5},{30,6},{31,7}} | collective-permute-start | bytes 589832 | tf_op jit(solution)/shard_map/ppermute | solution.py:1548
  477.9 14.7 %copy-start.5 = (bf16[1024,512]{1,0:T(8,128)(2,1)}, bf16[1024,512]{1,0:T(8,128)(2,1)S(1)}, u32[]{:S(2)}) copy-start(bf16[1024,512]{1,0:T(8,128)(2,1)S(1)} %pad_maximum_fusion.4.left_b) | copy-start | bytes 3145732
  498.9 172.5 %reduce-scatter.12.cloned.1.call-start = ((), (), s32[]{:S(2)}) async-start(), calls=%async_computation.11 | async-start | bytes 3276800 | tf_op jit(solution)/shard_map/reduce_scatter | solution.py:1694
  501.9 32.0 %collective-permute-start.7 = (bf16[4,512,128]{2,1,0:T(8,128)(2,1)}, bf16[4,512,128]{2,1,0:T(8,128)(2,1)}, u32[]{:S(2)}, u32[]{:S(2)}) collective-permute-start(bf16[4,512,128]{2,1,0:T(8,128)(2,1)} %get-tuple-element.288), channel_id=1, source_target_pairs={{0,6},{2,4},{4,2},{6,0},{1,7},{3,5},{5,3},{7,1},{8,14},{10,12},{12... | collective-permute-start | bytes 1572872 | tf_op jit(solution)/shard_map/ppermute | solution.py:1726
  504.1 29.7 %collective-permute-start.6 = (bf16[4,512,128]{2,1,0:T(8,128)(2,1)}, bf16[4,512,128]{2,1,0:T(8,128)(2,1)}, u32[]{:S(2)}, u32[]{:S(2)}) collective-permute-start(bf16[4,512,128]{2,1,0:T(8,128)(2,1)} %get-tuple-element.289), channel_id=1, source_target_pairs={{0,4},{2,6},{4,0},{6,2},{1,5},{3,7},{5,1},{7,3},{8,12},{10,14},{12... | collective-permute-start | bytes 1572872 | tf_op jit(solution)/shard_map/ppermute | solution.py:1726
  504.7 29.2 %collective-permute-start.5 = (bf16[4,512,128]{2,1,0:T(8,128)(2,1)}, bf16[4,512,128]{2,1,0:T(8,128)(2,1)}, u32[]{:S(2)}, u32[]{:S(2)}) collective-permute-start(bf16[4,512,128]{2,1,0:T(8,128)(2,1)} %get-tuple-element.290), channel_id=1, source_target_pairs={{0,2},{2,0},{4,6},{6,4},{1,3},{3,1},{5,7},{7,5},{8,10},{10,8},{12,... | collective-permute-start | bytes 1572872 | tf_op jit(solution)/shard_map/ppermute | solution.py:1726
  508.3 25.5 %copy-start.12 = (bf16[4,512,128]{2,1,0:T(8,128)(2,1)S(1)}, bf16[4,512,128]{2,1,0:T(8,128)(2,1)}, u32[]{:S(2)}) copy-start(bf16[4,512,128]{2,1,0:T(8,128)(2,1)} %get-tuple-element.147) | copy-start | bytes 1572868
  576.0 5.9 copy-start.4
  576.0 5.9 copy-start.16
  585.7 2.8 copy-start.6
  585.7 2.8 copy-start.7
  585.8 2.8 copy-start.8
  598.7 1.4 copy-start.29
  602.5 67.6 %copy-start.26 = (f32[1,2048]{1,0:T(1,128)S(1)}, f32[1,2048]{1,0:T(1,128)}, u32[]{:S(2)}) copy-start(f32[1,2048]{1,0:T(1,128)} %get-tuple-element.164) | copy-start | bytes 24580
  705.2 3.3 copy-start.9
  705.2 4.6 copy-start.1
  (3 other events, 3.0 us)
Sparse Core Ops, SparseCore 0:
  97.9 50.2 all-gather.3
  149.7 58.7 all-gather.5
  210.1 97.7 all-gather.7
  366.5 43.9 reduce-scatter.5
  412.7 88.7 reduce-scatter.7
  503.7 47.1 reduce-scatter.9
  553.2 43.8 reduce-scatter.13
  599.4 51.2 reduce-scatter.11

commit v5 on v4

--- a/solution.py
+++ b/solution.py
@@ -723,54 +723,90 @@
     return stage, done
 
 
-def share_rows(full_ref, half, own_sems, far_sems, near_sems, between=None):
+def share(block, part, far_sems, near_sems, own_sems=None):
     z, p, c = place()
     other = chip(z, p, 1 - c)
-    mine = full_ref.at[at_rows((p * 2 + c) * half, half), :]
-    copies = []
-    for i, d in enumerate(HOPS):
-        copies.append(send(mine, mine, far_sems.at[0, i], far_sems.at[1, i], chip(z, hop(p, d), c)))
-    copies.append(send(mine, mine, own_sems.at[0], own_sems.at[1], other))
-    if between is not None:
-        between()
-    onward = []
-    for i, d in ((1, 1), (2, 2), (0, 3)):
-        copies[i].wait_recv()
-        came = full_ref.at[at_rows((hop(p, d) * 2 + c) * half, half), :]
-        onward.append(send(came, came, near_sems.at[0, i], near_sems.at[1, i], other))
-    return copies, onward
-
-
-def finish_share(copies, onward):
-    for copy in copies[:3]:
-        copy.wait_send()
-    copies[3].wait()
-    for copy in onward:
-        copy.wait()
-
-
-def reduce_blocks(pairs, part, keep, sib_out, sib_in, out, came, near_sems, far_sems):
+    x, y, far = hop(p, 1), hop(p, 2), hop(p, 3)
+
+    def far_send(ref, i, q):
+        return send(ref, ref, far_sems.at[0, i], far_sems.at[1, i], chip(z, q, c))
+
+    def near_send(q, i):
+        return send(block(q), block(q), near_sems.at[0, i], near_sems.at[1, i], other)
+
+    out = [far_send(block(p), 0, x), far_send(block(p), 1, y)]
+    near = []
+    if own_sems is not None:
+        near.append(send(block(p), block(p), own_sems.at[0], own_sems.at[1], other))
+
+    def middle():
+        out[0].wait_recv()
+        out.append(far_send(part(x, 0), 2, y))
+        out[1].wait_recv()
+        out.append(far_send(part(y, 1), 3, x))
+        if near_sems is not None:
+            near.append(near_send(x, 0))
+            near.append(near_send(y, 1))
+
+    def end():
+        out[2].wait_recv()
+        out[3].wait_recv()
+        if near_sems is not None:
+            near.append(near_send(far, 2))
+        for copy in out:
+            copy.wait_send()
+        for copy in near:
+            copy.wait()
+
+    return middle, end
+
+
+def share_rows(full_ref, half, own_sems, far_sems, near_sems):
+    z, p, c = place()
+    rows = lambda q: (q * 2 + c) * half
+    return share(
+        lambda q: full_ref.at[at_rows(rows(q), half), :],
+        lambda q, i: full_ref.at[at_rows(rows(q) + i * (half // 2), half // 2), :],
+        far_sems, near_sems, own_sems,
+    )
+
+
+def reduce_blocks(pairs, part, keep, sib_out, sib_in, out, relay, came, near_sems, far_sems):
     z, p, c = place()
     other = chip(z, p, 1 - c)
-    half = keep.shape[1]
-    width = keep.shape[2]
-    tile = part.shape[1]
+    half, width = keep.shape[1], keep.shape[2]
+    tile, quarter = part.shape[1], half // 2
+    x, y = chip(z, hop(p, 1), c), chip(z, hop(p, 2), c)
+    first, second = at_rows(0, quarter), at_rows(quarter, quarter)
     near, far = [], []
 
-    def pass_on(i, d):
+    def far_send(src, dst, i, to):
+        far.append(send(src, dst, far_sems.at[0, i], far_sems.at[1, i], to))
+
+    def total_of(i, rows, extra=None):
+        @pl.loop(0, quarter // 16)
+        def _(r):
+            at = at_rows(rows + r * 16, 16)
+            total = keep[i, at, :] + sib_in[i, at, :].astype(f32)
+            if extra is not None:
+                total = total + relay[extra, at_rows(r * 16, 16), :].astype(f32)
+            out[i, at, :] = total.astype(bf16)
+
+    def pass_on(i):
         near[i].wait_recv()
-
-        @pl.loop(0, half // 16)
-        def _(r):
-            at = at_rows(r * 16, 16)
-            out[i, at, :] = (keep[i, at, :] + sib_in[i, at, :].astype(f32)).astype(bf16)
-
-        far.append(
-            send(out.at[i], came.at[i], far_sems.at[0, i], far_sems.at[1, i], chip(z, hop(p, d), c))
-        )
-
-    order = HOPS + (0,)
-    for i, d in enumerate(order):
+        if i == 0:
+            total_of(0, 0)
+            far_send(out.at[0, first, :], relay.at[0], 0, x)
+            total_of(0, quarter)
+            far_send(out.at[0, second, :], relay.at[1], 1, y)
+        if i == 1:
+            total_of(1, 0)
+            far_send(out.at[1, first, :], came.at[0, first, :], 2, x)
+        if i == 2:
+            total_of(2, quarter)
+            far_send(out.at[2, second, :], came.at[1, second, :], 3, y)
+
+    for i, d in enumerate((3, 1, 2, 0)):
         rows = at_rows(hop(p, d) * (2 * half), 2 * half)
 
         @pl.loop(0, width // tile)
@@ -787,21 +823,30 @@
             send(sib_out.at[i], sib_in.at[i], near_sems.at[0, i], near_sems.at[1, i], other)
         )
         if i:
-            pass_on(i - 1, order[i - 1])
+            pass_on(i - 1)
+
+    def middle():
+        far[1].wait_recv()
+        total_of(1, quarter, 1)
+        far_send(out.at[1, second, :], came.at[0, second, :], 4, x)
+        far[0].wait_recv()
+        total_of(2, 0, 0)
+        far_send(out.at[2, first, :], came.at[1, first, :], 5, y)
+
     def finish():
         near[3].wait_recv()
-        for copy in far:
+        for copy in far[2:]:
             copy.wait_recv()
 
     def total_rows(at):
         total = keep[3, at, :] + sib_in[3, at, :].astype(f32)
-        return total + came[0, at, :].astype(f32) + came[1, at, :].astype(f32) + came[2, at, :].astype(f32)
+        return total + came[0, at, :].astype(f32) + came[1, at, :].astype(f32)
 
     def done():
         for copy in near + far:
             copy.wait_send()
 
-    return total_rows, finish, done
+    return total_rows, middle, finish, done
 
 
 def greet():
@@ -814,27 +859,16 @@
 
 
 def mid_kernel(
-    left, right, resid, gain, w_ref, mid_ref, full_ref, w_out,
-    part, keep, sib_out, sib_in, out, came, n_sems, f_sems, own_sems, far_sems, near_sems,
-    up_sems, down_sems, loc_sems,
+    left, right, resid, gain, mid_ref, full_ref,
+    part, keep, sib_out, sib_in, out, relay, came, n_sems, f_sems, own_sems, far_sems, near_sems,
 ):
+    greet()
     z, p, c = place()
-    nz = w_out.shape[0]
-    meet(
-        [chip(z, p, 1 - c)]
-        + [chip(z, hop(p, d), c) for d in HOPS]
-        + [chip(lax.rem(z + d, nz), p, c) for d in (1, nz - 1)]
-    )
-    local = pltpu.make_async_copy(w_ref, w_out.at[z], loc_sems.at[0])
-    local.start()
-    local.wait()
-    stage, chain_done = z_chain(w_out, up_sems, down_sems)
-    stage(0)
     half = keep.shape[1]
-    total_rows, finish, done = reduce_blocks(
-        [(left, right)], part, keep, sib_out, sib_in, out, came, n_sems, f_sems
-    )
-    stage(1)
+    total_rows, middle, finish, done = reduce_blocks(
+        [(left, right)], part, keep, sib_out, sib_in, out, relay, came, n_sems, f_sems
+    )
+    middle()
     finish()
     g = gain[...]
 
@@ -845,25 +879,23 @@
         mid_ref[at, :] = mid
         full_ref[at_rows((p * 2 + c) * half + r * 16, 16), :] = (mid * rms(mid) * g).astype(bf16)
 
-    between = lambda: stage(2) if nz > 2 else None
-    copies, onward = share_rows(full_ref, half, own_sems, far_sems, near_sems, between)
-    for k in range(3, nz):
-        stage(k)
+    share_middle, share_end = share_rows(full_ref, half, own_sems, far_sems, near_sems)
+    share_middle()
     done()
-    finish_share(copies, onward)
-    chain_done()
+    share_end()
 
 
 def two_kernel(
     left, right, mid_own, grad_own, gain, dmid_ref, ggain_ref, full_ref,
-    part, keep, sib_out, sib_in, out, came, n_sems, f_sems, own_sems, far_sems, near_sems,
+    part, keep, sib_out, sib_in, out, relay, came, n_sems, f_sems, own_sems, far_sems, near_sems,
 ):
     greet()
     z, p, c = place()
     half = keep.shape[1]
-    total_rows, finish, done = reduce_blocks(
-        [(left, right)], part, keep, sib_out, sib_in, out, came, n_sems, f_sems
-    )
+    total_rows, middle, finish, done = reduce_blocks(
+        [(left, right)], part, keep, sib_out, sib_in, out, relay, came, n_sems, f_sems
+    )
+    middle()
     finish()
     g = gain[...]
     ggain_ref[...] = jnp.zeros_like(ggain_ref)
@@ -881,25 +913,30 @@
         dmid_ref[at, :] = d_mid
         full_ref[at_rows((p * 2 + c) * half + r * 16, 16), :] = d_mid.astype(bf16)
 
-    copies, onward = share_rows(full_ref, half, own_sems, far_sems, near_sems)
+    share_middle, share_end = share_rows(full_ref, half, own_sems, far_sems, near_sems)
+    share_middle()
     done()
-    finish_share(copies, onward)
+    share_end()
 
 
 def one_kernel(
     n, left_a, right_a, left_b, right_b, hidden_own, dmid_own, gain, act, w_act, mid_own, *refs
 ):
     ins, (grad_ref, block_ref, ggain_ref), outs = refs[:n], refs[n : n + 3], refs[n + 3 : 2 * n + 3]
-    first, second = refs[2 * n + 3 : 2 * n + 11], refs[2 * n + 11 : 2 * n + 19]
-    own_sems, w_sems, loc_sems = refs[2 * n + 19 :]
+    first, second = refs[2 * n + 3 : 2 * n + 12], refs[2 * n + 12 : 2 * n + 21]
+    own_sems, w_sems, loc_sems = refs[2 * n + 21 :]
     greet()
     z, p, c = place()
     half = hidden_own.shape[0]
-    total_rows, finish, done = reduce_blocks([(left_a, right_a), (left_b, right_b)], *first)
-    total_out, finish_out, done_out = reduce_blocks([(act, w_act)], *second)
+    total_rows, middle, finish, done = reduce_blocks(
+        [(left_a, right_a), (left_b, right_b)], *first
+    )
+    middle()
+    total_out, middle_out, finish_out, done_out = reduce_blocks([(act, w_act)], *second)
     moved = swap_begin(ins, outs, w_sems, loc_sems)
     g = gain[...]
     ggain_ref[...] = jnp.zeros_like(ggain_ref)
+    middle_out()
     finish()
 
     @pl.loop(0, half // 16)
@@ -965,15 +1002,16 @@
         pltpu.VMEM((4, half, width), bf16),
         pltpu.VMEM((4, half, width), bf16),
         pltpu.VMEM((3, half, width), bf16),
-        pltpu.VMEM((3, half, width), bf16),
+        pltpu.VMEM((2, half // 2, width), bf16),
+        pltpu.VMEM((2, half, width), bf16),
         pltpu.SemaphoreType.DMA((2, 4)),
-        pltpu.SemaphoreType.DMA((2, 3)),
+        pltpu.SemaphoreType.DMA((2, 6)),
     ]
 
 
 SHARE_SEMS = [
     pltpu.SemaphoreType.DMA((2,)),
-    pltpu.SemaphoreType.DMA((2, 3)),
+    pltpu.SemaphoreType.DMA((2, 4)),
     pltpu.SemaphoreType.DMA((2, 3)),
 ]
 
@@ -985,7 +1023,7 @@
         scratch = scratch + swap_sems(n)
     return pl.pallas_call(
         kernel,
-        in_specs=[VM] * len(args) + [ANYWHERE] * n,
+        in_specs=[VM] * (len(args) + n),
         out_specs=[VM] * len(shapes) + [ANYWHERE] * n,
         out_shape=[jax.ShapeDtypeStruct(s, t) for s, t in shapes]
         + [jax.ShapeDtypeStruct(m.shape, m.dtype) for m in moved],
@@ -998,28 +1036,14 @@
     )(*args, *moved)
 
 
-def mid_step(mixed, w, resid_own, gain, piece, nz):
+def mid_step(mixed, w, resid_own, gain):
     tok, width = mixed.shape[0], w.shape[0]
     half = resid_own.shape[0]
-    dma = pltpu.SemaphoreType.DMA
-    return pl.pallas_call(
-        mid_kernel,
-        in_specs=[VM] * 4 + [ANYWHERE],
-        out_specs=[VM] * 2 + [ANYWHERE],
-        out_shape=[
-            jax.ShapeDtypeStruct((half, width), f32),
-            jax.ShapeDtypeStruct((tok, width), bf16),
-            jax.ShapeDtypeStruct((nz,) + piece.shape, bf16),
-        ],
-        scratch_shapes=reduce_scratch(half, width)
-        + SHARE_SEMS
-        + [dma((2, nz)), dma((2, nz)), dma((1,))],
-        compiler_params=pltpu.CompilerParams(
-            collective_id=1, has_side_effects=True, vmem_limit_bytes=VMEM_LIMIT
-        ),
-        cost_estimate=pl.CostEstimate(flops=0, bytes_accessed=150_000_000, transcendentals=0),
-        name="mid_step",
-    )(mixed, w, resid_own, gain, piece)
+    return plane_call(
+        mid_kernel, "mid_step", 1, (mixed, w, resid_own, gain),
+        [((half, width), f32), ((tok, width), bf16)],
+        reduce_scratch(half, width) + SHARE_SEMS,
+    )
 
 
 def two_step(d_gu, w, mid_own, grad_own, gain):
@@ -1101,25 +1125,16 @@
             rows_in * rms(rows_in) * g
         ).astype(bf16)
 
-    other = chip(z, p, 1 - c)
-    mine = full_ref.at[at_rows((p * 2 + c) * half, half), :]
-    rows_out = [
-        send(mine, mine, far_sems.at[0, i], far_sems.at[1, i], flat[i]) for i in range(3)
-    ] + [send(mine, mine, own_sems.at[0], own_sems.at[1], other)]
+    share_middle, share_end = share_rows(full_ref, half, own_sems, far_sems, near_sems)
 
     stage, chain_done = z_chain(a_out, up_sems, down_sems)
     for copy in to_plane:
         copy.wait_recv()
-    for copy in local:
-        copy.wait()
+    local[0].wait()
     stage(0)
+    share_middle()
     if nz > 2:
         stage(1)
-    onward = []
-    for i, d in ((1, 1), (2, 2), (0, 3)):
-        rows_out[i].wait_recv()
-        came = full_ref.at[at_rows((hop(p, d) * 2 + c) * half, half), :]
-        onward.append(send(came, came, near_sems.at[0, i], near_sems.at[1, i], other))
     moved = []
     for j in range(n):
         for i, d in enumerate(HOPS):
@@ -1129,7 +1144,7 @@
                     w_sems.at[1, j, i], flat[i],
                 )
             )
-    finish_share(rows_out, onward)
+    share_end()
     halo_from = full_ref.at[at_rows(tok - HALO, HALO), :]
     halo_to = full_ref.at[at_rows(tok, HALO), :]
 
@@ -1159,7 +1174,7 @@
         halo(chip(z + 1, p, c)).wait_send()
 
     chain_done()
-    for copy in moved:
+    for copy in moved + local[1:]:
         copy.wait()
     for copy in gz + gp + to_plane:
         copy.wait_send()
@@ -1171,7 +1186,7 @@
     dma = pltpu.SemaphoreType.DMA
     return pl.pallas_call(
         functools.partial(open_kernel, n),
-        in_specs=[VM, VM] + [anywhere] * (n + 1),
+        in_specs=[VM] * (n + 3),
         out_specs=[VM, VM] + [anywhere] * (n + 1),
         out_shape=[
             jax.ShapeDtypeStruct((n_p, nz) + gains.shape, f32),
@@ -1221,20 +1236,17 @@
 
     half = x_ref.shape[0] // 2
     full_ref[p] = x_ref[...]
-    rows = at_rows(c * half, half)
-    mine = full_ref.at[p, rows, :]
-    copies = [
-        send(mine, mine, far_sems.at[0, i], far_sems.at[1, i], chip(z, hop(p, d), c))
-        for i, d in enumerate(HOPS)
-    ]
-    onward = []
-    for i, d in ((1, 1), (2, 2), (0, 3)):
-        copies[i].wait_recv()
-        came = full_ref.at[hop(p, d), rows, :]
-        onward.append(send(came, came, near_sems.at[0, i], near_sems.at[1, i], other))
+    bc_middle, bc_end = share(
+        lambda q: full_ref.at[q, at_rows(c * half, half), :],
+        lambda q, i: full_ref.at[q, at_rows(c * half + i * (half // 2), half // 2), :],
+        far_sems, near_sems,
+    )
+    bc_middle()
     g_half = grad_ref.shape[0]
     g_ref[at_rows((p * 2 + c) * g_half, g_half), :] = grad_ref[...].astype(bf16)
-    g_copies, g_onward = share_rows(g_ref, g_half, own_g, far_g, near_g)
+    g_middle, g_end = share_rows(g_ref, g_half, own_g, far_g, near_g)
+    bc_end()
+    g_middle()
     for d in range(1, nz):
 
         @pl.when(z - d >= 0)
@@ -1249,11 +1261,7 @@
             kvz_ref[z + d] = jnp.zeros(kv_ref.shape, kv_ref.dtype)
             up(d).wait_send()
 
-    for copy in copies:
-        copy.wait_send()
-    for copy in onward:
-        copy.wait()
-    finish_share(g_copies, g_onward)
+    g_end()
 
 
 def gather_bc(x, at, n_p, kv, nz, grad):
@@ -1274,7 +1282,7 @@
             jax.ShapeDtypeStruct((nz,) + kv.shape, bf16),
             jax.ShapeDtypeStruct((tok, grad.shape[1]), bf16),
         ],
-        scratch_shapes=[dma((2, 3)), dma((2, 3)), dma((2, nz - 1))] + SHARE_SEMS,
+        scratch_shapes=[dma((2, 4)), dma((2, 3)), dma((2, nz - 1))] + SHARE_SEMS,
         compiler_params=pltpu.CompilerParams(
             collective_id=5, has_side_effects=True, vmem_limit_bytes=VMEM_LIMIT
         ),
@@ -1283,68 +1291,64 @@
     )(x, kv, grad)
 
 
-def carry_kernel(state_ref, rate_ref, kvz_ref, in_ref, kv_ref, low, came, rates, factor, s_sems, r_sems, p_sems):
+def carry_kernel(
+    state_ref, rate_ref, kvz_ref, in_ref, kv_ref, rates_ref,
+    low, came, factor, s_sems, r_sems, p_sems,
+):
     z, p, c = place()
     nz = kvz_ref.shape[0]
-    meet(
-        [chip(z, hop(p, d), c) for d in HOPS]
-        + [chip(lax.rem(z + d, nz), p, c) for d in range(1, nz)]
-    )
+    ups = [chip(lax.rem(z + d, nz), p, c) for d in range(1, nz)]
+    meet([chip(z, hop(p, d), c) for d in (1, 2)] + ups)
     low[...] = state_ref[...].astype(bf16)
+    rates_ref[z] = rate_ref[...]
+    rates = [
+        send(rates_ref.at[z], rates_ref.at[z], r_sems.at[0, d], r_sems.at[1, d], ups[d])
+        for d in range(nz - 1)
+    ]
 
     def up(d):
-        to = chip(z + d, p, c)
-        return (
-            pltpu.make_async_remote_copy(
-                src_ref=low, dst_ref=came.at[d - 1], send_sem=s_sems.at[0, d - 1],
-                recv_sem=s_sems.at[1, d - 1], device_id=to, device_id_type=MESH,
-            ),
-            pltpu.make_async_remote_copy(
-                src_ref=rate_ref, dst_ref=rates.at[d - 1], send_sem=r_sems.at[0, d - 1],
-                recv_sem=r_sems.at[1, d - 1], device_id=to, device_id_type=MESH,
-            ),
+        return pltpu.make_async_remote_copy(
+            src_ref=low, dst_ref=came.at[d - 1], send_sem=s_sems.at[0, d - 1],
+            recv_sem=s_sems.at[1, d - 1], device_id=chip(z + d, p, c), device_id_type=MESH,
         )
 
     for d in range(1, nz):
 
         @pl.when(z + d < nz)
         def _():
-            for copy in up(d):
-                copy.start()
+            up(d).start()
 
     kv_ref[p] = kvz_ref[...]
-    mine = kv_ref.at[p]
-    copies = [
-        send(mine, mine, p_sems.at[0, i], p_sems.at[1, i], chip(z, hop(p, d), c))
-        for i, d in enumerate(HOPS)
-    ]
+    kv_middle, kv_end = share(
+        lambda q: kv_ref.at[q],
+        lambda q, i: kv_ref.at[q, pl.ds(i * (nz // 2), nz // 2)],
+        p_sems, None,
+    )
     in_ref[...] = jnp.zeros_like(in_ref)
     factor[...] = jnp.ones_like(factor)
     lane_head, row_head = head_maps(state_ref.shape[0])
+    kv_middle()
+    for copy in rates:
+        copy.wait_recv()
     for d in range(1, nz):
 
         @pl.when(z - d >= 0)
         def _():
-            fro = chip(z - d, p, c)
             pltpu.make_async_remote_copy(
                 src_ref=low, dst_ref=came.at[d - 1], send_sem=s_sems.at[0, d - 1],
-                recv_sem=s_sems.at[1, d - 1], device_id=fro, device_id_type=MESH,
-            ).wait_recv()
-            pltpu.make_async_remote_copy(
-                src_ref=rate_ref, dst_ref=rates.at[d - 1], send_sem=r_sems.at[0, d - 1],
-                recv_sem=r_sems.at[1, d - 1], device_id=fro, device_id_type=MESH,
+                recv_sem=s_sems.at[1, d - 1], device_id=chip(z - d, p, c), device_id_type=MESH,
             ).wait_recv()
             scale = jnp.sum(row_head * factor[0:1, :], axis=1, keepdims=True)
             in_ref[...] += scale * came[d - 1].astype(f32)
-            factor[...] = factor[...] * rates[d - 1]
+            factor[...] = factor[...] * rates_ref[z - d]
 
         @pl.when(z + d < nz)
         def _():
-            for copy in up(d):
-                copy.wait_send()
-
-    for copy in copies:
-        copy.wait()
+            up(d).wait_send()
+
+    kv_end()
+    for copy in rates:
+        copy.wait_send()
 
 
 def carry_step(state, rate, kvz, n_p):
@@ -1352,13 +1356,12 @@
     dma = pltpu.SemaphoreType.DMA
     return plane_call(
         carry_kernel, "carry_step", 8, (state, rate, kvz),
-        [(state.shape, f32), ((n_p,) + kvz.shape, bf16)],
+        [(state.shape, f32), ((n_p,) + kvz.shape, bf16), ((nz,) + rate.shape, f32)],
         [
             pltpu.VMEM(state.shape, bf16),
             pltpu.VMEM((nz - 1,) + state.shape, bf16),
-            pltpu.VMEM((nz - 1,) + rate.shape, f32),
             pltpu.VMEM(rate.shape, f32),
-            dma((2, nz - 1)), dma((2, nz - 1)), dma((2, 3)),
+            dma((2, nz - 1)), dma((2, nz - 1)), dma((2, 4)),
         ],
         nbytes=80_000_000,
     )
@@ -1539,15 +1542,14 @@
     return jnp.cos(angles), jnp.sin(angles)
 
 
-def carry_states(state, decays, sign):
-    nz = lax.axis_size("z")
+def carry_back(state, rates):
+    nz, zi = lax.axis_size("z"), lax.axis_index("z")
     low = state.astype(bf16)
     total, factor = None, None
     for d in range(1, nz):
-        route = [(i, i + sign * d) for i in range(nz) if 0 <= i + sign * d < nz]
-        came = lax.ppermute(low, "z", route).astype(f32)
-        rate = lax.ppermute(decays, "z", route)
+        came = lax.ppermute(low, "z", [(i, i - d) for i in range(d, nz)]).astype(f32)
         total = came if total is None else total + factor * came
+        rate = lax.dynamic_index_in_dim(rates, (zi + d) % nz, 0, keepdims=False)
         factor = rate if factor is None else factor * rate
     return total
 
@@ -1614,7 +1616,7 @@
     w_a = w_a.reshape(nz * n_p * rows, w_a.shape[3])
     gains = gains.transpose(2, 1, 0, 3)[:, :, :, :rows].reshape(8, 1, width)
     gain_mix, gain_ffn = gains[0], gains[1]
-    w_b, w_c, w_d = [along_z(piece) for piece in rest[:3]]
+    w_b, w_c, w_d, w_e = [along_z(piece) for piece in rest]
 
     in_ext = product(normed_one, w_a)
     in_b = product(normed_one, w_b)[:tok]
@@ -1664,9 +1666,8 @@
     y_local, span_starts, local_state, dev_decay, decay_full, c_mat = ssd_forward(
         base_arr, doc_starts, ssm, bc_all, dt_pre, neg_rate, skip_full
     )
-    total_decay = decay_full[-1][:, None]
     rate = jnp.broadcast_to(dev_decay[tok - 1 :], (8, 128))
-    in_state, kv = carry_step(local_state, rate, kvz, n_p)
+    in_state, kv, rates = carry_step(local_state, rate, kvz, n_p)
 
     attn_f32, lse, keys, values = attend(base_arr, doc_starts, queries, kv)
     attn_low = attn_f32.astype(bf16)
@@ -1675,20 +1676,20 @@
     gated = (y_flat * silu_z).astype(bf16)
     mixed = jnp.concatenate([gated, attn_low], axis=1)
 
-    mid_own, normed_two, w_e = mid_step(mixed, w_c, hidden_own, gain_ffn, rest[3], nz)
-    w_e = w_e.reshape(width, -1)
+    mid_own, normed_two = mid_step(mixed, w_c, hidden_own, gain_ffn)
     gu = product(normed_two, w_d)
     ffw = gu.shape[1] // 2
     gate_val, up_val = gu[:, :ffw], gu[:, ffw:]
     silu_gate = jax.nn.silu(gate_val)
     activated = (silu_gate * up_val).astype(bf16)
+    grad_e = product_t(g_ffn, activated).astype(bf16)
+    g_ffn, grad_e = lax.optimization_barrier((g_ffn, grad_e))
     d_act = product(g_ffn, w_e)
     d_gu = jnp.concatenate(
         [d_act * up_val * silu_slope(gate_val), d_act * silu_gate], axis=1
     ).astype(bf16)
-    grad_e = product_t(g_ffn, activated).astype(bf16)
     grad_d = product_t(normed_two, d_gu).astype(bf16)
-    d_gu, grad_e, grad_d = lax.optimization_barrier((d_gu, grad_e, grad_d))
+    d_gu, grad_d = lax.optimization_barrier((d_gu, grad_d))
 
     def scattered(grad):
         return lax.psum_scatter(grad, "z", scatter_dimension=0, tiled=True)
@@ -1710,7 +1711,8 @@
     d_z = (d_gated * y_flat * silu_slope(gate_z)).astype(bf16)
     d_in_local = product_t((d_y_flat * decay_full).astype(bf16), c_mat)
     d_in_local, d_attn = lax.optimization_barrier((d_in_local, d_attn))
-    state_grad = carry_states(d_in_local, total_decay, -1)
+    rates = jnp.repeat(rates[:, 0, :n_heads], MHDIM, axis=1)[:, :, None]
+    state_grad = carry_back(d_in_local, rates)
     d_query, d_kv = attend_back(
         base_arr, doc_starts, queries, d_attn, attn_f32, lse, keys, values, kv.shape
     )
@@ -1754,10 +1756,10 @@
     ga = scattered(grad_a)
     once = jnp.where(ci == 0, d_pre[:, xw:], jnp.zeros((), bf16))
     d_a_once = jnp.concatenate([d_pre[:, :xw], once, d_last], axis=1)
-    d_a_once, grad_a, gc = lax.optimization_barrier((d_a_once, grad_a, gc))
-    grad_in, block_out, grad_gain_mix, gc = one_step(
+    d_a_once, grad_a, gc, gb = lax.optimization_barrier((d_a_once, grad_a, gc, gb))
+    grad_in, block_out, grad_gain_mix, gc, gb = one_step(
         d_a_once, w_a, d_b, w_b, hidden_own, d_mid_own, gain_mix, activated, w_e, mid_own,
-        (by_owner(gc),),
+        (by_owner(gc), by_owner(gb)),
     )
 
     flat = jnp.concatenate(
@@ -1770,7 +1772,7 @@
         ]
     )
     flat = jnp.pad(flat, ((0, -flat.shape[0] % 8), (0, 0)))
-    summed, ga, gb = sums_step(flat, nz, n_p, (by_owner(ga), by_owner(gb)))
+    summed, ga = sums_step(flat, nz, n_p, (by_owner(ga),))
     g_rows = width // 128
     t_rows = grad_taps.size // 128
     si = zi * n_p + pi

time: 727 us -> 679 us (0.934)
  Pallas kernels: 509 us -> 420 us
  waiting for transfers between devices: 20 us -> 60.7 us
    pallas_call x7, Pallas kernels: 406 us -> 324 us  [the longest x6 256 us: plane_call(): pl.pallas_call(kernel, in_specs=[VM] * (len(args) + n), out_specs=[VM] *...]
    all_gather x3 -> x4, waiting for transfers between devices: 0.04 us -> 43.6 us  [along_z(): return lax.all_gather(piece, 'z', axis=0, tiled=True)]
    ppermute x5 -> x3, waiting for transfers between devices: 18 us -> 11.3 us  [carry_back(): lax.ppermute(low, 'z', [(i, i - d) for i in range(d, nz)]).astype(f32)]
    unnamed x74 -> x68, local copies, waits for them, and re-layouts: 12.5 us -> 17.2 us
  transfers between devices with their start and end apart: 16 -> 15, of which waited for: 5 -> 7; matrix products, arithmetic and copies ran while one was open for 16% -> 21% of each run, Pallas kernels for 55% -> 49%
where the time goes in v5:
time: 679 us; the launch traced here: 670 us
  Pallas kernels  420 us (62%)
  matrix products  67.8 us (10%)
  waiting for transfers between devices  60.7 us (9%)
  local copies, waits for them, and re-layouts  58.1 us (9%)
  other arithmetic  40.3 us (6%)
  between operations  15 us (2%)
  starting transfers between devices  8.1 us (1%)
    pallas_call x6, Pallas kernels, plane_call(): pl.pallas_call(kernel, in_specs=[VM] * (len(args) + n), out_specs=[VM] *...  256 us
    pallas_call x1, Pallas kernels, open_step(): pl.pallas_call(functools.partial(open_kernel, n), in_specs=[VM] * (n + 3)...  68.6 us
    all_gather x4, waiting for transfers between devices, along_z(): return lax.all_gather(piece, 'z', axis=0, tiled=True)  43.6 us
    dot_general x5, matrix products, product(): return jnp.dot(left, right, preferred_element_type=f32)  32.4 us
    dot_general x6, matrix products, product_t(): lax.dot_general(left, right, (((0,), (0,)), ((), ())), preferred_element_...  31.8 us
    pallas_call x1, Pallas kernels, gather_bc(): pl.pallas_call(gather_bc_kernel, grid=(1,), in_specs=[pl.BlockSpec((tok,...  30.8 us
    pallas_call x1, Pallas kernels, ssd_backward(): pl.pallas_call(functools.partial(ssd_backward_kernel, n_heads), grid=(nsp...  22.4 us
    unnamed x68, local copies, waits for them, and re-layouts  17.2 us
  transfers between devices with their start and end apart: 15, of which 7 were waited for; matrix products, arithmetic and copies ran while one was open for 21% of the time, Pallas kernels for 49%

profile of v5, /device:TPU:0, one launch (start us, length us, event | category | flops | bytes accessed | tf_op | source)
XLA Modules:
  0.0 670.2 jit_solution(16424527916293358562)
XLA Ops:
  11.2 5.5 pack.1
  16.7 68.6 %open_step.1 = (f32[4,4,8,128]{3,2,1,0:T(8,128)}, bf16[1040,2048]{1,0:T(8,128)(2,1)}, bf16[4,4,128,640]{3,2,1,0:T(8,128)(2,1)}, bf16[4,128,512]{2,1,0:T(8,128)(2...) custom-call(f32[128,2048]{1,0:T(8,128)} %constant_dynamic-slice_fusion.7.refs_0_.resi, ...), custom_call_target="tpu_custom_call" | custom-call | bytes 250000000 | tf_op jit(solution)/shard_map/open_step/pallas_call | solution.py:1187
  87.5 7.2 %fusion.81 = (bf16[1040,640]{1,0:T(8,128)(2,1)S(1)}, f32[1040,640]{1,0:T(8,128)}) fusion(bf16[1040,2048]{1,0:T(8,128)(2,1)} %get-tuple-element.110, bf16[2048,640]{1,0:T(8,128)(2,1)S(1)} %bitcast.83), kind=kOutput, calls=%fused_computation.178 | convolution fusion | flops 2726963200 | bytes 10874880 | tf_op jit(solution)/shard_map/dot_general | solution.py:32
  98.5 2.3 constant_dynamic-slice_fusion.3.grad_ref.grad_own
  103.6 3.8 fusion.43
  107.7 3.8 add_multiply_fusion
  114.5 30.8 %gather_bc.1 = (bf16[4,1024,128]{2,1,0:T(8,128)(2,1)}, bf16[4,512,128]{2,1,0:T(8,128)(2,1)}, bf16[1024,2048]{1,0:T(8,128)(2,1)}) custom-call(bf16[1024,512]{1,0:T(8,128)(2,1)} %multiply_convert_fusion.3.x_ref, bf16[512,128]{1,0:T(8,128)(2,1)} %pad_maximum_fusion.9.kv_ref, f32[128,2048]{1,0:T(8,128)} %constant_dynamic-slice_fusion.3.grad_ref.grad_own), custom_call_target="tpu_custom_call" | custom-call | bytes 40000000 | tf_op jit(solution)/shard_map/gather_bc/pallas_call | solution.py:1271
  145.4 13.7 %ssd_forward.1 = (f32[1024,384]{1,0:T(8,128)}, f32[8,384,256]{2,1,0:T(8,128)}, f32[384,256]{1,0:T(8,128)}, f32[1024,128]{1,0:T(8,128)}, f32[1024,384]{1,0:T(8,128)}, /*index=5*/bf16[1024,256]{1,0:T(8,128)(2,1)}) custom-call(s32[1]{0:T(128)} %bitcast.base_ref, s32[8]{0:T(128)} %starts_ref.7, bf16[1024,512]{1,0:T(8,128)(2,1)} %multiply_convert_fusion.3.x_ref, ...), custom_call_target="tpu_custom_call" | custom-call | flops 603979776 | bytes 40000000 | tf_op jit(solution)/shard_map/ssd_forward/pallas_call | solution.py:195
  160.4 31.1 %carry_step.1 = (f32[384,256]{1,0:T(8,128)}, bf16[4,4,512,128]{3,2,1,0:T(8,128)(2,1)}, f32[4,8,128]{2,1,0:T(8,128)}) custom-call(f32[384,256]{1,0:T(8,128)} %get-tuple-element.116.state_ref, f32[8,128]{1,0:T(8,128)} %broadcast_in_dim.122.rate_ref, bf16[4,512,128]{2,1,0:T(8,128)(2,1)} %get-tuple-element.118.kvz_ref), custom_call_target="tpu_custom_call" | custom-call | bytes 80000000 | tf_op jit(solution)/shard_map/carry_step/pallas_call | solution.py:1024
  191.5 5.3 fusion.82
  199.0 2.0 copy.94
  201.0 2.1 fusion.60
  204.0 8.4 %attend.1 = (f32[1024,128]{1,0:T(8,128)}, f32[1024,128]{1,0:T(8,128)}, bf16[4096,128]{1,0:T(8,128)(2,1)}, bf16[4096,128]{1,0:T(8,128)(2,1)}) custom-call(s32[1]{0:T(128)} %bitcast.base_ref, s32[8]{0:T(128)} %starts_ref.7, bf16[1024,128]{1,0:T(8,128)(2,1)} %copy.95.q_ref, bf16[4,4,512,128]{3,2,1,0:T(8,128)(2,1)} %get-tuple-element.122.kv_ref), custom_call_target="tpu_custom_call" | custom-call | flops 2147483648 | bytes 30000000 | tf_op jit(solution)/shard_map/attend/pallas_call | solution.py:416
  213.5 3.6 multiply_convert_fusion.6
  219.1 52.1 %mid_step.1 = (f32[128,2048]{1,0:T(8,128)}, bf16[1024,2048]{1,0:T(8,128)(2,1)}) custom-call(bf16[1024,512]{1,0:T(8,128)(2,1)} %pad_maximum_fusion.3.left, bf16[2048,512]{1,0:T(8,128)(2,1)} %all-gather.7.cloned.1.call-done.right, f32[128,2048]{1,0:T(8,128)} %constant_dynamic-slice_fusion.7.refs_0_.resid.hidden_own, f32[1,2048]{1,0:T(1,128)} %bitcast.98), custom_call_target="tpu_custom_call" | custom-call | bytes 150000000 | tf_op jit(solution)/shard_map/mid_step/pallas_call | solution.py:1024
  271.2 13.8 %all-gather.9.cloned.1.call-done.right = bf16[2048,1024]{1,0:T(8,128)(2,1)} async-done(((bf16[512,1024]{1,0:T(8,128)(2,1)}), bf16[2048,1024]{1,0:T(8,128)(2,1)}) %all-gather.9.cloned.1.call-update) | async-done | bytes 4194320 | tf_op jit(solution)/shard_map/all_gather | solution.py:1608
  285.0 7.5 %fusion.83 = f32[1024,1024]{1,0:T(8,128)S(1)} fusion(bf16[1024,2048]{1,0:T(8,128)(2,1)} %get-tuple-element.126, bf16[2048,1024]{1,0:T(8,128)(2,1)} %all-gather.9.cloned.1.call-done.right), kind=kOutput, calls=%fused_computation.180 | convolution fusion | flops 4294967296 | bytes 12582912 | tf_op jit(solution)/shard_map/dot_general | solution.py:32
  292.5 2.0 copy-done.6
  297.1 3.8 convolution_convert_fusion.4
  301.1 29.8 %all-gather.11.cloned.1.call-done.w_act = bf16[2048,512]{1,0:T(8,128)(2,1)} async-done(((bf16[512,512]{1,0:T(8,128)(2,1)}), bf16[2048,512]{1,0:T(8,128)(2,1)}) %all-gather.11.cloned.1.call-update) | async-done | bytes 2097168 | tf_op jit(solution)/shard_map/all_gather | solution.py:1608
  330.9 7.1 %multiply_convert_fusion.1 = (bf16[1024,512]{1,0:T(8,128)(2,1)S(1)}, bf16[1024,512]{1,0:T(8,128)(2,1)S(1)}) fusion(f32[1024,1024]{1,0:T(8,128)} %copy-done.6, bf16[1024,2048]{1,0:T(8,128)(2,1)} %get-tuple-element.128, bf16[2048,512]{1,0:T(8,128)(2,1)} %all-gather.11.cloned.1.call-done.w_act), kind=kOutput, calls=%fused_computation.45 | convolution fusion | flops 2154299392 | bytes 12582912 | tf_op jit(solution)/shard_map/dot_general | solution.py:32
  341.0 6.4 convolution_convert_fusion
  347.5 52.3 %two_step.1 = (f32[128,2048]{1,0:T(8,128)}, f32[1,2048]{1,0:T(1,128)}, bf16[1024,2048]{1,0:T(8,128)(2,1)}) custom-call(bf16[1024,1024]{1,0:T(8,128)(2,1)} %pad_maximum_fusion.1.left, bf16[2048,1024]{1,0:T(8,128)(2,1)} %all-gather.9.cloned.1.call-done.right, f32[128,2048]{1,0:T(8,128)} %get-tuple-element.131.mid_own, ...), custom_call_target="tpu_custom_call" | custom-call | bytes 150000000 | tf_op jit(solution)/shard_map/two_step/pallas_call | solution.py:1024
  399.8 6.1 convolution_convert_fusion.3
  407.2 5.3 fusion.84
  421.1 9.6 %attend_back.1 = (f32[1024,128]{1,0:T(8,128)}, bf16[4,4,512,128]{3,2,1,0:T(8,128)(2,1)}) custom-call(s32[1]{0:T(128)} %bitcast.base_ref, s32[8]{0:T(128)} %starts_ref.7, bf16[1024,128]{1,0:T(8,128)(2,1)} %copy.95.q_ref, bf16[1024,128]{1,0:T(8,128)(2,1)} %slice.482.do_ref, f32[1024,128]{1,0:T(8,128)} %get-tuple-element.123.o_ref, ...), custom_call_target="tpu_custom_call" | custom-call | flops 5368709120 | bytes 40000000 | tf_op jit(solution)/shard_map/attend_back/pallas_call | solution.py:482
  430.7 2.0 copy.104
  432.7 2.1 fusion.64
  437.0 2.8 collective-permute-done.1
  440.7 7.6 %collective-permute-done.2 = bf16[384,256]{1,0:T(8,128)(2,1)} collective-permute-done((bf16[384,256]{1,0:T(8,128)(2,1)}, bf16[384,256]{1,0:T(8,128)(2,1)}, u32[]{:S(2)}, u32[]{:S(2)}) %collective-permute-start.2) | collective-permute-done | bytes 196640 | tf_op jit(solution)/shard_map/ppermute | solution.py:1550
  448.3 2.0 multiply_add_fusion.1.grad_ref
  450.3 6.3 convolution_convert_fusion.2
  456.7 2.9 dynamic-slice_bitcast_fusion
  466.7 22.4 %ssd_backward.1 = (f32[1024,384]{1,0:T(8,128)}, f32[4,1024,128]{2,1,0:T(8,128)}, f32[1024,128]{1,0:T(8,128)}, f32[8,128]{1,0:T(8,128)}, f32[1,384]{1,0:T(1,128)}) custom-call(s32[1]{0:T(128)} %bitcast.base_ref, s32[8]{0:T(128)} %starts_ref.7, bf16[1024,512]{1,0:T(8,128)(2,1)} %multiply_convert_fusion.3.x_ref, ...), custom_call_target="tpu_custom_call" | custom-call | flops 1610612736 | bytes 80000000 | tf_op jit(solution)/shard_map/ssd_backward/pallas_call | solution.py:325
  490.5 1.8 slice.481
  492.3 2.4 add_convert_fusion.dkv_ref
  494.7 41.5 %reduce_bc.1 = (f32[1024,128]{1,0:T(8,128)}, f32[512,128]{1,0:T(8,128)}, f32[8,512]{1,0:T(8,128)}, bf16[4,128,512]{2,1,0:T(8,128)(2,1)}, bf16[4,128,1024]{2,1,0:T(8,128)(2,1)}) custom-call(f32[4,1024,128]{2,1,0:T(8,128)} %get-tuple-element.149.x_ref, bf16[4,512,128]{2,1,0:T(8,128)(2,1)} %add_convert_fusion.dkv_ref, f32[8,384]{1,0:T(8,128)} %slice.264.dx_ref, ...), custom_call_target="tpu_custom_call" | custom-call | bytes 100000000 | tf_op jit(solution)/shard_map/reduce_bc/pallas_call | solution.py:1024
  538.4 3.7 fusion.49
  542.1 3.8 fusion.6
  545.9 2.7 fusion.18
  548.7 2.1 concatenate.63
  550.8 8.1 %convolution_convert_fusion.1 = bf16[2048,640]{1,0:T(8,128)(2,1)} fusion(bf16[1040,2048]{1,0:T(8,128)(2,1)} %get-tuple-element.110, bf16[1024,640]{1,0:T(8,128)(2,1)} %concatenate.63), kind=kOutput, calls=%fused_computation.1 | convolution fusion | flops 2727608320 | bytes 8192000 | tf_op jit(solution)/shard_map/dot_general | solution.py:36
  560.6 2.1 concatenate.62.left_a
  562.7 3.1 reduce-scatter.12.cloned.1.call-done
  565.8 63.4 %one_step.1 = (f32[256,2048]{1,0:T(8,128)}, f32[256,2048]{1,0:T(8,128)}, f32[1,2048]{1,0:T(1,128)}, bf16[4,128,512]{2,1,0:T(8,128)(2,1)}, bf16[4,128,512]{2,1,0:T(8,128)(2,1)}) custom-call(bf16[1024,640]{1,0:T(8,128)(2,1)} %concatenate.62.left_a, bf16[2048,640]{1,0:T(8,128)(2,1)} %bitcast.82, bf16[1024,512]{1,0:T(8,128)(2,1)} %copy-done.7, ...), custom_call_target="tpu_custom_call" | custom-call | bytes 150000000 | tf_op jit(solution)/shard_map/one_step/pallas_call | solution.py:1024
  630.5 15.4 %sums_step.1 = (f32[2,4,56,128]{3,2,1,0:T(8,128)}, bf16[4,128,640]{2,1,0:T(8,128)(2,1)}) custom-call(f32[56,128]{1,0:T(8,128)} %pad.41.v_ref, bf16[4,128,640]{2,1,0:T(8,128)(2,1)} %bitcast.90), custom_call_target="tpu_custom_call" | custom-call | bytes 150000000 | tf_op jit(solution)/shard_map/sums_step/pallas_call | solution.py:1024
  651.7 5.3 unpack.1
  658.6 3.3 copy.118
  (191 shorter events, 64.2 us)
Async XLA Ops:
  7.2 2.9 copy-start
  7.2 184.3 %all-gather.5.cloned.1.call-start = ((), (), s32[]{:S(2)}) async-start(), calls=%async_computation.5 | async-start | bytes 2621440 | tf_op jit(solution)/shard_map/all_gather | solution.py:1608
  85.4 2.2 copy-start.8
  85.4 133.7 %all-gather.7.cloned.1.call-start = ((), (), s32[]{:S(2)}) async-start(), calls=%async_computation.6 | async-start | bytes 2621440 | tf_op jit(solution)/shard_map/all_gather | solution.py:1608
  86.1 198.9 %all-gather.9.cloned.1.call-start = ((), (), s32[]{:S(2)}) async-start(), calls=%async_computation.7 | async-start | bytes 5242880 | tf_op jit(solution)/shard_map/all_gather | solution.py:1608
  86.9 244.1 %all-gather.11.cloned.1.call-start = ((), (), s32[]{:S(2)}) async-start(), calls=%async_computation.8 | async-start | bytes 2621440 | tf_op jit(solution)/shard_map/all_gather | solution.py:1608
  87.5 312.4 %reduce-scatter.6.cloned.1.call-start = ((), (), s32[]{:S(2)}) async-start(), calls=%async_computation.9 | async-start | bytes 2621440 | tf_op jit(solution)/shard_map/reduce_scatter | solution.py:1695
  94.7 1.1 copy-start.3
  94.7 1.3 copy-start.29
  94.7 1.9 copy-start.30
  94.7 1.9 copy-start.31
  94.7 3.4 copy-start.25
  94.7 3.6 copy-start.24
  196.8 1.3 copy-start.14
  204.0 9.5 %copy-start.15 = (f32[1040,512]{1,0:T(8,128)S(1)}, f32[1040,512]{1,0:T(8,128)}, u32[]{:S(2)}) copy-start(f32[1040,512]{1,0:T(8,128)} %copy-done.14) | copy-start | bytes 6389764
  204.0 9.5 %copy-start.19 = (f32[1024,384]{1,0:T(8,128)S(1)}, f32[1024,384]{1,0:T(8,128)}, u32[]{:S(2)}) copy-start(f32[1024,384]{1,0:T(8,128)} %get-tuple-element.120) | copy-start | bytes 4718596
  217.1 0.9 copy-start.21
  292.5 2.0 copy-start.6
  294.5 2.6 copy-start.27
  295.2 1.0 copy-start.5
  300.9 165.8 %reduce-scatter.8.cloned.1.call-start = ((), (), s32[]{:S(2)}) async-start(), calls=%async_computation.10 | async-start | bytes 5242880 | tf_op jit(solution)/shard_map/reduce_scatter | solution.py:1695
  338.1 3.0 copy-start.28
  347.4 215.3 %reduce-scatter.10.cloned.1.call-start = ((), (), s32[]{:S(2)}) async-start(), calls=%async_computation.11 | async-start | bytes 2621440 | tf_op jit(solution)/shard_map/reduce_scatter | solution.py:1695
  406.0 159.8 %reduce-scatter.12.cloned.1.call-start = ((), (), s32[]{:S(2)}) async-start(), calls=%async_computation.12 | async-start | bytes 2621440 | tf_op jit(solution)/shard_map/reduce_scatter | solution.py:1695
  407.2 6.1 copy-start.16
  407.2 6.1 copy-start.18
  413.3 2.8 copy-start.20
  413.3 2.8 copy-start.22
  415.0 1.1 copy-start.2
  417.2 22.6 %collective-permute-start.1 = (bf16[384,256]{1,0:T(8,128)(2,1)}, bf16[384,256]{1,0:T(8,128)(2,1)}, u32[]{:S(2)}, u32[]{:S(2)}) collective-permute-start(bf16[384,256]{1,0:T(8,128)(2,1)} %fusion.31), channel_id=1, source_target_pairs={{16,0},{24,8},{17,1},{25,9},{18,2},{26,10},{19,3},{27,11},{20,4},{... | collective-permute-start | bytes 589832 | tf_op jit(solution)/shard_map/ppermute | solution.py:1550
  418.5 22.2 %collective-permute-start = (bf16[384,256]{1,0:T(8,128)(2,1)}, bf16[384,256]{1,0:T(8,128)(2,1)}, u32[]{:S(2)}, u32[]{:S(2)}) collective-permute-start(bf16[384,256]{1,0:T(8,128)(2,1)} %fusion.31), channel_id=1, source_target_pairs={{8,0},{16,8},{24,16},{9,1},{17,9},{25,17},{10,2},{18,10},{26,18},{... | collective-permute-start | bytes 589832 | tf_op jit(solution)/shard_map/ppermute | solution.py:1550
  419.8 28.5 %collective-permute-start.2 = (bf16[384,256]{1,0:T(8,128)(2,1)}, bf16[384,256]{1,0:T(8,128)(2,1)}, u32[]{:S(2)}, u32[]{:S(2)}) collective-permute-start(bf16[384,256]{1,0:T(8,128)(2,1)} %fusion.31), channel_id=1, source_target_pairs={{24,0},{25,1},{26,2},{27,3},{28,4},{29,5},{30,6},{31,7}} | collective-permute-start | bytes 589832 | tf_op jit(solution)/shard_map/ppermute | solution.py:1550
  437.0 13.3 %copy-start.7 = (bf16[1024,512]{1,0:T(8,128)(2,1)}, bf16[1024,512]{1,0:T(8,128)(2,1)S(1)}, u32[]{:S(2)}) copy-start(bf16[1024,512]{1,0:T(8,128)(2,1)S(1)} %pad_maximum_fusion.4.left_b) | copy-start | bytes 3145732
  456.7 173.9 %reduce-scatter.14.cloned.1.call-start = ((), (), s32[]{:S(2)}) async-start(), calls=%async_computation.13 | async-start | bytes 3276800 | tf_op jit(solution)/shard_map/reduce_scatter | solution.py:1695
  459.6 32.6 %collective-permute-start.5 = (bf16[4,512,128]{2,1,0:T(8,128)(2,1)}, bf16[4,512,128]{2,1,0:T(8,128)(2,1)}, u32[]{:S(2)}, u32[]{:S(2)}) collective-permute-start(bf16[4,512,128]{2,1,0:T(8,128)(2,1)} %get-tuple-element.291), channel_id=1, source_target_pairs={{0,6},{2,4},{4,2},{6,0},{1,7},{3,5},{5,3},{7,1},{8,14},{10,12},{12... | collective-permute-start | bytes 1572872 | tf_op jit(solution)/shard_map/ppermute | solution.py:1728
  461.3 31.0 %collective-permute-start.4 = (bf16[4,512,128]{2,1,0:T(8,128)(2,1)}, bf16[4,512,128]{2,1,0:T(8,128)(2,1)}, u32[]{:S(2)}, u32[]{:S(2)}) collective-permute-start(bf16[4,512,128]{2,1,0:T(8,128)(2,1)} %get-tuple-element.292), channel_id=1, source_target_pairs={{0,4},{2,6},{4,0},{6,2},{1,5},{3,7},{5,1},{7,3},{8,12},{10,14},{12... | collective-permute-start | bytes 1572872 | tf_op jit(solution)/shard_map/ppermute | solution.py:1728
  462.5 29.8 %collective-permute-start.3 = (bf16[4,512,128]{2,1,0:T(8,128)(2,1)}, bf16[4,512,128]{2,1,0:T(8,128)(2,1)}, u32[]{:S(2)}, u32[]{:S(2)}) collective-permute-start(bf16[4,512,128]{2,1,0:T(8,128)(2,1)} %get-tuple-element.293), channel_id=1, source_target_pairs={{0,2},{2,0},{4,6},{6,4},{1,3},{3,1},{5,7},{7,5},{8,10},{10,8},{12,... | collective-permute-start | bytes 1572872 | tf_op jit(solution)/shard_map/ppermute | solution.py:1728
  466.7 25.5 %copy-start.13 = (bf16[4,512,128]{2,1,0:T(8,128)(2,1)S(1)}, bf16[4,512,128]{2,1,0:T(8,128)(2,1)}, u32[]{:S(2)}) copy-start(bf16[4,512,128]{2,1,0:T(8,128)(2,1)} %get-tuple-element.150) | copy-start | bytes 1572868
  536.2 5.9 copy-start.4
  536.2 5.9 copy-start.17
  545.9 2.8 copy-start.9
  545.9 2.8 copy-start.10
  545.9 2.8 copy-start.11
  558.9 1.4 copy-start.26
  565.8 63.4 %copy-start.23 = (f32[1,2048]{1,0:T(1,128)S(1)}, f32[1,2048]{1,0:T(1,128)}, u32[]{:S(2)}) copy-start(f32[1,2048]{1,0:T(1,128)} %get-tuple-element.168) | copy-start | bytes 24580
  658.6 3.3 copy-start.12
  658.6 4.6 copy-start.1
Sparse Core Ops, SparseCore 0:
  85.5 48.8 all-gather.4
  136.0 60.1 all-gather.6
  197.8 87.1 all-gather.8
  286.4 44.4 all-gather.10
  333.1 42.5 reduce-scatter.5
  378.0 88.7 reduce-scatter.7
  469.0 49.7 reduce-scatter.9
  521.2 44.5 reduce-scatter.11
  568.1 51.4 reduce-scatter.13

commit v6 on v5

--- a/solution.py
+++ b/solution.py
@@ -577,10 +577,12 @@
 
 
 def unpack_kernel(
-    a_ref, b_ref, c_ref, d_ref, e_ref,
+    a_ref, b_ref, c_ref, d_ref, e_ref, row_ref, grow_ref,
     x_ref, bc_ref, k_ref, v_ref, dt_ref, q_ref, z_ref, mout_ref, aout_ref, gate_ref, up_ref,
-    down_ref,
+    down_ref, row_out, grow_out,
 ):
+    row_out[...] = row_ref[...]
+    grow_out[...] = grow_ref[...]
     n_p, rows = a_ref.shape[0], a_ref.shape[1]
     xw, bw, kw = x_ref.shape[1] // n_p, bc_ref.shape[1] // (2 * n_p), HDIM // n_p
     n_heads, ff, aw = dt_ref.shape[1] // n_p, gate_ref.shape[1] // n_p, q_ref.shape[1] // n_p
@@ -610,8 +612,8 @@
     vm = pl.BlockSpec(memory_space=pltpu.VMEM)
     return pl.pallas_call(
         unpack_kernel,
-        in_specs=[vm] * 5,
-        out_specs=[vm] * 12,
+        in_specs=[vm] * 7,
+        out_specs=[vm] * 14,
         out_shape=[jax.ShapeDtypeStruct(w.shape, f32) for w in like],
         compiler_params=pltpu.CompilerParams(vmem_limit_bytes=VMEM_LIMIT),
         cost_estimate=pl.CostEstimate(flops=0, bytes_accessed=10_000_000, transcendentals=0),
@@ -655,7 +657,7 @@
 HOPS = (3, 1, 2)
 
 
-def z_chain(ref, up_sems, down_sems):
+def z_chain(ref, up_sems, down_sems, since=0):
     z, p, c = place()
     nz = ref.shape[0]
 
@@ -689,7 +691,7 @@
         ).wait_recv()
 
     def stage(k):
-        if k:
+        if k > since:
 
             @pl.when(z - k >= 0)
             def _():
@@ -699,7 +701,7 @@
         def _():
             block_up(k).start()
 
-        if k:
+        if k > since:
 
             @pl.when(z + k < nz)
             def _():
@@ -710,7 +712,7 @@
             block_down(k).start()
 
     def done():
-        for k in range(nz):
+        for k in range(since, nz):
 
             @pl.when((z - k >= 0) & (z + 1 < nz))
             def _():
@@ -721,6 +723,46 @@
                 block_down(k).wait_send()
 
     return stage, done
+
+
+def z_hop(ref, k, sems):
+    z, p, c = place()
+    nz = ref.shape[0]
+
+    def move(slot, i, to):
+        return pltpu.make_async_remote_copy(
+            src_ref=ref.at[slot], dst_ref=ref.at[slot], send_sem=sems.at[0, i],
+            recv_sem=sems.at[1, i], device_id=chip(to, p, c), device_id_type=MESH,
+        )
+
+    goes_up, goes_down = (z - k >= 0) & (z + 1 < nz), (z + k < nz) & (z > 0)
+
+    @pl.when(goes_up)
+    def _():
+        move(z - k, 0, z + 1).start()
+
+    @pl.when(goes_down)
+    def _():
+        move(z + k, 1, z - 1).start()
+
+    def end():
+        @pl.when(z - k - 1 >= 0)
+        def _():
+            move(z - k - 1, 0, z - 1).wait_recv()
+
+        @pl.when(z + k + 1 < nz)
+        def _():
+            move(z + k + 1, 1, z + 1).wait_recv()
+
+        @pl.when(goes_up)
+        def _():
+            move(z - k, 0, z + 1).wait_send()
+
+        @pl.when(goes_down)
+        def _():
+            move(z + k, 1, z - 1).wait_send()
+
+    return end
 
 
 def share(block, part, far_sems, near_sems, own_sems=None):
@@ -859,11 +901,19 @@
 
 
 def mid_kernel(
-    left, right, resid, gain, mid_ref, full_ref,
+    left, right, resid, gain, e_given, mid_ref, full_ref, e_ref,
     part, keep, sib_out, sib_in, out, relay, came, n_sems, f_sems, own_sems, far_sems, near_sems,
+    up_sems, down_sems,
 ):
-    greet()
     z, p, c = place()
+    nz = e_ref.shape[0]
+    meet(
+        [chip(z, p, 1 - c)]
+        + [chip(z, hop(p, d), c) for d in HOPS]
+        + [chip(lax.rem(z + d, nz), p, c) for d in (1, nz - 1)]
+    )
+    stage, chain_done = z_chain(e_ref, up_sems, down_sems, 2)
+    stage(2)
     half = keep.shape[1]
     total_rows, middle, finish, done = reduce_blocks(
         [(left, right)], part, keep, sib_out, sib_in, out, relay, came, n_sems, f_sems
@@ -881,8 +931,11 @@
 
     share_middle, share_end = share_rows(full_ref, half, own_sems, far_sems, near_sems)
     share_middle()
+    for k in range(3, nz):
+        stage(k)
     done()
     share_end()
+    chain_done()
 
 
 def two_kernel(
@@ -1036,14 +1089,28 @@
     )(*args, *moved)
 
 
-def mid_step(mixed, w, resid_own, gain):
+def mid_step(mixed, w, resid_own, gain, piece):
     tok, width = mixed.shape[0], w.shape[0]
-    half = resid_own.shape[0]
-    return plane_call(
-        mid_kernel, "mid_step", 1, (mixed, w, resid_own, gain),
-        [((half, width), f32), ((tok, width), bf16)],
-        reduce_scratch(half, width) + SHARE_SEMS,
-    )
+    half, nz = resid_own.shape[0], piece.shape[0]
+    return pl.pallas_call(
+        mid_kernel,
+        in_specs=[VM] * 4 + [ANYWHERE],
+        out_specs=[VM] * 2 + [ANYWHERE],
+        out_shape=[
+            jax.ShapeDtypeStruct((half, width), f32),
+            jax.ShapeDtypeStruct((tok, width), bf16),
+            jax.ShapeDtypeStruct(piece.shape, bf16),
+        ],
+        scratch_shapes=reduce_scratch(half, width)
+        + SHARE_SEMS
+        + [pltpu.SemaphoreType.DMA((2, nz))] * 2,
+        input_output_aliases={4: 2},
+        compiler_params=pltpu.CompilerParams(
+            collective_id=1, has_side_effects=True, vmem_limit_bytes=VMEM_LIMIT
+        ),
+        cost_estimate=pl.CostEstimate(flops=0, bytes_accessed=150_000_000, transcendentals=0),
+        name="mid_step",
+    )(mixed, w, resid_own, gain, piece)
 
 
 def two_step(d_gu, w, mid_own, grad_own, gain):
@@ -1209,8 +1276,8 @@
 
 
 def gather_bc_kernel(
-    x_ref, kv_ref, grad_ref, full_ref, kvz_ref, g_ref,
-    far_sems, near_sems, z_sems, own_g, far_g, near_g,
+    x_ref, kv_ref, grad_ref, e_ref, full_ref, kvz_ref, g_ref, e_out,
+    far_sems, near_sems, z_sems, e_sems, loc_sems, own_g, far_g, near_g,
 ):
     z, p, c = place()
     nz = kvz_ref.shape[0]
@@ -1220,6 +1287,8 @@
         + [chip(z, hop(p, d), c) for d in HOPS]
         + [chip(lax.rem(z + d, nz), p, c) for d in range(1, nz)]
     )
+    local = pltpu.make_async_copy(e_ref, e_out.at[z], loc_sems.at[0])
+    local.start()
     kvz_ref[z] = kv_ref[...]
 
     def up(d):
@@ -1241,6 +1310,8 @@
         lambda q, i: full_ref.at[q, at_rows(c * half + i * (half // 2), half // 2), :],
         far_sems, near_sems,
     )
+    local.wait()
+    e_end = z_hop(e_out, 0, e_sems)
     bc_middle()
     g_half = grad_ref.shape[0]
     g_ref[at_rows((p * 2 + c) * g_half, g_half), :] = grad_ref[...].astype(bf16)
@@ -1262,9 +1333,10 @@
             up(d).wait_send()
 
     g_end()
-
-
-def gather_bc(x, at, n_p, kv, nz, grad):
+    e_end()
+
+
+def gather_bc(x, at, n_p, kv, nz, grad, piece):
     tok = x.shape[0]
     dma = pltpu.SemaphoreType.DMA
     whole = lambda s: pl.BlockSpec(s, lambda i: (0,) * len(s))
@@ -1272,28 +1344,32 @@
         gather_bc_kernel,
         grid=(1,),
         in_specs=[
-            pl.BlockSpec((tok, 128), lambda i: (0, at)), whole(kv.shape), whole(grad.shape)
+            pl.BlockSpec((tok, 128), lambda i: (0, at)), whole(kv.shape), whole(grad.shape),
+            whole(piece.shape),
         ],
         out_specs=[
-            whole((n_p, tok, 128)), whole((nz,) + kv.shape), whole((tok, grad.shape[1]))
+            whole((n_p, tok, 128)), whole((nz,) + kv.shape), whole((tok, grad.shape[1])),
+            ANYWHERE,
         ],
         out_shape=[
             jax.ShapeDtypeStruct((n_p, tok, 128), bf16),
             jax.ShapeDtypeStruct((nz,) + kv.shape, bf16),
             jax.ShapeDtypeStruct((tok, grad.shape[1]), bf16),
+            jax.ShapeDtypeStruct((nz,) + piece.shape, bf16),
         ],
-        scratch_shapes=[dma((2, 4)), dma((2, 3)), dma((2, nz - 1))] + SHARE_SEMS,
+        scratch_shapes=[dma((2, 4)), dma((2, 3)), dma((2, nz - 1)), dma((2, 2)), dma((1,))]
+        + SHARE_SEMS,
         compiler_params=pltpu.CompilerParams(
             collective_id=5, has_side_effects=True, vmem_limit_bytes=VMEM_LIMIT
         ),
         cost_estimate=pl.CostEstimate(flops=0, bytes_accessed=40_000_000, transcendentals=0),
         name="gather_bc",
-    )(x, kv, grad)
+    )(x, kv, grad, piece)
 
 
 def carry_kernel(
-    state_ref, rate_ref, kvz_ref, in_ref, kv_ref, rates_ref,
-    low, came, factor, s_sems, r_sems, p_sems,
+    state_ref, rate_ref, kvz_ref, e_given, in_ref, kv_ref, rates_ref, e_ref,
+    low, came, factor, s_sems, r_sems, p_sems, e_sems,
 ):
     z, p, c = place()
     nz = kvz_ref.shape[0]
@@ -1318,6 +1394,7 @@
         def _():
             up(d).start()
 
+    e_end = z_hop(e_ref, 1, e_sems)
     kv_ref[p] = kvz_ref[...]
     kv_middle, kv_end = share(
         lambda q: kv_ref.at[q],
@@ -1347,24 +1424,37 @@
             up(d).wait_send()
 
     kv_end()
+    e_end()
     for copy in rates:
         copy.wait_send()
 
 
-def carry_step(state, rate, kvz, n_p):
+def carry_step(state, rate, kvz, n_p, piece):
     nz = kvz.shape[0]
     dma = pltpu.SemaphoreType.DMA
-    return plane_call(
-        carry_kernel, "carry_step", 8, (state, rate, kvz),
-        [(state.shape, f32), ((n_p,) + kvz.shape, bf16), ((nz,) + rate.shape, f32)],
-        [
+    return pl.pallas_call(
+        carry_kernel,
+        in_specs=[VM] * 3 + [ANYWHERE],
+        out_specs=[VM] * 3 + [ANYWHERE],
+        out_shape=[
+            jax.ShapeDtypeStruct(state.shape, f32),
+            jax.ShapeDtypeStruct((n_p,) + kvz.shape, bf16),
+            jax.ShapeDtypeStruct((nz,) + rate.shape, f32),
+            jax.ShapeDtypeStruct(piece.shape, bf16),
+        ],
+        scratch_shapes=[
             pltpu.VMEM(state.shape, bf16),
             pltpu.VMEM((nz - 1,) + state.shape, bf16),
             pltpu.VMEM(rate.shape, f32),
-            dma((2, nz - 1)), dma((2, nz - 1)), dma((2, 4)),
+            dma((2, nz - 1)), dma((2, nz - 1)), dma((2, 4)), dma((2, 2)),
         ],
-        nbytes=80_000_000,
-    )
+        input_output_aliases={3: 3},
+        compiler_params=pltpu.CompilerParams(
+            collective_id=8, has_side_effects=True, vmem_limit_bytes=VMEM_LIMIT
+        ),
+        cost_estimate=pl.CostEstimate(flops=0, bytes_accessed=80_000_000, transcendentals=0),
+        name="carry_step",
+    )(state, rate, kvz, piece)
 
 
 def reduce_bc_kernel(n, x_ref, dkv_ref, dx_ref, slope_ref, *refs):
@@ -1616,7 +1706,7 @@
     w_a = w_a.reshape(nz * n_p * rows, w_a.shape[3])
     gains = gains.transpose(2, 1, 0, 3)[:, :, :, :rows].reshape(8, 1, width)
     gain_mix, gain_ffn = gains[0], gains[1]
-    w_b, w_c, w_d, w_e = [along_z(piece) for piece in rest]
+    w_b, w_c, w_d = [along_z(piece) for piece in rest[:3]]
 
     in_ext = product(normed_one, w_a)
     in_b = product(normed_one, w_b)[:tok]
@@ -1649,7 +1739,9 @@
     val_own = in_a[:, cw + kw : cw + 2 * kw]
     kv_own = jnp.concatenate([key_own, val_own], axis=1).astype(bf16)
     kv_own = jnp.concatenate([kv_own[: tok // 2], kv_own[tok // 2 :]], axis=1)
-    bc_all, kvz, g_ffn = gather_bc(ssm, xw // 128, n_p, kv_own, nz, grad_own)
+    bc_all, kvz, g_ffn, w_e = gather_bc(
+        ssm, xw // 128, n_p, kv_own, nz, grad_own, rest[3]
+    )
     cos_q, sin_q = rope_tables(positions, jnp.arange(HDIM // 2))
     cos_q, sin_q = cos_q.reshape(tok, n_p, hk), sin_q.reshape(tok, n_p, hk)
 
@@ -1667,7 +1759,7 @@
         base_arr, doc_starts, ssm, bc_all, dt_pre, neg_rate, skip_full
     )
     rate = jnp.broadcast_to(dev_decay[tok - 1 :], (8, 128))
-    in_state, kv, rates = carry_step(local_state, rate, kvz, n_p)
+    in_state, kv, rates, w_e = carry_step(local_state, rate, kvz, n_p, w_e)
 
     attn_f32, lse, keys, values = attend(base_arr, doc_starts, queries, kv)
     attn_low = attn_f32.astype(bf16)
@@ -1676,7 +1768,8 @@
     gated = (y_flat * silu_z).astype(bf16)
     mixed = jnp.concatenate([gated, attn_low], axis=1)
 
-    mid_own, normed_two = mid_step(mixed, w_c, hidden_own, gain_ffn)
+    mid_own, normed_two, w_e = mid_step(mixed, w_c, hidden_own, gain_ffn, w_e)
+    w_e = w_e.reshape(width, -1)
     gu = product(normed_two, w_d)
     ffw = gu.shape[1] // 2
     gate_val, up_val = gu[:, :ffw], gu[:, ffw:]
@@ -1787,9 +1880,10 @@
     s_bc = s_bc[:, :, xw:].reshape(n_p, edge + 1, 2, bw).transpose(1, 2, 0, 3)
     s_bc = s_bc.reshape(edge + 1, 2 * n_p * bw)
 
-    g_x, g_bc, g_k, g_v, g_dt, g_q, g_z, g_mout, g_aout, g_gate, g_up, g_down = unpack(
-        (ga, gb, gc, gd, ge), weights
-    )
+    (
+        g_x, g_bc, g_k, g_v, g_dt, g_q, g_z, g_mout, g_aout, g_gate, g_up, g_down, block_out,
+        grad_in,
+    ) = unpack((ga, gb, gc, gd, ge, block_out, grad_in), weights + (block_out, grad_in))
     return (
         block_out,
         grad_in,

time: 679 us -> 662 us (0.975)
  waiting for transfers between devices: 60.7 us -> 28.5 us
  Pallas kernels: 420 us -> 452 us
  local copies, waits for them, and re-layouts: 58.1 us -> 48.5 us
    pallas_call x1 -> x3, Pallas kernels: 5.32 us -> 117 us  [the longest x1 75.1 us: mid_step(): pl.pallas_call(mid_kernel, in_specs=[VM] * 4 + [ANYWHERE], out_specs=[VM]...]
    pallas_call x6 -> x4, Pallas kernels: 256 us -> 170 us  [plane_call(): pl.pallas_call(kernel, in_specs=[VM] * (len(args) + n), out_specs=[VM] *...]
    all_gather x4 -> x3, waiting for transfers between devices: 43.6 us -> 0.04 us  [along_z(): return lax.all_gather(piece, 'z', axis=0, tiled=True)]
    ppermute x3, waiting for transfers between devices: 11.3 us -> 18.2 us  [carry_back(): lax.ppermute(low, 'z', [(i, i - d) for i in range(d, nz)]).astype(f32)]
    unnamed x68 -> x86, local copies, waits for them, and re-layouts: 17.2 us -> 14.6 us
  transfers between devices with their start and end apart: 15 -> 14, of which waited for: 7 -> 4; matrix products, arithmetic and copies ran while one was open for 21% -> 18% of each run, Pallas kernels for 49% -> 54%
where the time goes in v6:
time: 662 us; the launch traced here: 653 us
  Pallas kernels  452 us (68%)
  matrix products  66.8 us (10%)
  local copies, waits for them, and re-layouts  48.5 us (7%)
  other arithmetic  33.8 us (5%)
  waiting for transfers between devices  28.5 us (4%)
  between operations  15.5 us (2%)
  starting transfers between devices  8.06 us (1%)
    pallas_call x4, Pallas kernels, plane_call(): pl.pallas_call(kernel, in_specs=[VM] * (len(args) + n), out_specs=[VM] *...  170 us
    pallas_call x1, Pallas kernels, mid_step(): pl.pallas_call(mid_kernel, in_specs=[VM] * 4 + [ANYWHERE], out_specs=[VM]...  75.1 us
    pallas_call x1, Pallas kernels, open_step(): pl.pallas_call(functools.partial(open_kernel, n), in_specs=[VM] * (n + 3)...  68.7 us
    pallas_call x1, Pallas kernels, gather_bc(): pl.pallas_call(gather_bc_kernel, grid=(1,), in_specs=[pl.BlockSpec((tok,...  35.8 us
    pallas_call x1, Pallas kernels, carry_step(): pl.pallas_call(carry_kernel, in_specs=[VM] * 3 + [ANYWHERE], out_specs=[V...  34 us
    dot_general x5, matrix products, product(): return jnp.dot(left, right, preferred_element_type=f32)  32 us
    dot_general x6, matrix products, product_t(): lax.dot_general(left, right, (((0,), (0,)), ((), ())), preferred_element_...  31.6 us
    pallas_call x1, Pallas kernels, ssd_backward(): pl.pallas_call(functools.partial(ssd_backward_kernel, n_heads), grid=(nsp...  22.4 us
  transfers between devices with their start and end apart: 14, of which 4 were waited for; matrix products, arithmetic and copies ran while one was open for 18% of the time, Pallas kernels for 54%

profile of v6, /device:TPU:0, one launch (start us, length us, event | category | flops | bytes accessed | tf_op | source)
XLA Modules:
  0.0 652.8 jit_solution(18416501820663636375)
XLA Ops:
  7.3 1.6 copy.93.dt_ref
  11.2 5.5 pack.1
  16.7 68.7 %open_step.1 = (f32[4,4,8,128]{3,2,1,0:T(8,128)}, bf16[1040,2048]{1,0:T(8,128)(2,1)}, bf16[4,4,128,640]{3,2,1,0:T(8,128)(2,1)}, bf16[4,128,512]{2,1,0:T(8,128)(2...) custom-call(f32[128,2048]{1,0:T(8,128)} %constant_dynamic-slice_fusion.7.refs_0_.resi, ...), custom_call_target="tpu_custom_call" | custom-call | bytes 250000000 | tf_op jit(solution)/shard_map/open_step/pallas_call | solution.py:1254
  86.9 8.0 %fusion.81 = (bf16[1040,640]{1,0:T(8,128)(2,1)S(1)}, f32[1040,640]{1,0:T(8,128)}) fusion(bf16[1040,2048]{1,0:T(8,128)(2,1)} %get-tuple-element.115, bf16[2048,640]{1,0:T(8,128)(2,1)} %bitcast.84), kind=kOutput, calls=%fused_computation.178 | convolution fusion | flops 2726963200 | bytes 10874880 | tf_op jit(solution)/shard_map/dot_general | solution.py:32
  100.3 3.8 fusion.43
  106.3 3.7 add_multiply_fusion
  111.4 1.5 multiply_convert_fusion.3.x_ref
  112.9 35.8 %gather_bc.1 = (bf16[4,1024,128]{2,1,0:T(8,128)(2,1)}, bf16[4,512,128]{2,1,0:T(8,128)(2,1)}, bf16[1024,2048]{1,0:T(8,128)(2,1)}, bf16[4,4,128,512]{3,2,1,0:T(8,128)(2,1)}) custom-call(bf16[1024,512]{1,0:T(8,128)(2,1)} %multiply_convert_fusion.3.x_ref, bf16[512,128]{1,0:T(8,128)(2,1)} %pad_maximum_fusion.9.kv_ref, ...), custom_call_target="tpu_custom_call" | custom-call | bytes 40000000 | tf_op jit(solution)/shard_map/gather_bc/pallas_call | solution.py:1343
  150.2 13.8 %ssd_forward.1 = (f32[1024,384]{1,0:T(8,128)}, f32[8,384,256]{2,1,0:T(8,128)}, f32[384,256]{1,0:T(8,128)}, f32[1024,128]{1,0:T(8,128)}, f32[1024,384]{1,0:T(8,128)}, /*index=5*/bf16[1024,256]{1,0:T(8,128)(2,1)}) custom-call(s32[1]{0:T(128)} %bitcast.base_ref, s32[8]{0:T(128)} %starts_ref.7, bf16[1024,512]{1,0:T(8,128)(2,1)} %multiply_convert_fusion.3.x_ref, ...), custom_call_target="tpu_custom_call" | custom-call | flops 603979776 | bytes 40000000 | tf_op jit(solution)/shard_map/ssd_forward/pallas_call | solution.py:195
  165.2 34.0 %carry_step.1 = (f32[384,256]{1,0:T(8,128)}, bf16[4,4,512,128]{3,2,1,0:T(8,128)(2,1)}, f32[4,8,128]{2,1,0:T(8,128)}, bf16[4,4,128,512]{3,2,1,0:T(8,128)(2,1)}) custom-call(f32[384,256]{1,0:T(8,128)} %get-tuple-element.122.state_ref, f32[8,128]{1,0:T(8,128)} %broadcast_in_dim.122.rate_ref, ...), custom_call_target="tpu_custom_call", output_to_operand_aliasing={{3}: (3, {})} | custom-call | bytes 80000000 | tf_op jit(solution)/shard_map/carry_step/pallas_call | solution.py:1435
  199.3 5.3 fusion.82
  204.6 1.4 copy-done.19
  208.2 8.5 %attend.1 = (f32[1024,128]{1,0:T(8,128)}, f32[1024,128]{1,0:T(8,128)}, bf16[4096,128]{1,0:T(8,128)(2,1)}, bf16[4096,128]{1,0:T(8,128)(2,1)}) custom-call(s32[1]{0:T(128)} %bitcast.base_ref, s32[8]{0:T(128)} %starts_ref.7, bf16[1024,128]{1,0:T(8,128)(2,1)} %copy.97.q_ref, bf16[4,4,512,128]{3,2,1,0:T(8,128)(2,1)} %get-tuple-element.129.kv_ref), custom_call_target="tpu_custom_call" | custom-call | flops 2147483648 | bytes 30000000 | tf_op jit(solution)/shard_map/attend/pallas_call | solution.py:416
  217.8 3.2 multiply_convert_fusion.6
  222.9 75.1 %mid_step.1 = (f32[128,2048]{1,0:T(8,128)}, bf16[1024,2048]{1,0:T(8,128)(2,1)}, bf16[4,4,128,512]{3,2,1,0:T(8,128)(2,1)}) custom-call(bf16[1024,512]{1,0:T(8,128)(2,1)} %pad_maximum_fusion.3.left, bf16[2048,512]{1,0:T(8,128)(2,1)} %all-gather.6.cloned.1.call-done.right, ...), custom_call_target="tpu_custom_call", output_to_operand_aliasing={{2}: (4, {})} | custom-call | bytes 150000000 | tf_op jit(solution)/shard_map/mid_step/pallas_call | solution.py:1095
  298.0 7.5 %fusion.83 = f32[1024,1024]{1,0:T(8,128)S(1)} fusion(bf16[1024,2048]{1,0:T(8,128)(2,1)} %get-tuple-element.134, bf16[2048,1024]{1,0:T(8,128)(2,1)} %all-gather.8.cloned.1.call-done.right), kind=kOutput, calls=%fused_computation.180 | convolution fusion | flops 4294967296 | bytes 12582912 | tf_op jit(solution)/shard_map/dot_general | solution.py:32
  306.3 1.4 copy-done.9
  308.2 1.4 copy-done.37
  309.6 3.7 convolution_convert_fusion.4
  313.6 1.3 copy-done.2
  315.0 6.5 multiply_convert_fusion.1
  321.5 1.6 pad_maximum_fusion.1.left
  324.4 6.3 convolution_convert_fusion
  330.8 53.2 %two_step.1 = (f32[128,2048]{1,0:T(8,128)}, f32[1,2048]{1,0:T(1,128)}, bf16[1024,2048]{1,0:T(8,128)(2,1)}) custom-call(bf16[1024,1024]{1,0:T(8,128)(2,1)} %pad_maximum_fusion.1.left, bf16[2048,1024]{1,0:T(8,128)(2,1)} %all-gather.8.cloned.1.call-done.right, f32[128,2048]{1,0:T(8,128)} %get-tuple-element.139.mid_own, ...), custom_call_target="tpu_custom_call" | custom-call | bytes 150000000 | tf_op jit(solution)/shard_map/two_step/pallas_call | solution.py:1077
  384.1 5.9 convolution_convert_fusion.3
  391.6 4.7 fusion.84
  397.1 1.7 multiply_convert_fusion.4
  403.9 9.6 %attend_back.1 = (f32[1024,128]{1,0:T(8,128)}, bf16[4,4,512,128]{3,2,1,0:T(8,128)(2,1)}) custom-call(s32[1]{0:T(128)} %bitcast.base_ref, s32[8]{0:T(128)} %starts_ref.7, bf16[1024,128]{1,0:T(8,128)(2,1)} %copy.97.q_ref, bf16[1024,128]{1,0:T(8,128)(2,1)} %slice.482.do_ref, f32[1024,128]{1,0:T(8,128)} %get-tuple-element.130.o_ref, ...), custom_call_target="tpu_custom_call" | custom-call | flops 5368709120 | bytes 40000000 | tf_op jit(solution)/shard_map/attend_back/pallas_call | solution.py:482
  416.3 8.0 %collective-permute-done.1 = bf16[384,256]{1,0:T(8,128)(2,1)} collective-permute-done((bf16[384,256]{1,0:T(8,128)(2,1)}, bf16[384,256]{1,0:T(8,128)(2,1)}, u32[]{:S(2)}, u32[]{:S(2)}) %collective-permute-start.1) | collective-permute-done | bytes 196640 | tf_op jit(solution)/shard_map/ppermute | solution.py:1640
  425.2 9.3 %collective-permute-done.2 = bf16[384,256]{1,0:T(8,128)(2,1)} collective-permute-done((bf16[384,256]{1,0:T(8,128)(2,1)}, bf16[384,256]{1,0:T(8,128)(2,1)}, u32[]{:S(2)}, u32[]{:S(2)}) %collective-permute-start.2) | collective-permute-done | bytes 196640 | tf_op jit(solution)/shard_map/ppermute | solution.py:1640
  434.5 2.1 multiply_add_fusion.1.grad_ref
  436.6 6.4 convolution_convert_fusion.2
  443.1 1.6 copy-done.17
  444.6 1.4 dynamic-slice_bitcast_fusion
  447.8 1.7 collective-permute-start.3
  452.5 22.4 %ssd_backward.1 = (f32[1024,384]{1,0:T(8,128)}, f32[4,1024,128]{2,1,0:T(8,128)}, f32[1024,128]{1,0:T(8,128)}, f32[8,128]{1,0:T(8,128)}, f32[1,384]{1,0:T(1,128)}) custom-call(s32[1]{0:T(128)} %bitcast.base_ref, s32[8]{0:T(128)} %starts_ref.7, bf16[1024,512]{1,0:T(8,128)(2,1)} %multiply_convert_fusion.3.x_ref, ...), custom_call_target="tpu_custom_call" | custom-call | flops 1610612736 | bytes 80000000 | tf_op jit(solution)/shard_map/ssd_backward/pallas_call | solution.py:325
  478.4 38.3 %reduce_bc.1 = (f32[1024,128]{1,0:T(8,128)}, f32[512,128]{1,0:T(8,128)}, f32[8,512]{1,0:T(8,128)}, bf16[4,128,512]{2,1,0:T(8,128)(2,1)}, bf16[4,128,1024]{2,1,0:T(8,128)(2,1)}) custom-call(f32[4,1024,128]{2,1,0:T(8,128)} %get-tuple-element.157.x_ref, bf16[4,512,128]{2,1,0:T(8,128)(2,1)} %add_convert_fusion.dkv_ref, f32[8,384]{1,0:T(8,128)} %slice.264.dx_ref, ...), custom_call_target="tpu_custom_call" | custom-call | bytes 100000000 | tf_op jit(solution)/shard_map/reduce_bc/pallas_call | solution.py:1077
  518.9 2.8 fusion.49
  521.8 2.7 fusion.6
  524.5 2.7 fusion.18
  527.3 2.1 concatenate.63
  529.3 8.1 %convolution_convert_fusion.1 = bf16[2048,640]{1,0:T(8,128)(2,1)} fusion(bf16[1040,2048]{1,0:T(8,128)(2,1)} %get-tuple-element.115, bf16[1024,640]{1,0:T(8,128)(2,1)} %concatenate.63), kind=kOutput, calls=%fused_computation.1 | convolution fusion | flops 2727608320 | bytes 8192000 | tf_op jit(solution)/shard_map/dot_general | solution.py:36
  539.1 2.1 concatenate.62.left_a
  541.2 8.7 %reduce-scatter.12.cloned.1.call-done = bf16[512,512]{1,0:T(8,128)(2,1)} async-done(((bf16[2048,512]{1,0:T(8,128)(2,1)}), bf16[512,512]{1,0:T(8,128)(2,1)}) %reduce-scatter.12.cloned.1.call-update) | async-done | bytes 524304 | tf_op jit(solution)/shard_map/reduce_scatter | solution.py:1788
  549.9 63.4 %one_step.1 = (f32[256,2048]{1,0:T(8,128)}, f32[256,2048]{1,0:T(8,128)}, f32[1,2048]{1,0:T(1,128)}, bf16[4,128,512]{2,1,0:T(8,128)(2,1)}, bf16[4,128,512]{2,1,0:T(8,128)(2,1)}) custom-call(bf16[1024,640]{1,0:T(8,128)(2,1)} %concatenate.62.left_a, bf16[2048,640]{1,0:T(8,128)(2,1)} %bitcast.85, bf16[1024,512]{1,0:T(8,128)(2,1)} %copy-done.10, ...), custom_call_target="tpu_custom_call" | custom-call | bytes 150000000 | tf_op jit(solution)/shard_map/one_step/pallas_call | solution.py:1077
  614.7 15.4 %sums_step.1 = (f32[2,4,56,128]{3,2,1,0:T(8,128)}, bf16[4,128,640]{2,1,0:T(8,128)(2,1)}) custom-call(f32[56,128]{1,0:T(8,128)} %pad.41.v_ref, bf16[4,128,640]{2,1,0:T(8,128)(2,1)} %bitcast.92), custom_call_target="tpu_custom_call" | custom-call | bytes 150000000 | tf_op jit(solution)/shard_map/sums_step/pallas_call | solution.py:1077
  635.9 8.1 %unpack.1 = (f32[128,1536]{1,0:T(8,128)}, f32[128,512]{1,0:T(8,128)}, f32[128,128]{1,0:T(8,128)}, f32[128,128]{1,0:T(8,128)}, f32[128,24]{1,0:T(8,128)}, /*index...) custom-call(bf16[4,128,640]{2,1,0:T(8,128)(2,1)} %get-tuple-element., ...), custom_call_target="tpu_custom_call" | custom-call | bytes 10000000 | tf_op jit(solution)/shard_map/unpack/pallas_call | solution.py:613
  644.0 1.5 copy.111
  (206 shorter events, 54.0 us)
Async XLA Ops:
  7.2 2.9 copy-start
  7.2 192.1 %all-gather.4.cloned.1.call-start = ((), (), s32[]{:S(2)}) async-start(), calls=%async_computation.5 | async-start | bytes 2621440 | tf_op jit(solution)/shard_map/all_gather | solution.py:1698
  85.4 137.5 %all-gather.6.cloned.1.call-start = ((), (), s32[]{:S(2)}) async-start(), calls=%async_computation.6 | async-start | bytes 2621440 | tf_op jit(solution)/shard_map/all_gather | solution.py:1698
  86.2 211.9 %all-gather.8.cloned.1.call-start = ((), (), s32[]{:S(2)}) async-start(), calls=%async_computation.7 | async-start | bytes 5242880 | tf_op jit(solution)/shard_map/all_gather | solution.py:1698
  86.9 297.2 %reduce-scatter.6.cloned.1.call-start = ((), (), s32[]{:S(2)}) async-start(), calls=%async_computation.8 | async-start | bytes 2621440 | tf_op jit(solution)/shard_map/reduce_scatter | solution.py:1788
  94.9 9.2 %copy-start.6 = (bf16[1040,640]{1,0:T(8,128)(2,1)}, bf16[1040,640]{1,0:T(8,128)(2,1)S(1)}, u32[]{:S(2)}) copy-start(bf16[1040,640]{1,0:T(8,128)(2,1)S(1)} %get-tuple-element.333) | copy-start | bytes 3993604
  94.9 4.3 copy-start.35
  95.0 5.2 copy-start.34
  99.2 6.1 copy-start.28
  112.9 35.8 %copy-start.41 = (f32[24]{0:T(128)S(1)}, f32[24]{0:T(128)}, u32[]{:S(2)}) copy-start(f32[24]{0:T(128)} %param.33) | copy-start | bytes 292
  208.2 9.5 %copy-start.20 = (f32[1040,512]{1,0:T(8,128)S(1)}, f32[1040,512]{1,0:T(8,128)}, u32[]{:S(2)}) copy-start(f32[1040,512]{1,0:T(8,128)} %copy-done.19) | copy-start | bytes 6389764
  208.2 9.6 %copy-start.24 = (f32[1024,384]{1,0:T(8,128)S(1)}, f32[1024,384]{1,0:T(8,128)}, u32[]{:S(2)}) copy-start(f32[1024,384]{1,0:T(8,128)} %get-tuple-element.127) | copy-start | bytes 4718596
  208.2 9.6 %copy-start.29 = (bf16[1024,256]{1,0:T(8,128)(2,1)S(1)}, bf16[1024,256]{1,0:T(8,128)(2,1)}, u32[]{:S(2)}) copy-start(bf16[1024,256]{1,0:T(8,128)(2,1)} %get-tuple-element.121) | copy-start | bytes 1572868
  208.2 9.6 %copy-start.32 = (f32[384,256]{1,0:T(8,128)S(1)}, f32[384,256]{1,0:T(8,128)}, u32[]{:S(2)}) copy-start(f32[384,256]{1,0:T(8,128)} %get-tuple-element.126.in_ref) | copy-start | bytes 1179652
  305.6 2.1 copy-start.9
  305.6 4.1 copy-start.37
  306.3 1.9 copy-start.8
  313.4 139.1 %reduce-scatter.8.cloned.1.call-start = ((), (), s32[]{:S(2)}) async-start(), calls=%async_computation.9 | async-start | bytes 5242880 | tf_op jit(solution)/shard_map/reduce_scatter | solution.py:1788
  321.5 2.9 copy-start.38
  330.8 210.4 %reduce-scatter.10.cloned.1.call-start = ((), (), s32[]{:S(2)}) async-start(), calls=%async_computation.10 | async-start | bytes 2621440 | tf_op jit(solution)/shard_map/reduce_scatter | solution.py:1788
  330.8 53.3 %copy-start.27 = (bf16[1024,384]{1,0:T(8,128)(2,1)S(1)}, bf16[1024,384]{1,0:T(8,128)(2,1)}, u32[]{:S(2)}) copy-start(bf16[1024,384]{1,0:T(8,128)(2,1)} %copy-done.26) | copy-start | bytes 2359300
  390.0 159.9 %reduce-scatter.12.cloned.1.call-start = ((), (), s32[]{:S(2)}) async-start(), calls=%async_computation.11 | async-start | bytes 2621440 | tf_op jit(solution)/shard_map/reduce_scatter | solution.py:1788
  391.6 5.5 copy-start.21
  391.6 5.5 copy-start.23
  397.1 1.7 copy-start.25
  397.1 1.7 copy-start.30
  398.8 14.6 %copy-start.5 = (f32[1024,384]{1,0:T(8,128)}, f32[1024,384]{1,0:T(8,128)S(1)}, u32[]{:S(2)}) copy-start(f32[1024,384]{1,0:T(8,128)S(1)} %get-tuple-element.144.dy_ref) | copy-start | bytes 4718596
  400.0 24.2 %collective-permute-start.1 = (bf16[384,256]{1,0:T(8,128)(2,1)}, bf16[384,256]{1,0:T(8,128)(2,1)}, u32[]{:S(2)}, u32[]{:S(2)}) collective-permute-start(bf16[384,256]{1,0:T(8,128)(2,1)} %fusion.31), channel_id=1, source_target_pairs={{16,0},{24,8},{17,1},{25,9},{18,2},{26,10},{19,3},{27,11},{20,4},{... | collective-permute-start | bytes 589832 | tf_op jit(solution)/shard_map/ppermute | solution.py:1640
  401.3 23.9 %collective-permute-start = (bf16[384,256]{1,0:T(8,128)(2,1)}, bf16[384,256]{1,0:T(8,128)(2,1)}, u32[]{:S(2)}, u32[]{:S(2)}) collective-permute-start(bf16[384,256]{1,0:T(8,128)(2,1)} %fusion.31), channel_id=1, source_target_pairs={{8,0},{16,8},{24,16},{9,1},{17,9},{25,17},{10,2},{18,10},{26,18},{... | collective-permute-start | bytes 589832 | tf_op jit(solution)/shard_map/ppermute | solution.py:1640
  402.6 31.9 %collective-permute-start.2 = (bf16[384,256]{1,0:T(8,128)(2,1)}, bf16[384,256]{1,0:T(8,128)(2,1)}, u32[]{:S(2)}, u32[]{:S(2)}) collective-permute-start(bf16[384,256]{1,0:T(8,128)(2,1)} %fusion.31), channel_id=1, source_target_pairs={{24,0},{25,1},{26,2},{27,3},{28,4},{29,5},{30,6},{31,7}} | collective-permute-start | bytes 589832 | tf_op jit(solution)/shard_map/ppermute | solution.py:1640
  413.4 2.7 copy-start.11
  416.3 26.7 %copy-start.10 = (bf16[1024,512]{1,0:T(8,128)(2,1)}, bf16[1024,512]{1,0:T(8,128)(2,1)S(1)}, u32[]{:S(2)}) copy-start(bf16[1024,512]{1,0:T(8,128)(2,1)S(1)} %pad_maximum_fusion.4.left_b) | copy-start | bytes 3145732
  443.0 1.7 copy-start.17
  443.0 171.7 %reduce-scatter.14.cloned.1.call-start = ((), (), s32[]{:S(2)}) async-start(), calls=%async_computation.12 | async-start | bytes 3276800 | tf_op jit(solution)/shard_map/reduce_scatter | solution.py:1788
  446.0 31.3 %collective-permute-start.5 = (bf16[4,512,128]{2,1,0:T(8,128)(2,1)}, bf16[4,512,128]{2,1,0:T(8,128)(2,1)S(1)}, u32[]{:S(2)}, u32[]{:S(2)}) collective-permute-start(bf16[4,512,128]{2,1,0:T(8,128)(2,1)} %get-tuple-element.301), channel_id=1, source_target_pairs={{0,6},{2,4},{4,2},{6,0},{1,7},{3,5},{5,3},{7,1},{8,14},{10,12},{12... | collective-permute-start | bytes 1572872 | tf_op jit(solution)/shard_map/ppermute | solution.py:1821
  447.2 30.1 %collective-permute-start.4 = (bf16[4,512,128]{2,1,0:T(8,128)(2,1)}, bf16[4,512,128]{2,1,0:T(8,128)(2,1)S(1)}, u32[]{:S(2)}, u32[]{:S(2)}) collective-permute-start(bf16[4,512,128]{2,1,0:T(8,128)(2,1)} %get-tuple-element.302), channel_id=1, source_target_pairs={{0,4},{2,6},{4,0},{6,2},{1,5},{3,7},{5,1},{7,3},{8,12},{10,14},{12... | collective-permute-start | bytes 1572872 | tf_op jit(solution)/shard_map/ppermute | solution.py:1821
  447.8 29.5 %collective-permute-start.3 = (bf16[4,512,128]{2,1,0:T(8,128)(2,1)}, bf16[4,512,128]{2,1,0:T(8,128)(2,1)S(1)}, u32[]{:S(2)}, u32[]{:S(2)}) collective-permute-start(bf16[4,512,128]{2,1,0:T(8,128)(2,1)} %get-tuple-element.303), channel_id=1, source_target_pairs={{0,2},{2,0},{4,6},{6,4},{1,3},{3,1},{5,7},{7,5},{8,10},{10,8},{12,... | collective-permute-start | bytes 1572872 | tf_op jit(solution)/shard_map/ppermute | solution.py:1821
  452.5 24.9 %copy-start.18 = (bf16[4,512,128]{2,1,0:T(8,128)(2,1)S(1)}, bf16[4,512,128]{2,1,0:T(8,128)(2,1)}, u32[]{:S(2)}) copy-start(bf16[4,512,128]{2,1,0:T(8,128)(2,1)} %get-tuple-element.158) | copy-start | bytes 1572868
  478.4 43.4 %copy-start.7 = (bf16[1040,640]{1,0:T(8,128)(2,1)S(1)}, bf16[1040,640]{1,0:T(8,128)(2,1)}, u32[]{:S(2)}) copy-start(bf16[1040,640]{1,0:T(8,128)(2,1)} %copy-done.6) | copy-start | bytes 3993604
  478.4 43.4 %copy-start.22 = (f32[1024,384]{1,0:T(8,128)S(1)}, f32[1024,384]{1,0:T(8,128)}, u32[]{:S(2)}) copy-start(f32[1024,384]{1,0:T(8,128)} %get-tuple-element.154) | copy-start | bytes 4718596
  516.7 5.0 copy-start.4
  516.7 5.0 copy-start.31
  521.7 5.5 copy-start.12
  521.7 5.5 copy-start.14
  537.4 1.7 copy-start.13
  537.4 1.7 copy-start.15
  549.9 63.4 %copy-start.33 = (f32[1,2048]{1,0:T(1,128)S(1)}, f32[1,2048]{1,0:T(1,128)}, u32[]{:S(2)}) copy-start(f32[1,2048]{1,0:T(1,128)} %get-tuple-element.174) | copy-start | bytes 24580
  635.9 9.6 %copy-start.1 = (f32[256,2048]{1,0:T(8,128)S(1)}, f32[256,2048]{1,0:T(8,128)}, u32[]{:S(2)}) copy-start(f32[256,2048]{1,0:T(8,128)} %param.22) | copy-start | bytes 6291460
  (8 other events, 11.2 us)
Sparse Core Ops, SparseCore 0:
  85.5 50.6 all-gather.3
  137.8 57.5 all-gather.5
  197.0 96.3 all-gather.7
  313.5 44.7 reduce-scatter.5
  360.5 88.6 reduce-scatter.7
  451.4 51.3 reduce-scatter.9
  505.1 44.7 reduce-scatter.11
  552.2 51.4 reduce-scatter.13

commit v7 on v6

--- a/solution.py
+++ b/solution.py
@@ -621,6 +621,53 @@
     )(*pieces)
 
 
+def ffn_kernel(x_ref, w_ref, g_ref, gu_ref, act_ref, grad_ref, total):
+    i = pl.program_id(0)
+    ff = act_ref.shape[1]
+    gu = dot_nn(x_ref[...], w_ref[...])
+    gu_ref[...] = gu
+    gate = gu[:, :ff]
+    act = (gate * jax.nn.sigmoid(gate) * gu[:, ff:]).astype(bf16)
+    act_ref[...] = act
+    part = dot_tn(g_ref[...], act)
+
+    @pl.when(i == 0)
+    def _():
+        total[...] = part
+
+    @pl.when(i > 0)
+    def _():
+        total[...] += part
+
+    @pl.when(i == pl.num_programs(0) - 1)
+    def _():
+        grad_ref[...] = total[...].astype(bf16)
+
+
+def ffn_forward(x, w, g):
+    tok, width = x.shape
+    ff, block = w.shape[1] // 2, 256
+    row = lambda n: pl.BlockSpec((block, n), lambda i: (i, 0))
+    whole = lambda *s: pl.BlockSpec(s, lambda i: (0,) * len(s))
+    return pl.pallas_call(
+        ffn_kernel,
+        grid=(tok // block,),
+        in_specs=[row(width), whole(*w.shape), row(width)],
+        out_specs=[row(2 * ff), row(ff), whole(width, ff)],
+        out_shape=[
+            jax.ShapeDtypeStruct((tok, 2 * ff), f32),
+            jax.ShapeDtypeStruct((tok, ff), bf16),
+            jax.ShapeDtypeStruct((width, ff), bf16),
+        ],
+        scratch_shapes=[pltpu.VMEM((width, ff), f32)],
+        compiler_params=pltpu.CompilerParams(vmem_limit_bytes=VMEM_LIMIT),
+        cost_estimate=pl.CostEstimate(
+            flops=6 * tok * width * ff, bytes_accessed=25_000_000, transcendentals=0
+        ),
+        name="ffn_forward",
+    )(x, w, g)
+
+
 def at_rows(first, count):
     return pl.ds(pl.multiple_of(first, count), count)
 
@@ -973,13 +1020,18 @@
 
 
 def one_kernel(
-    n, left_a, right_a, left_b, right_b, hidden_own, dmid_own, gain, act, w_act, mid_own, *refs
+    n, left_a, right_a, left_b, right_b, hidden_own, dmid_own, gain, act, w_act, mid_own, rest,
+    *refs
 ):
-    ins, (grad_ref, block_ref, ggain_ref), outs = refs[:n], refs[n : n + 3], refs[n + 3 : 2 * n + 3]
+    ins, (grad_ref, block_ref, sums_ref), outs = refs[:n], refs[n : n + 3], refs[n + 3 : 2 * n + 3]
     first, second = refs[2 * n + 3 : 2 * n + 12], refs[2 * n + 12 : 2 * n + 21]
-    own_sems, w_sems, loc_sems = refs[2 * n + 21 :]
-    greet()
+    own_sems, ggain_ref, flat, flat_came, z_sems, p_sems, c_sems, w_sems, loc_sems = refs[
+        2 * n + 21 :
+    ]
     z, p, c = place()
+    nz = flat_came.shape[0] + 1
+    ups = [chip(lax.rem(z + d, nz), p, c) for d in range(1, nz)]
+    meet([chip(z, p, 1 - c)] + [chip(z, hop(p, d), c) for d in HOPS] + ups)
     half = hidden_own.shape[0]
     total_rows, middle, finish, done = reduce_blocks(
         [(left_a, right_a), (left_b, right_b)], *first
@@ -1009,6 +1061,26 @@
     copies = [
         send(grad_ref.at[mine, :], grad_ref.at[mine, :], own_sems.at[0, 0], own_sems.at[1, 0], other)
     ]
+    g_rows = ggain_ref.shape[1] // 128
+    for i in range(g_rows):
+        flat[i : i + 1, :] = ggain_ref[:, i * 128 : i * 128 + 128]
+    flat[g_rows:, :] = rest[...]
+    up = [
+        send(flat, flat_came.at[d], z_sems.at[0, d], z_sems.at[1, d], ups[d])
+        for d in range(nz - 1)
+    ]
+    total = flat[...]
+    for d in range(nz - 1):
+        up[d].wait_recv()
+        total = total + flat_came[d]
+    sums_ref[c, p] = total
+    around = [
+        send(
+            sums_ref.at[c, p], sums_ref.at[c, p], p_sems.at[0, i], p_sems.at[1, i],
+            chip(z, hop(p, d), c),
+        )
+        for i, d in enumerate(HOPS)
+    ]
     finish_out()
 
     @pl.loop(0, half // 16)
@@ -1019,8 +1091,13 @@
     copies.append(
         send(block_ref.at[mine, :], block_ref.at[mine, :], own_sems.at[0, 1], own_sems.at[1, 1], other)
     )
+    for copy in around:
+        copy.wait_recv()
+    copies.append(send(sums_ref.at[c], sums_ref.at[c], c_sems.at[0], c_sems.at[1], other))
     done()
     done_out()
+    for copy in up + around:
+        copy.wait_send()
     for copy in copies + moved:
         copy.wait()
 
@@ -1123,16 +1200,23 @@
     )
 
 
-def one_step(d_a, w_a, d_b, w_b, hidden_own, dmid_own, gain, act, w_act, mid_own, moved):
+def one_step(
+    d_a, w_a, d_b, w_b, hidden_own, dmid_own, gain, act, w_act, mid_own, rest, nz, n_p, moved
+):
     width = w_a.shape[0]
     half = hidden_own.shape[0]
+    flat = (width // 128 + rest.shape[0], 128)
+    dma = pltpu.SemaphoreType.DMA
     return plane_call(
         one_kernel, "one_step", 3,
-        (d_a, w_a, d_b, w_b, hidden_own, dmid_own, gain, act, w_act, mid_own),
-        [((2 * half, width), f32), ((2 * half, width), f32), ((1, width), f32)],
+        (d_a, w_a, d_b, w_b, hidden_own, dmid_own, gain, act, w_act, mid_own, rest),
+        [((2 * half, width), f32), ((2 * half, width), f32), ((2, n_p) + flat, f32)],
         reduce_scratch(half, width)
         + reduce_scratch(half, width)
-        + [pltpu.SemaphoreType.DMA((2, 2))],
+        + [
+            dma((2, 2)), pltpu.VMEM((1, width), f32), pltpu.VMEM(flat, f32),
+            pltpu.VMEM((nz - 1,) + flat, f32), dma((2, nz - 1)), dma((2, 3)), dma((2,)),
+        ],
         moved=moved,
     )
 
@@ -1177,6 +1261,11 @@
         send(gain_out.at[p], gain_out.at[p], gp_sems.at[0, i], gp_sems.at[1, i], flat[i])
         for i in range(3)
     ]
+    stage, chain_done = z_chain(a_out, up_sems, down_sems)
+    for copy in to_plane:
+        copy.wait_recv()
+    local[0].wait()
+    stage(0)
     for copy in gp:
         copy.wait_recv()
     for i in range(nz):
@@ -1194,11 +1283,6 @@
 
     share_middle, share_end = share_rows(full_ref, half, own_sems, far_sems, near_sems)
 
-    stage, chain_done = z_chain(a_out, up_sems, down_sems)
-    for copy in to_plane:
-        copy.wait_recv()
-    local[0].wait()
-    stage(0)
     share_middle()
     if nz > 2:
         stage(1)
@@ -1578,52 +1662,16 @@
     )
 
 
-def sums_kernel(n, v_ref, *refs):
-    ins, out_ref, outs = refs[:n], refs[n], refs[n + 1 : 2 * n + 1]
-    came, z_sems, p_sems, c_sems, w_sems, loc_sems = refs[2 * n + 1 :]
+def swap_kernel(n, *refs):
+    ins, outs, sems = refs[:n], refs[n : 2 * n], refs[2 * n :]
     z, p, c = place()
-    nz = came.shape[0]
-    ups = [chip(lax.rem(z + d, nz), p, c) for d in range(1, nz)]
-    other = chip(z, p, 1 - c)
-    meet(ups + [chip(z, hop(p, d), c) for d in HOPS] + [other])
-    moved = swap_begin(ins, outs, w_sems, loc_sems)
-    copies = []
-    for d in range(1, nz):
-        copies.append(
-            send(v_ref, came.at[d], z_sems.at[0, d - 1], z_sems.at[1, d - 1], ups[d - 1])
-        )
-    total = v_ref[...]
-    for d in range(1, nz):
-        copies[d - 1].wait_recv()
-        total = total + came[d]
-    out_ref[c, p] = total
-    far = []
-    for i, d in enumerate(HOPS):
-        far.append(
-            send(out_ref.at[c, p], out_ref.at[c, p], p_sems.at[0, i], p_sems.at[1, i], chip(z, hop(p, d), c))
-        )
-    for copy in far:
-        copy.wait_recv()
-    near = send(out_ref.at[c], out_ref.at[c], c_sems.at[0], c_sems.at[1], other)
-    for copy in copies + far:
-        copy.wait_send()
-    near.wait()
-    for copy in moved:
+    meet([chip(z, hop(p, d), c) for d in HOPS])
+    for copy in swap_begin(ins, outs, *sems):
         copy.wait()
 
 
-def sums_step(v, nz, n_p, moved):
-    return plane_call(
-        sums_kernel, "sums_step", 6, (v,),
-        [((2, n_p) + v.shape, f32)],
-        [
-            pltpu.VMEM((nz,) + v.shape, f32),
-            pltpu.SemaphoreType.DMA((2, nz - 1)),
-            pltpu.SemaphoreType.DMA((2, 3)),
-            pltpu.SemaphoreType.DMA((2,)),
-        ],
-        moved=moved,
-    )
+def swap_step(*moved):
+    return plane_call(swap_kernel, "swap_step", 6, (), [], [], nbytes=20_000_000, moved=moved)
 
 
 def rope_tables(positions, pairs):
@@ -1770,12 +1818,10 @@
 
     mid_own, normed_two, w_e = mid_step(mixed, w_c, hidden_own, gain_ffn, w_e)
     w_e = w_e.reshape(width, -1)
-    gu = product(normed_two, w_d)
+    gu, activated, grad_e = ffn_forward(normed_two, w_d, g_ffn)
     ffw = gu.shape[1] // 2
     gate_val, up_val = gu[:, :ffw], gu[:, ffw:]
     silu_gate = jax.nn.silu(gate_val)
-    activated = (silu_gate * up_val).astype(bf16)
-    grad_e = product_t(g_ffn, activated).astype(bf16)
     g_ffn, grad_e = lax.optimization_barrier((g_ffn, grad_e))
     d_act = product(g_ffn, w_e)
     d_gu = jnp.concatenate(
@@ -1849,23 +1895,21 @@
     ga = scattered(grad_a)
     once = jnp.where(ci == 0, d_pre[:, xw:], jnp.zeros((), bf16))
     d_a_once = jnp.concatenate([d_pre[:, :xw], once, d_last], axis=1)
-    d_a_once, grad_a, gc, gb = lax.optimization_barrier((d_a_once, grad_a, gc, gb))
-    grad_in, block_out, grad_gain_mix, gc, gb = one_step(
-        d_a_once, w_a, d_b, w_b, hidden_own, d_mid_own, gain_mix, activated, w_e, mid_own,
-        (by_owner(gc), by_owner(gb)),
-    )
-
-    flat = jnp.concatenate(
+    d_a_once, grad_a, gc = lax.optimization_barrier((d_a_once, grad_a, gc))
+    rest = jnp.concatenate(
         [
-            grad_gain_mix.reshape(-1, 128),
             grad_gain_ffn.reshape(-1, 128),
             grad_taps.reshape(-1, 128),
             sums[:2],
             jnp.pad(jnp.sum(skip_sums.reshape(n_heads, MHDIM), axis=1), (0, 128 - n_heads))[None],
         ]
     )
-    flat = jnp.pad(flat, ((0, -flat.shape[0] % 8), (0, 0)))
-    summed, ga = sums_step(flat, nz, n_p, (by_owner(ga),))
+    rest = jnp.pad(rest, ((0, -rest.shape[0] % 8), (0, 0)))
+    grad_in, block_out, summed, gc = one_step(
+        d_a_once, w_a, d_b, w_b, hidden_own, d_mid_own, gain_mix, activated, w_e, mid_own, rest,
+        nz, n_p, (by_owner(gc),),
+    )
+
     g_rows = width // 128
     t_rows = grad_taps.size // 128
     si = zi * n_p + pi
@@ -1880,6 +1924,7 @@
     s_bc = s_bc[:, :, xw:].reshape(n_p, edge + 1, 2, bw).transpose(1, 2, 0, 3)
     s_bc = s_bc.reshape(edge + 1, 2 * n_p * bw)
 
+    ga, gb = swap_step(by_owner(ga), by_owner(gb))
     (
         g_x, g_bc, g_k, g_v, g_dt, g_q, g_z, g_mout, g_aout, g_gate, g_up, g_down, block_out,
         grad_in,

time: 662 us -> 660 us (level)
  Pallas kernels: 452 us -> 470 us
  waiting for transfers between devices: 28.5 us -> 13.7 us
  matrix products: 66.8 us -> 57.3 us
    pallas_call x0 -> x1, Pallas kernels: none -> 14 us  [ffn_forward(): pl.pallas_call(ffn_kernel, grid=(tok // block,), in_specs=[row(width), wh...]
    reduce_scatter x5, waiting for transfers between devices: 8.73 us -> 0.03 us  [scattered(): return lax.psum_scatter(grad, 'z', scatter_dimension=0, tiled=True)]
    unnamed x86 -> x60, local copies, waits for them, and re-layouts: 14.6 us -> 7.84 us
    dot_general x5 -> x4, matrix products: 32 us -> 25.8 us  [product(): return jnp.dot(left, right, preferred_element_type=f32)]
    dot_general x6 -> x5, matrix products: 31.6 us -> 28.1 us  [product_t(): lax.dot_general(left, right, (((0,), (0,)), ((), ())), preferred_element_...]
  transfers between devices with their start and end apart: 14 -> 14, of which waited for: 4 -> 3; matrix products, arithmetic and copies ran while one was open for 18% -> 21% of each run, Pallas kernels for 54% -> 55%
where the time goes in v7:
time: 660 us; the launch traced here: 652 us
  Pallas kernels  470 us (71%)
  matrix products  57.3 us (9%)
  local copies, waits for them, and re-layouts  47.4 us (7%)
  other arithmetic  40.1 us (6%)
  between operations  15.3 us (2%)
  waiting for transfers between devices  13.7 us (2%)
  starting transfers between devices  8.06 us (1%)
    pallas_call x4, Pallas kernels, plane_call(): pl.pallas_call(kernel, in_specs=[VM] * (len(args) + n), out_specs=[VM] *...  174 us
    pallas_call x1, Pallas kernels, mid_step(): pl.pallas_call(mid_kernel, in_specs=[VM] * 4 + [ANYWHERE], out_specs=[VM]...  75 us
    pallas_call x1, Pallas kernels, open_step(): pl.pallas_call(functools.partial(open_kernel, n), in_specs=[VM] * (n + 3)...  68.6 us
    pallas_call x1, Pallas kernels, gather_bc(): pl.pallas_call(gather_bc_kernel, grid=(1,), in_specs=[pl.BlockSpec((tok,...  36.3 us
    pallas_call x1, Pallas kernels, carry_step(): pl.pallas_call(carry_kernel, in_specs=[VM] * 3 + [ANYWHERE], out_specs=[V...  34.5 us
    dot_general x5, matrix products, product_t(): lax.dot_general(left, right, (((0,), (0,)), ((), ())), preferred_element_...  28.1 us
    dot_general x4, matrix products, product(): return jnp.dot(left, right, preferred_element_type=f32)  25.8 us
    pallas_call x1, Pallas kernels, ssd_backward(): pl.pallas_call(functools.partial(ssd_backward_kernel, n_heads), grid=(nsp...  22.4 us
  transfers between devices with their start and end apart: 14, of which 3 were waited for; matrix products, arithmetic and copies ran while one was open for 21% of the time, Pallas kernels for 55%

profile of v7, /device:TPU:0, one launch (start us, length us, event | category | flops | bytes accessed | tf_op | source)
XLA Modules:
  0.0 651.9 jit_solution(4086059198066927498)
XLA Ops:
  7.3 1.6 copy.87.dt_ref
  11.2 5.5 pack.1
  16.7 68.6 %open_step.1 = (f32[4,4,8,128]{3,2,1,0:T(8,128)}, bf16[1040,2048]{1,0:T(8,128)(2,1)}, bf16[4,4,128,640]{3,2,1,0:T(8,128)(2,1)}, bf16[4,128,512]{2,1,0:T(8,128)(2...) custom-call(f32[128,2048]{1,0:T(8,128)} %constant_dynamic-slice_fusion.7.refs_0_.resi, ...), custom_call_target="tpu_custom_call" | custom-call | bytes 250000000 | tf_op jit(solution)/shard_map/open_step/pallas_call | solution.py:1338
  86.9 8.0 %fusion.80 = (bf16[1040,640]{1,0:T(8,128)(2,1)S(1)}, f32[1040,640]{1,0:T(8,128)}) fusion(bf16[1040,2048]{1,0:T(8,128)(2,1)} %get-tuple-element.116, bf16[2048,640]{1,0:T(8,128)(2,1)} %bitcast.79), kind=kOutput, calls=%fused_computation.179 | convolution fusion | flops 2726963200 | bytes 10874880 | tf_op jit(solution)/shard_map/dot_general | solution.py:32
  97.9 2.0 slice.314
  101.1 3.8 fusion.42
  107.1 3.7 add_multiply_fusion
  110.9 1.5 multiply_convert_fusion.2.x_ref
  112.4 36.3 %gather_bc.1 = (bf16[4,1024,128]{2,1,0:T(8,128)(2,1)}, bf16[4,512,128]{2,1,0:T(8,128)(2,1)}, bf16[1024,2048]{1,0:T(8,128)(2,1)}, bf16[4,4,128,512]{3,2,1,0:T(8,128)(2,1)}) custom-call(bf16[1024,512]{1,0:T(8,128)(2,1)} %multiply_convert_fusion.2.x_ref, bf16[512,128]{1,0:T(8,128)(2,1)} %pad_maximum_fusion.9.kv_ref, ...), custom_call_target="tpu_custom_call" | custom-call | bytes 40000000 | tf_op jit(solution)/shard_map/gather_bc/pallas_call | solution.py:1427
  150.1 13.7 %ssd_forward.1 = (f32[1024,384]{1,0:T(8,128)}, f32[8,384,256]{2,1,0:T(8,128)}, f32[384,256]{1,0:T(8,128)}, f32[1024,128]{1,0:T(8,128)}, f32[1024,384]{1,0:T(8,128)}, /*index=5*/bf16[1024,256]{1,0:T(8,128)(2,1)}) custom-call(s32[1]{0:T(128)} %bitcast.2.base_ref, s32[8]{0:T(128)} %starts_ref.7, bf16[1024,512]{1,0:T(8,128)(2,1)} %multiply_convert_fusion.2.x_ref, ...), custom_call_target="tpu_custom_call" | custom-call | flops 603979776 | bytes 40000000 | tf_op jit(solution)/shard_map/ssd_forward/pallas_call | solution.py:195
  165.2 34.5 %carry_step.1 = (f32[384,256]{1,0:T(8,128)}, bf16[4,4,512,128]{3,2,1,0:T(8,128)(2,1)}, f32[4,8,128]{2,1,0:T(8,128)}, bf16[4,4,128,512]{3,2,1,0:T(8,128)(2,1)}) custom-call(f32[384,256]{1,0:T(8,128)} %get-tuple-element.123.state_ref, f32[8,128]{1,0:T(8,128)} %broadcast_in_dim.122.rate_ref, ...), custom_call_target="tpu_custom_call", output_to_operand_aliasing={{3}: (3, {})} | custom-call | bytes 80000000 | tf_op jit(solution)/shard_map/carry_step/pallas_call | solution.py:1519
  199.7 5.3 fusion.81
  207.2 2.1 copy.90
  209.2 2.1 fusion.59
  212.3 8.5 %attend.1 = (f32[1024,128]{1,0:T(8,128)}, f32[1024,128]{1,0:T(8,128)}, bf16[4096,128]{1,0:T(8,128)(2,1)}, bf16[4096,128]{1,0:T(8,128)(2,1)}) custom-call(s32[1]{0:T(128)} %bitcast.2.base_ref, s32[8]{0:T(128)} %starts_ref.7, bf16[1024,128]{1,0:T(8,128)(2,1)} %copy.91.q_ref, bf16[4,4,512,128]{3,2,1,0:T(8,128)(2,1)} %get-tuple-element.130.kv_ref), custom_call_target="tpu_custom_call" | custom-call | flops 2147483648 | bytes 30000000 | tf_op jit(solution)/shard_map/attend/pallas_call | solution.py:416
  221.8 3.4 multiply_convert_fusion.5
  227.2 75.0 %mid_step.1 = (f32[128,2048]{1,0:T(8,128)}, bf16[1024,2048]{1,0:T(8,128)(2,1)}, bf16[4,4,128,512]{3,2,1,0:T(8,128)(2,1)}) custom-call(bf16[1024,512]{1,0:T(8,128)(2,1)} %pad_maximum_fusion.3.left, bf16[2048,512]{1,0:T(8,128)(2,1)} %all-gather.6.cloned.1.call-done.right, ...), custom_call_target="tpu_custom_call", output_to_operand_aliasing={{2}: (4, {})} | custom-call | bytes 150000000 | tf_op jit(solution)/shard_map/mid_step/pallas_call | solution.py:1172
  302.3 14.0 %ffn_forward.1 = (f32[1024,1024]{1,0:T(8,128)}, bf16[1024,512]{1,0:T(8,128)(2,1)}, bf16[2048,512]{1,0:T(8,128)(2,1)}) custom-call(bf16[1024,2048]{1,0:T(8,128)(2,1)} %get-tuple-element.135.x_ref, bf16[2048,1024]{1,0:T(8,128)(2,1)} %all-gather.8.cloned.1.call-done.w_ref.right, bf16[1024,2048]{1,0:T(8,128)(2,1)} %get-tuple-element.138.g_ref), custom_call_target="tpu_custom_call" | custom-call | flops 6442450944 | bytes 25000000 | tf_op jit(solution)/shard_map/ffn_forward/pallas_call | solution.py:652
  316.6 7.1 %multiply_convert_fusion.1 = (bf16[1024,512]{1,0:T(8,128)(2,1)S(1)}, bf16[1024,512]{1,0:T(8,128)(2,1)S(1)}) fusion(f32[1024,1024]{1,0:T(8,128)} %get-tuple-element.140, bf16[1024,2048]{1,0:T(8,128)(2,1)} %get-tuple-element.138.g_ref, bf16[2048,512]{1,0:T(8,128)(2,1)} %bitcast.77), kind=kOutput, calls=%fused_computation.44 | convolution fusion | flops 2154299392 | bytes 12582912 | tf_op jit(solution)/shard_map/dot_general | solution.py:32
  323.7 1.7 pad_maximum_fusion.1.left
  326.6 6.4 convolution_convert_fusion
  333.1 53.3 %two_step.1 = (f32[128,2048]{1,0:T(8,128)}, f32[1,2048]{1,0:T(1,128)}, bf16[1024,2048]{1,0:T(8,128)(2,1)}) custom-call(bf16[1024,1024]{1,0:T(8,128)(2,1)} %pad_maximum_fusion.1.left, bf16[2048,1024]{1,0:T(8,128)(2,1)} %all-gather.8.cloned.1.call-done.w_ref.right, f32[128,2048]{1,0:T(8,128)} %get-tuple-element.142.mid_own, ...), custom_call_target="tpu_custom_call" | custom-call | bytes 150000000 | tf_op jit(solution)/shard_map/two_step/pallas_call | solution.py:1154
  386.4 6.2 convolution_convert_fusion.2
  393.8 5.4 fusion.82
  400.0 1.7 multiply_convert_fusion.3
  407.9 9.6 %attend_back.1 = (f32[1024,128]{1,0:T(8,128)}, bf16[4,4,512,128]{3,2,1,0:T(8,128)(2,1)}) custom-call(s32[1]{0:T(128)} %bitcast.2.base_ref, s32[8]{0:T(128)} %starts_ref.7, bf16[1024,128]{1,0:T(8,128)(2,1)} %copy.91.q_ref, bf16[1024,128]{1,0:T(8,128)(2,1)} %slice.475.do_ref, f32[1024,128]{1,0:T(8,128)} %get-tuple-element.131.o_ref, ...), custom_call_target="tpu_custom_call" | custom-call | flops 5368709120 | bytes 40000000 | tf_op jit(solution)/shard_map/attend_back/pallas_call | solution.py:482
  417.4 2.1 copy.98
  419.5 2.1 fusion.63
  423.8 5.4 collective-permute-done.1
  429.5 6.4 collective-permute-done.2
  436.0 2.1 multiply_add_fusion.1.grad_ref
  438.0 6.3 convolution_convert_fusion.3
  444.5 2.9 dynamic-slice_bitcast_fusion
  449.3 1.6 collective-permute-start.3
  453.8 22.4 %ssd_backward.1 = (f32[1024,384]{1,0:T(8,128)}, f32[4,1024,128]{2,1,0:T(8,128)}, f32[1024,128]{1,0:T(8,128)}, f32[8,128]{1,0:T(8,128)}, f32[1,384]{1,0:T(1,128)}) custom-call(s32[1]{0:T(128)} %bitcast.2.base_ref, s32[8]{0:T(128)} %starts_ref.7, bf16[1024,512]{1,0:T(8,128)(2,1)} %multiply_convert_fusion.2.x_ref, ...), custom_call_target="tpu_custom_call" | custom-call | flops 1610612736 | bytes 80000000 | tf_op jit(solution)/shard_map/ssd_backward/pallas_call | solution.py:325
  477.6 1.8 slice.474
  479.4 2.4 add_convert_fusion.dkv_ref
  481.8 42.2 %reduce_bc.1 = (f32[1024,128]{1,0:T(8,128)}, f32[512,128]{1,0:T(8,128)}, f32[8,512]{1,0:T(8,128)}, bf16[4,128,512]{2,1,0:T(8,128)(2,1)}, bf16[4,128,1024]{2,1,0:T(8,128)(2,1)}) custom-call(f32[4,1024,128]{2,1,0:T(8,128)} %get-tuple-element.160.x_ref, bf16[4,512,128]{2,1,0:T(8,128)(2,1)} %add_convert_fusion.dkv_ref, f32[8,384]{1,0:T(8,128)} %slice.264.dx_ref, ...), custom_call_target="tpu_custom_call" | custom-call | bytes 100000000 | tf_op jit(solution)/shard_map/reduce_bc/pallas_call | solution.py:1154
  526.2 3.7 fusion.48
  529.9 3.8 fusion.6
  533.7 2.7 fusion.18
  536.5 2.1 concatenate.62
  538.6 8.1 %convolution_convert_fusion.1 = bf16[2048,640]{1,0:T(8,128)(2,1)} fusion(bf16[1040,2048]{1,0:T(8,128)(2,1)} %get-tuple-element.116, bf16[1024,640]{1,0:T(8,128)(2,1)} %concatenate.62), kind=kOutput, calls=%fused_computation.1 | convolution fusion | flops 2727608320 | bytes 8192000 | tf_op jit(solution)/shard_map/dot_general | solution.py:36
  548.4 2.1 concatenate.63.left_a
  551.1 61.0 %one_step.1 = (f32[256,2048]{1,0:T(8,128)}, f32[256,2048]{1,0:T(8,128)}, f32[2,4,56,128]{3,2,1,0:T(8,128)}, bf16[4,128,512]{2,1,0:T(8,128)(2,1)}) custom-call(bf16[1024,640]{1,0:T(8,128)(2,1)} %concatenate.63.left_a, bf16[2048,640]{1,0:T(8,128)(2,1)} %bitcast.80, bf16[1024,512]{1,0:T(8,128)(2,1)} %copy-done.5, ...), custom_call_target="tpu_custom_call" | custom-call | bytes 150000000 | tf_op jit(solution)/shard_map/one_step/pallas_call | solution.py:1154
  617.9 17.2 %swap_step.1 = (bf16[4,128,640]{2,1,0:T(8,128)(2,1)}, bf16[4,128,512]{2,1,0:T(8,128)(2,1)}) custom-call(bf16[4,128,640]{2,1,0:T(8,128)(2,1)} %bitcast.87, bf16[4,128,512]{2,1,0:T(8,128)(2,1)} %bitcast.90), custom_call_target="tpu_custom_call" | custom-call | bytes 20000000 | tf_op jit(solution)/shard_map/swap_step/pallas_call | solution.py:1154
  635.1 8.1 %unpack.1 = (f32[128,1536]{1,0:T(8,128)}, f32[128,512]{1,0:T(8,128)}, f32[128,128]{1,0:T(8,128)}, f32[128,128]{1,0:T(8,128)}, f32[128,24]{1,0:T(8,128)}, /*index...) custom-call(bf16[4,128,640]{2,1,0:T(8,128)(2,1)} %get-tuple-element., ...), custom_call_target="tpu_custom_call" | custom-call | bytes 10000000 | tf_op jit(solution)/shard_map/unpack/pallas_call | solution.py:613
  643.1 1.5 copy.103
  (177 shorter events, 47.6 us)
Async XLA Ops:
  7.2 2.9 copy-start
  7.2 192.5 %all-gather.4.cloned.1.call-start = ((), (), s32[]{:S(2)}) async-start(), calls=%async_computation.5 | async-start | bytes 2621440 | tf_op jit(solution)/shard_map/all_gather | solution.py:1746
  85.4 141.8 %all-gather.6.cloned.1.call-start = ((), (), s32[]{:S(2)}) async-start(), calls=%async_computation.6 | async-start | bytes 2621440 | tf_op jit(solution)/shard_map/all_gather | solution.py:1746
  86.2 216.1 %all-gather.8.cloned.1.call-start = ((), (), s32[]{:S(2)}) async-start(), calls=%async_computation.7 | async-start | bytes 5242880 | tf_op jit(solution)/shard_map/all_gather | solution.py:1746
  86.9 299.5 %reduce-scatter.6.cloned.1.call-start = ((), (), s32[]{:S(2)}) async-start(), calls=%async_computation.8 | async-start | bytes 2621440 | tf_op jit(solution)/shard_map/reduce_scatter | solution.py:1834
  95.0 9.9 %copy-start.3 = (bf16[1040,640]{1,0:T(8,128)(2,1)}, bf16[1040,640]{1,0:T(8,128)(2,1)S(1)}, u32[]{:S(2)}) copy-start(bf16[1040,640]{1,0:T(8,128)(2,1)S(1)} %get-tuple-element.335) | copy-start | bytes 3993604
  95.0 1.5 copy-start.26
  95.0 1.6 copy-start.27
  95.0 5.0 copy-start.23
  95.0 6.0 copy-start.22
  100.0 6.1 copy-start.19
  112.4 36.3 %copy-start.28 = (f32[24]{0:T(128)S(1)}, f32[24]{0:T(128)}, u32[]{:S(2)}) copy-start(f32[24]{0:T(128)} %param.33) | copy-start | bytes 292
  112.4 36.9 %copy-start.9 = (f32[1024,6]{1,0:T(8,128)S(1)}, f32[1024,6]{1,0:T(8,128)}, u32[]{:S(2)}) copy-start(f32[1024,6]{1,0:T(8,128)} %slice.314) | copy-start | bytes 73732
  205.0 1.3 copy-start.11
  212.2 9.6 %copy-start.12 = (f32[1040,512]{1,0:T(8,128)S(1)}, f32[1040,512]{1,0:T(8,128)}, u32[]{:S(2)}) copy-start(f32[1040,512]{1,0:T(8,128)} %copy-done.11) | copy-start | bytes 6389764
  212.2 9.6 %copy-start.16 = (f32[1024,384]{1,0:T(8,128)S(1)}, f32[1024,384]{1,0:T(8,128)}, u32[]{:S(2)}) copy-start(f32[1024,384]{1,0:T(8,128)} %get-tuple-element.128) | copy-start | bytes 4718596
  225.3 0.9 copy-start.18
  316.3 137.5 %reduce-scatter.8.cloned.1.call-start = ((), (), s32[]{:S(2)}) async-start(), calls=%async_computation.9 | async-start | bytes 5242880 | tf_op jit(solution)/shard_map/reduce_scatter | solution.py:1834
  323.7 2.9 copy-start.25
  333.0 217.4 %reduce-scatter.14.cloned.1.call-start = ((), (), s32[]{:S(2)}) async-start(), calls=%async_computation.12 | async-start | bytes 2621440 | tf_op jit(solution)/shard_map/reduce_scatter | solution.py:1834
  392.6 225.3 %reduce-scatter.12.cloned.1.call-start = ((), (), s32[]{:S(2)}) async-start(), calls=%async_computation.11 | async-start | bytes 2621440 | tf_op jit(solution)/shard_map/reduce_scatter | solution.py:1834
  393.8 6.2 copy-start.13
  393.8 6.2 copy-start.15
  400.0 2.8 copy-start.17
  400.0 2.8 copy-start.20
  401.7 1.1 copy-start.2
  404.0 25.2 %collective-permute-start.1 = (bf16[384,256]{1,0:T(8,128)(2,1)}, bf16[384,256]{1,0:T(8,128)(2,1)}, u32[]{:S(2)}, u32[]{:S(2)}) collective-permute-start(bf16[384,256]{1,0:T(8,128)(2,1)} %fusion.30), channel_id=1, source_target_pairs={{16,0},{24,8},{17,1},{25,9},{18,2},{26,10},{19,3},{27,11},{20,4},{... | collective-permute-start | bytes 589832 | tf_op jit(solution)/shard_map/ppermute | solution.py:1688
  405.3 24.3 %collective-permute-start = (bf16[384,256]{1,0:T(8,128)(2,1)}, bf16[384,256]{1,0:T(8,128)(2,1)}, u32[]{:S(2)}, u32[]{:S(2)}) collective-permute-start(bf16[384,256]{1,0:T(8,128)(2,1)} %fusion.30), channel_id=1, source_target_pairs={{8,0},{16,8},{24,16},{9,1},{17,9},{25,17},{10,2},{18,10},{26,18},{... | collective-permute-start | bytes 589832 | tf_op jit(solution)/shard_map/ppermute | solution.py:1688
  406.6 29.4 %collective-permute-start.2 = (bf16[384,256]{1,0:T(8,128)(2,1)}, bf16[384,256]{1,0:T(8,128)(2,1)}, u32[]{:S(2)}, u32[]{:S(2)}) collective-permute-start(bf16[384,256]{1,0:T(8,128)(2,1)} %fusion.30), channel_id=1, source_target_pairs={{24,0},{25,1},{26,2},{27,3},{28,4},{29,5},{30,6},{31,7}} | collective-permute-start | bytes 589832 | tf_op jit(solution)/shard_map/ppermute | solution.py:1688
  423.8 14.3 %copy-start.5 = (bf16[1024,512]{1,0:T(8,128)(2,1)}, bf16[1024,512]{1,0:T(8,128)(2,1)S(1)}, u32[]{:S(2)}) copy-start(bf16[1024,512]{1,0:T(8,128)(2,1)S(1)} %pad_maximum_fusion.4.left_b) | copy-start | bytes 3145732
  444.4 173.5 %reduce-scatter.10.cloned.1.call-start = ((), (), s32[]{:S(2)}) async-start(), calls=%async_computation.10 | async-start | bytes 3276800 | tf_op jit(solution)/shard_map/reduce_scatter | solution.py:1834
  447.4 32.0 %collective-permute-start.5 = (bf16[4,512,128]{2,1,0:T(8,128)(2,1)}, bf16[4,512,128]{2,1,0:T(8,128)(2,1)}, u32[]{:S(2)}, u32[]{:S(2)}) collective-permute-start(bf16[4,512,128]{2,1,0:T(8,128)(2,1)} %get-tuple-element.303), channel_id=1, source_target_pairs={{0,6},{2,4},{4,2},{6,0},{1,7},{3,5},{5,3},{7,1},{8,14},{10,12},{12... | collective-permute-start | bytes 1572872 | tf_op jit(solution)/shard_map/ppermute | solution.py:1867
  448.8 30.6 %collective-permute-start.4 = (bf16[4,512,128]{2,1,0:T(8,128)(2,1)}, bf16[4,512,128]{2,1,0:T(8,128)(2,1)}, u32[]{:S(2)}, u32[]{:S(2)}) collective-permute-start(bf16[4,512,128]{2,1,0:T(8,128)(2,1)} %get-tuple-element.304), channel_id=1, source_target_pairs={{0,4},{2,6},{4,0},{6,2},{1,5},{3,7},{5,1},{7,3},{8,12},{10,14},{12... | collective-permute-start | bytes 1572872 | tf_op jit(solution)/shard_map/ppermute | solution.py:1867
  449.3 30.1 %collective-permute-start.3 = (bf16[4,512,128]{2,1,0:T(8,128)(2,1)}, bf16[4,512,128]{2,1,0:T(8,128)(2,1)}, u32[]{:S(2)}, u32[]{:S(2)}) collective-permute-start(bf16[4,512,128]{2,1,0:T(8,128)(2,1)} %get-tuple-element.305), channel_id=1, source_target_pairs={{0,2},{2,0},{4,6},{6,4},{1,3},{3,1},{5,7},{7,5},{8,10},{10,8},{12,... | collective-permute-start | bytes 1572872 | tf_op jit(solution)/shard_map/ppermute | solution.py:1867
  453.8 25.5 %copy-start.10 = (bf16[4,512,128]{2,1,0:T(8,128)(2,1)S(1)}, bf16[4,512,128]{2,1,0:T(8,128)(2,1)}, u32[]{:S(2)}) copy-start(bf16[4,512,128]{2,1,0:T(8,128)(2,1)} %get-tuple-element.161) | copy-start | bytes 1572868
  524.0 5.9 copy-start.4
  524.0 5.9 copy-start.14
  533.7 2.8 copy-start.6
  533.7 2.8 copy-start.7
  533.7 2.8 copy-start.8
  546.6 1.4 copy-start.24
  548.3 2.2 copy-start.21
  635.0 9.6 %copy-start.1 = (f32[256,2048]{1,0:T(8,128)S(1)}, f32[256,2048]{1,0:T(8,128)}, u32[]{:S(2)}) copy-start(f32[256,2048]{1,0:T(8,128)} %param.22) | copy-start | bytes 6291460
Sparse Core Ops, SparseCore 0:
  85.5 51.2 all-gather.3
  138.4 57.9 all-gather.5
  198.0 96.1 all-gather.7
  316.5 42.1 reduce-scatter.5
  360.9 88.7 reduce-scatter.7
  451.8 47.1 reduce-scatter.13
  501.4 43.8 reduce-scatter.11
  547.5 52.9 reduce-scatter.9

commit v8 on v7

--- a/solution.py
+++ b/solution.py
@@ -365,7 +365,10 @@
     return (k_pos >= low) & (k_pos <= high)
 
 
-def attend_kernel(scale, base_ref, starts_ref, q_ref, kv_ref, o_ref, lse_ref, k_ref, v_ref):
+def attend_kernel(
+    scale, base_ref, starts_ref, raw_ref, cos_ref, sin_ref, kv_ref,
+    o_ref, lse_ref, k_ref, v_ref, q_ref,
+):
     i = pl.program_id(0)
 
     @pl.when(i == 0)
@@ -382,7 +385,12 @@
                 k_ref[at, :] = jnp.concatenate([v[:, lo : lo + kw] for v in parts], axis=1)
                 v_ref[at, :] = jnp.concatenate([v[:, lo + kw : lo + 2 * kw] for v in parts], axis=1)
 
-    q = q_ref[...]
+    raw = raw_ref[...]
+    hk = HDIM // kv_ref.shape[0] // 2
+    leading = iota2(raw.shape, 1) % (2 * hk) < hk
+    partner = jnp.where(leading, pltpu.roll(raw, HDIM - hk, 1), pltpu.roll(raw, hk, 1))
+    q = (raw * cos_ref[...] + partner * sin_ref[...]).astype(bf16)
+    q_ref[...] = q
     low, high = sight(base_ref, starts_ref, i * QB)
     blocks = (base_ref[0] + (i + 1) * QB + KB - 1) // KB
 
@@ -407,8 +415,8 @@
     lse_ref[...] = jnp.broadcast_to(m + jnp.log(l), (QB, 128))
 
 
-def attend(base, doc_starts, q, kv):
-    tok = q.shape[0]
+def attend(base, doc_starts, raw, cosine, sine, kv):
+    tok = cosine.shape[0]
     keys = kv.shape[1] * kv.shape[2] * 2
     row = pl.BlockSpec((QB, HDIM), lambda i: (i, 0))
     whole = lambda s: pl.BlockSpec(s, lambda i: (0,) * len(s))
@@ -416,16 +424,17 @@
     return pl.pallas_call(
         functools.partial(attend_kernel, HDIM ** (-0.5)),
         grid=(tok // QB,),
-        in_specs=[smem, smem, row, whole(kv.shape)],
-        out_specs=[row, row, whole((keys, HDIM)), whole((keys, HDIM))],
+        in_specs=[smem, smem, row, row, row, whole(kv.shape)],
+        out_specs=[row, row, whole((keys, HDIM)), whole((keys, HDIM)), row],
         out_shape=[jax.ShapeDtypeStruct((tok, HDIM), f32)] * 2
-        + [jax.ShapeDtypeStruct((keys, HDIM), bf16)] * 2,
+        + [jax.ShapeDtypeStruct((keys, HDIM), bf16)] * 2
+        + [jax.ShapeDtypeStruct((tok, HDIM), bf16)],
         compiler_params=pltpu.CompilerParams(vmem_limit_bytes=VMEM_LIMIT),
         cost_estimate=pl.CostEstimate(
             flops=4 * tok * keys * HDIM, bytes_accessed=30_000_000, transcendentals=0
         ),
         name="attend",
-    )(base, doc_starts, q, kv)
+    )(base, doc_starts, raw, cosine, sine, kv)
 
 
 def attend_back_kernel(
@@ -1757,7 +1766,8 @@
     w_b, w_c, w_d = [along_z(piece) for piece in rest[:3]]
 
     in_ext = product(normed_one, w_a)
-    in_b = product(normed_one, w_b)[:tok]
+    in_b_ext = product(normed_one, w_b)
+    in_b = in_b_ext[:tok]
     in_a = in_ext[:tok]
     pre_ext = in_ext[:, :cw].astype(bf16)
     gate_z = in_b[:, HDIM:]
@@ -1800,7 +1810,9 @@
             [a * cos_q - sign * b * sin_q, b * cos_q + sign * a * sin_q], axis=2
         ).reshape(tok, HDIM)
 
-    queries = rope_q(in_b[:, :HDIM], 1.0).astype(bf16)
+    lane = jnp.arange(HDIM)
+    cos_w, sin_w = rope_tables(positions, (lane // kw) * hk + lane % hk)
+    sin_w = jnp.where(lane % kw < hk, -1.0, 1.0)[None, :] * sin_w
 
     base_arr = jnp.reshape(base, (1,)).astype(jnp.int32)
     y_local, span_starts, local_state, dev_decay, decay_full, c_mat = ssd_forward(
@@ -1809,7 +1821,9 @@
     rate = jnp.broadcast_to(dev_decay[tok - 1 :], (8, 128))
     in_state, kv, rates, w_e = carry_step(local_state, rate, kvz, n_p, w_e)
 
-    attn_f32, lse, keys, values = attend(base_arr, doc_starts, queries, kv)
+    attn_f32, lse, keys, values, queries = attend(
+        base_arr, doc_starts, in_b_ext, cos_w, sin_w, kv
+    )
     attn_low = attn_f32.astype(bf16)
     y_flat = y_local + product_nt(c_mat, in_state.astype(bf16)) * decay_full
     silu_z = jax.nn.silu(gate_z)

time: 660 us -> 656 us (level)
  transfers between devices with their start and end apart: 14 -> 14, of which waited for: 3 -> 3; matrix products, arithmetic and copies ran while one was open for 21% -> 20% of each run, Pallas kernels for 55% -> 55%
where the time goes in v8:
time: 656 us; the launch traced here: 649 us
  Pallas kernels  469 us (71%)
  matrix products  58.7 us (9%)
  local copies, waits for them, and re-layouts  42.4 us (6%)
  other arithmetic  41.1 us (6%)
  between operations  15.3 us (2%)
  waiting for transfers between devices  14.1 us (2%)
  starting transfers between devices  8.06 us (1%)
    pallas_call x4, Pallas kernels, plane_call(): pl.pallas_call(kernel, in_specs=[VM] * (len(args) + n), out_specs=[VM] *...  173 us
    pallas_call x1, Pallas kernels, mid_step(): pl.pallas_call(mid_kernel, in_specs=[VM] * 4 + [ANYWHERE], out_specs=[VM]...  74.4 us
    pallas_call x1, Pallas kernels, open_step(): pl.pallas_call(functools.partial(open_kernel, n), in_specs=[VM] * (n + 3)...  68.6 us
    pallas_call x1, Pallas kernels, gather_bc(): pl.pallas_call(gather_bc_kernel, grid=(1,), in_specs=[pl.BlockSpec((tok,...  36.2 us
    pallas_call x1, Pallas kernels, carry_step(): pl.pallas_call(carry_kernel, in_specs=[VM] * 3 + [ANYWHERE], out_specs=[V...  34.4 us
    dot_general x5, matrix products, product_t(): lax.dot_general(left, right, (((0,), (0,)), ((), ())), preferred_element_...  28.1 us
    dot_general x4, matrix products, product(): return jnp.dot(left, right, preferred_element_type=f32)  27.2 us
    pallas_call x1, Pallas kernels, ssd_backward(): pl.pallas_call(functools.partial(ssd_backward_kernel, n_heads), grid=(nsp...  22.4 us
  transfers between devices with their start and end apart: 14, of which 3 were waited for; matrix products, arithmetic and copies ran while one was open for 20% of the time, Pallas kernels for 55%

profile of v8, /device:TPU:0, one launch (start us, length us, event | category | flops | bytes accessed | tf_op | source)
XLA Modules:
  0.0 649.0 jit_solution(15898474028346867596)
XLA Ops:
  7.3 1.6 copy.81.dt_ref
  11.2 5.5 pack.1
  16.7 68.6 %open_step.1 = (f32[4,4,8,128]{3,2,1,0:T(8,128)}, bf16[1040,2048]{1,0:T(8,128)(2,1)}, bf16[4,4,128,640]{3,2,1,0:T(8,128)(2,1)}, bf16[4,128,512]{2,1,0:T(8,128)(2...) custom-call(f32[128,2048]{1,0:T(8,128)} %constant_dynamic-slice_fusion.7.refs_0_.resi, ...), custom_call_target="tpu_custom_call" | custom-call | bytes 250000000 | tf_op jit(solution)/shard_map/open_step/pallas_call | solution.py:1347
  86.9 8.0 %fusion.78 = (bf16[1040,640]{1,0:T(8,128)(2,1)S(1)}, f32[1040,640]{1,0:T(8,128)}) fusion(bf16[1040,2048]{1,0:T(8,128)(2,1)} %get-tuple-element.117, bf16[2048,640]{1,0:T(8,128)(2,1)} %bitcast.77), kind=kOutput, calls=%fused_computation.186 | convolution fusion | flops 2726963200 | bytes 10874880 | tf_op jit(solution)/shard_map/dot_general | solution.py:32
  98.0 2.0 slice.301
  101.2 3.8 fusion.42
  107.2 3.7 add_multiply_fusion
  110.9 1.5 multiply_convert_fusion.2.x_ref
  112.5 36.2 %gather_bc.1 = (bf16[4,1024,128]{2,1,0:T(8,128)(2,1)}, bf16[4,512,128]{2,1,0:T(8,128)(2,1)}, bf16[1024,2048]{1,0:T(8,128)(2,1)}, bf16[4,4,128,512]{3,2,1,0:T(8,128)(2,1)}) custom-call(bf16[1024,512]{1,0:T(8,128)(2,1)} %multiply_convert_fusion.2.x_ref, bf16[512,128]{1,0:T(8,128)(2,1)} %pad_maximum_fusion.8.kv_ref, ...), custom_call_target="tpu_custom_call" | custom-call | bytes 40000000 | tf_op jit(solution)/shard_map/gather_bc/pallas_call | solution.py:1436
  150.1 13.8 %ssd_forward.1 = (f32[1024,384]{1,0:T(8,128)}, f32[8,384,256]{2,1,0:T(8,128)}, f32[384,256]{1,0:T(8,128)}, f32[1024,128]{1,0:T(8,128)}, f32[1024,384]{1,0:T(8,128)}, /*index=5*/bf16[1024,256]{1,0:T(8,128)(2,1)}) custom-call(s32[1]{0:T(128)} %bitcast.2.base_ref, s32[8]{0:T(128)} %starts_ref.7, bf16[1024,512]{1,0:T(8,128)(2,1)} %multiply_convert_fusion.2.x_ref, ...), custom_call_target="tpu_custom_call" | custom-call | flops 603979776 | bytes 40000000 | tf_op jit(solution)/shard_map/ssd_forward/pallas_call | solution.py:195
  165.2 34.4 %carry_step.1 = (f32[384,256]{1,0:T(8,128)}, bf16[4,4,512,128]{3,2,1,0:T(8,128)(2,1)}, f32[4,8,128]{2,1,0:T(8,128)}, bf16[4,4,128,512]{3,2,1,0:T(8,128)(2,1)}) custom-call(f32[384,256]{1,0:T(8,128)} %get-tuple-element.124.state_ref, f32[8,128]{1,0:T(8,128)} %broadcast_in_dim.133.rate_ref, ...), custom_call_target="tpu_custom_call", output_to_operand_aliasing={{3}: (3, {})} | custom-call | bytes 80000000 | tf_op jit(solution)/shard_map/carry_step/pallas_call | solution.py:1528
  199.6 3.1 fusion.49
  202.7 6.6 %fusion.79.raw_ref = f32[1040,512]{1,0:T(8,128)} fusion(bf16[1040,2048]{1,0:T(8,128)(2,1)} %get-tuple-element.117, bf16[2048,512]{1,0:T(8,128)(2,1)} %all-gather.4.cloned.1.call-done.right_b), kind=kOutput, calls=%fused_computation.187 | convolution fusion | flops 2181038080 | bytes 8486912 | tf_op jit(solution)/shard_map/dot_general | solution.py:32
  209.3 9.2 %attend.1 = (f32[1024,128]{1,0:T(8,128)}, f32[1024,128]{1,0:T(8,128)}, bf16[4096,128]{1,0:T(8,128)(2,1)}, bf16[4096,128]{1,0:T(8,128)(2,1)}, bf16[1024,128]{1,0:T(8,128)(2,1)}) custom-call(s32[1]{0:T(128)} %bitcast.2.base_ref, s32[8]{0:T(128)} %starts_ref.7, f32[1040,512]{1,0:T(8,128)} %fusion.79.raw_ref, f32[1024,128]{1,0:T(8,128)} %get-tuple-element.334.cos_ref, ...), custom_call_target="tpu_custom_call" | custom-call | flops 2147483648 | bytes 30000000 | tf_op jit(solution)/shard_map/attend/pallas_call | solution.py:424
  219.6 3.5 multiply_convert_fusion.5
  225.0 74.4 %mid_step.1 = (f32[128,2048]{1,0:T(8,128)}, bf16[1024,2048]{1,0:T(8,128)(2,1)}, bf16[4,4,128,512]{3,2,1,0:T(8,128)(2,1)}) custom-call(bf16[1024,512]{1,0:T(8,128)(2,1)} %pad_maximum_fusion.3.left, bf16[2048,512]{1,0:T(8,128)(2,1)} %all-gather.6.cloned.1.call-done.right, ...), custom_call_target="tpu_custom_call", output_to_operand_aliasing={{2}: (4, {})} | custom-call | bytes 150000000 | tf_op jit(solution)/shard_map/mid_step/pallas_call | solution.py:1181
  299.4 14.0 %ffn_forward.1 = (f32[1024,1024]{1,0:T(8,128)}, bf16[1024,512]{1,0:T(8,128)(2,1)}, bf16[2048,512]{1,0:T(8,128)(2,1)}) custom-call(bf16[1024,2048]{1,0:T(8,128)(2,1)} %get-tuple-element.136.x_ref, bf16[2048,1024]{1,0:T(8,128)(2,1)} %all-gather.8.cloned.1.call-done.w_ref.right, bf16[1024,2048]{1,0:T(8,128)(2,1)} %get-tuple-element.139.g_ref), custom_call_target="tpu_custom_call" | custom-call | flops 6442450944 | bytes 25000000 | tf_op jit(solution)/shard_map/ffn_forward/pallas_call | solution.py:661
  313.7 7.1 %multiply_convert_fusion.1 = (bf16[1024,512]{1,0:T(8,128)(2,1)S(1)}, bf16[1024,512]{1,0:T(8,128)(2,1)S(1)}) fusion(f32[1024,1024]{1,0:T(8,128)} %get-tuple-element.141, bf16[1024,2048]{1,0:T(8,128)(2,1)} %get-tuple-element.139.g_ref, bf16[2048,512]{1,0:T(8,128)(2,1)} %bitcast.75), kind=kOutput, calls=%fused_computation.44 | convolution fusion | flops 2154299392 | bytes 12582912 | tf_op jit(solution)/shard_map/dot_general | solution.py:32
  320.8 1.7 pad_maximum_fusion.1.left
  323.8 6.4 convolution_convert_fusion
  330.2 53.2 %two_step.1 = (f32[128,2048]{1,0:T(8,128)}, f32[1,2048]{1,0:T(1,128)}, bf16[1024,2048]{1,0:T(8,128)(2,1)}) custom-call(bf16[1024,1024]{1,0:T(8,128)(2,1)} %pad_maximum_fusion.1.left, bf16[2048,1024]{1,0:T(8,128)(2,1)} %all-gather.8.cloned.1.call-done.w_ref.right, f32[128,2048]{1,0:T(8,128)} %get-tuple-element.143.mid_own, ...), custom_call_target="tpu_custom_call" | custom-call | bytes 150000000 | tf_op jit(solution)/shard_map/two_step/pallas_call | solution.py:1163
  383.4 6.2 convolution_convert_fusion.2
  390.8 5.4 fusion.80
  397.0 1.7 multiply_convert_fusion.3
  404.9 9.6 %attend_back.1 = (f32[1024,128]{1,0:T(8,128)}, bf16[4,4,512,128]{3,2,1,0:T(8,128)(2,1)}) custom-call(s32[1]{0:T(128)} %bitcast.2.base_ref, s32[8]{0:T(128)} %starts_ref.7, bf16[1024,128]{1,0:T(8,128)(2,1)} %get-tuple-element.150.q_ref, bf16[1024,128]{1,0:T(8,128)(2,1)} %slice.455.do_ref, f32[1024,128]{1,0:T(8,128)} %get-tuple-element.132.o_ref, ...), custom_call_target="tpu_custom_call" | custom-call | flops 5368709120 | bytes 40000000 | tf_op jit(solution)/shard_map/attend_back/pallas_call | solution.py:491
  414.4 2.1 copy.89
  416.5 2.1 fusion.56
  420.8 5.5 collective-permute-done.1
  426.5 6.8 %collective-permute-done.2 = bf16[384,256]{1,0:T(8,128)(2,1)} collective-permute-done((bf16[384,256]{1,0:T(8,128)(2,1)}, bf16[384,256]{1,0:T(8,128)(2,1)}, u32[]{:S(2)}, u32[]{:S(2)}) %collective-permute-start.2) | collective-permute-done | bytes 196640 | tf_op jit(solution)/shard_map/ppermute | solution.py:1697
  433.3 2.1 multiply_add_fusion.1.grad_ref
  435.4 6.3 convolution_convert_fusion.3
  441.8 2.9 dynamic-slice_bitcast_fusion
  444.8 1.4 collective-permute-start.5
  446.7 1.6 collective-permute-start.3
  451.2 22.4 %ssd_backward.1 = (f32[1024,384]{1,0:T(8,128)}, f32[4,1024,128]{2,1,0:T(8,128)}, f32[1024,128]{1,0:T(8,128)}, f32[8,128]{1,0:T(8,128)}, f32[1,384]{1,0:T(1,128)}) custom-call(s32[1]{0:T(128)} %bitcast.2.base_ref, s32[8]{0:T(128)} %starts_ref.7, bf16[1024,512]{1,0:T(8,128)(2,1)} %multiply_convert_fusion.2.x_ref, ...), custom_call_target="tpu_custom_call" | custom-call | flops 1610612736 | bytes 80000000 | tf_op jit(solution)/shard_map/ssd_backward/pallas_call | solution.py:325
  474.9 1.8 slice.454
  476.7 2.4 add_convert_fusion.dkv_ref
  479.2 41.8 %reduce_bc.1 = (f32[1024,128]{1,0:T(8,128)}, f32[512,128]{1,0:T(8,128)}, f32[8,512]{1,0:T(8,128)}, bf16[4,128,512]{2,1,0:T(8,128)(2,1)}, bf16[4,128,1024]{2,1,0:T(8,128)(2,1)}) custom-call(f32[4,1024,128]{2,1,0:T(8,128)} %get-tuple-element.162.x_ref, bf16[4,512,128]{2,1,0:T(8,128)(2,1)} %add_convert_fusion.dkv_ref, f32[8,384]{1,0:T(8,128)} %slice.251.dx_ref, ...), custom_call_target="tpu_custom_call" | custom-call | bytes 100000000 | tf_op jit(solution)/shard_map/reduce_bc/pallas_call | solution.py:1163
  523.2 3.7 fusion.48
  526.9 3.8 fusion.6
  530.8 2.7 fusion.18
  533.5 2.1 concatenate.62
  535.6 8.1 %convolution_convert_fusion.1 = bf16[2048,640]{1,0:T(8,128)(2,1)} fusion(bf16[1040,2048]{1,0:T(8,128)(2,1)} %get-tuple-element.117, bf16[1024,640]{1,0:T(8,128)(2,1)} %concatenate.62), kind=kOutput, calls=%fused_computation.1 | convolution fusion | flops 2727608320 | bytes 8192000 | tf_op jit(solution)/shard_map/dot_general | solution.py:36
  545.4 2.1 concatenate.63.left_a
  548.1 61.1 %one_step.1 = (f32[256,2048]{1,0:T(8,128)}, f32[256,2048]{1,0:T(8,128)}, f32[2,4,56,128]{3,2,1,0:T(8,128)}, bf16[4,128,512]{2,1,0:T(8,128)(2,1)}) custom-call(bf16[1024,640]{1,0:T(8,128)(2,1)} %concatenate.63.left_a, bf16[2048,640]{1,0:T(8,128)(2,1)} %bitcast.78, bf16[1024,512]{1,0:T(8,128)(2,1)} %copy-done.5, ...), custom_call_target="tpu_custom_call" | custom-call | bytes 150000000 | tf_op jit(solution)/shard_map/one_step/pallas_call | solution.py:1163
  615.0 17.1 %swap_step.1 = (bf16[4,128,640]{2,1,0:T(8,128)(2,1)}, bf16[4,128,512]{2,1,0:T(8,128)(2,1)}) custom-call(bf16[4,128,640]{2,1,0:T(8,128)(2,1)} %bitcast.83, bf16[4,128,512]{2,1,0:T(8,128)(2,1)} %bitcast.86), custom_call_target="tpu_custom_call" | custom-call | bytes 20000000 | tf_op jit(solution)/shard_map/swap_step/pallas_call | solution.py:1163
  632.1 8.1 %unpack.1 = (f32[128,1536]{1,0:T(8,128)}, f32[128,512]{1,0:T(8,128)}, f32[128,128]{1,0:T(8,128)}, f32[128,128]{1,0:T(8,128)}, f32[128,24]{1,0:T(8,128)}, /*index...) custom-call(bf16[4,128,640]{2,1,0:T(8,128)(2,1)} %get-tuple-element., ...), custom_call_target="tpu_custom_call" | custom-call | bytes 10000000 | tf_op jit(solution)/shard_map/unpack/pallas_call | solution.py:622
  640.2 1.5 copy.94
  (172 shorter events, 43.1 us)
Async XLA Ops:
  7.2 2.9 copy-start
  7.2 195.5 %all-gather.4.cloned.1.call-start = ((), (), s32[]{:S(2)}) async-start(), calls=%async_computation.5 | async-start | bytes 2621440 | tf_op jit(solution)/shard_map/all_gather | solution.py:1755
  85.4 139.6 %all-gather.6.cloned.1.call-start = ((), (), s32[]{:S(2)}) async-start(), calls=%async_computation.6 | async-start | bytes 2621440 | tf_op jit(solution)/shard_map/all_gather | solution.py:1755
  86.2 213.2 %all-gather.8.cloned.1.call-start = ((), (), s32[]{:S(2)}) async-start(), calls=%async_computation.7 | async-start | bytes 5242880 | tf_op jit(solution)/shard_map/all_gather | solution.py:1755
  86.9 296.5 %reduce-scatter.6.cloned.1.call-start = ((), (), s32[]{:S(2)}) async-start(), calls=%async_computation.8 | async-start | bytes 2621440 | tf_op jit(solution)/shard_map/reduce_scatter | solution.py:1848
  95.0 10.0 %copy-start.3 = (bf16[1040,640]{1,0:T(8,128)(2,1)}, bf16[1040,640]{1,0:T(8,128)(2,1)S(1)}, u32[]{:S(2)}) copy-start(bf16[1040,640]{1,0:T(8,128)(2,1)S(1)} %get-tuple-element.337) | copy-start | bytes 3993604
  95.0 0.7 copy-start.25
  95.0 0.7 copy-start.26
  95.0 5.1 copy-start.22
  95.0 6.1 copy-start.21
  100.1 6.1 copy-start.18
  112.5 36.2 %copy-start.27 = (f32[24]{0:T(128)S(1)}, f32[24]{0:T(128)}, u32[]{:S(2)}) copy-start(f32[24]{0:T(128)} %param.33) | copy-start | bytes 292
  112.5 36.8 %copy-start.9 = (f32[1024,6]{1,0:T(8,128)S(1)}, f32[1024,6]{1,0:T(8,128)}, u32[]{:S(2)}) copy-start(f32[1024,6]{1,0:T(8,128)} %slice.301) | copy-start | bytes 73732
  209.3 10.3 %copy-start.13 = (f32[1024,384]{1,0:T(8,128)S(1)}, f32[1024,384]{1,0:T(8,128)}, u32[]{:S(2)}) copy-start(f32[1024,384]{1,0:T(8,128)} %get-tuple-element.129) | copy-start | bytes 4718596
  209.3 10.3 %copy-start.15 = (f32[1040,512]{1,0:T(8,128)S(1)}, f32[1040,512]{1,0:T(8,128)}, u32[]{:S(2)}) copy-start(f32[1040,512]{1,0:T(8,128)} %fusion.79.raw_ref) | copy-start | bytes 6389764
  223.1 0.9 copy-start.17
  313.5 137.7 %reduce-scatter.8.cloned.1.call-start = ((), (), s32[]{:S(2)}) async-start(), calls=%async_computation.9 | async-start | bytes 5242880 | tf_op jit(solution)/shard_map/reduce_scatter | solution.py:1848
  320.8 2.9 copy-start.24
  330.2 217.4 %reduce-scatter.14.cloned.1.call-start = ((), (), s32[]{:S(2)}) async-start(), calls=%async_computation.12 | async-start | bytes 2621440 | tf_op jit(solution)/shard_map/reduce_scatter | solution.py:1848
  389.6 225.4 %reduce-scatter.12.cloned.1.call-start = ((), (), s32[]{:S(2)}) async-start(), calls=%async_computation.11 | async-start | bytes 2621440 | tf_op jit(solution)/shard_map/reduce_scatter | solution.py:1848
  390.8 6.2 copy-start.12
  390.8 6.2 copy-start.16
  397.0 2.8 copy-start.14
  397.0 2.8 copy-start.19
  398.7 1.1 copy-start.2
  401.0 25.3 %collective-permute-start.1 = (bf16[384,256]{1,0:T(8,128)(2,1)}, bf16[384,256]{1,0:T(8,128)(2,1)}, u32[]{:S(2)}, u32[]{:S(2)}) collective-permute-start(bf16[384,256]{1,0:T(8,128)(2,1)} %fusion.30), channel_id=1, source_target_pairs={{16,0},{24,8},{17,1},{25,9},{18,2},{26,10},{19,3},{27,11},{20,4},{... | collective-permute-start | bytes 589832 | tf_op jit(solution)/shard_map/ppermute | solution.py:1697
  402.3 24.2 %collective-permute-start = (bf16[384,256]{1,0:T(8,128)(2,1)}, bf16[384,256]{1,0:T(8,128)(2,1)}, u32[]{:S(2)}, u32[]{:S(2)}) collective-permute-start(bf16[384,256]{1,0:T(8,128)(2,1)} %fusion.30), channel_id=1, source_target_pairs={{8,0},{16,8},{24,16},{9,1},{17,9},{25,17},{10,2},{18,10},{26,18},{... | collective-permute-start | bytes 589832 | tf_op jit(solution)/shard_map/ppermute | solution.py:1697
  403.6 29.8 %collective-permute-start.2 = (bf16[384,256]{1,0:T(8,128)(2,1)}, bf16[384,256]{1,0:T(8,128)(2,1)}, u32[]{:S(2)}, u32[]{:S(2)}) collective-permute-start(bf16[384,256]{1,0:T(8,128)(2,1)} %fusion.30), channel_id=1, source_target_pairs={{24,0},{25,1},{26,2},{27,3},{28,4},{29,5},{30,6},{31,7}} | collective-permute-start | bytes 589832 | tf_op jit(solution)/shard_map/ppermute | solution.py:1697
  420.8 14.6 %copy-start.5 = (bf16[1024,512]{1,0:T(8,128)(2,1)}, bf16[1024,512]{1,0:T(8,128)(2,1)S(1)}, u32[]{:S(2)}) copy-start(bf16[1024,512]{1,0:T(8,128)(2,1)S(1)} %pad_maximum_fusion.4.left_b) | copy-start | bytes 3145732
  441.8 173.2 %reduce-scatter.10.cloned.1.call-start = ((), (), s32[]{:S(2)}) async-start(), calls=%async_computation.10 | async-start | bytes 3276800 | tf_op jit(solution)/shard_map/reduce_scatter | solution.py:1848
  444.8 32.0 %collective-permute-start.5 = (bf16[4,512,128]{2,1,0:T(8,128)(2,1)}, bf16[4,512,128]{2,1,0:T(8,128)(2,1)}, u32[]{:S(2)}, u32[]{:S(2)}) collective-permute-start(bf16[4,512,128]{2,1,0:T(8,128)(2,1)} %get-tuple-element.305), channel_id=1, source_target_pairs={{0,6},{2,4},{4,2},{6,0},{1,7},{3,5},{5,3},{7,1},{8,14},{10,12},{12... | collective-permute-start | bytes 1572872 | tf_op jit(solution)/shard_map/ppermute | solution.py:1881
  446.2 30.6 %collective-permute-start.4 = (bf16[4,512,128]{2,1,0:T(8,128)(2,1)}, bf16[4,512,128]{2,1,0:T(8,128)(2,1)}, u32[]{:S(2)}, u32[]{:S(2)}) collective-permute-start(bf16[4,512,128]{2,1,0:T(8,128)(2,1)} %get-tuple-element.306), channel_id=1, source_target_pairs={{0,4},{2,6},{4,0},{6,2},{1,5},{3,7},{5,1},{7,3},{8,12},{10,14},{12... | collective-permute-start | bytes 1572872 | tf_op jit(solution)/shard_map/ppermute | solution.py:1881
  446.7 30.1 %collective-permute-start.3 = (bf16[4,512,128]{2,1,0:T(8,128)(2,1)}, bf16[4,512,128]{2,1,0:T(8,128)(2,1)}, u32[]{:S(2)}, u32[]{:S(2)}) collective-permute-start(bf16[4,512,128]{2,1,0:T(8,128)(2,1)} %get-tuple-element.307), channel_id=1, source_target_pairs={{0,2},{2,0},{4,6},{6,4},{1,3},{3,1},{5,7},{7,5},{8,10},{10,8},{12,... | collective-permute-start | bytes 1572872 | tf_op jit(solution)/shard_map/ppermute | solution.py:1881
  451.2 25.5 %copy-start.10 = (bf16[4,512,128]{2,1,0:T(8,128)(2,1)S(1)}, bf16[4,512,128]{2,1,0:T(8,128)(2,1)}, u32[]{:S(2)}) copy-start(bf16[4,512,128]{2,1,0:T(8,128)(2,1)} %get-tuple-element.163) | copy-start | bytes 1572868
  521.0 5.9 copy-start.4
  521.0 5.9 copy-start.11
  530.7 2.8 copy-start.6
  530.7 2.8 copy-start.7
  530.7 2.8 copy-start.8
  543.7 1.4 copy-start.23
  545.4 2.2 copy-start.20
  632.1 9.6 %copy-start.1 = (f32[256,2048]{1,0:T(8,128)S(1)}, f32[256,2048]{1,0:T(8,128)}, u32[]{:S(2)}) copy-start(f32[256,2048]{1,0:T(8,128)} %param.22) | copy-start | bytes 6291460
Sparse Core Ops, SparseCore 0:
  85.5 51.1 all-gather.3
  138.3 57.9 all-gather.5
  197.9 96.0 all-gather.7
  313.6 42.3 reduce-scatter.5
  358.2 88.7 reduce-scatter.7
  449.1 47.1 reduce-scatter.13
  498.7 43.8 reduce-scatter.11
  544.9 52.9 reduce-scatter.9
